TPU v7x, 32 devices: a whole 2x2x4 slice. The times are simulated.
32 devices in a mesh: wide: 8 (over y, x, core), narrow: 4 (over z).
Axes of the slice: x: 2, y: 2, z: 4, core: 2. Of those that a mesh axis runs over, the one named last changes fastest.
Arguments:
- inputs: bfloat16 [896, 16384], P('wide', 'narrow'), may hold values from -6 to 6
- grad_out: bfloat16 [896, 53248], P('narrow', 'wide'), may hold values from -6 to 6
- w_base: bfloat16 [16384, 53248], P('narrow', 'wide'), may hold values from -0.046875 to 0.046875
- adapter_down_matrix: bfloat16 [16384, 256], P('narrow'), may hold values from -0.046875 to 0.046875
- b_factor: bfloat16 [256, 53248], P(None, 'wide'), may hold values from -0.375 to 0.375
Outputs:
- input_gradient: bfloat16 [896, 16384], P('wide', 'narrow')
- grad_a: float32 [16384, 256], P('narrow')
- grad_b: float32 [256, 53248], P(None, 'wide')
All inputs are finite; a program needn't handle non-finite values.
Results may differ from a plain program's by a relative error of at most 0.0046.
Values may be sent and summed in bfloat16 or wider, within the bound.
No kernel may reach another device: no remote copies, remote signals or barrier semaphores. Data moves between devices by JAX's collectives and lax.ppermute only.
A program may use at most 192 MiB of HBM per device.

v0:
```python
import jax
import jax.numpy as jnp
from jax import lax
from jax.sharding import PartitionSpec as P

adapter_scale = 2.0


def contract_trailing_axis(left, right):
    return lax.dot_general(
        left, right, (((1,), (1,)), ((), ())), preferred_element_type=jnp.float32
    )


def contract_first(left, right):
    return lax.dot_general(
        left, right, (((0,), (0,)), ((), ())), preferred_element_type=jnp.float32
    )


def shards(inputs, grad_out, w_base, adapter_down_matrix, b_factor):
    width_in = w_base.shape[0]
    owner_rows = inputs.shape[0]
    token_total_count = owner_rows * lax.axis_size("wide")
    adapter_matrix = adapter_scale / token_total_count
    every_row = lax.all_gather(grad_out, "narrow", axis=0, tiled=True)
    base_part = contract_trailing_axis(every_row, w_base)
    low_part = contract_trailing_axis(every_row, b_factor)
    stacked = jnp.concatenate([base_part, low_part], axis=1)
    summed = lax.psum_scatter(stacked, "wide", scatter_dimension=0, tiled=True)
    frozen_weight_rows = summed[:, :width_in]
    low_rank_gradient = summed[:, width_in:].astype(jnp.bfloat16)
    input_gradient = (
        frozen_weight_rows
        + adapter_scale * contract_trailing_axis(low_rank_gradient, adapter_down_matrix)
    ).astype(jnp.bfloat16)
    grad_a = lax.psum(adapter_matrix * contract_first(inputs, low_rank_gradient), "wide")
    low_part = jnp.dot(inputs, adapter_down_matrix, preferred_element_type=jnp.float32)
    low_act = lax.psum(low_part, "narrow").astype(jnp.bfloat16)
    low_all = lax.all_gather(low_act, "wide", axis=0, tiled=True)
    grad_b = adapter_matrix * contract_first(low_all, every_row)
    return (input_gradient, grad_a, grad_b)


def solution(mesh):
    return jax.shard_map(
        shards,
        mesh=mesh,
        in_specs=(
            P("wide", "narrow"),
            P("narrow", "wide"),
            P("narrow", "wide"),
            P("narrow", None),
            P(None, "wide"),
        ),
        out_specs=(P("wide", "narrow"), P("narrow", None), P(None, "wide")),
        check_vma=False,
    )
```

profile of v0, /device:TPU:0, one launch (start us, length us, event | category | flops | bytes accessed | tf_op | source)
XLA Modules:
  0.0 500.3 jit_solution(8415087510198090936)
XLA Ops:
  7.2 0.0 copy-start
  7.2 0.0 all-gather.2.cloned.1.call-start
  7.2 0.7 all-gather.2.cloned.1.call-update
  7.9 0.0 reduce-scatter.2.cloned.1.call-start
  8.0 211.8 %all-gather.2.cloned.1.call-done = bf16[896,6656]{1,0:T(8,128)(2,1)} async-done(((bf16[224,6656]{1,0:T(8,128)(2,1)}), bf16[896,6656]{1,0:T(8,128)(2,1)}) %all-gather.2.cloned.1.call-update) | async-done | bytes 11927568 | tf_op jit(solution)/shard_map/all_gather | solution.py:26
  219.8 0.0 copy-done
  219.8 6.2 %fusion.4 = f32[896,256]{1,0:T(8,128)S(1)} fusion(bf16[896,6656]{1,0:T(8,128)(2,1)} %all-gather.2.cloned.1.call-done, bf16[256,6656]{1,0:T(8,128)(2,1)S(1)} %copy-done), kind=kOutput, calls=%fused_computation.9 | convolution fusion | flops 3053453312 | bytes 16252928 | tf_op jit(solution)/shard_map/dot_general | solution.py:10
  226.0 58.4 %fusion.3 = f32[896,4096]{1,0:T(8,128)} fusion(bf16[896,6656]{1,0:T(8,128)(2,1)} %all-gather.2.cloned.1.call-done, bf16[4096,6656]{1,0:T(8,128)(2,1)} %param.7), kind=kOutput, calls=%fused_computation.8 | convolution fusion | flops 48855252992 | bytes 81133568 | tf_op jit(solution)/shard_map/dot_general | solution.py:10
  284.4 10.6 %pad_maximum_fusion = f32[896,4352]{1,0:T(8,128)} fusion(f32[896,256]{1,0:T(8,128)S(1)} %fusion.4, f32[896,4096]{1,0:T(8,128)} %fusion.3), kind=kLoop, calls=%fused_computation | loop fusion | flops 3899392 | bytes 31195136 | tf_op jit(solution)/shard_map/concatenate | solution.py:29
  294.9 0.0 copy-start.4
  294.9 0.0 reduce-scatter.2.cloned.1.call-update
  295.0 0.0 copy-start.2
  295.0 0.0 all-reduce.2.cloned.1.call-start
  295.0 106.8 %reduce-scatter.2.cloned.1.call-done = f32[112,4352]{1,0:T(8,128)} async-done(((f32[896,4352]{1,0:T(8,128)}), f32[112,4352]{1,0:T(8,128)}) %reduce-scatter.2.cloned.1.call-update) | async-done | bytes 1949712 | tf_op jit(solution)/shard_map/reduce_scatter | solution.py:30
  401.8 0.0 copy-done.4
  401.8 3.6 fusion
  405.4 0.0 all-reduce.2.cloned.1.call-update
  405.4 0.0 copy-done.2
  405.5 0.4 fusion.5
  405.9 20.7 %psum.15 = bf16[112,256]{1,0:T(8,128)(2,1)S(1)} all-reduce(f32[112,256]{1,0:T(8,128)S(1)} %fusion.5), channel_id=1, replica_groups=mesh['wide'=8,'narrow'=4] {'narrow'}, use_global_device_ids=true, to_apply=%region_2.0 | all-reduce | flops 28672 | bytes 172032 | tf_op jit(solution)/shard_map/psum | solution.py:39
  426.6 9.5 %all_gather.7 = bf16[896,256]{1,0:T(8,128)(2,1)S(1)} all-gather(bf16[112,256]{1,0:T(8,128)(2,1)S(1)} %psum.15), channel_id=1, replica_groups=mesh['wide'=8,'narrow'=4] {'wide'}, dimensions={0}, use_global_device_ids=true | all-gather | bytes 516096 | tf_op jit(solution)/shard_map/all_gather | solution.py:40
  436.1 0.0 copy-start.3
  436.1 10.6 %convolution_multiply_fusion = f32[256,6656]{1,0:T(8,128)} fusion(bf16[896,256]{1,0:T(8,128)(2,1)S(1)} %all_gather.7, bf16[896,6656]{1,0:T(8,128)(2,1)} %all-gather.2.cloned.1.call-done), kind=kOutput, calls=%fused_computation.1 | convolution fusion | flops 3055157248 | bytes 19202048 | tf_op jit(solution)/shard_map/dot_general | solution.py:16
  446.7 0.0 copy-done.3
  446.7 0.0 copy-start.1
  446.8 3.5 fusion.2
  450.2 38.0 %all-reduce.2.cloned.1.call-done = f32[4096,256]{0,1:T(8,128)} async-done(((f32[4096,256]{0,1:T(8,128)}), f32[4096,256]{0,1:T(8,128)}) %all-reduce.2.cloned.1.call-update) | async-done | bytes 4194320 | tf_op jit(solution)/shard_map/psum | solution.py:37
  488.2 5.6 %copy.9 = f32[4096,256]{1,0:T(8,128)} copy(f32[4096,256]{0,1:T(8,128)} %all-reduce.2.cloned.1.call-done) | data formatting | bytes 8388608
  493.8 0.0 copy-done.1
Async XLA Ops:
  7.2 212.6 %copy-start = (bf16[256,6656]{1,0:T(8,128)(2,1)S(1)}, bf16[256,6656]{1,0:T(8,128)(2,1)}, u32[]{:S(2)}) copy-start(bf16[256,6656]{1,0:T(8,128)(2,1)} %param.9) | copy-start | bytes 10223620
  7.2 212.6 %all-gather.2.cloned.1.call-start = ((), (), s32[]{:S(2)}) async-start(), calls=%async_computation.1 | async-start | bytes 14909440 | tf_op jit(solution)/shard_map/all_gather | solution.py:26
  7.9 393.9 %reduce-scatter.2.cloned.1.call-start = ((), (), s32[]{:S(2)}) async-start(), calls=%async_computation.2 | async-start | bytes 17547264 | tf_op jit(solution)/shard_map/reduce_scatter | solution.py:30
  294.9 106.9 %copy-start.4 = (bf16[112,4096]{1,0:T(8,128)(2,1)S(1)}, bf16[112,4096]{1,0:T(8,128)(2,1)}, u32[]{:S(2)}) copy-start(bf16[112,4096]{1,0:T(8,128)(2,1)} %param.5) | copy-start | bytes 2752516
  295.0 110.5 %copy-start.2 = (bf16[4096,256]{1,0:T(8,128)(2,1)S(1)}, bf16[4096,256]{1,0:T(8,128)(2,1)}, u32[]{:S(2)}) copy-start(bf16[4096,256]{1,0:T(8,128)(2,1)} %param.8) | copy-start | bytes 6291460
  295.0 193.2 %all-reduce.2.cloned.1.call-start = ((), (), s32[]{:S(2)}) async-start(), calls=%async_computation.3 | async-start | bytes 8388608 | tf_op jit(solution)/shard_map/psum | solution.py:37
  436.1 10.6 %copy-start.3 = (bf16[4096,256]{1,0:T(8,128)(2,1)S(1)}, bf16[4096,256]{1,0:T(8,128)(2,1)}, u32[]{:S(2)}) copy-start(bf16[4096,256]{1,0:T(8,128)(2,1)} %param.8) | copy-start | bytes 6291460
  446.7 47.1 %copy-start.1 = (bf16[256,6656]{1,0:T(8,128)(2,1)S(1)}, bf16[256,6656]{1,0:T(8,128)(2,1)}, u32[]{:S(2)}) copy-start(bf16[256,6656]{1,0:T(8,128)(2,1)} %param.9) | copy-start | bytes 10223620
Sparse Core Ops, SparseCore 0:
  9.6 210.1 all-gather.1
  295.1 106.6 reduce-scatter.1
  406.0 82.1 all-reduce.1
where the time goes:
time: 501 us; the launch traced here: 500 us
  waiting for transfers between devices  357 us (71%)
  matrix products  82.7 us (17%)
  blocking collectives  30.2 us (6%)
  between operations  13.8 us (3%)
  other arithmetic  10.6 us (2%)
  local copies, waits for them, and re-layouts  5.62 us (1%)
    all_gather x1, waiting for transfers between devices, shards(): every_row = lax.all_gather(grad_out, 'narrow', axis=0, tiled=True)  212 us
    reduce_scatter x1, waiting for transfers between devices, shards(): summed = lax.psum_scatter(stacked, 'wide', scatter_dimension=0, tiled=True)  107 us
    dot_general x3, matrix products, contract_trailing_axis(): lax.dot_general(left, right, (((1,), (1,)), ((), ())), preferred_element_...  68 us
    psum x1, waiting for transfers between devices, shards(): lax.psum(adapter_matrix * contract_first(inputs, low_rank_gradient), 'wide')  38 us
    psum x1, blocking collectives, shards(): low_act = lax.psum(low_part, 'narrow').astype(jnp.bfloat16)  20.7 us
    dot_general x2, matrix products, contract_first(): lax.dot_general(left, right, (((0,), (0,)), ((), ())), preferred_element_...  14.3 us
    concatenate x1, other arithmetic, shards(): stacked = jnp.concatenate([base_part, low_part], axis=1)  10.6 us
  transfers between devices with their start and end apart: 3, of which 3 were waited for; matrix products, arithmetic and copies ran while one was open for 3% of the time, Pallas kernels for 0%

commit v1 on v0

v1 whole, which is shorter than its diff:
```python
import jax
import jax.numpy as jnp
from jax import lax
from jax.sharding import PartitionSpec as P

adapter_scale = 2.0
piece_rows = 32


def contract_trailing_axis(left, right):
    return lax.dot_general(
        left, right, (((1,), (1,)), ((), ())), preferred_element_type=jnp.float32
    )


def contract_first(left, right):
    return lax.dot_general(
        left, right, (((0,), (0,)), ((), ())), preferred_element_type=jnp.float32
    )


def swap(value, axis, bit):
    size = lax.axis_size(axis)
    return lax.ppermute(value, axis, [(i, i ^ bit) for i in range(size)])


def shift(value, axis, by):
    size = lax.axis_size(axis)
    return lax.ppermute(value, axis, [(i, (i + by) % size) for i in range(size)])


def sum_over(value, axis):
    bit = 1
    while bit < lax.axis_size(axis):
        value = value + swap(value, axis, bit)
        bit *= 2
    return value


def gather_over(value, axis):
    me = lax.axis_index(axis)
    bit = 1
    while bit < lax.axis_size(axis):
        other = swap(value, axis, bit)
        upper = (me & bit) != 0
        first = jnp.where(upper, other, value)
        second = jnp.where(upper, value, other)
        value = jnp.concatenate([first, second], axis=0)
        bit *= 2
    return value


def ring_gather(block, axis):
    size = lax.axis_size(axis)
    found = {0: block}
    up = down = block
    for step in range(1, (size - 1) // 2 + 1):
        up = shift(up, axis, 1)
        down = shift(down, axis, -1)
        found[size - step] = up
        found[step] = down
    if size % 2 == 0 and size > 1:
        half = block.shape[1] // 2
        left = shift(up[:, :half], axis, 1)
        right = shift(down[:, half:], axis, -1)
        found[size // 2] = jnp.concatenate([left, right], axis=1)
    return [found[k] for k in range(size)]


def scatter_sum(parts, axis):
    size = lax.axis_size(axis)
    bits = []
    bit = 1
    while bit < size:
        bits.append(bit)
        bit *= 2
    sent = jnp.stack([parts[p].astype(jnp.bfloat16) for p in range(size) if p & 1])
    got = swap(sent, axis, 1)
    kept = [parts[p] + got[i] for i, p in enumerate(range(0, size, 2))]
    half = kept[0].shape[1] // 2
    done = []
    for side, order in ((0, bits[1:]), (1, bits[1:][::-1])):
        live = {
            p: kept[p // 2][:, side * half : (side + 1) * half] for p in range(0, size, 2)
        }
        for bit in order:
            stay = [p for p in live if not p & bit]
            sent = jnp.stack([live[p ^ bit].astype(jnp.bfloat16) for p in stay])
            got = swap(sent, axis, bit)
            live = {p: live[p] + got[i] for i, p in enumerate(stay)}
        done.append(live[0])
    return jnp.concatenate(done, axis=1)


def shards(inputs, grad_out, w_base, adapter_down_matrix, b_factor):
    width_in = w_base.shape[0]
    owner_rows = inputs.shape[0]
    wide_count = lax.axis_size("wide")
    narrow_count = lax.axis_size("narrow")
    me_wide = lax.axis_index("wide")
    me_narrow = lax.axis_index("narrow")
    token_total_count = owner_rows * wide_count
    adapter_matrix = adapter_scale / token_total_count
    share = grad_out.shape[0] // owner_rows

    starts = list(range(0, owner_rows, piece_rows))
    rows_of = [min(piece_rows, owner_rows - s) for s in starts]
    own = grad_out.reshape(share, owner_rows, grad_out.shape[1])
    gathered = []
    for s, r in zip(starts, rows_of):
        block = own[:, s : s + r].reshape(share * r, -1)
        if len(gathered) > 1:
            block, *earlier = lax.optimization_barrier([block] + gathered[-2])
            gathered[-2] = earlier
        gathered.append(ring_gather(block, "narrow"))

    low_rank_gradient = sum_over(contract_trailing_axis(grad_out, b_factor), "wide").astype(jnp.bfloat16)
    low_rank_all = gather_over(low_rank_gradient, "narrow")
    low_rank_own = lax.dynamic_slice_in_dim(low_rank_all, me_wide * owner_rows, owner_rows)
    low_term = adapter_scale * contract_trailing_axis(low_rank_own, adapter_down_matrix)

    low_act = sum_over(
        jnp.dot(inputs, adapter_down_matrix, preferred_element_type=jnp.float32), "narrow"
    ).astype(jnp.bfloat16)
    low_act_all = gather_over(low_act, "wide")
    low_act_ring = jnp.roll(
        low_act_all.reshape(narrow_count, share, owner_rows, -1), -me_narrow, axis=0
    )

    columns = lax.all_to_all(inputs, "wide", split_axis=1, concat_axis=0, tiled=True)
    grad_a = lax.all_gather(
        adapter_matrix * contract_first(columns, low_rank_all), "wide", axis=0, tiled=True
    )

    grad_b = None
    results = []
    for s, r, blocks in zip(starts, rows_of, gathered):
        tokens = jnp.concatenate(blocks, axis=0)
        part = contract_trailing_axis(tokens, w_base).reshape(narrow_count, share, r, width_in)
        parts = []
        for p in range(wide_count):
            owner = me_wide ^ p
            distance = (owner // share - me_narrow) % narrow_count
            picked = lax.dynamic_slice(
                part, (distance, owner % share, 0, 0), (1, 1, r, width_in)
            )
            parts.append(picked.reshape(r, width_in))
        summed = scatter_sum(parts, "wide")
        results.append((summed + low_term[s : s + r]).astype(jnp.bfloat16))
        acts = low_act_ring[:, :, s : s + r].reshape(narrow_count * share * r, -1)
        term = contract_first(acts, tokens)
        grad_b = term if grad_b is None else grad_b + term
    input_gradient = jnp.concatenate(results, axis=0)
    return (input_gradient, grad_a, adapter_matrix * grad_b)


def solution(mesh):
    return jax.shard_map(
        shards,
        mesh=mesh,
        in_specs=(
            P("wide", "narrow"),
            P("narrow", "wide"),
            P("narrow", "wide"),
            P("narrow", None),
            P(None, "wide"),
        ),
        out_specs=(P("wide", "narrow"), P("narrow", None), P(None, "wide")),
        check_vma=False,
    )
```

time: 501 us -> 406 us (0.81)
  waiting for transfers between devices: 357 us -> 134 us
  starting transfers between devices: 0.12 us -> 65.4 us
  matrix products: 82.7 us -> 132 us
  local copies, waits for them, and re-layouts: 5.62 us -> 37.9 us
  blocking collectives: 30.2 us -> 0 us
  other arithmetic: 10.6 us -> 20.8 us
    all_gather x1, waiting for transfers between devices: 212 us -> 0.01 us  [shards(): lax.all_gather(adapter_matrix * contract_first(columns, low_rank_all), 'w...]
    ppermute x0 -> x46, waiting for transfers between devices: none -> 134 us  [the longest x30 90.7 us: swap(): return lax.ppermute(value, axis, [(i, i ^ bit) for i in range(size)])]
    reduce_scatter x1 -> x0, waiting for transfers between devices: 107 us -> none  [shards(): summed = lax.psum_scatter(stacked, 'wide', scatter_dimension=0, tiled=True)]
    ppermute x0 -> x46, starting transfers between devices: none -> 61.1 us  [the longest x16 31 us: shift(): lax.ppermute(value, axis, [(i, (i + by) % size) for i in range(size)])]
    psum x1 -> x0, waiting for transfers between devices: 38 us -> none  [shards(): lax.psum(adapter_matrix * contract_first(inputs, low_rank_gradient), 'wide')]
    dot_general x3 -> x6, matrix products: 68 us -> 101 us  [contract_trailing_axis(): lax.dot_general(left, right, (((1,), (1,)), ((), ())), preferred_element_...]
    psum x1 -> x0, blocking collectives: 20.7 us -> none  [shards(): low_act = lax.psum(low_part, 'narrow').astype(jnp.bfloat16)]
    slice x0 -> x13, local copies, waits for them, and re-layouts: none -> 16 us  [the longest x4 5.76 us: ring_gather(): left = shift(up[:, :half], axis, 1)]
  transfers between devices with their start and end apart: 3 -> 48, of which waited for: 3 -> 20; matrix products, arithmetic and copies ran while one was open for 3% -> 44% of each run, Pallas kernels for 0% -> 0%
where the time goes in v1:
time: 406 us; the launch traced here: 405 us
  waiting for transfers between devices  134 us (33%)
  matrix products  132 us (33%)
  starting transfers between devices  65.4 us (16%)
  local copies, waits for them, and re-layouts  37.9 us (9%)
  other arithmetic  20.8 us (5%)
  between operations  14.8 us (4%)
    dot_general x6, matrix products, contract_trailing_axis(): lax.dot_general(left, right, (((1,), (1,)), ((), ())), preferred_element_...  101 us
    ppermute x30, waiting for transfers between devices, swap(): return lax.ppermute(value, axis, [(i, i ^ bit) for i in range(size)])  90.7 us
    ppermute x16, waiting for transfers between devices, shift(): lax.ppermute(value, axis, [(i, (i + by) % size) for i in range(size)])  43.1 us
    ppermute x16, starting transfers between devices, shift(): lax.ppermute(value, axis, [(i, (i + by) % size) for i in range(size)])  31 us
    ppermute x30, starting transfers between devices, swap(): return lax.ppermute(value, axis, [(i, i ^ bit) for i in range(size)])  30 us
    dot_general x5, matrix products, contract_first(): lax.dot_general(left, right, (((0,), (0,)), ((), ())), preferred_element_...  28.4 us
    unnamed x59, local copies, waits for them, and re-layouts  13.1 us
  transfers between devices with their start and end apart: 48, of which 20 were waited for; matrix products, arithmetic and copies ran while one was open for 44% of the time, Pallas kernels for 0%

profile of v1, /device:TPU:0, one launch (start us, length us, event | category | flops | bytes accessed | tf_op | source)
XLA Modules:
  0.0 404.9 jit_solution(5931186932282053326)
XLA Ops:
  7.2 2.5 fusion.73
  9.7 3.1 collective-permute-start.41
  12.8 3.1 collective-permute-done.41
  15.9 2.8 collective-permute-start.42
  18.7 4.9 %collective-permute-done.42 = f32[112,256]{1,0:T(8,128)S(1)} collective-permute-done((f32[112,256]{1,0:T(8,128)S(1)}, f32[112,256]{1,0:T(8,128)S(1)}, u32[]{:S(2)}, u32[]{:S(2)}) %collective-permute-start.42) | collective-permute-done | bytes 114720 | tf_op jit(solution)/shard_map/ppermute | solution.py:24
  23.8 1.9 fusion.71
  32.8 3.0 fusion.68
  36.5 3.1 collective-permute-start.14
  40.7 4.2 %all-to-all-start = ((bf16[112,8,512]{2,0,1:T(8,128)(2,1)}), bf16[112,8,512]{2,0,1:T(8,128)(2,1)}, u32[]{:S(2)}, u32[]{:S(2)}) async-start(bf16[112,8,512]{2,0,1:T(8,128)(2,1)} %bitcast.336), calls=%async_computation | async-start | bytes 1835008 | tf_op jit(solution)/shard_map/all_to_all | solution.py:130
  46.8 3.8 collective-permute-start
  50.7 1.9 collective-permute-start.11
  52.8 10.1 %collective-permute-done.11 = f32[224,256]{1,0:T(8,128)S(1)} collective-permute-done((f32[224,256]{1,0:T(8,128)S(1)}, f32[224,256]{1,0:T(8,128)S(1)}, u32[]{:S(2)}, u32[]{:S(2)}) %collective-permute-start.11) | collective-permute-done | bytes 229408 | tf_op jit(solution)/shard_map/ppermute | solution.py:24
  63.9 49.6 %collective-permute-done.12 = bf16[224,256]{1,0:T(8,128)(2,1)S(1)} collective-permute-done((bf16[224,256]{1,0:T(8,128)(2,1)S(1)}, bf16[224,256]{1,0:T(8,128)(2,1)S(1)}, u32[]{:S(2)}, u32[]{:S(2)}) %collective-permute-start.12) | collective-permute-done | bytes 114720 | tf_op jit(solution)/shard_map/ppermute | solution.py:24
  113.5 2.1 collective-permute-start.13
  116.4 2.0 slice.375
  119.9 1.8 slice.376
  121.8 2.2 collective-permute-start.17
  127.6 3.8 collective-permute-start.3
  131.4 3.2 collective-permute-done.13
  134.7 2.4 fusion.2
  137.2 2.0 convolution_multiply_fusion
  139.2 13.1 %collective-permute-done.17 = bf16[64,3328]{1,0:T(8,128)(2,1)} collective-permute-done((bf16[64,3328]{1,0:T(8,128)(2,1)}, bf16[64,3328]{1,0:T(8,128)(2,1)}, u32[]{:S(2)}, u32[]{:S(2)}) %collective-permute-start.17) | collective-permute-done | bytes 426016 | tf_op jit(solution)/shard_map/ppermute | solution.py:29
  154.8 2.6 collective-permute-start.32
  157.4 13.2 %collective-permute-done.3 = bf16[64,3328]{1,0:T(8,128)(2,1)} collective-permute-done((bf16[64,3328]{1,0:T(8,128)(2,1)}, bf16[64,3328]{1,0:T(8,128)(2,1)}, u32[]{:S(2)}, u32[]{:S(2)}) %collective-permute-start.3) | collective-permute-done | bytes 426016 | tf_op jit(solution)/shard_map/ppermute | solution.py:29
  170.6 2.1 pad_maximum_fusion.6
  173.9 2.6 collective-permute-start.23
  181.2 4.0 fusion.74
  185.2 24.2 %fusion.72 = f32[256,4096]{1,0:T(8,128)} fusion(bf16[256,6656]{1,0:T(8,128)(2,1)S(1)} %constant_dynamic-update-slice_fusion.4, bf16[4096,6656]{1,0:T(8,128)(2,1)} %param.7), kind=kOutput, calls=%fused_computation.222 | convolution fusion | flops 13958643712 | bytes 62128128 | tf_op jit(solution)/shard_map/dot_general | solution.py:11
  214.8 24.3 %fusion.70 = f32[256,4096]{1,0:T(8,128)} fusion(bf16[256,6656]{1,0:T(8,128)(2,1)S(1)} %constant_dynamic-update-slice_fusion, bf16[4096,6656]{1,0:T(8,128)(2,1)} %param.7), kind=kOutput, calls=%fused_computation.220 | convolution fusion | flops 13958643712 | bytes 62128128 | tf_op jit(solution)/shard_map/dot_general | solution.py:11
  239.1 6.8 %convolution_add_fusion.1 = f32[256,6656]{1,0:T(8,128)} fusion(f32[256,6656]{1,0:T(8,128)} %fusion.74, bf16[256,256]{1,0:T(8,128)(2,1)} %bitcast.354, bf16[256,6656]{1,0:T(8,128)(2,1)S(1)} %constant_dynamic-update-slice_fusion), kind=kOutput, calls=%fused_computation.3 | convolution fusion | flops 874119168 | bytes 17170432 | tf_op jit(solution)/shard_map/dot_general | solution.py:17
  249.6 4.1 %collective-permute-start.35 = (bf16[32,3328]{1,0:T(8,128)(2,1)S(1)}, bf16[32,3328]{1,0:T(8,128)(2,1)}, u32[]{:S(2)}, u32[]{:S(2)}) collective-permute-start(bf16[32,3328]{1,0:T(8,128)(2,1)S(1)} %slice.414), channel_id=1, source_target_pairs={{0,3},{1,0},{2,1},{3,2},{4,7},{5,4},{6,5},{7,6},{8,11},{9,8},{10,9... | collective-permute-start | bytes 638984 | tf_op jit(solution)/shard_map/ppermute | solution.py:29
  253.8 4.7 %collective-permute-done.34 = bf16[32,3328]{1,0:T(8,128)(2,1)S(1)} collective-permute-done((bf16[32,3328]{1,0:T(8,128)(2,1)S(1)}, bf16[32,3328]{1,0:T(8,128)(2,1)S(1)}, u32[]{:S(2)}, u32[]{:S(2)}) %collective-permute-start.34) | collective-permute-done | bytes 213024 | tf_op jit(solution)/shard_map/ppermute | solution.py:29
  259.2 3.0 collective-permute-done.35
  262.2 23.5 %fusion.66 = f32[128,4096]{1,0:T(8,128)S(1)} fusion(bf16[4096,6656]{1,0:T(8,128)(2,1)} %param.7, bf16[32,6656]{1,0:T(8,128)(2,1)} %collective-permute-done.33, bf16[32,3328]{1,0:T(8,128)(2,1)} %collective-permute-done.35, bf16[32,3328]{1,0:T(8,128)(2,1)} %copy-done.25, bf16[32,6656]{1,0:T(8,128)(2,1)} %collective-permute-done.32, bf16[32,6656]{1,0:T(8,128)(2,1)} %bitcast.28), kind=kOutput, calls=%fused_computation.216 | convolution fusion | flops 6987841536 | bytes 58327040 | tf_op jit(solution)/shard_map/dot_general | solution.py:11
  286.0 5.9 %fusion.65 = f32[256,6656]{1,0:T(8,128)} fusion(bf16[128,256]{1,0:T(8,128)(2,1)S(1)} %bitcast.349, bf16[32,6656]{1,0:T(8,128)(2,1)} %collective-permute-done.33, bf16[32,3328]{1,0:T(8,128)(2,1)} %collective-permute-done.35, bf16[32,3328]{1,0:T(8,128)(2,1)} %copy-done.25, bf16[32,6656]{1,0:T(8,128)(2,1)} %collective-permute-done.32, ...), kind=kOutput, calls=%fused_computation.215 | convolution fusion | flops 444727296 | bytes 8585216 | tf_op jit(solution)/shard_map/dot_general | solution.py:17
  294.1 3.9 collective-permute-start.26
  305.3 2.2 collective-permute-done.25
  308.2 6.9 %collective-permute-done.26 = bf16[64,3328]{1,0:T(8,128)(2,1)S(1)} collective-permute-done((bf16[64,3328]{1,0:T(8,128)(2,1)S(1)}, bf16[64,3328]{1,0:T(8,128)(2,1)S(1)}, u32[]{:S(2)}, u32[]{:S(2)}) %collective-permute-start.26) | collective-permute-done | bytes 426016 | tf_op jit(solution)/shard_map/ppermute | solution.py:29
  315.8 2.2 collective-permute-start.37
  318.0 25.4 %fusion.67 = f32[256,4096]{1,0:T(8,128)} fusion(bf16[4096,6656]{1,0:T(8,128)(2,1)} %param.7, bf16[64,6656]{1,0:T(8,128)(2,1)} %collective-permute-done.24, bf16[64,3328]{1,0:T(8,128)(2,1)} %copy-done.23, bf16[64,3328]{1,0:T(8,128)(2,1)S(1)} %collective-permute-done.25, bf16[64,6656]{1,0:T(8,128)(2,1)} %collective-permute-done.23, bf16[64,6656]{1,0:T(8,128)(2,1)} %bitcast.1), kind=kOutput, calls=%fused_computation.217 | convolution fusion | flops 13975683072 | bytes 62128128 | tf_op jit(solution)/shard_map/dot_general | solution.py:11
  345.1 9.2 %fusion.1 = f32[256,6656]{1,0:T(8,128)} fusion(f32[256,6656]{1,0:T(8,128)} %fusion.65, f32[256,6656]{1,0:T(8,128)} %convolution_add_fusion.1, bf16[256,256]{1,0:T(8,128)(2,1)S(1)} %bitcast.353, bf16[64,6656]{1,0:T(8,128)(2,1)} %collective-permute-done.24, bf16[64,3328]{1,0:T(8,128)(2,1)S(1)} %copy-done.24, bf16[64,3328]{1,0:T(8,128)(2,1)S(1)} %collective-permute-done.25, ...), kind=kOutput, calls=%fused_computation.2 | convolution fusion | flops 894566400 | bytes 23986176 | tf_op jit(solution)/shard_map/dot_general | solution.py:17
  360.6 2.1 collective-permute-start.6
  363.7 2.4 collective-permute-done.6
  373.5 4.8 %collective-permute-done.21 = bf16[2,32,2048]{2,1,0:T(8,128)(2,1)S(1)} collective-permute-done((bf16[2,32,2048]{2,1,0:T(8,128)(2,1)S(1)}, bf16[2,32,2048]{2,1,0:T(8,128)(2,1)S(1)}, u32[]{:S(2)}, u32[]{:S(2)}) %collective-permute-start.21) | collective-permute-done | bytes 262176 | tf_op jit(solution)/shard_map/ppermute | solution.py:24
  380.5 2.9 collective-permute-done.30
  383.5 2.2 collective-permute-done.28
  388.9 2.0 collective-permute-done.29
  392.1 5.9 %copy.13 = f32[4096,256]{1,0:T(8,128)} copy(f32[4096,256]{0,1:T(8,128)} %all-gather.2.cloned.1.call-done) | data formatting | bytes 8388608
  (199 shorter events, 70.3 us)
Async XLA Ops:
  9.7 6.2 %collective-permute-start.41 = (f32[112,256]{1,0:T(8,128)S(1)}, f32[112,256]{1,0:T(8,128)S(1)}, u32[]{:S(2)}, u32[]{:S(2)}) collective-permute-start(f32[112,256]{1,0:T(8,128)S(1)} %fusion.73), channel_id=1, source_target_pairs={{0,1},{1,0},{2,3},{3,2},{4,5},{5,4},{6,7},{7,6},{8,9},{9,8},{10,11... | collective-permute-start | bytes 344072 | tf_op jit(solution)/shard_map/ppermute | solution.py:24
  15.9 7.7 %collective-permute-start.42 = (f32[112,256]{1,0:T(8,128)S(1)}, f32[112,256]{1,0:T(8,128)S(1)}, u32[]{:S(2)}, u32[]{:S(2)}) collective-permute-start(f32[112,256]{1,0:T(8,128)S(1)} %add.450), channel_id=1, source_target_pairs={{0,2},{1,3},{2,0},{3,1},{4,6},{5,7},{6,4},{7,5},{8,10},{9,11},{10,... | collective-permute-start | bytes 344072 | tf_op jit(solution)/shard_map/ppermute | solution.py:24
  23.7 2.4 collective-permute-start.43
  25.6 1.9 collective-permute-start.9
  26.2 5.1 %collective-permute-start.44 = (bf16[224,256]{1,0:T(8,128)(2,1)S(1)}, bf16[224,256]{1,0:T(8,128)(2,1)S(1)}, u32[]{:S(2)}, u32[]{:S(2)}) collective-permute-start(bf16[224,256]{1,0:T(8,128)(2,1)S(1)} %pad_maximum_fusion.22), channel_id=1, source_target_pairs={{0,8},{4,12},{8,0},{12,4},{16,24},{20,28},{24,16},{28,20},{1,9},{5... | collective-permute-start | bytes 344072 | tf_op jit(solution)/shard_map/ppermute | solution.py:24
  28.6 18.3 %collective-permute-start.10 = (f32[224,256]{1,0:T(8,128)S(1)}, f32[224,256]{1,0:T(8,128)S(1)}, u32[]{:S(2)}, u32[]{:S(2)}) collective-permute-start(f32[224,256]{1,0:T(8,128)S(1)} %add.412), channel_id=1, source_target_pairs={{0,8},{4,12},{8,0},{12,4},{16,24},{20,28},{24,16},{28,20},{1,9},{5... | collective-permute-start | bytes 688136 | tf_op jit(solution)/shard_map/ppermute | solution.py:24
  31.4 19.3 %collective-permute-start.45 = (bf16[448,256]{1,0:T(8,128)(2,1)S(1)}, bf16[448,256]{1,0:T(8,128)(2,1)S(1)}, u32[]{:S(2)}, u32[]{:S(2)}) collective-permute-start(bf16[448,256]{1,0:T(8,128)(2,1)S(1)} %pad_maximum_fusion.19), channel_id=1, source_target_pairs={{0,16},{4,20},{8,24},{12,28},{16,0},{20,4},{24,8},{28,12},{1,17},{... | collective-permute-start | bytes 688136 | tf_op jit(solution)/shard_map/ppermute | solution.py:24
  35.9 80.5 %collective-permute-start.15 = (bf16[64,6656]{1,0:T(8,128)(2,1)}, bf16[64,6656]{1,0:T(8,128)(2,1)}, u32[]{:S(2)}, u32[]{:S(2)}) collective-permute-start(bf16[64,6656]{1,0:T(8,128)(2,1)} %bitcast.29), channel_id=1, source_target_pairs={{0,1},{1,2},{2,3},{3,0},{4,5},{5,6},{6,7},{7,4},{8,9},{9,10},{10,1... | collective-permute-start | bytes 2555912 | tf_op jit(solution)/shard_map/ppermute | solution.py:29
  36.5 83.4 %collective-permute-start.14 = (bf16[64,6656]{1,0:T(8,128)(2,1)}, bf16[64,6656]{1,0:T(8,128)(2,1)}, u32[]{:S(2)}, u32[]{:S(2)}) collective-permute-start(bf16[64,6656]{1,0:T(8,128)(2,1)} %bitcast.29), channel_id=1, source_target_pairs={{0,3},{1,0},{2,1},{3,2},{4,7},{5,4},{6,5},{7,6},{8,11},{9,8},{10,9... | collective-permute-start | bytes 2555912 | tf_op jit(solution)/shard_map/ppermute | solution.py:29
  39.7 84.3 %collective-permute-start.1 = (bf16[64,6656]{1,0:T(8,128)(2,1)S(1)}, bf16[64,6656]{1,0:T(8,128)(2,1)}, u32[]{:S(2)}, u32[]{:S(2)}) collective-permute-start(bf16[64,6656]{1,0:T(8,128)(2,1)S(1)} %bitcast.338), channel_id=1, source_target_pairs={{0,1},{1,2},{2,3},{3,0},{4,5},{5,6},{6,7},{7,4},{8,9},{9,10},{10,1... | collective-permute-start | bytes 2555912 | tf_op jit(solution)/shard_map/ppermute | solution.py:29
  40.7 94.0 %all-to-all-start = ((bf16[112,8,512]{2,0,1:T(8,128)(2,1)}), bf16[112,8,512]{2,0,1:T(8,128)(2,1)}, u32[]{:S(2)}, u32[]{:S(2)}) async-start(bf16[112,8,512]{2,0,1:T(8,128)(2,1)} %bitcast.336), calls=%async_computation | async-start | bytes 1835008 | tf_op jit(solution)/shard_map/all_to_all | solution.py:130
  44.9 347.2 %all-gather.2.cloned.1.call-start = ((), (), s32[]{:S(2)}) async-start(), calls=%async_computation.1 | async-start | bytes 4718592 | tf_op jit(solution)/shard_map/all_gather | solution.py:131
  46.8 79.0 %collective-permute-start = (bf16[64,6656]{1,0:T(8,128)(2,1)S(1)}, bf16[64,6656]{1,0:T(8,128)(2,1)S(1)}, u32[]{:S(2)}, u32[]{:S(2)}) collective-permute-start(bf16[64,6656]{1,0:T(8,128)(2,1)S(1)} %bitcast.339), channel_id=1, source_target_pairs={{0,3},{1,0},{2,1},{3,2},{4,7},{5,4},{6,5},{7,6},{8,11},{9,8},{10,9... | collective-permute-start | bytes 2555912 | tf_op jit(solution)/shard_map/ppermute | solution.py:29
  50.7 12.1 %collective-permute-start.11 = (f32[224,256]{1,0:T(8,128)S(1)}, f32[224,256]{1,0:T(8,128)S(1)}, u32[]{:S(2)}, u32[]{:S(2)}) collective-permute-start(f32[224,256]{1,0:T(8,128)S(1)} %add.413), channel_id=1, source_target_pairs={{0,16},{4,20},{8,24},{12,28},{16,0},{20,4},{24,8},{28,12},{1,17},{... | collective-permute-start | bytes 688136 | tf_op jit(solution)/shard_map/ppermute | solution.py:24
  62.8 50.6 %collective-permute-start.12 = (bf16[224,256]{1,0:T(8,128)(2,1)S(1)}, bf16[224,256]{1,0:T(8,128)(2,1)S(1)}, u32[]{:S(2)}, u32[]{:S(2)}) collective-permute-start(bf16[224,256]{1,0:T(8,128)(2,1)S(1)} %add_convert_fusion), channel_id=1, source_target_pairs={{0,1},{1,0},{2,3},{3,2},{4,5},{5,4},{6,7},{7,6},{8,9},{9,8},{10,11... | collective-permute-start | bytes 344072 | tf_op jit(solution)/shard_map/ppermute | solution.py:24
  113.5 21.1 %collective-permute-start.13 = (bf16[448,256]{1,0:T(8,128)(2,1)S(1)}, bf16[448,256]{1,0:T(8,128)(2,1)S(1)}, u32[]{:S(2)}, u32[]{:S(2)}) collective-permute-start(bf16[448,256]{1,0:T(8,128)(2,1)S(1)} %pad_maximum_fusion.18), channel_id=1, source_target_pairs={{0,2},{1,3},{2,0},{3,1},{4,6},{5,7},{6,4},{7,5},{8,10},{9,11},{10,... | collective-permute-start | bytes 688136 | tf_op jit(solution)/shard_map/ppermute | solution.py:24
  118.3 20.9 %collective-permute-start.16 = (bf16[64,3328]{1,0:T(8,128)(2,1)}, bf16[64,3328]{1,0:T(8,128)(2,1)}, u32[]{:S(2)}, u32[]{:S(2)}) collective-permute-start(bf16[64,3328]{1,0:T(8,128)(2,1)} %slice.375), channel_id=1, source_target_pairs={{0,1},{1,2},{2,3},{3,0},{4,5},{5,6},{6,7},{7,4},{8,9},{9,10},{10,1... | collective-permute-start | bytes 1277960 | tf_op jit(solution)/shard_map/ppermute | solution.py:29
  121.8 30.6 %collective-permute-start.17 = (bf16[64,3328]{1,0:T(8,128)(2,1)}, bf16[64,3328]{1,0:T(8,128)(2,1)}, u32[]{:S(2)}, u32[]{:S(2)}) collective-permute-start(bf16[64,3328]{1,0:T(8,128)(2,1)} %slice.376), channel_id=1, source_target_pairs={{0,3},{1,0},{2,1},{3,2},{4,7},{5,4},{6,5},{7,6},{8,11},{9,8},{10,9... | collective-permute-start | bytes 1277960 | tf_op jit(solution)/shard_map/ppermute | solution.py:29
  125.8 31.6 %collective-permute-start.2 = (bf16[64,3328]{1,0:T(8,128)(2,1)}, bf16[64,3328]{1,0:T(8,128)(2,1)}, u32[]{:S(2)}, u32[]{:S(2)}) collective-permute-start(bf16[64,3328]{1,0:T(8,128)(2,1)} %slice.354), channel_id=1, source_target_pairs={{0,1},{1,2},{2,3},{3,0},{4,5},{5,6},{6,7},{7,4},{8,9},{9,10},{10,1... | collective-permute-start | bytes 1277960 | tf_op jit(solution)/shard_map/ppermute | solution.py:29
  127.6 43.0 %collective-permute-start.3 = (bf16[64,3328]{1,0:T(8,128)(2,1)}, bf16[64,3328]{1,0:T(8,128)(2,1)}, u32[]{:S(2)}, u32[]{:S(2)}) collective-permute-start(bf16[64,3328]{1,0:T(8,128)(2,1)} %slice.355), channel_id=1, source_target_pairs={{0,3},{1,0},{2,1},{3,2},{4,7},{5,4},{6,5},{7,6},{8,11},{9,8},{10,9... | collective-permute-start | bytes 1277960 | tf_op jit(solution)/shard_map/ppermute | solution.py:29
  153.5 94.1 %collective-permute-start.33 = (bf16[32,6656]{1,0:T(8,128)(2,1)}, bf16[32,6656]{1,0:T(8,128)(2,1)}, u32[]{:S(2)}, u32[]{:S(2)}) collective-permute-start(bf16[32,6656]{1,0:T(8,128)(2,1)} %bitcast.28), channel_id=1, source_target_pairs={{0,1},{1,2},{2,3},{3,0},{4,5},{5,6},{6,7},{7,4},{8,9},{9,10},{10,1... | collective-permute-start | bytes 1277960 | tf_op jit(solution)/shard_map/ppermute | solution.py:29
  154.8 93.9 %collective-permute-start.32 = (bf16[32,6656]{1,0:T(8,128)(2,1)}, bf16[32,6656]{1,0:T(8,128)(2,1)}, u32[]{:S(2)}, u32[]{:S(2)}) collective-permute-start(bf16[32,6656]{1,0:T(8,128)(2,1)} %bitcast.28), channel_id=1, source_target_pairs={{0,3},{1,0},{2,1},{3,2},{4,7},{5,4},{6,5},{7,6},{8,11},{9,8},{10,9... | collective-permute-start | bytes 1277960 | tf_op jit(solution)/shard_map/ppermute | solution.py:29
  172.7 119.2 %collective-permute-start.24 = (bf16[64,6656]{1,0:T(8,128)(2,1)}, bf16[64,6656]{1,0:T(8,128)(2,1)}, u32[]{:S(2)}, u32[]{:S(2)}) collective-permute-start(bf16[64,6656]{1,0:T(8,128)(2,1)} %bitcast.1), channel_id=1, source_target_pairs={{0,1},{1,2},{2,3},{3,0},{4,5},{5,6},{6,7},{7,4},{8,9},{9,10},{10,1... | collective-permute-start | bytes 2555912 | tf_op jit(solution)/shard_map/ppermute | solution.py:29
  173.9 119.1 %collective-permute-start.23 = (bf16[64,6656]{1,0:T(8,128)(2,1)}, bf16[64,6656]{1,0:T(8,128)(2,1)}, u32[]{:S(2)}, u32[]{:S(2)}) collective-permute-start(bf16[64,6656]{1,0:T(8,128)(2,1)} %bitcast.1), channel_id=1, source_target_pairs={{0,3},{1,0},{2,1},{3,2},{4,7},{5,4},{6,5},{7,6},{8,11},{9,8},{10,9... | collective-permute-start | bytes 2555912 | tf_op jit(solution)/shard_map/ppermute | solution.py:29
  212.3 154.8 %collective-permute-start.18 = (bf16[4,32,4096]{2,1,0:T(8,128)(2,1)}, bf16[4,32,4096]{2,1,0:T(8,128)(2,1)}, u32[]{:S(2)}, u32[]{:S(2)}) collective-permute-start(bf16[4,32,4096]{2,1,0:T(8,128)(2,1)} %pad_maximum_fusion.3), channel_id=1, source_target_pairs={{0,4},{4,0},{8,12},{12,8},{16,20},{20,16},{24,28},{28,24},{1,5},{5... | collective-permute-start | bytes 3145736 | tf_op jit(solution)/shard_map/ppermute | solution.py:24
  248.6 9.9 %collective-permute-start.34 = (bf16[32,3328]{1,0:T(8,128)(2,1)S(1)}, bf16[32,3328]{1,0:T(8,128)(2,1)S(1)}, u32[]{:S(2)}, u32[]{:S(2)}) collective-permute-start(bf16[32,3328]{1,0:T(8,128)(2,1)S(1)} %slice.413), channel_id=1, source_target_pairs={{0,1},{1,2},{2,3},{3,0},{4,5},{5,6},{6,7},{7,4},{8,9},{9,10},{10,1... | collective-permute-start | bytes 638984 | tf_op jit(solution)/shard_map/ppermute | solution.py:29
  249.6 12.6 %collective-permute-start.35 = (bf16[32,3328]{1,0:T(8,128)(2,1)S(1)}, bf16[32,3328]{1,0:T(8,128)(2,1)}, u32[]{:S(2)}, u32[]{:S(2)}) collective-permute-start(bf16[32,3328]{1,0:T(8,128)(2,1)S(1)} %slice.414), channel_id=1, source_target_pairs={{0,3},{1,0},{2,1},{3,2},{4,7},{5,4},{6,5},{7,6},{8,11},{9,8},{10,9... | collective-permute-start | bytes 638984 | tf_op jit(solution)/shard_map/ppermute | solution.py:29
  258.5 39.4 %collective-permute-start.4 = (bf16[4,32,4096]{2,1,0:T(8,128)(2,1)S(1)}, bf16[4,32,4096]{2,1,0:T(8,128)(2,1)}, u32[]{:S(2)}, u32[]{:S(2)}) collective-permute-start(bf16[4,32,4096]{2,1,0:T(8,128)(2,1)S(1)} %pad_maximum_fusion.2), channel_id=1, source_target_pairs={{0,4},{4,0},{8,12},{12,8},{16,20},{20,16},{24,28},{28,24},{1,5},{5... | collective-permute-start | bytes 3145736 | tf_op jit(solution)/shard_map/ppermute | solution.py:24
  285.9 15.7 %collective-permute-start.36 = (bf16[4,16,4096]{2,1,0:T(8,128)(2,1)S(1)}, bf16[4,16,4096]{2,1,0:T(8,128)(2,1)S(1)}, u32[]{:S(2)}, u32[]{:S(2)}) collective-permute-start(bf16[4,16,4096]{2,1,0:T(8,128)(2,1)S(1)} %pad_maximum_fusion.8), channel_id=1, source_target_pairs={{0,4},{4,0},{8,12},{12,8},{16,20},{20,16},{24,28},{28,24},{1,5},{5... | collective-permute-start | bytes 1572872 | tf_op jit(solution)/shard_map/ppermute | solution.py:24
  292.9 14.6 %collective-permute-start.25 = (bf16[64,3328]{1,0:T(8,128)(2,1)S(1)}, bf16[64,3328]{1,0:T(8,128)(2,1)S(1)}, u32[]{:S(2)}, u32[]{:S(2)}) collective-permute-start(bf16[64,3328]{1,0:T(8,128)(2,1)S(1)} %slice.394), channel_id=1, source_target_pairs={{0,1},{1,2},{2,3},{3,0},{4,5},{5,6},{6,7},{7,4},{8,9},{9,10},{10,1... | collective-permute-start | bytes 1277960 | tf_op jit(solution)/shard_map/ppermute | solution.py:29
  294.1 21.0 %collective-permute-start.26 = (bf16[64,3328]{1,0:T(8,128)(2,1)S(1)}, bf16[64,3328]{1,0:T(8,128)(2,1)S(1)}, u32[]{:S(2)}, u32[]{:S(2)}) collective-permute-start(bf16[64,3328]{1,0:T(8,128)(2,1)S(1)} %slice.395), channel_id=1, source_target_pairs={{0,3},{1,0},{2,1},{3,2},{4,7},{5,4},{6,5},{7,6},{8,11},{9,8},{10,9... | collective-permute-start | bytes 1277960 | tf_op jit(solution)/shard_map/ppermute | solution.py:29
  300.1 56.8 %collective-permute-start.7 = (bf16[2,32,2048]{2,1,0:T(8,128)(2,1)}, bf16[2,32,2048]{2,1,0:T(8,128)(2,1)}, u32[]{:S(2)}, u32[]{:S(2)}) collective-permute-start(bf16[2,32,2048]{2,1,0:T(8,128)(2,1)} %pad_maximum_fusion.13), channel_id=1, source_target_pairs={{0,16},{4,20},{8,24},{12,28},{16,0},{20,4},{24,8},{28,12},{1,17},{... | collective-permute-start | bytes 786440 | tf_op jit(solution)/shard_map/ppermute | solution.py:24
  301.5 56.6 %collective-permute-start.5 = (bf16[2,32,2048]{2,1,0:T(8,128)(2,1)}, bf16[2,32,2048]{2,1,0:T(8,128)(2,1)}, u32[]{:S(2)}, u32[]{:S(2)}) collective-permute-start(bf16[2,32,2048]{2,1,0:T(8,128)(2,1)} %pad_maximum_fusion.12), channel_id=1, source_target_pairs={{0,8},{4,12},{8,0},{12,4},{16,24},{20,28},{24,16},{28,20},{1,9},{5... | collective-permute-start | bytes 786440 | tf_op jit(solution)/shard_map/ppermute | solution.py:24
  307.5 47.0 %collective-permute-start.39 = (bf16[2,16,2048]{2,1,0:T(8,128)(2,1)}, bf16[2,16,2048]{2,1,0:T(8,128)(2,1)}, u32[]{:S(2)}, u32[]{:S(2)}) collective-permute-start(bf16[2,16,2048]{2,1,0:T(8,128)(2,1)} %pad_maximum_fusion.21), channel_id=1, source_target_pairs={{0,16},{4,20},{8,24},{12,28},{16,0},{20,4},{24,8},{28,12},{1,17},{... | collective-permute-start | bytes 393224 | tf_op jit(solution)/shard_map/ppermute | solution.py:24
  315.8 39.8 %collective-permute-start.37 = (bf16[2,16,2048]{2,1,0:T(8,128)(2,1)}, bf16[2,16,2048]{2,1,0:T(8,128)(2,1)}, u32[]{:S(2)}, u32[]{:S(2)}) collective-permute-start(bf16[2,16,2048]{2,1,0:T(8,128)(2,1)} %pad_maximum_fusion.20), channel_id=1, source_target_pairs={{0,8},{4,12},{8,0},{12,4},{16,24},{20,28},{24,16},{28,20},{1,9},{5... | collective-permute-start | bytes 393224 | tf_op jit(solution)/shard_map/ppermute | solution.py:24
  354.5 12.6 %collective-permute-start.27 = (bf16[4,32,4096]{2,1,0:T(8,128)(2,1)S(1)}, bf16[4,32,4096]{2,1,0:T(8,128)(2,1)S(1)}, u32[]{:S(2)}, u32[]{:S(2)}) collective-permute-start(bf16[4,32,4096]{2,1,0:T(8,128)(2,1)S(1)} %pad_maximum_fusion.4), channel_id=1, source_target_pairs={{0,4},{4,0},{8,12},{12,8},{16,20},{20,16},{24,28},{28,24},{1,5},{5... | collective-permute-start | bytes 3145736 | tf_op jit(solution)/shard_map/ppermute | solution.py:24
  355.6 5.0 %collective-permute-start.40 = (bf16[1,16,2048]{2,1,0:T(8,128)(2,1)S(1)}, bf16[1,16,2048]{2,1,0:T(8,128)(2,1)S(1)}, u32[]{:S(2)}, u32[]{:S(2)}) collective-permute-start(bf16[1,16,2048]{2,1,0:T(8,128)(2,1)S(1)} %fusion.59), channel_id=1, source_target_pairs={{0,8},{4,12},{8,0},{12,4},{16,24},{20,28},{24,16},{28,20},{1,9},{5... | collective-permute-start | bytes 196616 | tf_op jit(solution)/shard_map/ppermute | solution.py:24
  357.0 5.7 %collective-permute-start.38 = (bf16[1,16,2048]{2,1,0:T(8,128)(2,1)S(1)}, bf16[1,16,2048]{2,1,0:T(8,128)(2,1)S(1)}, u32[]{:S(2)}, u32[]{:S(2)}) collective-permute-start(bf16[1,16,2048]{2,1,0:T(8,128)(2,1)S(1)} %fusion.57), channel_id=1, source_target_pairs={{0,16},{4,20},{8,24},{12,28},{16,0},{20,4},{24,8},{28,12},{1,17},{... | collective-permute-start | bytes 196616 | tf_op jit(solution)/shard_map/ppermute | solution.py:24
  358.1 5.6 %collective-permute-start.8 = (bf16[1,32,2048]{2,1,0:T(8,128)(2,1)S(1)}, bf16[1,32,2048]{2,1,0:T(8,128)(2,1)S(1)}, u32[]{:S(2)}, u32[]{:S(2)}) collective-permute-start(bf16[1,32,2048]{2,1,0:T(8,128)(2,1)S(1)} %fusion.43), channel_id=1, source_target_pairs={{0,8},{4,12},{8,0},{12,4},{16,24},{20,28},{24,16},{28,20},{1,9},{5... | collective-permute-start | bytes 393224 | tf_op jit(solution)/shard_map/ppermute | solution.py:24
  360.6 5.4 %collective-permute-start.6 = (bf16[1,32,2048]{2,1,0:T(8,128)(2,1)S(1)}, bf16[1,32,2048]{2,1,0:T(8,128)(2,1)S(1)}, u32[]{:S(2)}, u32[]{:S(2)}) collective-permute-start(bf16[1,32,2048]{2,1,0:T(8,128)(2,1)S(1)} %fusion.41), channel_id=1, source_target_pairs={{0,16},{4,20},{8,24},{12,28},{16,0},{20,4},{24,8},{28,12},{1,17},{... | collective-permute-start | bytes 393224 | tf_op jit(solution)/shard_map/ppermute | solution.py:24
  369.0 9.3 %collective-permute-start.21 = (bf16[2,32,2048]{2,1,0:T(8,128)(2,1)S(1)}, bf16[2,32,2048]{2,1,0:T(8,128)(2,1)S(1)}, u32[]{:S(2)}, u32[]{:S(2)}) collective-permute-start(bf16[2,32,2048]{2,1,0:T(8,128)(2,1)S(1)} %pad_maximum_fusion.15), channel_id=1, source_target_pairs={{0,16},{4,20},{8,24},{12,28},{16,0},{20,4},{24,8},{28,12},{1,17},{... | collective-permute-start | bytes 786440 | tf_op jit(solution)/shard_map/ppermute | solution.py:24
  370.8 9.3 %collective-permute-start.19 = (bf16[2,32,2048]{2,1,0:T(8,128)(2,1)S(1)}, bf16[2,32,2048]{2,1,0:T(8,128)(2,1)S(1)}, u32[]{:S(2)}, u32[]{:S(2)}) collective-permute-start(bf16[2,32,2048]{2,1,0:T(8,128)(2,1)S(1)} %pad_maximum_fusion.14), channel_id=1, source_target_pairs={{0,8},{4,12},{8,0},{12,4},{16,24},{20,28},{24,16},{28,20},{1,9},{5... | collective-permute-start | bytes 786440 | tf_op jit(solution)/shard_map/ppermute | solution.py:24
  371.3 12.1 %collective-permute-start.30 = (bf16[2,32,2048]{2,1,0:T(8,128)(2,1)S(1)}, bf16[2,32,2048]{2,1,0:T(8,128)(2,1)S(1)}, u32[]{:S(2)}, u32[]{:S(2)}) collective-permute-start(bf16[2,32,2048]{2,1,0:T(8,128)(2,1)S(1)} %pad_maximum_fusion.17), channel_id=1, source_target_pairs={{0,16},{4,20},{8,24},{12,28},{16,0},{20,4},{24,8},{28,12},{1,17},{... | collective-permute-start | bytes 786440 | tf_op jit(solution)/shard_map/ppermute | solution.py:24
  371.7 14.1 %collective-permute-start.28 = (bf16[2,32,2048]{2,1,0:T(8,128)(2,1)S(1)}, bf16[2,32,2048]{2,1,0:T(8,128)(2,1)S(1)}, u32[]{:S(2)}, u32[]{:S(2)}) collective-permute-start(bf16[2,32,2048]{2,1,0:T(8,128)(2,1)S(1)} %pad_maximum_fusion.16), channel_id=1, source_target_pairs={{0,8},{4,12},{8,0},{12,4},{16,24},{20,28},{24,16},{28,20},{1,9},{5... | collective-permute-start | bytes 786440 | tf_op jit(solution)/shard_map/ppermute | solution.py:24
  378.3 9.1 %collective-permute-start.22 = (bf16[1,32,2048]{2,1,0:T(8,128)(2,1)S(1)}, bf16[1,32,2048]{2,1,0:T(8,128)(2,1)S(1)}, u32[]{:S(2)}, u32[]{:S(2)}) collective-permute-start(bf16[1,32,2048]{2,1,0:T(8,128)(2,1)S(1)} %fusion.47), channel_id=1, source_target_pairs={{0,8},{4,12},{8,0},{12,4},{16,24},{20,28},{24,16},{28,20},{1,9},{5... | collective-permute-start | bytes 393224 | tf_op jit(solution)/shard_map/ppermute | solution.py:24
  380.2 7.3 %collective-permute-start.20 = (bf16[1,32,2048]{2,1,0:T(8,128)(2,1)S(1)}, bf16[1,32,2048]{2,1,0:T(8,128)(2,1)S(1)}, u32[]{:S(2)}, u32[]{:S(2)}) collective-permute-start(bf16[1,32,2048]{2,1,0:T(8,128)(2,1)S(1)} %fusion.45), channel_id=1, source_target_pairs={{0,16},{4,20},{8,24},{12,28},{16,0},{20,4},{24,8},{28,12},{1,17},{... | collective-permute-start | bytes 393224 | tf_op jit(solution)/shard_map/ppermute | solution.py:24
  383.4 5.4 %collective-permute-start.31 = (bf16[1,32,2048]{2,1,0:T(8,128)(2,1)S(1)}, bf16[1,32,2048]{2,1,0:T(8,128)(2,1)S(1)}, u32[]{:S(2)}, u32[]{:S(2)}) collective-permute-start(bf16[1,32,2048]{2,1,0:T(8,128)(2,1)S(1)} %fusion.51), channel_id=1, source_target_pairs={{0,8},{4,12},{8,0},{12,4},{16,24},{20,28},{24,16},{28,20},{1,9},{5... | collective-permute-start | bytes 393224 | tf_op jit(solution)/shard_map/ppermute | solution.py:24
  385.8 5.0 %collective-permute-start.29 = (bf16[1,32,2048]{2,1,0:T(8,128)(2,1)S(1)}, bf16[1,32,2048]{2,1,0:T(8,128)(2,1)S(1)}, u32[]{:S(2)}, u32[]{:S(2)}) collective-permute-start(bf16[1,32,2048]{2,1,0:T(8,128)(2,1)S(1)} %fusion.49), channel_id=1, source_target_pairs={{0,16},{4,20},{8,24},{12,28},{16,0},{20,4},{24,8},{28,12},{1,17},{... | collective-permute-start | bytes 393224 | tf_op jit(solution)/shard_map/ppermute | solution.py:24
  (27 other events, 463.4 us)
Sparse Core Ops, SparseCore 0:
  137.3 34.0 all-gather.1

commit v2 on v0

v2 whole, which is shorter than its diff:
```python
import functools

import jax
import jax.numpy as jnp
from jax import lax
from jax.experimental import pallas as pl
from jax.experimental.pallas import tpu as pltpu
from jax.sharding import PartitionSpec as P

adapter_scale = 2.0
piece_rows = 32
weight_rows = 256
vmem_bytes = 40 * 2**20


def contract_trailing_axis(left, right):
    return lax.dot_general(
        left, right, (((1,), (1,)), ((), ())), preferred_element_type=jnp.float32
    )


def contract_first(left, right):
    return lax.dot_general(
        left, right, (((0,), (0,)), ((), ())), preferred_element_type=jnp.float32
    )


def bits_of(axis):
    size = lax.axis_size(axis)
    return [1 << i for i in range(size.bit_length() - 1)]


def swap(value, axis, bit):
    size = lax.axis_size(axis)
    return lax.ppermute(value, axis, [(i, i ^ bit) for i in range(size)])


def shift(value, axis, by):
    size = lax.axis_size(axis)
    return lax.ppermute(value, axis, [(i, (i + by) % size) for i in range(size)])


def scatter_small(value, axis):
    me = lax.axis_index(axis)
    for bit in reversed(bits_of(axis)):
        pair = value.reshape(2, value.shape[0] // 2, value.shape[1])
        mine = ((me & bit) != 0).astype(jnp.int32)
        kept = lax.dynamic_index_in_dim(pair, mine, 0, keepdims=False)
        sent = lax.dynamic_index_in_dim(pair, 1 - mine, 0, keepdims=False)
        value = kept + swap(sent, axis, bit)
    return value


def scatter_direct(value, axis):
    size = lax.axis_size(axis)
    me = lax.axis_index(axis)
    rows = value.shape[0] // size
    blocks = value.reshape(size, rows, value.shape[1])
    found = [
        swap(lax.dynamic_index_in_dim(blocks, me ^ p, 0, keepdims=False), axis, p)
        for p in range(1, size)
    ]
    return lax.dynamic_index_in_dim(blocks, me, 0, keepdims=False), found


def gather_direct(value, axis):
    return [value] + [swap(value, axis, p) for p in range(1, lax.axis_size(axis))]


def by_index(blocks, axis):
    value = jnp.stack(blocks)
    me = lax.axis_index(axis)
    for bit in bits_of(axis):
        pair = value.reshape(value.shape[0] // (2 * bit), 2, bit, *value.shape[1:])
        value = jnp.where((me & bit) != 0, pair[:, ::-1], pair).reshape(value.shape)
    return value


def gather_relative(value, axis, order):
    value = value[None]
    for bit in order:
        value = jnp.concatenate([value, swap(value, axis, bit)], axis=0)
    return value


def gather_ordered(value, axis, order):
    me = lax.axis_index(axis)
    for bit in order:
        other = swap(value, axis, bit)
        upper = (me & bit) != 0
        value = jnp.concatenate(
            [jnp.where(upper, other, value), jnp.where(upper, value, other)], axis=0
        )
    return value


def first_hops(block, axis):
    size = lax.axis_size(axis)
    if size == 4:
        far = swap(block, axis, 2)
        near = swap(block, axis, 1)
        middle = lax.ppermute(block, axis, [(1, 2), (2, 1)])
        return [far, near, middle]
    return [shift(block, axis, 1), shift(block, axis, -1)]


def last_hops(block, hops, axis):
    size = lax.axis_size(axis)
    me = lax.axis_index(axis)
    if size == 4:
        far, near, middle = hops
        ends = (me == 0) | (me == 3)
        onward = lax.ppermute(far, axis, [(1, 0), (2, 3)])
        return [
            (block, me, True),
            (near, me ^ 1, True),
            (far, me ^ 2, True),
            (middle, me ^ 3, ~ends),
            (onward, me ^ 3, ends),
        ]
    up, down = hops
    found = [(block, me, True)]
    for step in range(1, size):
        if step % 2:
            found.append((up, (me + size - (step + 1) // 2) % size, True))
            if step + 2 < size:
                up = shift(up, axis, 1)
        else:
            found.append((down, (me + step // 2) % size, True))
            if step + 2 < size:
                down = shift(down, axis, -1)
    return found


def pass_kernel(places, *refs, sources, share, rows, final, summed):
    source_refs, refs = refs[:sources], refs[sources:]
    weight, refs = refs[0], refs[1:]
    before, refs = (refs[0], refs[1:]) if summed else (None, refs)
    tokens, outs = refs[0], refs[1:]

    @pl.when(pl.program_id(0) == 0)
    def _():
        for i, source in enumerate(source_refs):
            for h in range(share):
                place = places[i * share + h]

                @pl.when(place >= 0)
                def _():
                    start = pl.multiple_of(place * rows, rows)
                    tokens[pl.ds(start, rows), :] = source[h * rows : (h + 1) * rows, :]

    product = contract_trailing_axis(tokens[...], weight[...])
    if summed:
        product = product + before[...]
    if final:
        half = product.shape[0] // 2
        outs[0][...] = product[:half]
        outs[1][...] = product[half:].astype(jnp.bfloat16)
    else:
        outs[0][...] = product


def weight_pass(places, sources, weight, depth_block, share, rows, owners, final, before=None):
    depth = sources[0].shape[1]
    width = weight.shape[0]
    total = owners * rows
    column = lambda i, *_: (0, i)
    whole = lambda i, *_: (0, 0)
    operands = [*sources, weight]
    in_specs = [pl.BlockSpec(s.shape, whole) for s in sources]
    in_specs.append(pl.BlockSpec((weight_rows, depth), lambda i, *_: (i, depth_block)))
    if before is not None:
        operands.append(before)
        in_specs.append(pl.BlockSpec((total, weight_rows), column))
    out_shape = [jax.ShapeDtypeStruct((total, depth), jnp.bfloat16)]
    out_specs = [pl.BlockSpec((total, depth), whole)]
    if final:
        out_shape += [
            jax.ShapeDtypeStruct((total // 2, width), jnp.float32),
            jax.ShapeDtypeStruct((total // 2, width), jnp.bfloat16),
        ]
        out_specs += [pl.BlockSpec((total // 2, weight_rows), column)] * 2
    else:
        out_shape.append(jax.ShapeDtypeStruct((total, width), jnp.float32))
        out_specs.append(pl.BlockSpec((total, weight_rows), column))
    return pl.pallas_call(
        functools.partial(
            pass_kernel,
            sources=len(sources),
            share=share,
            rows=rows,
            final=final,
            summed=before is not None,
        ),
        grid_spec=pltpu.PrefetchScalarGridSpec(
            num_scalar_prefetch=1,
            grid=(width // weight_rows,),
            in_specs=in_specs,
            out_specs=out_specs,
        ),
        out_shape=out_shape,
        compiler_params=pltpu.CompilerParams(vmem_limit_bytes=vmem_bytes),
        cost_estimate=pl.CostEstimate(
            flops=2 * total * depth * width,
            bytes_accessed=2 * width * depth + 4 * total * depth,
            transcendentals=0,
        ),
        name="weight_pass",
    )(places, *operands)


def scatter_sum(kept, sent, axis, owners, rows):
    bits = bits_of(axis)
    live = (kept + swap(sent, axis, 1)).reshape(owners // 2, rows, -1)
    half = live.shape[2] // 2
    done = []
    for side, order in ((0, bits[:-1]), (1, bits[:-1][::-1])):
        part = {p: live[p, :, side * half : (side + 1) * half] for p in range(owners // 2)}
        for bit in order:
            stay = [p for p in part if not p & bit]
            away = jnp.stack([part[p ^ bit].astype(jnp.bfloat16) for p in stay])
            got = swap(away, axis, 2 * bit)
            part = {p: part[p] + got[i] for i, p in enumerate(stay)}
        done.append(part[0])
    return done


def hold(*groups):
    leaves, tree = jax.tree.flatten(groups)
    return jax.tree.unflatten(tree, lax.optimization_barrier(leaves))


def cut_rows(owner_rows, depth):
    sizes = []
    left = owner_rows
    while left:
        sizes.insert(0, min(left, piece_rows))
        left -= sizes[0]
    if len(sizes) > 2 and sizes[0] < piece_rows:
        sizes = [sizes[0] + sizes[1], *sizes[2:]]
    cuts = max(c for c in (4, 2, 1) if depth % (c * 128) == 0)
    tail = depth // cuts
    pieces = []
    start = 0
    for rows in sizes:
        pieces.append((start, rows, 0, depth))
        start += rows
    if cuts > 1:
        start, rows, _, _ = pieces.pop()
        pieces += [(start, rows, 0, depth - tail), (start, rows, depth - tail, depth)]
    return pieces


def shards(inputs, grad_out, w_base, adapter_down_matrix, b_factor):
    owner_rows = inputs.shape[0]
    owners = lax.axis_size("wide")
    me_wide = lax.axis_index("wide")
    adapter_matrix = adapter_scale / (owner_rows * owners)
    share = grad_out.shape[0] // owner_rows
    rank = b_factor.shape[0]
    depth = grad_out.shape[1]
    wide_bits = bits_of("wide")
    pieces = cut_rows(owner_rows, depth)
    count = len(pieces)

    def block_of(source, piece):
        start, rows, low, high = piece
        own = source.reshape(share, owner_rows, depth)
        return own[:, start : start + rows, low:high].reshape(share * rows, high - low)

    blocks = {0: block_of(grad_out, pieces[0])}
    hops = {0: first_hops(blocks[0], "narrow")}

    act_own, act_others = scatter_direct(
        jnp.dot(inputs, adapter_down_matrix, preferred_element_type=jnp.float32), "narrow"
    )
    low_small = scatter_small(contract_trailing_axis(grad_out, b_factor), "wide").astype(jnp.bfloat16)
    grad_out, low_small = hold(grad_out, low_small)
    low_blocks = gather_direct(low_small, "narrow")
    blocks[1] = block_of(grad_out, pieces[1])
    hops[1] = first_hops(blocks[1], "narrow")

    hops[0], act_own, act_others, low_blocks, grad_out, inputs = hold(
        hops[0], act_own, act_others, low_blocks, grad_out, inputs
    )
    found = {0: last_hops(blocks[0], hops[0], "narrow")}
    places = []
    for _, block, valid in found[0]:
        for h in range(share):
            p = (block * share + h) ^ me_wide
            place = (p & 1) * (owners // 2) + (p >> 1)
            places.append(jnp.where(valid, place, -1).astype(jnp.int32))
    places = jnp.stack(places)
    found[0] = [array for array, _, _ in found[0]]
    blocks[2] = block_of(grad_out, pieces[2])
    hops[2] = first_hops(blocks[2], "narrow")
    act_blocks = gather_direct((act_own + sum(act_others)).astype(jnp.bfloat16), "narrow")

    low_wide = gather_ordered(by_index(low_blocks, "narrow")[None], "wide", wide_bits)
    low_rank_all = jnp.swapaxes(low_wide, 0, 1).reshape(owner_rows * owners, rank)
    low_rank_own = lax.dynamic_slice_in_dim(low_rank_all, me_wide * owner_rows, owner_rows)
    low_term = adapter_scale * contract_trailing_axis(low_rank_own, adapter_down_matrix)
    shares = inputs.reshape(owner_rows, owners, -1)
    flipped = [
        sum(bit for i, bit in enumerate(wide_bits) if w & wide_bits[len(wide_bits) - 1 - i])
        for w in range(owners)
    ]
    columns = lax.all_to_all(
        jnp.stack([shares[:, f] for f in flipped], axis=0), "wide", split_axis=0, concat_axis=0
    ).reshape(owner_rows * owners, -1)
    grad_a = adapter_matrix * contract_first(columns, low_rank_all)
    grad_a_steps = wide_bits[::-1]

    sums, tokens, grad_b, results = {}, {}, None, {}
    acts = None

    def run_pass(i):
        _, rows, low, high = pieces[i]
        final = high == depth
        before = None if low == 0 else sums.pop(i - 1)[0]
        tokens[i], *sums[i] = weight_pass(
            places, found[i], w_base, low // (high - low), share, rows, owners, final, before
        )

    def finish(i, acc):
        start, rows, low, _ = pieces[i]
        held = tokens[i] if low == 0 else jnp.concatenate([tokens[i - 1], tokens[i]], axis=1)
        piece_acts = acts[:, start : start + rows].reshape(owners * rows, rank)
        term = contract_first(piece_acts, held)
        acc = term if acc is None else acc + term
        sides = scatter_sum(*sums.pop(i), "wide", owners, rows)
        half = sides[0].shape[1]
        mine = low_term[start : start + rows]
        results[i] = jnp.concatenate(
            [
                (side + mine[:, j * half : (j + 1) * half]).astype(jnp.bfloat16)
                for j, side in enumerate(sides)
            ],
            axis=1,
        )
        return acc

    for i in range(1, count):
        hops[i], found[i - 1], grad_out, grad_a, act_blocks, sums, grad_b, results, acts, low_term = hold(
            hops[i], found[i - 1], grad_out, grad_a, act_blocks, sums, grad_b, results, acts, low_term
        )
        found[i] = [array for array, _, _ in last_hops(blocks[i], hops[i], "narrow")]
        if i + 2 < count:
            blocks[i + 2] = block_of(grad_out, pieces[i + 2])
            hops[i + 2] = first_hops(blocks[i + 2], "narrow")
        if i >= 2 and pieces[i - 2][3] == depth:
            grad_b = finish(i - 2, grad_b)
        run_pass(i - 1)
        if acts is None:
            act_rows = by_index(act_blocks, "narrow").reshape(owner_rows, rank)
            acts = gather_relative(act_rows, "wide", wide_bits[1:] + wide_bits[:1])
        if grad_a_steps:
            grad_a = gather_ordered(grad_a, "wide", grad_a_steps[:1])
            grad_a_steps = grad_a_steps[1:]
    grad_a = gather_ordered(grad_a, "wide", grad_a_steps)
    found[count - 1], sums, grad_b, results, grad_a = hold(
        found[count - 1], sums, grad_b, results, grad_a
    )
    for i in range(count - 2, count - 1):
        if pieces[i][3] == depth:
            grad_b = finish(i, grad_b)
    run_pass(count - 1)
    grad_b = adapter_matrix * finish(count - 1, grad_b)
    return (jnp.concatenate([results[i] for i in sorted(results)], axis=0), grad_a, grad_b)


def solution(mesh):
    return jax.shard_map(
        shards,
        mesh=mesh,
        in_specs=(
            P("wide", "narrow"),
            P("narrow", "wide"),
            P("narrow", "wide"),
            P("narrow", None),
            P(None, "wide"),
        ),
        out_specs=(P("wide", "narrow"), P("narrow", None), P(None, "wide")),
        check_vma=False,
    )
```

time: 501 us -> 393 us (0.78)
  waiting for transfers between devices: 357 us -> 133 us
  Pallas kernels: 0 us -> 100 us
  starting transfers between devices: 0.12 us -> 73.4 us
  matrix products: 82.7 us -> 24.5 us
  blocking collectives: 30.2 us -> 0 us
  other arithmetic: 10.6 us -> 37.8 us
  local copies, waits for them, and re-layouts: 5.62 us -> 20.6 us
  between operations: 13.8 us -> 1.36 us
    all_gather x1 -> x0, waiting for transfers between devices: 212 us -> none  [shards(): every_row = lax.all_gather(grad_out, 'narrow', axis=0, tiled=True)]
    ppermute x0 -> x52, waiting for transfers between devices: none -> 133 us  [the longest x44 115 us: swap(): return lax.ppermute(value, axis, [(i, i ^ bit) for i in range(size)])]
    reduce_scatter x1 -> x0, waiting for transfers between devices: 107 us -> none  [shards(): summed = lax.psum_scatter(stacked, 'wide', scatter_dimension=0, tiled=True)]
    pallas_call x0 -> x4, Pallas kernels: none -> 100 us  [weight_pass(): pl.pallas_call(functools.partial(pass_kernel, sources=len(sources), share...]
    ppermute x0 -> x52, starting transfers between devices: none -> 69.1 us  [the longest x44 59.8 us: swap(): return lax.ppermute(value, axis, [(i, i ^ bit) for i in range(size)])]
    dot_general x3 -> x2, matrix products: 68 us -> 7.41 us  [contract_trailing_axis(): lax.dot_general(left, right, (((1,), (1,)), ((), ())), preferred_element_...]
    psum x1 -> x0, waiting for transfers between devices: 38 us -> none  [shards(): lax.psum(adapter_matrix * contract_first(inputs, low_rank_gradient), 'wide')]
    psum x1 -> x0, blocking collectives: 20.7 us -> none  [shards(): low_act = lax.psum(low_part, 'narrow').astype(jnp.bfloat16)]
  transfers between devices with their start and end apart: 3 -> 53, of which waited for: 3 -> 21; matrix products, arithmetic and copies ran while one was open for 3% -> 19% of each run, Pallas kernels for 0% -> 22%
where the time goes in v2:
time: 393 us; the launch traced here: 391 us
  waiting for transfers between devices  133 us (34%)
  Pallas kernels  100 us (25%)
  starting transfers between devices  73.4 us (19%)
  other arithmetic  37.8 us (10%)
  matrix products  24.5 us (6%)
  local copies, waits for them, and re-layouts  20.6 us (5%)
    ppermute x44, waiting for transfers between devices, swap(): return lax.ppermute(value, axis, [(i, i ^ bit) for i in range(size)])  115 us
    pallas_call x4, Pallas kernels, weight_pass(): pl.pallas_call(functools.partial(pass_kernel, sources=len(sources), share...  100 us
    ppermute x44, starting transfers between devices, swap(): return lax.ppermute(value, axis, [(i, i ^ bit) for i in range(size)])  59.8 us
    ppermute x4, waiting for transfers between devices, last_hops(): onward = lax.ppermute(far, axis, [(1, 0), (2, 3)])  17.8 us
    dot_general x4, matrix products, contract_first(): lax.dot_general(left, right, (((0,), (0,)), ((), ())), preferred_element_...  14.8 us
    unnamed x44, local copies, waits for them, and re-layouts  8.63 us
  transfers between devices with their start and end apart: 53, of which 21 were waited for; matrix products, arithmetic and copies ran while one was open for 19% of the time, Pallas kernels for 22%

profile of v2, /device:TPU:0, one launch (start us, length us, event | category | flops | bytes accessed | tf_op | source)
XLA Modules:
  0.0 390.7 jit_solution(11271422603830498039)
XLA Ops:
  0.6 2.6 slice.253
  3.2 4.0 %collective-permute-start.6 = (bf16[96,6656]{1,0:T(8,128)(2,1)}, bf16[96,6656]{1,0:T(8,128)(2,1)}, u32[]{:S(2)}, u32[]{:S(2)}) collective-permute-start(bf16[96,6656]{1,0:T(8,128)(2,1)} %bitcast.11.refs_0_), channel_id=1, source_target_pairs={{0,2},{1,3},{2,0},{3,1},{4,6},{5,7},{6,4},{7,5},{8,10},{9,11},{10,... | collective-permute-start | bytes 3833864 | tf_op jit(solution)/shard_map/ppermute | solution.py:35
  7.3 1.6 collective-permute-start.7
  8.8 1.7 collective-permute-start.8
  10.5 3.7 fusion.45
  16.7 2.3 fusion.46
  22.2 2.1 collective-permute-start.10
  24.5 67.3 %collective-permute-done.10 = f32[28,256]{1,0:T(8,128)S(1)} collective-permute-done((f32[28,256]{1,0:T(8,128)S(1)}, f32[28,256]{1,0:T(8,128)S(1)}, u32[]{:S(2)}, u32[]{:S(2)}) %collective-permute-start.10) | collective-permute-done | bytes 28704 | tf_op jit(solution)/shard_map/ppermute | solution.py:35
  91.8 3.5 collective-permute-start.11
  95.3 2.2 collective-permute-done.11
  97.5 1.9 collective-permute-done.9
  99.4 2.2 collective-permute-start.13
  101.6 3.2 collective-permute-start.14
  109.7 1.7 fusion.43
  118.9 3.7 collective-permute-done.17
  126.2 4.2 %all-to-all-start = ((bf16[8,112,512]{2,1,0:T(8,128)(2,1)}), bf16[8,112,512]{2,1,0:T(8,128)(2,1)}, u32[]{:S(2)}, u32[]{:S(2)}) async-start(bf16[8,112,512]{2,1,0:T(8,128)(2,1)} %bitcast_dynamic-update-slice_fusion), calls=%async_computation | async-start | bytes 1835008 | tf_op jit(solution)/shard_map/all_to_all | solution.py:308
  132.3 6.7 %collective-permute-start.19 = (bf16[28,256]{1,0:T(8,128)(2,1)S(1)}, bf16[28,256]{1,0:T(8,128)(2,1)}, u32[]{:S(2)}, u32[]{:S(2)}) collective-permute-start(bf16[28,256]{1,0:T(8,128)(2,1)S(1)} %add_convert_fusion), channel_id=1, source_target_pairs={{0,1},{1,0},{2,3},{3,2},{4,5},{5,4},{6,7},{7,6},{8,9},{9,8},{10,11... | collective-permute-start | bytes 43016 | tf_op jit(solution)/shard_map/ppermute | solution.py:35
  140.8 1.9 reshape.110
  142.7 3.7 convolution_multiply_fusion
  147.4 3.2 collective-permute-start.21
  150.6 2.6 convolution_multiply_fusion.1
  153.2 18.9 %collective-permute-done.19 = bf16[28,256]{1,0:T(8,128)(2,1)} collective-permute-done((bf16[28,256]{1,0:T(8,128)(2,1)S(1)}, bf16[28,256]{1,0:T(8,128)(2,1)}, u32[]{:S(2)}, u32[]{:S(2)}) %collective-permute-start.19) | collective-permute-done | bytes 14368 | tf_op jit(solution)/shard_map/ppermute | solution.py:35
  174.5 2.7 collective-permute-done.30
  177.2 1.6 collective-permute-start.31
  178.8 3.3 collective-permute-done.31
  185.2 2.6 collective-permute-start.26
  188.5 1.6 collective-permute-start.29
  191.6 34.9 %weight_pass.4 = (bf16[384,6656]{1,0:T(8,128)(2,1)}, f32[192,4096]{1,0:T(8,128)S(1)}, bf16[192,4096]{1,0:T(8,128)(2,1)S(1)}) custom-call(s32[10]{0:T(128)S(1)} %stack.118.places, bf16[96,6656]{1,0:T(8,128)(2,1)} %bitcast.11.refs_0_, bf16[96,6656]{1,0:T(8,128)(2,1)} %collective-permute-done.7.refs_1_, bf16[96,6656]{1,0:T(8,128)(2,1)} %collective-permute-done.6.refs_2_, ...), custom_call_target="tpu_custom_call" | custom-call | flops 20937965568 | bytes 64749568 | tf_op jit(solution)/shard_map/weight_pass/pallas_call | solution.py:186
  228.6 5.9 %collective-permute-done.28.refs_4_ = bf16[64,6656]{1,0:T(8,128)(2,1)S(1)} collective-permute-done((bf16[64,6656]{1,0:T(8,128)(2,1)S(1)}, bf16[64,6656]{1,0:T(8,128)(2,1)S(1)}, u32[]{:S(2)}, u32[]{:S(2)}) %collective-permute-start.28) | collective-permute-done | bytes 852000 | tf_op jit(solution)/shard_map/ppermute | solution.py:113
  235.6 2.1 collective-permute-start.23
  239.2 27.4 %weight_pass.5 = (bf16[256,6656]{1,0:T(8,128)(2,1)S(1)}, f32[128,4096]{1,0:T(8,128)S(1)}, bf16[128,4096]{1,0:T(8,128)(2,1)S(1)}) custom-call(s32[10]{0:T(128)S(1)} %stack.118.places, bf16[64,6656]{1,0:T(8,128)(2,1)S(1)} %bitcast.139, bf16[64,6656]{1,0:T(8,128)(2,1)S(1)} %collective-permute-done.4.refs_1_, ...), custom_call_target="tpu_custom_call" | custom-call | flops 13958643712 | bytes 61341696 | tf_op jit(solution)/shard_map/weight_pass/pallas_call | solution.py:186
  269.4 4.4 %fusion.47 = f32[256,6656]{1,0:T(8,128)S(1)} fusion(bf16[384,256]{1,0:T(8,128)(2,1)S(1)} %bitcast.165, bf16[384,6656]{1,0:T(8,128)(2,1)} %get-tuple-element.126), kind=kOutput, calls=%fused_computation.117 | convolution fusion | flops 1308622848 | bytes 12124160 | tf_op jit(solution)/shard_map/dot_general | solution.py:23
  274.5 1.7 broadcast_select_fusion.3
  276.2 1.8 collective-permute-done.36
  278.4 1.6 collective-permute-start.37
  287.8 11.9 %collective-permute-done.33.refs_4_ = bf16[64,4992]{1,0:T(8,128)(2,1)S(1)} collective-permute-done((bf16[64,4992]{1,0:T(8,128)(2,1)S(1)}, bf16[64,4992]{1,0:T(8,128)(2,1)S(1)}, u32[]{:S(2)}, u32[]{:S(2)}) %collective-permute-start.33) | collective-permute-done | bytes 639008 | tf_op jit(solution)/shard_map/ppermute | solution.py:113
  301.7 2.1 collective-permute-done.41
  308.4 23.6 %weight_pass.6 = (bf16[256,4992]{1,0:T(8,128)(2,1)S(1)}, f32[256,4096]{1,0:T(8,128)S(1)}) custom-call(s32[10]{0:T(128)S(1)} %stack.118.places, bf16[64,4992]{1,0:T(8,128)(2,1)S(1)} %bitcast.143, bf16[64,4992]{1,0:T(8,128)(2,1)S(1)} %collective-permute-done.26.refs_1_, bf16[64,4992]{1,0:T(8,128)(2,1)S(1)} %collective-permute-done.25.refs_2_, ...), custom_call_target="tpu_custom_call" | custom-call | flops 10468982784 | bytes 46006272 | tf_op jit(solution)/shard_map/weight_pass/pallas_call | solution.py:186
  334.4 3.9 %fusion.48 = f32[256,6656]{1,0:T(8,128)} fusion(bf16[256,256]{1,0:T(8,128)(2,1)S(1)} %bitcast.167, bf16[256,6656]{1,0:T(8,128)(2,1)S(1)} %get-tuple-element.141), kind=kOutput, calls=%fused_computation.118 | convolution fusion | flops 872415232 | bytes 10354688 | tf_op jit(solution)/shard_map/dot_general | solution.py:23
  338.4 6.9 %add.254 = f32[256,6656]{1,0:T(8,128)} add(f32[256,6656]{1,0:T(8,128)S(1)} %fusion.47, f32[256,6656]{1,0:T(8,128)} %fusion.48) | non-fusion elementwise | flops 1703936 | bytes 20447232 | tf_op jit(solution)/shard_map/add | solution.py:330
  347.3 2.5 broadcast_select_fusion.1
  349.8 2.3 pad_maximum_fusion
  352.1 14.6 %weight_pass.7 = (bf16[256,1664]{1,0:T(8,128)(2,1)S(1)}, f32[128,4096]{1,0:T(8,128)S(1)}, bf16[128,4096]{1,0:T(8,128)(2,1)S(1)}) custom-call(s32[10]{0:T(128)S(1)} %stack.118.places, bf16[64,1664]{1,0:T(8,128)(2,1)S(1)} %bitcast.147, bf16[64,1664]{1,0:T(8,128)(2,1)S(1)} %collective-permute-done.23.refs_1_, ...), custom_call_target="tpu_custom_call" | custom-call | flops 3489660928 | bytes 15335424 | tf_op jit(solution)/shard_map/weight_pass/pallas_call | solution.py:186
  366.7 2.6 collective-permute-done.47
  372.8 3.8 fusion
  376.6 1.6 collective-permute-done.48
  379.4 1.6 collective-permute-start.49
  381.6 6.9 %add_multiply_fusion = f32[256,6656]{1,0:T(8,128)} fusion(f32[256,6656]{1,0:T(8,128)S(1)} %bitcast.149, f32[256,6656]{1,0:T(8,128)} %fusion), kind=kLoop, calls=%fused_computation | loop fusion | flops 3407872 | bytes 20447232 | tf_op jit(solution)/shard_map/mul | solution.py:368
  (183 shorter events, 68.7 us)
Async XLA Ops:
  3.2 104.1 %collective-permute-start.6 = (bf16[96,6656]{1,0:T(8,128)(2,1)}, bf16[96,6656]{1,0:T(8,128)(2,1)}, u32[]{:S(2)}, u32[]{:S(2)}) collective-permute-start(bf16[96,6656]{1,0:T(8,128)(2,1)} %bitcast.11.refs_0_), channel_id=1, source_target_pairs={{0,2},{1,3},{2,0},{3,1},{4,6},{5,7},{6,4},{7,5},{8,10},{9,11},{10,... | collective-permute-start | bytes 3833864 | tf_op jit(solution)/shard_map/ppermute | solution.py:35
  7.3 100.8 %collective-permute-start.7 = (bf16[96,6656]{1,0:T(8,128)(2,1)}, bf16[96,6656]{1,0:T(8,128)(2,1)}, u32[]{:S(2)}, u32[]{:S(2)}) collective-permute-start(bf16[96,6656]{1,0:T(8,128)(2,1)} %bitcast.11.refs_0_), channel_id=1, source_target_pairs={{0,1},{1,0},{2,3},{3,2},{4,5},{5,4},{6,7},{7,6},{8,9},{9,8},{10,11... | collective-permute-start | bytes 3833864 | tf_op jit(solution)/shard_map/ppermute | solution.py:35
  8.8 99.2 %collective-permute-start.8 = (bf16[96,6656]{1,0:T(8,128)(2,1)}, bf16[96,6656]{1,0:T(8,128)(2,1)}, u32[]{:S(2)}, u32[]{:S(2)}) collective-permute-start(bf16[96,6656]{1,0:T(8,128)(2,1)} %bitcast.11.refs_0_), channel_id=1, source_target_pairs={{1,2},{2,1},{5,6},{6,5},{9,10},{10,9},{13,14},{14,13},{17,18},{18,... | collective-permute-start | bytes 3833864 | tf_op jit(solution)/shard_map/ppermute | solution.py:102
  15.2 4.8 %collective-permute-start = (f32[112,256]{1,0:T(8,128)S(1)}, f32[112,256]{1,0:T(8,128)S(1)}, u32[]{:S(2)}, u32[]{:S(2)}) collective-permute-start(f32[112,256]{1,0:T(8,128)S(1)} %dynamic-slice_bitcast_fusion), channel_id=1, source_target_pairs={{0,16},{4,20},{8,24},{12,28},{16,0},{20,4},{24,8},{28,12},{1,17},{... | collective-permute-start | bytes 344072 | tf_op jit(solution)/shard_map/ppermute | solution.py:35
  20.1 4.3 %collective-permute-start.1 = (f32[56,256]{1,0:T(8,128)S(1)}, f32[56,256]{1,0:T(8,128)S(1)}, u32[]{:S(2)}, u32[]{:S(2)}) collective-permute-start(f32[56,256]{1,0:T(8,128)S(1)} %dynamic-slice_bitcast_fusion.1), channel_id=1, source_target_pairs={{0,8},{4,12},{8,0},{12,4},{16,24},{20,28},{24,16},{28,20},{1,9},{5... | collective-permute-start | bytes 172040 | tf_op jit(solution)/shard_map/ppermute | solution.py:35
  22.2 69.5 %collective-permute-start.10 = (f32[28,256]{1,0:T(8,128)S(1)}, f32[28,256]{1,0:T(8,128)S(1)}, u32[]{:S(2)}, u32[]{:S(2)}) collective-permute-start(f32[28,256]{1,0:T(8,128)S(1)} %get-tuple-element.202), channel_id=1, source_target_pairs={{0,2},{1,3},{2,0},{3,1},{4,6},{5,7},{6,4},{7,5},{8,10},{9,11},{10,... | collective-permute-start | bytes 86024 | tf_op jit(solution)/shard_map/ppermute | solution.py:35
  24.4 70.8 %collective-permute-start.2 = (f32[28,256]{1,0:T(8,128)S(1)}, f32[28,256]{1,0:T(8,128)S(1)}, u32[]{:S(2)}, u32[]{:S(2)}) collective-permute-start(f32[28,256]{1,0:T(8,128)S(1)} %dynamic-slice_bitcast_fusion.6), channel_id=1, source_target_pairs={{0,4},{4,0},{8,12},{12,8},{16,20},{20,16},{24,28},{28,24},{1,5},{5... | collective-permute-start | bytes 86024 | tf_op jit(solution)/shard_map/ppermute | solution.py:35
  91.8 5.7 %collective-permute-start.11 = (f32[28,256]{1,0:T(8,128)S(1)}, f32[28,256]{1,0:T(8,128)S(1)}, u32[]{:S(2)}, u32[]{:S(2)}) collective-permute-start(f32[28,256]{1,0:T(8,128)S(1)} %get-tuple-element.201), channel_id=1, source_target_pairs={{0,3},{1,2},{2,1},{3,0},{4,7},{5,6},{6,5},{7,4},{8,11},{9,10},{10,... | collective-permute-start | bytes 86024 | tf_op jit(solution)/shard_map/ppermute | solution.py:35
  99.4 6.6 %collective-permute-start.13 = (bf16[28,256]{1,0:T(8,128)(2,1)S(1)}, bf16[28,256]{1,0:T(8,128)(2,1)S(1)}, u32[]{:S(2)}, u32[]{:S(2)}) collective-permute-start(bf16[28,256]{1,0:T(8,128)(2,1)S(1)} %fusion.37), channel_id=1, source_target_pairs={{0,2},{1,3},{2,0},{3,1},{4,6},{5,7},{6,4},{7,5},{8,10},{9,11},{10,... | collective-permute-start | bytes 43016 | tf_op jit(solution)/shard_map/ppermute | solution.py:35
  101.6 5.8 %collective-permute-start.14 = (bf16[28,256]{1,0:T(8,128)(2,1)S(1)}, bf16[28,256]{1,0:T(8,128)(2,1)S(1)}, u32[]{:S(2)}, u32[]{:S(2)}) collective-permute-start(bf16[28,256]{1,0:T(8,128)(2,1)S(1)} %fusion.37), channel_id=1, source_target_pairs={{0,3},{1,2},{2,1},{3,0},{4,7},{5,6},{6,5},{7,4},{8,11},{9,10},{10,... | collective-permute-start | bytes 43016 | tf_op jit(solution)/shard_map/ppermute | solution.py:35
  106.0 40.5 %collective-permute-start.3 = (bf16[64,6656]{1,0:T(8,128)(2,1)S(1)}, bf16[64,6656]{1,0:T(8,128)(2,1)S(1)}, u32[]{:S(2)}, u32[]{:S(2)}) collective-permute-start(bf16[64,6656]{1,0:T(8,128)(2,1)S(1)} %bitcast.136), channel_id=1, source_target_pairs={{0,2},{1,3},{2,0},{3,1},{4,6},{5,7},{6,4},{7,5},{8,10},{9,11},{10,... | collective-permute-start | bytes 2555912 | tf_op jit(solution)/shard_map/ppermute | solution.py:35
  107.3 40.0 %collective-permute-start.4 = (bf16[64,6656]{1,0:T(8,128)(2,1)S(1)}, bf16[64,6656]{1,0:T(8,128)(2,1)S(1)}, u32[]{:S(2)}, u32[]{:S(2)}) collective-permute-start(bf16[64,6656]{1,0:T(8,128)(2,1)S(1)} %bitcast.137), channel_id=1, source_target_pairs={{0,1},{1,0},{2,3},{3,2},{4,5},{5,4},{6,7},{7,6},{8,9},{9,8},{10,11... | collective-permute-start | bytes 2555912 | tf_op jit(solution)/shard_map/ppermute | solution.py:35
  107.3 45.9 %collective-permute-start.5 = (bf16[64,6656]{1,0:T(8,128)(2,1)S(1)}, bf16[64,6656]{1,0:T(8,128)(2,1)S(1)}, u32[]{:S(2)}, u32[]{:S(2)}) collective-permute-start(bf16[64,6656]{1,0:T(8,128)(2,1)S(1)} %bitcast.138), channel_id=1, source_target_pairs={{1,2},{2,1},{5,6},{6,5},{9,10},{10,9},{13,14},{14,13},{17,18},{18,... | collective-permute-start | bytes 2555912 | tf_op jit(solution)/shard_map/ppermute | solution.py:102
  108.1 8.5 %collective-permute-start.16 = (bf16[1,4,28,256]{3,2,0,1:T(8,128)(2,1)S(1)}, bf16[1,4,28,256]{3,2,0,1:T(8,128)(2,1)S(1)}, u32[]{:S(2)}, u32[]{:S(2)}) collective-permute-start(bf16[1,4,28,256]{3,2,0,1:T(8,128)(2,1)S(1)} %bitcast.172), channel_id=1, source_target_pairs={{0,4},{4,0},{8,12},{12,8},{16,20},{20,16},{24,28},{28,24},{1,5},{5... | collective-permute-start | bytes 172040 | tf_op jit(solution)/shard_map/ppermute | solution.py:35
  112.0 60.0 %collective-permute-start.15 = (bf16[96,6656]{1,0:T(8,128)(2,1)}, bf16[96,6656]{1,0:T(8,128)(2,1)}, u32[]{:S(2)}, u32[]{:S(2)}) collective-permute-start(bf16[96,6656]{1,0:T(8,128)(2,1)} %collective-permute-done.6.refs_2_), channel_id=1, source_target_pairs={{1,0},{2,3},{5,4},{6,7},{9,8},{10,11},{13,12},{14,15},{17,16},{18,... | collective-permute-start | bytes 3833864 | tf_op jit(solution)/shard_map/ppermute | solution.py:113
  116.7 6.0 %collective-permute-start.17 = (bf16[2,4,28,256]{3,2,0,1:T(8,128)(2,1)S(1)}, bf16[2,4,28,256]{3,2,0,1:T(8,128)(2,1)S(1)}, u32[]{:S(2)}, u32[]{:S(2)}) collective-permute-start(bf16[2,4,28,256]{3,2,0,1:T(8,128)(2,1)S(1)} %pad_maximum_fusion.11), channel_id=1, source_target_pairs={{0,8},{4,12},{8,0},{12,4},{16,24},{20,28},{24,16},{28,20},{1,9},{5... | collective-permute-start | bytes 344072 | tf_op jit(solution)/shard_map/ppermute | solution.py:35
  124.1 8.2 %collective-permute-start.18 = (bf16[4,4,28,256]{3,2,0,1:T(8,128)(2,1)}, bf16[4,4,28,256]{3,2,0,1:T(8,128)(2,1)}, u32[]{:S(2)}, u32[]{:S(2)}) collective-permute-start(bf16[4,4,28,256]{3,2,0,1:T(8,128)(2,1)} %pad_maximum_fusion.6), channel_id=1, source_target_pairs={{0,16},{4,20},{8,24},{12,28},{16,0},{20,4},{24,8},{28,12},{1,17},{... | collective-permute-start | bytes 688136 | tf_op jit(solution)/shard_map/ppermute | solution.py:35
  126.2 24.4 %all-to-all-start = ((bf16[8,112,512]{2,1,0:T(8,128)(2,1)}), bf16[8,112,512]{2,1,0:T(8,128)(2,1)}, u32[]{:S(2)}, u32[]{:S(2)}) async-start(bf16[8,112,512]{2,1,0:T(8,128)(2,1)} %bitcast_dynamic-update-slice_fusion), calls=%async_computation | async-start | bytes 1835008 | tf_op jit(solution)/shard_map/all_to_all | solution.py:308
  132.3 39.8 %collective-permute-start.19 = (bf16[28,256]{1,0:T(8,128)(2,1)S(1)}, bf16[28,256]{1,0:T(8,128)(2,1)}, u32[]{:S(2)}, u32[]{:S(2)}) collective-permute-start(bf16[28,256]{1,0:T(8,128)(2,1)S(1)} %add_convert_fusion), channel_id=1, source_target_pairs={{0,1},{1,0},{2,3},{3,2},{4,5},{5,4},{6,7},{7,6},{8,9},{9,8},{10,11... | collective-permute-start | bytes 43016 | tf_op jit(solution)/shard_map/ppermute | solution.py:35
  146.5 25.6 %collective-permute-start.20 = (bf16[28,256]{1,0:T(8,128)(2,1)S(1)}, bf16[28,256]{1,0:T(8,128)(2,1)S(1)}, u32[]{:S(2)}, u32[]{:S(2)}) collective-permute-start(bf16[28,256]{1,0:T(8,128)(2,1)S(1)} %add_convert_fusion), channel_id=1, source_target_pairs={{0,2},{1,3},{2,0},{3,1},{4,6},{5,7},{6,4},{7,5},{8,10},{9,11},{10,... | collective-permute-start | bytes 43016 | tf_op jit(solution)/shard_map/ppermute | solution.py:35
  147.4 24.7 %collective-permute-start.21 = (bf16[28,256]{1,0:T(8,128)(2,1)S(1)}, bf16[28,256]{1,0:T(8,128)(2,1)S(1)}, u32[]{:S(2)}, u32[]{:S(2)}) collective-permute-start(bf16[28,256]{1,0:T(8,128)(2,1)S(1)} %add_convert_fusion), channel_id=1, source_target_pairs={{0,3},{1,2},{2,1},{3,0},{4,7},{5,6},{6,5},{7,4},{8,11},{9,10},{10,... | collective-permute-start | bytes 43016 | tf_op jit(solution)/shard_map/ppermute | solution.py:35
  177.2 4.9 %collective-permute-start.31 = (bf16[2,112,256]{2,1,0:T(8,128)(2,1)S(1)}, bf16[2,112,256]{2,1,0:T(8,128)(2,1)S(1)}, u32[]{:S(2)}, u32[]{:S(2)}) collective-permute-start(bf16[2,112,256]{2,1,0:T(8,128)(2,1)S(1)} %pad_maximum_fusion.12), channel_id=1, source_target_pairs={{0,16},{4,20},{8,24},{12,28},{16,0},{20,4},{24,8},{28,12},{1,17},{... | collective-permute-start | bytes 344072 | tf_op jit(solution)/shard_map/ppermute | solution.py:35
  183.4 6.7 %collective-permute-start.32 = (bf16[4,112,256]{2,1,0:T(8,128)(2,1)}, bf16[4,112,256]{2,1,0:T(8,128)(2,1)}, u32[]{:S(2)}, u32[]{:S(2)}) collective-permute-start(bf16[4,112,256]{2,1,0:T(8,128)(2,1)} %pad_maximum_fusion.10), channel_id=1, source_target_pairs={{0,4},{4,0},{8,12},{12,8},{16,20},{20,16},{24,28},{28,24},{1,5},{5... | collective-permute-start | bytes 688136 | tf_op jit(solution)/shard_map/ppermute | solution.py:35
  184.6 44.0 %collective-permute-start.25 = (bf16[64,4992]{1,0:T(8,128)(2,1)S(1)}, bf16[64,4992]{1,0:T(8,128)(2,1)S(1)}, u32[]{:S(2)}, u32[]{:S(2)}) collective-permute-start(bf16[64,4992]{1,0:T(8,128)(2,1)S(1)} %bitcast.140), channel_id=1, source_target_pairs={{0,2},{1,3},{2,0},{3,1},{4,6},{5,7},{6,4},{7,5},{8,10},{9,11},{10,... | collective-permute-start | bytes 1916936 | tf_op jit(solution)/shard_map/ppermute | solution.py:35
  185.2 43.4 %collective-permute-start.26 = (bf16[64,4992]{1,0:T(8,128)(2,1)S(1)}, bf16[64,4992]{1,0:T(8,128)(2,1)S(1)}, u32[]{:S(2)}, u32[]{:S(2)}) collective-permute-start(bf16[64,4992]{1,0:T(8,128)(2,1)S(1)} %bitcast.141), channel_id=1, source_target_pairs={{0,1},{1,0},{2,3},{3,2},{4,5},{5,4},{6,7},{7,6},{8,9},{9,8},{10,11... | collective-permute-start | bytes 1916936 | tf_op jit(solution)/shard_map/ppermute | solution.py:35
  187.8 40.8 %collective-permute-start.27 = (bf16[64,4992]{1,0:T(8,128)(2,1)S(1)}, bf16[64,4992]{1,0:T(8,128)(2,1)S(1)}, u32[]{:S(2)}, u32[]{:S(2)}) collective-permute-start(bf16[64,4992]{1,0:T(8,128)(2,1)S(1)} %bitcast.142), channel_id=1, source_target_pairs={{1,2},{2,1},{5,6},{6,5},{9,10},{10,9},{13,14},{14,13},{17,18},{18,... | collective-permute-start | bytes 1916936 | tf_op jit(solution)/shard_map/ppermute | solution.py:102
  188.5 38.9 %collective-permute-start.29 = (f32[512,256]{1,0:T(8,128)}, f32[512,256]{1,0:T(8,128)S(1)}, u32[]{:S(2)}, u32[]{:S(2)}) collective-permute-start(f32[512,256]{1,0:T(8,128)} %convolution_multiply_fusion.1), channel_id=1, source_target_pairs={{0,16},{4,20},{8,24},{12,28},{16,0},{20,4},{24,8},{28,12},{1,17},{... | collective-permute-start | bytes 1572872 | tf_op jit(solution)/shard_map/ppermute | solution.py:35
  190.1 44.4 %collective-permute-start.28 = (bf16[64,6656]{1,0:T(8,128)(2,1)S(1)}, bf16[64,6656]{1,0:T(8,128)(2,1)S(1)}, u32[]{:S(2)}, u32[]{:S(2)}) collective-permute-start(bf16[64,6656]{1,0:T(8,128)(2,1)S(1)} %collective-permute-done.3.refs_2_), channel_id=1, source_target_pairs={{1,0},{2,3},{5,4},{6,7},{9,8},{10,11},{13,12},{14,15},{17,16},{18,... | collective-permute-start | bytes 2555912 | tf_op jit(solution)/shard_map/ppermute | solution.py:113
  234.5 32.1 %collective-permute-start.35 = (bf16[192,4096]{1,0:T(8,128)(2,1)S(1)}, bf16[192,4096]{1,0:T(8,128)(2,1)S(1)}, u32[]{:S(2)}, u32[]{:S(2)}) collective-permute-start(bf16[192,4096]{1,0:T(8,128)(2,1)S(1)} %get-tuple-element.128), channel_id=1, source_target_pairs={{0,4},{4,0},{8,12},{12,8},{16,20},{20,16},{24,28},{28,24},{1,5},{5... | collective-permute-start | bytes 4718600 | tf_op jit(solution)/shard_map/ppermute | solution.py:35
  235.5 52.3 %collective-permute-start.22 = (bf16[64,1664]{1,0:T(8,128)(2,1)S(1)}, bf16[64,1664]{1,0:T(8,128)(2,1)S(1)}, u32[]{:S(2)}, u32[]{:S(2)}) collective-permute-start(bf16[64,1664]{1,0:T(8,128)(2,1)S(1)} %bitcast.144), channel_id=1, source_target_pairs={{0,2},{1,3},{2,0},{3,1},{4,6},{5,7},{6,4},{7,5},{8,10},{9,11},{10,... | collective-permute-start | bytes 638984 | tf_op jit(solution)/shard_map/ppermute | solution.py:35
  235.6 52.2 %collective-permute-start.23 = (bf16[64,1664]{1,0:T(8,128)(2,1)S(1)}, bf16[64,1664]{1,0:T(8,128)(2,1)S(1)}, u32[]{:S(2)}, u32[]{:S(2)}) collective-permute-start(bf16[64,1664]{1,0:T(8,128)(2,1)S(1)} %bitcast.145), channel_id=1, source_target_pairs={{0,1},{1,0},{2,3},{3,2},{4,5},{5,4},{6,7},{7,6},{8,9},{9,8},{10,11... | collective-permute-start | bytes 638984 | tf_op jit(solution)/shard_map/ppermute | solution.py:35
  237.7 36.2 %collective-permute-start.34 = (f32[1024,256]{1,0:T(8,128)}, f32[1024,256]{1,0:T(8,128)}, u32[]{:S(2)}, u32[]{:S(2)}) collective-permute-start(f32[1024,256]{1,0:T(8,128)} %pad_maximum_fusion.2), channel_id=1, source_target_pairs={{0,8},{4,12},{8,0},{12,4},{16,24},{20,28},{24,16},{28,20},{1,9},{5... | collective-permute-start | bytes 3145736 | tf_op jit(solution)/shard_map/ppermute | solution.py:35
  267.3 10.8 %collective-permute-start.36 = (bf16[2,48,2048]{2,1,0:T(8,128)(2,1)S(1)}, bf16[2,48,2048]{2,1,0:T(8,128)(2,1)S(1)}, u32[]{:S(2)}, u32[]{:S(2)}) collective-permute-start(bf16[2,48,2048]{2,1,0:T(8,128)(2,1)S(1)} %pad_maximum_fusion.4), channel_id=1, source_target_pairs={{0,8},{4,12},{8,0},{12,4},{16,24},{20,28},{24,16},{28,20},{1,9},{5... | collective-permute-start | bytes 1179656 | tf_op jit(solution)/shard_map/ppermute | solution.py:35
  267.9 10.4 %collective-permute-start.38 = (bf16[2,48,2048]{2,1,0:T(8,128)(2,1)S(1)}, bf16[2,48,2048]{2,1,0:T(8,128)(2,1)S(1)}, u32[]{:S(2)}, u32[]{:S(2)}) collective-permute-start(bf16[2,48,2048]{2,1,0:T(8,128)(2,1)S(1)} %slice.271), channel_id=1, source_target_pairs={{0,16},{4,20},{8,24},{12,28},{16,0},{20,4},{24,8},{28,12},{1,17},{... | collective-permute-start | bytes 1179656 | tf_op jit(solution)/shard_map/ppermute | solution.py:35
  273.9 13.9 %collective-permute-start.24 = (bf16[64,1664]{1,0:T(8,128)(2,1)S(1)}, bf16[64,1664]{1,0:T(8,128)(2,1)S(1)}, u32[]{:S(2)}, u32[]{:S(2)}) collective-permute-start(bf16[64,1664]{1,0:T(8,128)(2,1)S(1)} %bitcast.146), channel_id=1, source_target_pairs={{1,2},{2,1},{5,6},{6,5},{9,10},{10,9},{13,14},{14,13},{17,18},{18,... | collective-permute-start | bytes 638984 | tf_op jit(solution)/shard_map/ppermute | solution.py:102
  278.4 5.7 %collective-permute-start.37 = (bf16[1,48,2048]{2,1,0:T(8,128)(2,1)S(1)}, bf16[1,48,2048]{2,1,0:T(8,128)(2,1)S(1)}, u32[]{:S(2)}, u32[]{:S(2)}) collective-permute-start(bf16[1,48,2048]{2,1,0:T(8,128)(2,1)S(1)} %get-tuple-element.169), channel_id=1, source_target_pairs={{0,16},{4,20},{8,24},{12,28},{16,0},{20,4},{24,8},{28,12},{1,17},{... | collective-permute-start | bytes 589832 | tf_op jit(solution)/shard_map/ppermute | solution.py:35
  280.0 5.7 %collective-permute-start.39 = (bf16[1,48,2048]{2,1,0:T(8,128)(2,1)S(1)}, bf16[1,48,2048]{2,1,0:T(8,128)(2,1)S(1)}, u32[]{:S(2)}, u32[]{:S(2)}) collective-permute-start(bf16[1,48,2048]{2,1,0:T(8,128)(2,1)S(1)} %get-tuple-element.170), channel_id=1, source_target_pairs={{0,8},{4,12},{8,0},{12,4},{16,24},{20,28},{24,16},{28,20},{1,9},{5... | collective-permute-start | bytes 589832 | tf_op jit(solution)/shard_map/ppermute | solution.py:35
  284.1 15.5 %collective-permute-start.33 = (bf16[64,4992]{1,0:T(8,128)(2,1)S(1)}, bf16[64,4992]{1,0:T(8,128)(2,1)S(1)}, u32[]{:S(2)}, u32[]{:S(2)}) collective-permute-start(bf16[64,4992]{1,0:T(8,128)(2,1)S(1)} %collective-permute-done.25.refs_2_), channel_id=1, source_target_pairs={{1,0},{2,3},{5,4},{6,7},{9,8},{10,11},{13,12},{14,15},{17,16},{18,... | collective-permute-start | bytes 1916936 | tf_op jit(solution)/shard_map/ppermute | solution.py:113
  299.7 47.6 %collective-permute-start.46 = (f32[2048,256]{1,0:T(8,128)}, f32[2048,256]{1,0:T(8,128)}, u32[]{:S(2)}, u32[]{:S(2)}) collective-permute-start(f32[2048,256]{1,0:T(8,128)} %pad_maximum_fusion.1), channel_id=1, source_target_pairs={{0,4},{4,0},{8,12},{12,8},{16,20},{20,16},{24,28},{28,24},{1,5},{5... | collective-permute-start | bytes 6291464 | tf_op jit(solution)/shard_map/ppermute | solution.py:35
  300.2 51.9 %collective-permute-start.40 = (bf16[64,1664]{1,0:T(8,128)(2,1)S(1)}, bf16[64,1664]{1,0:T(8,128)(2,1)S(1)}, u32[]{:S(2)}, u32[]{:S(2)}) collective-permute-start(bf16[64,1664]{1,0:T(8,128)(2,1)S(1)} %collective-permute-done.22.refs_2_), channel_id=1, source_target_pairs={{1,0},{2,3},{5,4},{6,7},{9,8},{10,11},{13,12},{14,15},{17,16},{18,... | collective-permute-start | bytes 638984 | tf_op jit(solution)/shard_map/ppermute | solution.py:113
  305.4 26.6 %collective-permute-start.42 = (bf16[2,32,2048]{2,1,0:T(8,128)(2,1)S(1)}, bf16[2,32,2048]{2,1,0:T(8,128)(2,1)S(1)}, u32[]{:S(2)}, u32[]{:S(2)}) collective-permute-start(bf16[2,32,2048]{2,1,0:T(8,128)(2,1)S(1)} %pad_maximum_fusion.7), channel_id=1, source_target_pairs={{0,8},{4,12},{8,0},{12,4},{16,24},{20,28},{24,16},{28,20},{1,9},{5... | collective-permute-start | bytes 786440 | tf_op jit(solution)/shard_map/ppermute | solution.py:35
  306.9 25.1 %collective-permute-start.44 = (bf16[2,32,2048]{2,1,0:T(8,128)(2,1)S(1)}, bf16[2,32,2048]{2,1,0:T(8,128)(2,1)S(1)}, u32[]{:S(2)}, u32[]{:S(2)}) collective-permute-start(bf16[2,32,2048]{2,1,0:T(8,128)(2,1)S(1)} %slice.282), channel_id=1, source_target_pairs={{0,16},{4,20},{8,24},{12,28},{16,0},{20,4},{24,8},{28,12},{1,17},{... | collective-permute-start | bytes 786440 | tf_op jit(solution)/shard_map/ppermute | solution.py:35
  333.2 12.0 %collective-permute-start.43 = (bf16[1,32,2048]{2,1,0:T(8,128)(2,1)S(1)}, bf16[1,32,2048]{2,1,0:T(8,128)(2,1)S(1)}, u32[]{:S(2)}, u32[]{:S(2)}) collective-permute-start(bf16[1,32,2048]{2,1,0:T(8,128)(2,1)S(1)} %get-tuple-element.173), channel_id=1, source_target_pairs={{0,16},{4,20},{8,24},{12,28},{16,0},{20,4},{24,8},{28,12},{1,17},{... | collective-permute-start | bytes 393224 | tf_op jit(solution)/shard_map/ppermute | solution.py:35
  333.8 11.4 %collective-permute-start.45 = (bf16[1,32,2048]{2,1,0:T(8,128)(2,1)S(1)}, bf16[1,32,2048]{2,1,0:T(8,128)(2,1)S(1)}, u32[]{:S(2)}, u32[]{:S(2)}) collective-permute-start(bf16[1,32,2048]{2,1,0:T(8,128)(2,1)S(1)} %get-tuple-element.174), channel_id=1, source_target_pairs={{0,8},{4,12},{8,0},{12,4},{16,24},{20,28},{24,16},{28,20},{1,9},{5... | collective-permute-start | bytes 393224 | tf_op jit(solution)/shard_map/ppermute | solution.py:35
  369.8 8.4 %collective-permute-start.48 = (bf16[2,32,2048]{2,1,0:T(8,128)(2,1)S(1)}, bf16[2,32,2048]{2,1,0:T(8,128)(2,1)S(1)}, u32[]{:S(2)}, u32[]{:S(2)}) collective-permute-start(bf16[2,32,2048]{2,1,0:T(8,128)(2,1)S(1)} %pad_maximum_fusion.9), channel_id=1, source_target_pairs={{0,8},{4,12},{8,0},{12,4},{16,24},{20,28},{24,16},{28,20},{1,9},{5... | collective-permute-start | bytes 786440 | tf_op jit(solution)/shard_map/ppermute | solution.py:35
  371.3 8.1 %collective-permute-start.50 = (bf16[2,32,2048]{2,1,0:T(8,128)(2,1)S(1)}, bf16[2,32,2048]{2,1,0:T(8,128)(2,1)S(1)}, u32[]{:S(2)}, u32[]{:S(2)}) collective-permute-start(bf16[2,32,2048]{2,1,0:T(8,128)(2,1)S(1)} %slice.293), channel_id=1, source_target_pairs={{0,16},{4,20},{8,24},{12,28},{16,0},{20,4},{24,8},{28,12},{1,17},{... | collective-permute-start | bytes 786440 | tf_op jit(solution)/shard_map/ppermute | solution.py:35
  379.4 9.1 %collective-permute-start.49 = (bf16[1,32,2048]{2,1,0:T(8,128)(2,1)S(1)}, bf16[1,32,2048]{2,1,0:T(8,128)(2,1)S(1)}, u32[]{:S(2)}, u32[]{:S(2)}) collective-permute-start(bf16[1,32,2048]{2,1,0:T(8,128)(2,1)S(1)} %get-tuple-element.171), channel_id=1, source_target_pairs={{0,16},{4,20},{8,24},{12,28},{16,0},{20,4},{24,8},{28,12},{1,17},{... | collective-permute-start | bytes 393224 | tf_op jit(solution)/shard_map/ppermute | solution.py:35
  381.0 7.5 %collective-permute-start.51 = (bf16[1,32,2048]{2,1,0:T(8,128)(2,1)S(1)}, bf16[1,32,2048]{2,1,0:T(8,128)(2,1)S(1)}, u32[]{:S(2)}, u32[]{:S(2)}) collective-permute-start(bf16[1,32,2048]{2,1,0:T(8,128)(2,1)S(1)} %get-tuple-element.172), channel_id=1, source_target_pairs={{0,8},{4,12},{8,0},{12,4},{16,24},{20,28},{24,16},{28,20},{1,9},{5... | collective-permute-start | bytes 393224 | tf_op jit(solution)/shard_map/ppermute | solution.py:35
  (24 other events, 233.0 us)

commit v3 on v2

v3 whole, which is shorter than its diff:
```python
import functools

import jax
import jax.numpy as jnp
from jax import lax
from jax.experimental import pallas as pl
from jax.experimental.pallas import tpu as pltpu
from jax.sharding import PartitionSpec as P

adapter_scale = 2.0
piece_rows = 32
weight_rows = 512
vmem_bytes = 40 * 2**20
light = pl.CostEstimate(flops=0, bytes_accessed=2**16, transcendentals=0)


def contract_trailing_axis(left, right):
    return lax.dot_general(
        left, right, (((1,), (1,)), ((), ())), preferred_element_type=jnp.float32
    )


def contract_first(left, right):
    return lax.dot_general(
        left, right, (((0,), (0,)), ((), ())), preferred_element_type=jnp.float32
    )


def bits_of(axis):
    size = lax.axis_size(axis)
    return [1 << i for i in range(size.bit_length() - 1)]


def swap(value, axis, bit):
    size = lax.axis_size(axis)
    return lax.ppermute(value, axis, [(i, i ^ bit) for i in range(size)])


def scatter_small(value, axis):
    me = lax.axis_index(axis)
    for bit in reversed(bits_of(axis)):
        pair = value.reshape(2, value.shape[0] // 2, value.shape[1])
        mine = ((me & bit) != 0).astype(jnp.int32)
        kept = lax.dynamic_index_in_dim(pair, mine, 0, keepdims=False)
        sent = lax.dynamic_index_in_dim(pair, 1 - mine, 0, keepdims=False)
        value = kept + swap(sent, axis, bit)
    return value


def scatter_direct(value, axis):
    size = lax.axis_size(axis)
    me = lax.axis_index(axis)
    rows = value.shape[0] // size
    blocks = value.reshape(size, rows, value.shape[1])
    found = [
        swap(lax.dynamic_index_in_dim(blocks, me ^ p, 0, keepdims=False), axis, p)
        for p in range(1, size)
    ]
    return lax.dynamic_index_in_dim(blocks, me, 0, keepdims=False), found


def gather_direct(value, axis):
    return [value] + [swap(value, axis, p) for p in range(1, lax.axis_size(axis))]


def by_index(blocks, axis):
    value = jnp.stack(blocks)
    me = lax.axis_index(axis)
    for bit in bits_of(axis):
        pair = value.reshape(value.shape[0] // (2 * bit), 2, bit, *value.shape[1:])
        value = jnp.where((me & bit) != 0, pair[:, ::-1], pair).reshape(value.shape)
    return value


def gather_relative(value, axis, order):
    value = value[None]
    for bit in order:
        value = jnp.concatenate([value, swap(value, axis, bit)], axis=0)
    return value


def gather_ordered(value, axis, order):
    me = lax.axis_index(axis)
    for bit in order:
        other = swap(value, axis, bit)
        upper = (me & bit) != 0
        value = jnp.concatenate(
            [jnp.where(upper, other, value), jnp.where(upper, value, other)], axis=0
        )
    return value


def pass_kernel(me, tokens, weight, *refs, owners, rows, final, summed):
    product = contract_trailing_axis(tokens[...], weight[...])
    if summed:
        product = product + refs[0][...]
        refs = refs[1:]
    if not final:
        refs[0][...] = product
        return
    kept, sent = refs
    for core in range(2):

        @pl.when((me[0] & 1) == core)
        def _():
            for owner in range(owners):
                place = (owner ^ me[0]) >> 1
                part = product[owner * rows : (owner + 1) * rows]
                if owner % 2 == core:
                    kept[place] = part
                else:
                    sent[place] = part.astype(jnp.bfloat16)


def weight_pass(me, tokens, weight, depth_block, owners, final, before=None):
    total, depth = tokens.shape
    width = weight.shape[0]
    rows = total // owners
    step = min(weight_rows, width)
    column = lambda i, *_: (0, i)
    operands = [tokens, weight]
    in_specs = [
        pl.BlockSpec((total, depth), lambda i, *_: (0, 0), pipeline_mode=pl.Buffered(1)),
        pl.BlockSpec((step, depth), lambda i, *_: (i, depth_block)),
    ]
    if before is not None:
        operands.append(before)
        in_specs.append(pl.BlockSpec((total, step), column))
    if final:
        half = (owners // 2, rows, width)
        out_shape = [
            jax.ShapeDtypeStruct(half, jnp.float32),
            jax.ShapeDtypeStruct(half, jnp.bfloat16),
        ]
        out_specs = [pl.BlockSpec((owners // 2, rows, step), lambda i, *_: (0, 0, i))] * 2
    else:
        out_shape = [jax.ShapeDtypeStruct((total, width), jnp.float32)]
        out_specs = [pl.BlockSpec((total, step), column)]
    return pl.pallas_call(
        functools.partial(
            pass_kernel, owners=owners, rows=rows, final=final, summed=before is not None
        ),
        grid_spec=pltpu.PrefetchScalarGridSpec(
            num_scalar_prefetch=1,
            grid=(width // step,),
            in_specs=in_specs,
            out_specs=out_specs,
        ),
        out_shape=out_shape,
        compiler_params=pltpu.CompilerParams(vmem_limit_bytes=vmem_bytes),
        cost_estimate=light,
        name="weight_pass",
    )(me, *operands)


def factor_kernel(*refs, count, scale):
    acts, tokens, out = refs[:count], refs[count : 2 * count], refs[-1]
    out[...] = scale * sum(
        jnp.dot(a[...], t[...], preferred_element_type=jnp.float32) for a, t in zip(acts, tokens)
    )


def factor_gradient(acts, tokens, places, scale, depth, step, first, blocks, into=None):
    rank = acts[0].shape[0]
    whole = lambda i: (0, 0)
    in_specs = [pl.BlockSpec(a.shape, whole, pipeline_mode=pl.Buffered(1)) for a in acts]
    in_specs += [
        pl.BlockSpec((t.shape[0], step), lambda i, place=place: (0, first + i - place))
        for t, place in zip(tokens, places)
    ]
    operands = [*acts, *tokens]
    aliases = {}
    if into is not None:
        aliases = {len(operands): 0}
        operands.append(into)
        in_specs.append(pl.BlockSpec(memory_space=pl.ANY))
    return pl.pallas_call(
        functools.partial(factor_kernel, count=len(acts), scale=scale),
        grid=(blocks,),
        in_specs=in_specs,
        out_specs=pl.BlockSpec((rank, step), lambda i: (0, first + i)),
        out_shape=jax.ShapeDtypeStruct((rank, depth), jnp.float32),
        input_output_aliases=aliases,
        compiler_params=pltpu.CompilerParams(vmem_limit_bytes=vmem_bytes),
        cost_estimate=light,
        name="factor_gradient",
    )(*operands)


def scatter_sum(kept, sent, axis):
    bits = bits_of(axis)
    live = kept + swap(sent, axis, 1)
    half = live.shape[2] // 2
    done = []
    for side, order in ((0, bits[:-1]), (1, bits[:-1][::-1])):
        part = {p: live[p, :, side * half : (side + 1) * half] for p in range(live.shape[0])}
        for bit in order:
            stay = [p for p in part if not p & bit]
            away = jnp.stack([part[p ^ bit].astype(jnp.bfloat16) for p in stay])
            got = swap(away, axis, 2 * bit)
            part = {p: part[p] + got[i] for i, p in enumerate(stay)}
        done.append(part[0])
    return done


def hold(*groups):
    leaves, tree = jax.tree.flatten(groups)
    return jax.tree.unflatten(tree, lax.optimization_barrier(leaves))


def cut_rows(owner_rows, depth):
    sizes = []
    left = owner_rows
    while left:
        sizes.insert(0, min(left, piece_rows))
        left -= sizes[0]
    if len(sizes) > 2 and sizes[0] < piece_rows:
        sizes = [sizes[0] + sizes[1], *sizes[2:]]
    cuts = max(c for c in (4, 2, 1) if depth % (c * 128) == 0)
    tail = depth // cuts
    pieces = []
    start = 0
    for rows in sizes:
        pieces.append((start, rows, 0, depth))
        start += rows
    if cuts > 1:
        start, rows, _, _ = pieces.pop()
        pieces += [(start, rows, 0, depth - tail), (start, rows, depth - tail, depth)]
    return pieces


def shards(inputs, grad_out, w_base, adapter_down_matrix, b_factor):
    owner_rows = inputs.shape[0]
    owners = lax.axis_size("wide")
    me_wide = lax.axis_index("wide")
    adapter_matrix = adapter_scale / (owner_rows * owners)
    share = grad_out.shape[0] // owner_rows
    rank = b_factor.shape[0]
    depth = grad_out.shape[1]
    wide_bits = bits_of("wide")
    pieces = cut_rows(owner_rows, depth)
    count = len(pieces)
    me = me_wide.astype(jnp.int32).reshape(1)

    def gather(source, piece):
        start, rows, low, high = piece
        own = source.reshape(share, owner_rows, depth)
        block = own[:, start : start + rows, low:high].reshape(share * rows, high - low)
        return lax.all_gather(block, "narrow", axis=0, tiled=True)

    tokens = {0: gather(grad_out, pieces[0])}

    act_own, act_others = scatter_direct(
        jnp.dot(inputs, adapter_down_matrix, preferred_element_type=jnp.float32), "narrow"
    )
    low_small = scatter_small(contract_trailing_axis(grad_out, b_factor), "wide").astype(jnp.bfloat16)
    low_small, act_own, act_others, grad_out = hold(low_small, act_own, act_others, grad_out)
    for i in range(1, count):
        tokens[i] = gather(grad_out, pieces[i])
    low_blocks = gather_direct(low_small, "narrow")
    act_blocks = gather_direct((act_own + sum(act_others)).astype(jnp.bfloat16), "narrow")

    low_wide = gather_ordered(by_index(low_blocks, "narrow")[None], "wide", wide_bits)
    low_rank_all = jnp.swapaxes(low_wide, 0, 1).reshape(owner_rows * owners, rank)
    low_rank_own = lax.dynamic_slice_in_dim(low_rank_all, me_wide * owner_rows, owner_rows)
    low_term = adapter_scale * contract_trailing_axis(low_rank_own, adapter_down_matrix)
    shares = inputs.reshape(owner_rows, owners, -1)
    flipped = [
        sum(bit for i, bit in enumerate(wide_bits) if w & wide_bits[len(wide_bits) - 1 - i])
        for w in range(owners)
    ]
    columns = lax.all_to_all(
        jnp.stack([shares[:, f] for f in flipped], axis=0), "wide", split_axis=0, concat_axis=0
    ).reshape(owner_rows * owners, -1)
    grad_a = adapter_matrix * contract_first(columns, low_rank_all)
    grad_a_steps = wide_bits[::-1]

    act_rows = by_index(act_blocks, "narrow").reshape(owner_rows, rank)
    acts = gather_ordered(act_rows[None], "wide", wide_bits)
    turned = []
    for start, rows, _, _ in pieces:
        turned.append(acts[:, start : start + rows].reshape(owners * rows, rank).T)

    sums, results, grad_b = {}, {}, None
    tail = pieces[-1][3] - pieces[-1][2]

    def run_pass(i):
        _, _, low, high = pieces[i]
        final = high == depth
        before = None if low == 0 else sums.pop(i - 1)[0]
        sums[i] = weight_pass(me, tokens[i], w_base, low // (high - low), owners, final, before)

    def finish(i):
        start, rows, _, _ = pieces[i]
        sides = scatter_sum(*sums.pop(i), "wide")
        half = sides[0].shape[1]
        mine = low_term[start : start + rows]
        results[i] = jnp.concatenate(
            [
                (side + mine[:, j * half : (j + 1) * half]).astype(jnp.bfloat16)
                for j, side in enumerate(sides)
            ],
            axis=1,
        )

    def factor(low, high, into):
        used = [i for i, piece in enumerate(pieces) if piece[2] <= low and piece[3] >= high]
        return factor_gradient(
            [turned[i] for i in used],
            [tokens[i] for i in used],
            [pieces[i][2] // tail for i in used],
            adapter_matrix,
            depth,
            tail,
            low // tail,
            (high - low) // tail,
            into,
        )

    for i in range(count):
        tokens[i], grad_a, turned, sums, grad_b, results, low_term = hold(
            tokens[i], grad_a, turned, sums, grad_b, results, low_term
        )
        if i and pieces[i - 1][3] == depth:
            finish(i - 1)
        run_pass(i)
        if i == count - 2 and tail < depth:
            grad_b = factor(0, depth - tail, None)
        if grad_a_steps:
            grad_a = gather_ordered(grad_a, "wide", grad_a_steps[:1])
            grad_a_steps = grad_a_steps[1:]
    grad_a = gather_ordered(grad_a, "wide", grad_a_steps)
    grad_b = factor(depth - tail, depth, grad_b)
    finish(count - 1)
    return (jnp.concatenate([results[i] for i in sorted(results)], axis=0), grad_a, grad_b)


def solution(mesh):
    return jax.shard_map(
        shards,
        mesh=mesh,
        in_specs=(
            P("wide", "narrow"),
            P("narrow", "wide"),
            P("narrow", "wide"),
            P("narrow", None),
            P(None, "wide"),
        ),
        out_specs=(P("wide", "narrow"), P("narrow", None), P(None, "wide")),
        check_vma=False,
    )
```

time: 393 us -> 338 us (0.86)
  starting transfers between devices: 73.4 us -> 45.7 us
  other arithmetic: 37.8 us -> 19.4 us
  blocking collectives: 0 us -> 18 us
  Pallas kernels: 100 us -> 84.8 us
  matrix products: 24.5 us -> 9.8 us
  between operations: 1.36 us -> 14.5 us
  waiting for transfers between devices: 133 us -> 120 us
  local copies, waits for them, and re-layouts: 20.6 us -> 25 us
    all_gather x0 -> x3, waiting for transfers between devices: none -> 71.2 us  [gather(): return lax.all_gather(block, 'narrow', axis=0, tiled=True)]
    ppermute x44 -> x36, waiting for transfers between devices: 115 us -> 48.6 us  [swap(): return lax.ppermute(value, axis, [(i, i ^ bit) for i in range(size)])]
    ppermute x44 -> x36, starting transfers between devices: 59.8 us -> 41.1 us  [swap(): return lax.ppermute(value, axis, [(i, i ^ bit) for i in range(size)])]
    all_gather x0 -> x1, blocking collectives: none -> 18 us  [gather(): return lax.all_gather(block, 'narrow', axis=0, tiled=True)]
    ppermute x8 -> x0, waiting for transfers between devices: 17.8 us -> none  [the longest x4 17.8 us: last_hops(): onward = lax.ppermute(far, axis, [(1, 0), (2, 3)])]
    pallas_call x4 -> x6, Pallas kernels: 100 us -> 84.8 us  [the longest x4 77.3 us: weight_pass(): pl.pallas_call(functools.partial(pass_kernel, owners=owners, rows=rows, f...]
    dot_general x4 -> x1, matrix products: 14.8 us -> 2.45 us  [contract_first(): lax.dot_general(left, right, (((0,), (0,)), ((), ())), preferred_element_...]
    ppermute x8 -> x0, starting transfers between devices: 9.29 us -> none  [the longest x4 5.52 us: last_hops(): onward = lax.ppermute(far, axis, [(1, 0), (2, 3)])]
  transfers between devices with their start and end apart: 53 -> 40, of which waited for: 21 -> 25; matrix products, arithmetic and copies ran while one was open for 19% -> 11% of each run, Pallas kernels for 22% -> 22%
where the time goes in v3:
time: 338 us; the launch traced here: 337 us
  waiting for transfers between devices  120 us (36%)
  Pallas kernels  84.8 us (25%)
  starting transfers between devices  45.7 us (14%)
  local copies, waits for them, and re-layouts  25 us (7%)
  other arithmetic  19.4 us (6%)
  blocking collectives  18 us (5%)
  between operations  14.5 us (4%)
  matrix products  9.8 us (3%)
    pallas_call x4, Pallas kernels, weight_pass(): pl.pallas_call(functools.partial(pass_kernel, owners=owners, rows=rows, f...  77.3 us
    all_gather x3, waiting for transfers between devices, gather(): return lax.all_gather(block, 'narrow', axis=0, tiled=True)  71.2 us
    ppermute x36, waiting for transfers between devices, swap(): return lax.ppermute(value, axis, [(i, i ^ bit) for i in range(size)])  48.6 us
    ppermute x36, starting transfers between devices, swap(): return lax.ppermute(value, axis, [(i, i ^ bit) for i in range(size)])  41.1 us
    all_gather x1, blocking collectives, gather(): return lax.all_gather(block, 'narrow', axis=0, tiled=True)  18 us
    unnamed x54, local copies, waits for them, and re-layouts  12.2 us
    slice x4, local copies, waits for them, and re-layouts, gather(): own[:, start:start + rows, low:high].reshape(share * rows, high - low)  7.79 us
    pallas_call x2, Pallas kernels, factor_gradient(): pl.pallas_call(functools.partial(factor_kernel, count=len(acts), scale=sc...  7.52 us
  transfers between devices with their start and end apart: 40, of which 25 were waited for; matrix products, arithmetic and copies ran while one was open for 11% of the time, Pallas kernels for 22%

profile of v3, /device:TPU:0, one launch (start us, length us, event | category | flops | bytes accessed | tf_op | source)
XLA Modules:
  0.0 337.0 jit_solution(11665626642562118381)
XLA Ops:
  7.2 2.6 slice.256
  9.9 3.0 fusion.44
  13.6 3.0 collective-permute-start
  16.7 2.3 fusion.45
  19.1 1.6 collective-permute-start.3
  20.7 2.6 collective-permute-start.4
  23.9 1.7 fusion.43
  28.9 1.6 collective-permute-start.1
  31.1 2.0 collective-permute-done.1
  34.5 2.1 slice.255
  37.3 4.2 %all-to-all-start = ((bf16[8,112,512]{2,1,0:T(8,128)(2,1)}), bf16[8,112,512]{2,1,0:T(8,128)(2,1)}, u32[]{:S(2)}, u32[]{:S(2)}) async-start(bf16[8,112,512]{2,1,0:T(8,128)(2,1)} %bitcast_dynamic-update-slice_fusion), calls=%async_computation | async-start | bytes 1835008 | tf_op jit(solution)/shard_map/all_to_all | solution.py:272
  41.8 3.7 %collective-permute-start.8 = (bf16[28,256]{1,0:T(8,128)(2,1)S(1)}, bf16[28,256]{1,0:T(8,128)(2,1)S(1)}, u32[]{:S(2)}, u32[]{:S(2)}) collective-permute-start(bf16[28,256]{1,0:T(8,128)(2,1)S(1)} %fusion.35), channel_id=1, source_target_pairs={{0,3},{1,2},{2,1},{3,0},{4,7},{5,6},{6,5},{7,4},{8,11},{9,10},{10,... | collective-permute-start | bytes 43016 | tf_op jit(solution)/shard_map/ppermute | solution.py:36
  46.3 3.7 %collective-permute-start.14 = (bf16[28,256]{1,0:T(8,128)(2,1)S(1)}, bf16[28,256]{1,0:T(8,128)(2,1)S(1)}, u32[]{:S(2)}, u32[]{:S(2)}) collective-permute-start(bf16[28,256]{1,0:T(8,128)(2,1)S(1)} %add_convert_fusion), channel_id=1, source_target_pairs={{0,3},{1,2},{2,1},{3,0},{4,7},{5,6},{6,5},{7,4},{8,11},{9,10},{10,... | collective-permute-start | bytes 43016 | tf_op jit(solution)/shard_map/ppermute | solution.py:36
  50.7 2.0 collective-permute-done.7
  52.7 2.2 collective-permute-done.13
  54.9 1.9 collective-permute-done.12
  58.3 1.6 collective-permute-start.10
  60.5 4.2 %collective-permute-done.10 = bf16[2,4,28,256]{3,2,0,1:T(8,128)(2,1)S(1)} collective-permute-done((bf16[2,4,28,256]{3,2,0,1:T(8,128)(2,1)S(1)}, bf16[2,4,28,256]{3,2,0,1:T(8,128)(2,1)S(1)}, u32[]{:S(2)}, u32[]{:S(2)}) %collective-permute-start.10) | collective-permute-done | bytes 114720 | tf_op jit(solution)/shard_map/ppermute | solution.py:36
  68.3 5.7 %collective-permute-done.11 = bf16[4,4,28,256]{3,2,0,1:T(8,128)(2,1)S(1)} collective-permute-done((bf16[4,4,28,256]{3,2,0,1:T(8,128)(2,1)S(1)}, bf16[4,4,28,256]{3,2,0,1:T(8,128)(2,1)S(1)}, u32[]{:S(2)}, u32[]{:S(2)}) %collective-permute-start.11) | collective-permute-done | bytes 229408 | tf_op jit(solution)/shard_map/ppermute | solution.py:36
  75.0 1.7 collective-permute-done.17
  79.4 2.0 convolution_multiply_fusion
  81.4 2.4 convolution_multiply_fusion.1
  83.9 28.7 %all-gather.8.cloned.1.call-done.tokens.refs_3_ = bf16[384,6656]{1,0:T(8,128)(2,1)} async-done(((bf16[96,6656]{1,0:T(8,128)(2,1)}), bf16[384,6656]{1,0:T(8,128)(2,1)}) %all-gather.8.cloned.1.call-update) | async-done | bytes 5111824 | tf_op jit(solution)/shard_map/all_gather | solution.py:249
  114.0 2.4 copy-done.2
  116.4 26.5 %weight_pass.4 = (f32[4,48,4096]{2,1,0:T(8,128)S(1)}, bf16[4,48,4096]{2,1,0:T(8,128)(2,1)S(1)}) custom-call(s32[1]{0:T(128)} %bitcast.42.me, bf16[384,6656]{1,0:T(8,128)(2,1)S(1)} %copy-done.2, bf16[4096,6656]{1,0:T(8,128)(2,1)} %weight.7), custom_call_target="tpu_custom_call" | custom-call | bytes 65536 | tf_op jit(solution)/shard_map/weight_pass/pallas_call | solution.py:139
  146.6 34.2 %all-gather.6.cloned.1.call-done.tokens.refs_4_ = bf16[256,6656]{1,0:T(8,128)(2,1)} async-done(((bf16[64,6656]{1,0:T(8,128)(2,1)}), bf16[256,6656]{1,0:T(8,128)(2,1)}) %all-gather.6.cloned.1.call-update) | async-done | bytes 3407888 | tf_op jit(solution)/shard_map/all_gather | solution.py:249
  180.9 2.0 slice.254
  182.9 1.5 collective-permute-start.19
  184.6 3.1 fusion.39
  190.9 22.5 %weight_pass.5 = (f32[4,32,4096]{2,1,0:T(8,128)S(1)}, bf16[4,32,4096]{2,1,0:T(8,128)(2,1)S(1)}) custom-call(s32[1]{0:T(128)} %bitcast.42.me, bf16[256,6656]{1,0:T(8,128)(2,1)S(1)} %copy-done.3, bf16[4096,6656]{1,0:T(8,128)(2,1)} %weight.7), custom_call_target="tpu_custom_call" | custom-call | bytes 65536 | tf_op jit(solution)/shard_map/weight_pass/pallas_call | solution.py:139
  215.1 2.0 collective-permute-done.21
  217.2 1.5 collective-permute-start.22
  221.7 2.2 collective-permute-done.22
  227.2 8.3 %all-gather.4.cloned.1.call-done.tokens.refs_5_ = bf16[256,4992]{1,0:T(8,128)(2,1)} async-done(((bf16[64,4992]{1,0:T(8,128)(2,1)}), bf16[256,4992]{1,0:T(8,128)(2,1)}) %all-gather.4.cloned.1.call-update) | async-done | bytes 2555920 | tf_op jit(solution)/shard_map/all_gather | solution.py:249
  236.0 3.8 %collective-permute-done.26 = bf16[4,32,4096]{2,1,0:T(8,128)(2,1)S(1)} collective-permute-done((bf16[4,32,4096]{2,1,0:T(8,128)(2,1)}, bf16[4,32,4096]{2,1,0:T(8,128)(2,1)S(1)}, u32[]{:S(2)}, u32[]{:S(2)}) %collective-permute-start.26) | collective-permute-done | bytes 1048608 | tf_op jit(solution)/shard_map/ppermute | solution.py:36
  239.8 1.9 fusion.38
  241.9 1.5 collective-permute-start.27
  246.0 4.3 %collective-permute-done.27 = bf16[2,32,2048]{2,1,0:T(8,128)(2,1)S(1)} collective-permute-done((bf16[2,32,2048]{2,1,0:T(8,128)(2,1)S(1)}, bf16[2,32,2048]{2,1,0:T(8,128)(2,1)S(1)}, u32[]{:S(2)}, u32[]{:S(2)}) %collective-permute-start.27) | collective-permute-done | bytes 262176 | tf_op jit(solution)/shard_map/ppermute | solution.py:36
  251.5 1.5 collective-permute-start.28
  253.6 18.0 %all_gather.12.tokens.refs_5_ = bf16[256,1664]{1,0:T(8,128)(2,1)S(1)} all-gather(bf16[64,1664]{1,0:T(8,128)(2,1)S(1)} %bitcast.137), channel_id=1, replica_groups=mesh['wide'=8,'narrow'=4] {'narrow'}, dimensions={0}, use_global_device_ids=true | all-gather | bytes 1064960 | tf_op jit(solution)/shard_map/all_gather | solution.py:249
  271.7 18.4 %weight_pass.6.refs_0_ = f32[256,4096]{1,0:T(8,128)S(1)} custom-call(s32[1]{0:T(128)} %bitcast.42.me, bf16[256,4992]{1,0:T(8,128)(2,1)S(1)} %copy-done.5, bf16[4096,6656]{1,0:T(8,128)(2,1)} %weight.7), custom_call_target="tpu_custom_call" | custom-call | bytes 65536 | tf_op jit(solution)/shard_map/weight_pass/pallas_call | solution.py:139
  290.1 5.2 %factor_gradient.2.refs_6_ = f32[256,6656]{1,0:T(8,128)} custom-call(bf16[256,384]{1,0:T(8,128)(2,1)S(1)} %bitcast.122, bf16[256,256]{1,0:T(8,128)(2,1)S(1)} %bitcast.124, bf16[256,256]{1,0:T(8,128)(2,1)S(1)} %bitcast.126, bf16[384,6656]{1,0:T(8,128)(2,1)S(1)} %bitcast.121, bf16[256,6656]{1,0:T(8,128)(2,1)S(1)} %copy-done.3, bf16[256,4992]{1,0:T(8,128)(2,1)S(1)} %copy-done.5), custom_call_target="tpu_custom_call" | custom-call | bytes 65536 | tf_op jit(solution)/shard_map/factor_gradient/pallas_call | solution.py:177
  296.9 1.9 broadcast_select_fusion.1
  298.8 2.3 pad_maximum_fusion
  301.1 9.9 %weight_pass.7 = (f32[4,32,4096]{2,1,0:T(8,128)S(1)}, bf16[4,32,4096]{2,1,0:T(8,128)(2,1)S(1)}) custom-call(s32[1]{0:T(128)} %bitcast.42.me, bf16[256,1664]{1,0:T(8,128)(2,1)S(1)} %all_gather.12.tokens.refs_5_, bf16[4096,6656]{1,0:T(8,128)(2,1)} %weight.7, f32[256,4096]{1,0:T(8,128)S(1)} %weight_pass.6.refs_0_), custom_call_target="tpu_custom_call" | custom-call | bytes 65536 | tf_op jit(solution)/shard_map/weight_pass/pallas_call | solution.py:139
  311.1 2.6 collective-permute-done.31
  316.2 6.4 %collective-permute-done.32 = bf16[2,32,2048]{2,1,0:T(8,128)(2,1)S(1)} collective-permute-done((bf16[2,32,2048]{2,1,0:T(8,128)(2,1)S(1)}, bf16[2,32,2048]{2,1,0:T(8,128)(2,1)S(1)}, u32[]{:S(2)}, u32[]{:S(2)}) %collective-permute-start.32) | collective-permute-done | bytes 262176 | tf_op jit(solution)/shard_map/ppermute | solution.py:36
  325.1 2.3 factor_gradient.3
  (167 shorter events, 49.4 us)
Async XLA Ops:
  7.2 105.4 %all-gather.8.cloned.1.call-start = ((), (), s32[]{:S(2)}) async-start(), calls=%async_computation.3 | async-start | bytes 6389760 | tf_op jit(solution)/shard_map/all_gather | solution.py:249
  9.8 171.0 %all-gather.6.cloned.1.call-start = ((), (), s32[]{:S(2)}) async-start(), calls=%async_computation.2 | async-start | bytes 4259840 | tf_op jit(solution)/shard_map/all_gather | solution.py:249
  12.9 10.6 %copy-start.16 = (bf16[112,4096]{1,0:T(8,128)(2,1)S(1)}, bf16[112,4096]{1,0:T(8,128)(2,1)}, u32[]{:S(2)}) copy-start(bf16[112,4096]{1,0:T(8,128)(2,1)} %param.5) | copy-start | bytes 2752516
  13.6 15.2 %collective-permute-start = (f32[112,256]{1,0:T(8,128)S(1)}, f32[112,256]{1,0:T(8,128)S(1)}, u32[]{:S(2)}, u32[]{:S(2)}) collective-permute-start(f32[112,256]{1,0:T(8,128)S(1)} %dynamic-slice_bitcast_fusion), channel_id=1, source_target_pairs={{0,16},{4,20},{8,24},{12,28},{16,0},{20,4},{24,8},{28,12},{1,17},{... | collective-permute-start | bytes 344072 | tf_op jit(solution)/shard_map/ppermute | solution.py:36
  19.1 15.4 %collective-permute-start.3 = (f32[28,256]{1,0:T(8,128)S(1)}, f32[28,256]{1,0:T(8,128)S(1)}, u32[]{:S(2)}, u32[]{:S(2)}) collective-permute-start(f32[28,256]{1,0:T(8,128)S(1)} %get-tuple-element.151), channel_id=1, source_target_pairs={{0,1},{1,0},{2,3},{3,2},{4,5},{5,4},{6,7},{7,6},{8,9},{9,8},{10,11... | collective-permute-start | bytes 86024 | tf_op jit(solution)/shard_map/ppermute | solution.py:36
  20.7 13.8 %collective-permute-start.4 = (f32[28,256]{1,0:T(8,128)S(1)}, f32[28,256]{1,0:T(8,128)S(1)}, u32[]{:S(2)}, u32[]{:S(2)}) collective-permute-start(f32[28,256]{1,0:T(8,128)S(1)} %get-tuple-element.150), channel_id=1, source_target_pairs={{0,2},{1,3},{2,0},{3,1},{4,6},{5,7},{6,4},{7,5},{8,10},{9,11},{10,... | collective-permute-start | bytes 86024 | tf_op jit(solution)/shard_map/ppermute | solution.py:36
  23.3 11.2 %collective-permute-start.5 = (f32[28,256]{1,0:T(8,128)S(1)}, f32[28,256]{1,0:T(8,128)S(1)}, u32[]{:S(2)}, u32[]{:S(2)}) collective-permute-start(f32[28,256]{1,0:T(8,128)S(1)} %get-tuple-element.149), channel_id=1, source_target_pairs={{0,3},{1,2},{2,1},{3,0},{4,7},{5,6},{6,5},{7,4},{8,11},{9,10},{10,... | collective-permute-start | bytes 86024 | tf_op jit(solution)/shard_map/ppermute | solution.py:36
  28.9 4.2 %collective-permute-start.1 = (f32[56,256]{1,0:T(8,128)S(1)}, f32[56,256]{1,0:T(8,128)S(1)}, u32[]{:S(2)}, u32[]{:S(2)}) collective-permute-start(f32[56,256]{1,0:T(8,128)S(1)} %dynamic-slice_bitcast_fusion.1), channel_id=1, source_target_pairs={{0,8},{4,12},{8,0},{12,4},{16,24},{20,28},{24,16},{28,20},{1,9},{5... | collective-permute-start | bytes 172040 | tf_op jit(solution)/shard_map/ppermute | solution.py:36
  33.2 1.3 collective-permute-start.2
  37.3 44.1 %all-to-all-start = ((bf16[8,112,512]{2,1,0:T(8,128)(2,1)}), bf16[8,112,512]{2,1,0:T(8,128)(2,1)}, u32[]{:S(2)}, u32[]{:S(2)}) async-start(bf16[8,112,512]{2,1,0:T(8,128)(2,1)} %bitcast_dynamic-update-slice_fusion), calls=%async_computation | async-start | bytes 1835008 | tf_op jit(solution)/shard_map/all_to_all | solution.py:272
  41.5 194.0 %all-gather.4.cloned.1.call-start = ((), (), s32[]{:S(2)}) async-start(), calls=%async_computation.1 | async-start | bytes 3194880 | tf_op jit(solution)/shard_map/all_gather | solution.py:249
  41.8 8.1 %collective-permute-start.8 = (bf16[28,256]{1,0:T(8,128)(2,1)S(1)}, bf16[28,256]{1,0:T(8,128)(2,1)S(1)}, u32[]{:S(2)}, u32[]{:S(2)}) collective-permute-start(bf16[28,256]{1,0:T(8,128)(2,1)S(1)} %fusion.35), channel_id=1, source_target_pairs={{0,3},{1,2},{2,1},{3,0},{4,7},{5,6},{6,5},{7,4},{8,11},{9,10},{10,... | collective-permute-start | bytes 43016 | tf_op jit(solution)/shard_map/ppermute | solution.py:36
  45.5 7.2 %collective-permute-start.7 = (bf16[28,256]{1,0:T(8,128)(2,1)S(1)}, bf16[28,256]{1,0:T(8,128)(2,1)S(1)}, u32[]{:S(2)}, u32[]{:S(2)}) collective-permute-start(bf16[28,256]{1,0:T(8,128)(2,1)S(1)} %fusion.35), channel_id=1, source_target_pairs={{0,2},{1,3},{2,0},{3,1},{4,6},{5,7},{6,4},{7,5},{8,10},{9,11},{10,... | collective-permute-start | bytes 43016 | tf_op jit(solution)/shard_map/ppermute | solution.py:36
  45.5 7.2 %collective-permute-start.6 = (bf16[28,256]{1,0:T(8,128)(2,1)S(1)}, bf16[28,256]{1,0:T(8,128)(2,1)S(1)}, u32[]{:S(2)}, u32[]{:S(2)}) collective-permute-start(bf16[28,256]{1,0:T(8,128)(2,1)S(1)} %fusion.35), channel_id=1, source_target_pairs={{0,1},{1,0},{2,3},{3,2},{4,5},{5,4},{6,7},{7,6},{8,9},{9,8},{10,11... | collective-permute-start | bytes 43016 | tf_op jit(solution)/shard_map/ppermute | solution.py:36
  46.3 6.4 %collective-permute-start.14 = (bf16[28,256]{1,0:T(8,128)(2,1)S(1)}, bf16[28,256]{1,0:T(8,128)(2,1)S(1)}, u32[]{:S(2)}, u32[]{:S(2)}) collective-permute-start(bf16[28,256]{1,0:T(8,128)(2,1)S(1)} %add_convert_fusion), channel_id=1, source_target_pairs={{0,3},{1,2},{2,1},{3,0},{4,7},{5,6},{6,5},{7,4},{8,11},{9,10},{10,... | collective-permute-start | bytes 43016 | tf_op jit(solution)/shard_map/ppermute | solution.py:36
  49.9 5.0 %collective-permute-start.13 = (bf16[28,256]{1,0:T(8,128)(2,1)S(1)}, bf16[28,256]{1,0:T(8,128)(2,1)S(1)}, u32[]{:S(2)}, u32[]{:S(2)}) collective-permute-start(bf16[28,256]{1,0:T(8,128)(2,1)S(1)} %add_convert_fusion), channel_id=1, source_target_pairs={{0,2},{1,3},{2,0},{3,1},{4,6},{5,7},{6,4},{7,5},{8,10},{9,11},{10,... | collective-permute-start | bytes 43016 | tf_op jit(solution)/shard_map/ppermute | solution.py:36
  49.9 6.9 %collective-permute-start.12 = (bf16[28,256]{1,0:T(8,128)(2,1)S(1)}, bf16[28,256]{1,0:T(8,128)(2,1)S(1)}, u32[]{:S(2)}, u32[]{:S(2)}) collective-permute-start(bf16[28,256]{1,0:T(8,128)(2,1)S(1)} %add_convert_fusion), channel_id=1, source_target_pairs={{0,1},{1,0},{2,3},{3,2},{4,5},{5,4},{6,7},{7,6},{8,9},{9,8},{10,11... | collective-permute-start | bytes 43016 | tf_op jit(solution)/shard_map/ppermute | solution.py:36
  56.9 1.3 collective-permute-start.9
  57.1 2.8 collective-permute-start.15
  58.3 6.4 %collective-permute-start.10 = (bf16[2,4,28,256]{3,2,0,1:T(8,128)(2,1)S(1)}, bf16[2,4,28,256]{3,2,0,1:T(8,128)(2,1)S(1)}, u32[]{:S(2)}, u32[]{:S(2)}) collective-permute-start(bf16[2,4,28,256]{3,2,0,1:T(8,128)(2,1)S(1)} %pad_maximum_fusion.11), channel_id=1, source_target_pairs={{0,8},{4,12},{8,0},{12,4},{16,24},{20,28},{24,16},{28,20},{1,9},{5... | collective-permute-start | bytes 344072 | tf_op jit(solution)/shard_map/ppermute | solution.py:36
  59.9 6.5 %collective-permute-start.16 = (bf16[2,112,256]{2,1,0:T(8,128)(2,1)S(1)}, bf16[2,112,256]{2,1,0:T(8,128)(2,1)S(1)}, u32[]{:S(2)}, u32[]{:S(2)}) collective-permute-start(bf16[2,112,256]{2,1,0:T(8,128)(2,1)S(1)} %pad_maximum_fusion.12), channel_id=1, source_target_pairs={{0,8},{4,12},{8,0},{12,4},{16,24},{20,28},{24,16},{28,20},{1,9},{5... | collective-permute-start | bytes 344072 | tf_op jit(solution)/shard_map/ppermute | solution.py:36
  64.8 9.3 %collective-permute-start.11 = (bf16[4,4,28,256]{3,2,0,1:T(8,128)(2,1)S(1)}, bf16[4,4,28,256]{3,2,0,1:T(8,128)(2,1)S(1)}, u32[]{:S(2)}, u32[]{:S(2)}) collective-permute-start(bf16[4,4,28,256]{3,2,0,1:T(8,128)(2,1)S(1)} %pad_maximum_fusion.5), channel_id=1, source_target_pairs={{0,16},{4,20},{8,24},{12,28},{16,0},{20,4},{24,8},{28,12},{1,17},{... | collective-permute-start | bytes 688136 | tf_op jit(solution)/shard_map/ppermute | solution.py:36
  67.1 9.6 %collective-permute-start.17 = (bf16[4,112,256]{2,1,0:T(8,128)(2,1)}, bf16[4,112,256]{2,1,0:T(8,128)(2,1)}, u32[]{:S(2)}, u32[]{:S(2)}) collective-permute-start(bf16[4,112,256]{2,1,0:T(8,128)(2,1)} %pad_maximum_fusion.9), channel_id=1, source_target_pairs={{0,16},{4,20},{8,24},{12,28},{16,0},{20,4},{24,8},{28,12},{1,17},{... | collective-permute-start | bytes 688136 | tf_op jit(solution)/shard_map/ppermute | solution.py:36
  112.6 31.5 %collective-permute-start.18 = (f32[512,256]{1,0:T(8,128)}, f32[512,256]{1,0:T(8,128)S(1)}, u32[]{:S(2)}, u32[]{:S(2)}) collective-permute-start(f32[512,256]{1,0:T(8,128)} %convolution_multiply_fusion.1), channel_id=1, source_target_pairs={{0,16},{4,20},{8,24},{12,28},{16,0},{20,4},{24,8},{28,12},{1,17},{... | collective-permute-start | bytes 1572872 | tf_op jit(solution)/shard_map/ppermute | solution.py:36
  180.9 3.8 %collective-permute-start.20 = (bf16[4,48,4096]{2,1,0:T(8,128)(2,1)}, bf16[4,48,4096]{2,1,0:T(8,128)(2,1)}, u32[]{:S(2)}, u32[]{:S(2)}) collective-permute-start(bf16[4,48,4096]{2,1,0:T(8,128)(2,1)} %copy-done.10), channel_id=1, source_target_pairs={{0,4},{4,0},{8,12},{12,8},{16,20},{20,16},{24,28},{28,24},{1,5},{5... | collective-permute-start | bytes 4718600 | tf_op jit(solution)/shard_map/ppermute | solution.py:36
  182.9 30.6 %collective-permute-start.19 = (f32[1024,256]{1,0:T(8,128)}, f32[1024,256]{1,0:T(8,128)S(1)}, u32[]{:S(2)}, u32[]{:S(2)}) collective-permute-start(f32[1024,256]{1,0:T(8,128)} %pad_maximum_fusion.2), channel_id=1, source_target_pairs={{0,8},{4,12},{8,0},{12,4},{16,24},{20,28},{24,16},{28,20},{1,9},{5... | collective-permute-start | bytes 3145736 | tf_op jit(solution)/shard_map/ppermute | solution.py:36
  187.9 25.6 %copy-start.15 = (f32[1024,256]{1,0:T(8,128)S(1)}, f32[1024,256]{1,0:T(8,128)}, u32[]{:S(2)}) copy-start(f32[1024,256]{1,0:T(8,128)} %pad_maximum_fusion.2) | copy-start | bytes 3145732
  187.9 29.3 %collective-permute-start.21 = (bf16[2,48,2048]{2,1,0:T(8,128)(2,1)S(1)}, bf16[2,48,2048]{2,1,0:T(8,128)(2,1)S(1)}, u32[]{:S(2)}, u32[]{:S(2)}) collective-permute-start(bf16[2,48,2048]{2,1,0:T(8,128)(2,1)S(1)} %pad_maximum_fusion.3), channel_id=1, source_target_pairs={{0,8},{4,12},{8,0},{12,4},{16,24},{20,28},{24,16},{28,20},{1,9},{5... | collective-permute-start | bytes 1179656 | tf_op jit(solution)/shard_map/ppermute | solution.py:36
  189.4 27.7 %collective-permute-start.23 = (bf16[2,48,2048]{2,1,0:T(8,128)(2,1)S(1)}, bf16[2,48,2048]{2,1,0:T(8,128)(2,1)S(1)}, u32[]{:S(2)}, u32[]{:S(2)}) collective-permute-start(bf16[2,48,2048]{2,1,0:T(8,128)(2,1)S(1)} %slice.276), channel_id=1, source_target_pairs={{0,16},{4,20},{8,24},{12,28},{16,0},{20,4},{24,8},{28,12},{1,17},{... | collective-permute-start | bytes 1179656 | tf_op jit(solution)/shard_map/ppermute | solution.py:36
  217.2 6.7 %collective-permute-start.22 = (bf16[1,48,2048]{2,1,0:T(8,128)(2,1)S(1)}, bf16[1,48,2048]{2,1,0:T(8,128)(2,1)S(1)}, u32[]{:S(2)}, u32[]{:S(2)}) collective-permute-start(bf16[1,48,2048]{2,1,0:T(8,128)(2,1)S(1)} %get-tuple-element.113), channel_id=1, source_target_pairs={{0,16},{4,20},{8,24},{12,28},{16,0},{20,4},{24,8},{28,12},{1,17},{... | collective-permute-start | bytes 589832 | tf_op jit(solution)/shard_map/ppermute | solution.py:36
  218.8 6.4 %collective-permute-start.24 = (bf16[1,48,2048]{2,1,0:T(8,128)(2,1)S(1)}, bf16[1,48,2048]{2,1,0:T(8,128)(2,1)S(1)}, u32[]{:S(2)}, u32[]{:S(2)}) collective-permute-start(bf16[1,48,2048]{2,1,0:T(8,128)(2,1)S(1)} %get-tuple-element.114), channel_id=1, source_target_pairs={{0,8},{4,12},{8,0},{12,4},{16,24},{20,28},{24,16},{28,20},{1,9},{5... | collective-permute-start | bytes 589832 | tf_op jit(solution)/shard_map/ppermute | solution.py:36
  235.5 4.3 %collective-permute-start.26 = (bf16[4,32,4096]{2,1,0:T(8,128)(2,1)}, bf16[4,32,4096]{2,1,0:T(8,128)(2,1)S(1)}, u32[]{:S(2)}, u32[]{:S(2)}) collective-permute-start(bf16[4,32,4096]{2,1,0:T(8,128)(2,1)} %copy-done.11), channel_id=1, source_target_pairs={{0,4},{4,0},{8,12},{12,8},{16,20},{20,16},{24,28},{28,24},{1,5},{5... | collective-permute-start | bytes 3145736 | tf_op jit(solution)/shard_map/ppermute | solution.py:36
  235.5 60.0 %collective-permute-start.25 = (f32[2048,256]{1,0:T(8,128)}, f32[2048,256]{1,0:T(8,128)}, u32[]{:S(2)}, u32[]{:S(2)}) collective-permute-start(f32[2048,256]{1,0:T(8,128)} %pad_maximum_fusion.1), channel_id=1, source_target_pairs={{0,4},{4,0},{8,12},{12,8},{16,20},{20,16},{24,28},{28,24},{1,5},{5... | collective-permute-start | bytes 6291464 | tf_op jit(solution)/shard_map/ppermute | solution.py:36
  241.8 29.9 %copy-start.5 = (bf16[256,4992]{1,0:T(8,128)(2,1)S(1)}, bf16[256,4992]{1,0:T(8,128)(2,1)}, u32[]{:S(2)}) copy-start(bf16[256,4992]{1,0:T(8,128)(2,1)} %all-gather.4.cloned.1.call-done.tokens.refs_5_) | copy-start | bytes 7667716
  241.9 8.4 %collective-permute-start.27 = (bf16[2,32,2048]{2,1,0:T(8,128)(2,1)S(1)}, bf16[2,32,2048]{2,1,0:T(8,128)(2,1)S(1)}, u32[]{:S(2)}, u32[]{:S(2)}) collective-permute-start(bf16[2,32,2048]{2,1,0:T(8,128)(2,1)S(1)} %pad_maximum_fusion.6), channel_id=1, source_target_pairs={{0,8},{4,12},{8,0},{12,4},{16,24},{20,28},{24,16},{28,20},{1,9},{5... | collective-permute-start | bytes 786440 | tf_op jit(solution)/shard_map/ppermute | solution.py:36
  243.4 8.1 %collective-permute-start.29 = (bf16[2,32,2048]{2,1,0:T(8,128)(2,1)S(1)}, bf16[2,32,2048]{2,1,0:T(8,128)(2,1)S(1)}, u32[]{:S(2)}, u32[]{:S(2)}) collective-permute-start(bf16[2,32,2048]{2,1,0:T(8,128)(2,1)S(1)} %slice.287), channel_id=1, source_target_pairs={{0,16},{4,20},{8,24},{12,28},{16,0},{20,4},{24,8},{28,12},{1,17},{... | collective-permute-start | bytes 786440 | tf_op jit(solution)/shard_map/ppermute | solution.py:36
  244.9 45.2 %slice-start = ((s8[5111808]{0:T(1024)(128)(4,1)}), s8[4194304]{0:T(1024)(128)(4,1)S(1)}, s32[]{:S(2)}) async-start(s8[5111808]{0:T(1024)(128)(4,1)} %bitcast.120), calls=%async_computation.4 | async-start | bytes 8388608
  251.5 43.8 %collective-permute-start.28 = (bf16[1,32,2048]{2,1,0:T(8,128)(2,1)S(1)}, bf16[1,32,2048]{2,1,0:T(8,128)(2,1)S(1)}, u32[]{:S(2)}, u32[]{:S(2)}) collective-permute-start(bf16[1,32,2048]{2,1,0:T(8,128)(2,1)S(1)} %get-tuple-element.117), channel_id=1, source_target_pairs={{0,16},{4,20},{8,24},{12,28},{16,0},{20,4},{24,8},{28,12},{1,17},{... | collective-permute-start | bytes 393224 | tf_op jit(solution)/shard_map/ppermute | solution.py:36
  253.1 42.3 %collective-permute-start.30 = (bf16[1,32,2048]{2,1,0:T(8,128)(2,1)S(1)}, bf16[1,32,2048]{2,1,0:T(8,128)(2,1)S(1)}, u32[]{:S(2)}, u32[]{:S(2)}) collective-permute-start(bf16[1,32,2048]{2,1,0:T(8,128)(2,1)S(1)} %get-tuple-element.118), channel_id=1, source_target_pairs={{0,8},{4,12},{8,0},{12,4},{16,24},{20,28},{24,16},{28,20},{1,9},{5... | collective-permute-start | bytes 393224 | tf_op jit(solution)/shard_map/ppermute | solution.py:36
  271.7 18.4 %slice-start.1 = ((s8[5111808]{0:T(1024)(128)(4,1)}), s8[917504]{0:T(1024)(128)(4,1)S(1)}, s32[]{:S(2)}) async-start(s8[5111808]{0:T(1024)(128)(4,1)} %bitcast.120), calls=%async_computation.5 | async-start | bytes 1835008
  271.7 18.4 %copy-start.8 = (bf16[384,256]{0,1:T(8,128)(2,1)S(1)}, bf16[384,256]{0,1:T(8,128)(2,1)}, u32[]{:S(2)}) copy-start(bf16[384,256]{0,1:T(8,128)(2,1)} %copy.93) | copy-start | bytes 589828
  271.7 18.4 %copy-start.9 = (bf16[256,256]{0,1:T(8,128)(2,1)S(1)}, bf16[256,256]{0,1:T(8,128)(2,1)}, u32[]{:S(2)}) copy-start(bf16[256,256]{0,1:T(8,128)(2,1)} %copy.95) | copy-start | bytes 393220
  311.0 2.7 collective-permute-start.31
  313.8 11.3 %copy-start.4 = (bf16[256,6656]{1,0:T(8,128)(2,1)S(1)}, bf16[256,6656]{1,0:T(8,128)(2,1)}, u32[]{:S(2)}) copy-start(bf16[256,6656]{1,0:T(8,128)(2,1)} %all-gather.6.cloned.1.call-done.tokens.refs_4_) | copy-start | bytes 10223620
  314.2 8.4 %collective-permute-start.32 = (bf16[2,32,2048]{2,1,0:T(8,128)(2,1)S(1)}, bf16[2,32,2048]{2,1,0:T(8,128)(2,1)S(1)}, u32[]{:S(2)}, u32[]{:S(2)}) collective-permute-start(bf16[2,32,2048]{2,1,0:T(8,128)(2,1)S(1)} %pad_maximum_fusion.8), channel_id=1, source_target_pairs={{0,8},{4,12},{8,0},{12,4},{16,24},{20,28},{24,16},{28,20},{1,9},{5... | collective-permute-start | bytes 786440 | tf_op jit(solution)/shard_map/ppermute | solution.py:36
  315.7 8.1 %collective-permute-start.34 = (bf16[2,32,2048]{2,1,0:T(8,128)(2,1)S(1)}, bf16[2,32,2048]{2,1,0:T(8,128)(2,1)S(1)}, u32[]{:S(2)}, u32[]{:S(2)}) collective-permute-start(bf16[2,32,2048]{2,1,0:T(8,128)(2,1)S(1)} %slice.298), channel_id=1, source_target_pairs={{0,16},{4,20},{8,24},{12,28},{16,0},{20,4},{24,8},{28,12},{1,17},{... | collective-permute-start | bytes 786440 | tf_op jit(solution)/shard_map/ppermute | solution.py:36
  323.8 5.0 %collective-permute-start.33 = (bf16[1,32,2048]{2,1,0:T(8,128)(2,1)S(1)}, bf16[1,32,2048]{2,1,0:T(8,128)(2,1)S(1)}, u32[]{:S(2)}, u32[]{:S(2)}) collective-permute-start(bf16[1,32,2048]{2,1,0:T(8,128)(2,1)S(1)} %get-tuple-element.115), channel_id=1, source_target_pairs={{0,16},{4,20},{8,24},{12,28},{16,0},{20,4},{24,8},{28,12},{1,17},{... | collective-permute-start | bytes 393224 | tf_op jit(solution)/shard_map/ppermute | solution.py:36
  324.4 5.0 %collective-permute-start.35 = (bf16[1,32,2048]{2,1,0:T(8,128)(2,1)S(1)}, bf16[1,32,2048]{2,1,0:T(8,128)(2,1)S(1)}, u32[]{:S(2)}, u32[]{:S(2)}) collective-permute-start(bf16[1,32,2048]{2,1,0:T(8,128)(2,1)S(1)} %get-tuple-element.116), channel_id=1, source_target_pairs={{0,8},{4,12},{8,0},{12,4},{16,24},{20,28},{24,16},{28,20},{1,9},{5... | collective-permute-start | bytes 393224 | tf_op jit(solution)/shard_map/ppermute | solution.py:36
  (15 other events, 45.2 us)
Sparse Core Ops, SparseCore 0:
  10.2 102.3 all-gather.7
  114.1 66.6 all-gather.5
  183.0 52.4 all-gather.3

commit v4 on v0

v4 whole, which is shorter than its diff:
```python
import functools

import jax
import jax.numpy as jnp
from jax import lax
from jax.experimental import pallas as pl
from jax.experimental.pallas import tpu as pltpu
from jax.sharding import PartitionSpec as P

adapter_scale = 2.0
short_rows = 16
weight_rows = 512
vmem_bytes = 40 * 2**20
light = pl.CostEstimate(flops=0, bytes_accessed=2**16, transcendentals=0)


def contract_trailing_axis(left, right):
    return lax.dot_general(
        left, right, (((1,), (1,)), ((), ())), preferred_element_type=jnp.float32
    )


def contract_first(left, right):
    return lax.dot_general(
        left, right, (((0,), (0,)), ((), ())), preferred_element_type=jnp.float32
    )


def bits_of(axis):
    size = lax.axis_size(axis)
    return [1 << i for i in range(size.bit_length() - 1)]


def swap(value, axis, bit):
    size = lax.axis_size(axis)
    return lax.ppermute(value, axis, [(i, i ^ bit) for i in range(size)])


def scatter_small(value, axis):
    me = lax.axis_index(axis)
    for bit in reversed(bits_of(axis)):
        pair = value.reshape(2, value.shape[0] // 2, value.shape[1])
        mine = ((me & bit) != 0).astype(jnp.int32)
        kept = lax.dynamic_index_in_dim(pair, mine, 0, keepdims=False)
        sent = lax.dynamic_index_in_dim(pair, 1 - mine, 0, keepdims=False)
        value = kept + swap(sent, axis, bit)
    return value


def gather_ordered(value, axis, order):
    me = lax.axis_index(axis)
    for bit in order:
        other = swap(value, axis, bit)
        upper = (me & bit) != 0
        value = jnp.concatenate(
            [jnp.where(upper, other, value), jnp.where(upper, value, other)], axis=0
        )
    return value


def phase_a(block, axis):
    return swap(block, axis, 1), swap(block, axis, 2)


def phase_b(block, far, axis):
    return (
        lax.ppermute(block, axis, [(1, 2), (2, 1)]),
        lax.ppermute(far, axis, [(1, 0), (2, 3)]),
    )


def pass_kernel(table, *refs, sources, owners, rows):
    source_refs, refs = refs[:sources], refs[sources:]
    weight, refs = refs[0], refs[1:]
    if sources > 1:
        tokens, kept, sent = refs

        @pl.when(pl.program_id(0) == 0)
        def _():
            size = source_refs[0].shape[0]
            for i, source in enumerate(source_refs[: sources - 2]):
                tokens[i * size : (i + 1) * size] = source[...]
            for end in range(2):

                @pl.when(table[owners] == end)
                def _():
                    tokens[(sources - 2) * size :] = source_refs[sources - 2 + end][...]
    else:
        (tokens,) = source_refs
        kept, sent = refs
    product = contract_trailing_axis(tokens[...], weight[...])
    for i in range(owners):
        place = table[i]
        part = product[i * rows : (i + 1) * rows]

        @pl.when((place & 1) == 0)
        def _():
            kept[place >> 1] = part

        @pl.when((place & 1) == 1)
        def _():
            sent[place >> 1] = part.astype(jnp.bfloat16)


def weight_pass(table, sources, weight, owners):
    depth = weight.shape[1]
    width = weight.shape[0]
    total = sources[0].shape[0] * max(1, len(sources) - 1)
    rows = total // owners
    step = min(weight_rows, width)
    whole = lambda i, *_: (0, 0)
    once = pl.Buffered(1)
    in_specs = [pl.BlockSpec(s.shape, whole, pipeline_mode=once) for s in sources]
    in_specs.append(pl.BlockSpec((step, depth), lambda i, *_: (i, 0)))
    half = (owners // 2, rows, width)
    out_shape = [
        jax.ShapeDtypeStruct(half, jnp.float32),
        jax.ShapeDtypeStruct(half, jnp.bfloat16),
    ]
    out_specs = [pl.BlockSpec((owners // 2, rows, step), lambda i, *_: (0, 0, i))] * 2
    if len(sources) > 1:
        out_shape.insert(0, jax.ShapeDtypeStruct((total, depth), jnp.bfloat16))
        out_specs.insert(0, pl.BlockSpec((total, depth), whole, pipeline_mode=once))
    outs = pl.pallas_call(
        functools.partial(pass_kernel, sources=len(sources), owners=owners, rows=rows),
        grid_spec=pltpu.PrefetchScalarGridSpec(
            num_scalar_prefetch=1,
            grid=(width // step,),
            in_specs=in_specs,
            out_specs=out_specs,
        ),
        out_shape=out_shape,
        compiler_params=pltpu.CompilerParams(vmem_limit_bytes=vmem_bytes),
        cost_estimate=light,
        name="weight_pass",
    )(table, *sources, weight)
    return outs if len(sources) > 1 else [sources[0], *outs]


def factor_kernel(*refs, count, scale):
    acts, tokens, out = refs[:count], refs[count : 2 * count], refs[-1]
    out[...] = scale * sum(
        jnp.dot(a[...], t[...], preferred_element_type=jnp.float32) for a, t in zip(acts, tokens)
    )


def factor_gradient(acts, tokens, scale, step, first, blocks, into=None):
    rank, depth = acts[0].shape[0], tokens[0].shape[1]
    in_specs = [
        pl.BlockSpec(a.shape, lambda i: (0, 0), pipeline_mode=pl.Buffered(1)) for a in acts
    ]
    in_specs += [pl.BlockSpec((t.shape[0], step), lambda i: (0, first + i)) for t in tokens]
    operands = [*acts, *tokens]
    aliases = {}
    if into is not None:
        aliases = {len(operands): 0}
        operands.append(into)
        in_specs.append(pl.BlockSpec(memory_space=pl.ANY))
    return pl.pallas_call(
        functools.partial(factor_kernel, count=len(acts), scale=scale),
        grid=(blocks,),
        in_specs=in_specs,
        out_specs=pl.BlockSpec((rank, step), lambda i: (0, first + i)),
        out_shape=jax.ShapeDtypeStruct((rank, depth), jnp.float32),
        input_output_aliases=aliases,
        compiler_params=pltpu.CompilerParams(vmem_limit_bytes=vmem_bytes),
        cost_estimate=light,
        name="factor_gradient",
    )(*operands)


def scatter_sum(kept, sent, axis):
    bits = bits_of(axis)
    live = kept + swap(sent, axis, 1)
    half = live.shape[2] // 2
    done = []
    for side, order in ((0, bits[:-1]), (1, bits[:-1][::-1])):
        part = {p: live[p, :, side * half : (side + 1) * half] for p in range(live.shape[0])}
        for bit in order:
            stay = [p for p in part if not p & bit]
            away = jnp.stack([part[p ^ bit].astype(jnp.bfloat16) for p in stay])
            got = swap(away, axis, 2 * bit)
            part = {p: part[p] + got[i] for i, p in enumerate(stay)}
        done.append(part[0])
    return done


def hold(*groups):
    leaves, tree = jax.tree.flatten(groups)
    return jax.tree.unflatten(tree, lax.optimization_barrier(leaves))


def cut_rows(owner_rows):
    middle = owner_rows - 2 * short_rows
    sizes = [owner_rows]
    if middle >= 2 * short_rows:
        large = -(-middle * 3 // (5 * short_rows)) * short_rows
        sizes = [short_rows, large, middle - large, short_rows]
    starts = [sum(sizes[:i]) for i in range(len(sizes))]
    return list(zip(starts, sizes))


def shards(inputs, grad_out, w_base, adapter_down_matrix, b_factor):
    owner_rows = inputs.shape[0]
    owners = lax.axis_size("wide")
    groups = lax.axis_size("narrow")
    me_wide = lax.axis_index("wide")
    me_narrow = lax.axis_index("narrow")
    adapter_matrix = adapter_scale / (owner_rows * owners)
    share = grad_out.shape[0] // owner_rows
    rank = b_factor.shape[0]
    depth = grad_out.shape[1]
    wide_bits, narrow_bits = bits_of("wide"), bits_of("narrow")
    pieces = cut_rows(owner_rows)
    count = len(pieces)
    line = groups == 4

    held = [me_narrow ^ i if line else jnp.int32(i) for i in range(groups)]
    table = [(block * share + h) ^ me_wide for block in held for h in range(share)]
    table.append(((me_narrow == 0) | (me_narrow == groups - 1)).astype(jnp.int32))
    table = jnp.stack([entry.astype(jnp.int32) for entry in table])

    def block_of(source, i):
        start, rows = pieces[i]
        own = source.reshape(share, owner_rows, depth)
        return own[:, start : start + rows].reshape(share * rows, depth)

    blocks, near, far, middle, onward = {}, {}, {}, {}, {}

    def begin(i):
        blocks[i] = block_of(grad_out, i)
        if line:
            near[i], far[i] = phase_a(blocks[i], "narrow")
        else:
            near[i] = far[i] = lax.all_gather(blocks[i], "narrow", axis=0, tiled=True)

    def complete(i):
        if line:
            middle[i], onward[i] = phase_b(blocks[i], far[i], "narrow")
        else:
            middle[i], onward[i] = near[i], far[i]

    begin(0)

    act_part = jnp.dot(inputs, adapter_down_matrix, preferred_element_type=jnp.float32)
    act_small = scatter_small(act_part, "narrow").astype(jnp.bfloat16)
    low_part = contract_trailing_axis(grad_out, b_factor)
    low_small = scatter_small(low_part, "wide").astype(jnp.bfloat16)
    near[0], far[0], grad_out, low_small = hold(near[0], far[0], grad_out, low_small)
    complete(0)
    act_rows = gather_ordered(act_small, "narrow", narrow_bits)
    low_rows = gather_ordered(low_small[None], "narrow", narrow_bits)
    middle[0], onward[0], grad_out, act_rows, low_rows, inputs = hold(
        middle[0], onward[0], grad_out, act_rows, low_rows, inputs
    )
    if count > 1:
        begin(1)

    low_wide = gather_ordered(low_rows[None], "wide", wide_bits)
    low_rank_all = jnp.swapaxes(low_wide, 0, 1).reshape(owner_rows * owners, rank)
    low_rank_own = lax.dynamic_slice_in_dim(low_rank_all, me_wide * owner_rows, owner_rows)
    low_term = adapter_scale * contract_trailing_axis(low_rank_own, adapter_down_matrix)
    shares = inputs.reshape(owner_rows, owners, -1)
    flipped = [
        sum(bit for i, bit in enumerate(wide_bits) if w & wide_bits[len(wide_bits) - 1 - i])
        for w in range(owners)
    ]
    columns = lax.all_to_all(
        jnp.stack([shares[:, f] for f in flipped], axis=0), "wide", split_axis=0, concat_axis=0
    ).reshape(owner_rows * owners, -1)
    grad_a = adapter_matrix * contract_first(columns, low_rank_all)
    grad_a_steps = wide_bits[::-1]

    acts = gather_ordered(act_rows[None], "wide", wide_bits).reshape(groups, share, owner_rows, rank)
    if line:
        for bit in narrow_bits:
            pair = acts.reshape(groups // (2 * bit), 2, bit, share, owner_rows, rank)
            acts = jnp.where((me_narrow & bit) != 0, pair[:, ::-1], pair).reshape(acts.shape)
    turned = [
        acts[:, :, start : start + rows].reshape(owners * rows, rank).T for start, rows in pieces
    ]

    tokens, sums, results = {}, {}, {}

    def run_pass(i):
        sources = [blocks[i], near[i], far[i], middle[i], onward[i]] if line else [near[i]]
        tokens[i], *sums[i] = weight_pass(table, sources, w_base, owners)

    def finish(i):
        start, rows = pieces[i]
        sides = scatter_sum(*sums.pop(i), "wide")
        half = sides[0].shape[1]
        mine = low_term[start : start + rows]
        results[i] = jnp.concatenate(
            [
                (side + mine[:, j * half : (j + 1) * half]).astype(jnp.bfloat16)
                for j, side in enumerate(sides)
            ],
            axis=1,
        )

    run_pass(0)
    for i in range(1, count):
        near[i], far[i], grad_out, grad_a, turned, sums, low_term, results = hold(
            near[i], far[i], grad_out, grad_a, turned, sums, low_term, results
        )
        complete(i)
        if i + 1 < count:
            begin(i + 1)
            middle[i], onward[i], grad_a, sums, blocks[i + 1] = hold(
                middle[i], onward[i], grad_a, sums, blocks[i + 1]
            )
        else:
            middle[i], onward[i], grad_a, sums = hold(middle[i], onward[i], grad_a, sums)
        finish(i - 1)
        run_pass(i)
        if grad_a_steps:
            grad_a = gather_ordered(grad_a, "wide", grad_a_steps[:1])
            grad_a_steps = grad_a_steps[1:]
    grad_a = gather_ordered(grad_a, "wide", grad_a_steps)
    step = max(128 * c for c in range(1, 14) if depth % (128 * c) == 0)
    steps = depth // step
    turned = [turned[i] for i in range(count)]
    tokens = [tokens[i] for i in range(count)]
    grad_b = factor_gradient(turned, tokens, adapter_matrix, step, 0, steps // 2 or 1)
    if steps > 1:
        grad_b = factor_gradient(
            turned, tokens, adapter_matrix, step, steps // 2, steps - steps // 2, grad_b
        )
    finish(count - 1)
    return (jnp.concatenate([results[i] for i in range(count)], axis=0), grad_a, grad_b)


def solution(mesh):
    return jax.shard_map(
        shards,
        mesh=mesh,
        in_specs=(
            P("wide", "narrow"),
            P("narrow", "wide"),
            P("narrow", "wide"),
            P("narrow", None),
            P(None, "wide"),
        ),
        out_specs=(P("wide", "narrow"), P("narrow", None), P(None, "wide")),
        check_vma=False,
    )
```

time: 501 us -> 373 us (0.74)
  waiting for transfers between devices: 357 us -> 140 us
  Pallas kernels: 0 us -> 113 us
  matrix products: 82.7 us -> 9.78 us
  starting transfers between devices: 0.12 us -> 64.8 us
  blocking collectives: 30.2 us -> 0 us
  local copies, waits for them, and re-layouts: 5.62 us -> 22.9 us
  between operations: 13.8 us -> 1.45 us
  other arithmetic: 10.6 us -> 19 us
    all_gather x1 -> x0, waiting for transfers between devices: 212 us -> none  [shards(): every_row = lax.all_gather(grad_out, 'narrow', axis=0, tiled=True)]
    ppermute x0 -> x54, waiting for transfers between devices: none -> 140 us  [the longest x46 74.7 us: swap(): return lax.ppermute(value, axis, [(i, i ^ bit) for i in range(size)])]
    pallas_call x0 -> x6, Pallas kernels: none -> 113 us  [the longest x4 105 us: weight_pass(): pl.pallas_call(functools.partial(pass_kernel, sources=len(sources), owner...]
    reduce_scatter x1 -> x0, waiting for transfers between devices: 107 us -> none  [shards(): summed = lax.psum_scatter(stacked, 'wide', scatter_dimension=0, tiled=True)]
    dot_general x3 -> x2, matrix products: 68 us -> 5.49 us  [contract_trailing_axis(): lax.dot_general(left, right, (((1,), (1,)), ((), ())), preferred_element_...]
    ppermute x0 -> x54, starting transfers between devices: none -> 60.5 us  [the longest x46 50 us: swap(): return lax.ppermute(value, axis, [(i, i ^ bit) for i in range(size)])]
    psum x1 -> x0, waiting for transfers between devices: 38 us -> none  [shards(): lax.psum(adapter_matrix * contract_first(inputs, low_rank_gradient), 'wide')]
    psum x1 -> x0, blocking collectives: 20.7 us -> none  [shards(): low_act = lax.psum(low_part, 'narrow').astype(jnp.bfloat16)]
  transfers between devices with their start and end apart: 3 -> 55, of which waited for: 3 -> 27; matrix products, arithmetic and copies ran while one was open for 3% -> 12% of each run, Pallas kernels for 0% -> 24%
where the time goes in v4:
time: 373 us; the launch traced here: 371 us
  waiting for transfers between devices  140 us (38%)
  Pallas kernels  113 us (30%)
  starting transfers between devices  64.8 us (17%)
  local copies, waits for them, and re-layouts  22.9 us (6%)
  other arithmetic  19 us (5%)
  matrix products  9.78 us (3%)
    pallas_call x4, Pallas kernels, weight_pass(): pl.pallas_call(functools.partial(pass_kernel, sources=len(sources), owner...  105 us
    ppermute x46, waiting for transfers between devices, swap(): return lax.ppermute(value, axis, [(i, i ^ bit) for i in range(size)])  74.7 us
    ppermute x4, waiting for transfers between devices, phase_b(): lax.ppermute(far, axis, [(1, 0), (2, 3)])  65.6 us
    ppermute x46, starting transfers between devices, swap(): return lax.ppermute(value, axis, [(i, i ^ bit) for i in range(size)])  50 us
    pallas_call x2, Pallas kernels, factor_gradient(): pl.pallas_call(functools.partial(factor_kernel, count=len(acts), scale=sc...  8.5 us
  transfers between devices with their start and end apart: 55, of which 27 were waited for; matrix products, arithmetic and copies ran while one was open for 12% of the time, Pallas kernels for 24%

profile of v4, /device:TPU:0, one launch (start us, length us, event | category | flops | bytes accessed | tf_op | source)
XLA Modules:
  0.0 371.3 jit_solution(7303724778102245363)
XLA Ops:
  0.6 1.9 slice.320
  2.6 4.0 %collective-permute-start.2 = (bf16[32,6656]{1,0:T(8,128)(2,1)}, bf16[32,6656]{1,0:T(8,128)(2,1)}, u32[]{:S(2)}, u32[]{:S(2)}) collective-permute-start(bf16[32,6656]{1,0:T(8,128)(2,1)} %bitcast.1.refs_0_), channel_id=1, source_target_pairs={{0,2},{1,3},{2,0},{3,1},{4,6},{5,7},{6,4},{7,5},{8,10},{9,11},{10,... | collective-permute-start | bytes 1277960 | tf_op jit(solution)/shard_map/ppermute | solution.py:36
  6.6 1.6 collective-permute-start.1
  9.6 2.5 fusion.56
  12.7 2.4 collective-permute-start.7
  15.2 1.9 fusion.55
  17.0 20.5 %collective-permute-done.7 = f32[56,256]{1,0:T(8,128)} collective-permute-done((f32[56,256]{1,0:T(8,128)}, f32[56,256]{1,0:T(8,128)}, u32[]{:S(2)}, u32[]{:S(2)}) %collective-permute-start.7) | collective-permute-done | bytes 57376 | tf_op jit(solution)/shard_map/ppermute | solution.py:36
  43.1 1.7 collective-permute-done.3
  47.3 2.7 collective-permute-done.4
  50.1 3.4 collective-permute-start.10
  54.0 2.2 collective-permute-done.10
  57.5 3.2 collective-permute-start.12
  62.8 7.9 %collective-permute-done.6.refs_4_ = bf16[32,6656]{1,0:T(8,128)(2,1)S(1)} collective-permute-done((bf16[32,6656]{1,0:T(8,128)(2,1)}, bf16[32,6656]{1,0:T(8,128)(2,1)S(1)}, u32[]{:S(2)}, u32[]{:S(2)}) %collective-permute-start.6) | collective-permute-done | bytes 426016 | tf_op jit(solution)/shard_map/ppermute | solution.py:68
  72.1 1.7 collective-permute-start.23
  76.6 1.7 fusion.51
  83.6 4.2 %all-to-all-start = ((bf16[8,112,512]{2,1,0:T(8,128)(2,1)}), bf16[8,112,512]{2,1,0:T(8,128)(2,1)}, u32[]{:S(2)}, u32[]{:S(2)}) async-start(bf16[8,112,512]{2,1,0:T(8,128)(2,1)} %bitcast_dynamic-update-slice_fusion), calls=%async_computation | async-start | bytes 1835008 | tf_op jit(solution)/shard_map/all_to_all | solution.py:268
  87.8 25.2 %weight_pass.4 = (bf16[128,6656]{1,0:T(8,128)(2,1)S(1)}, f32[4,16,4096]{2,1,0:T(8,128)S(1)}, bf16[4,16,4096]{2,1,0:T(8,128)(2,1)S(1)}) custom-call(s32[9]{0:T(128)S(1)} %stack.95.table, bf16[32,6656]{1,0:T(8,128)(2,1)} %bitcast.1.refs_0_, bf16[32,6656]{1,0:T(8,128)(2,1)} %collective-permute-done.1.refs_1_, bf16[32,6656]{1,0:T(8,128)(2,1)} %collective-permute-done.2.refs_2_, ...), custom_call_target="tpu_custom_call" | custom-call | bytes 65536 | tf_op jit(solution)/shard_map/weight_pass/pallas_call | solution.py:124
  114.1 2.0 collective-permute-start.19
  117.1 2.5 collective-permute-done.19
  119.7 1.9 collective-permute-start.20
  123.2 1.7 collective-permute-start.17
  124.9 3.3 collective-permute-done.20
  135.6 2.0 reshape.112
  137.6 3.6 convolution_multiply_fusion
  141.2 1.8 convolution_multiply_fusion.1
  143.1 14.3 %collective-permute-done.14.refs_2_ = bf16[96,6656]{1,0:T(8,128)(2,1)} collective-permute-done((bf16[96,6656]{1,0:T(8,128)(2,1)S(1)}, bf16[96,6656]{1,0:T(8,128)(2,1)}, u32[]{:S(2)}, u32[]{:S(2)}) %collective-permute-start.14) | collective-permute-done | bytes 1277984 | tf_op jit(solution)/shard_map/ppermute | solution.py:36
  159.9 28.5 %collective-permute-done.24.refs_4_ = bf16[96,6656]{1,0:T(8,128)(2,1)S(1)} collective-permute-done((bf16[96,6656]{1,0:T(8,128)(2,1)}, bf16[96,6656]{1,0:T(8,128)(2,1)S(1)}, u32[]{:S(2)}, u32[]{:S(2)}) %collective-permute-start.24) | collective-permute-done | bytes 1277984 | tf_op jit(solution)/shard_map/ppermute | solution.py:68
  191.8 31.2 %weight_pass.5 = (bf16[384,6656]{1,0:T(8,128)(2,1)}, f32[4,48,4096]{2,1,0:T(8,128)S(1)}, bf16[4,48,4096]{2,1,0:T(8,128)(2,1)S(1)}) custom-call(s32[9]{0:T(128)S(1)} %stack.95.table, bf16[96,6656]{1,0:T(8,128)(2,1)S(1)} %bitcast.146, bf16[96,6656]{1,0:T(8,128)(2,1)} %collective-permute-done.13.refs_1_, bf16[96,6656]{1,0:T(8,128)(2,1)} %collective-permute-done.14.refs_2_, ...), custom_call_target="tpu_custom_call" | custom-call | bytes 65536 | tf_op jit(solution)/shard_map/weight_pass/pallas_call | solution.py:124
  223.3 1.6 collective-permute-start.27
  225.4 3.0 collective-permute-done.27
  231.2 2.9 collective-permute-done.28
  237.8 19.1 %collective-permute-done.34.refs_4_ = bf16[64,6656]{1,0:T(8,128)(2,1)S(1)} collective-permute-done((bf16[64,6656]{1,0:T(8,128)(2,1)S(1)}, bf16[64,6656]{1,0:T(8,128)(2,1)S(1)}, u32[]{:S(2)}, u32[]{:S(2)}) %collective-permute-start.34) | collective-permute-done | bytes 852000 | tf_op jit(solution)/shard_map/ppermute | solution.py:68
  257.5 2.7 collective-permute-done.36
  260.2 2.2 fusion.47
  264.6 2.3 collective-permute-start.31
  267.0 23.5 %weight_pass.6 = (bf16[256,6656]{1,0:T(8,128)(2,1)S(1)}, f32[4,32,4096]{2,1,0:T(8,128)S(1)}, bf16[4,32,4096]{2,1,0:T(8,128)(2,1)S(1)}) custom-call(s32[9]{0:T(128)S(1)} %stack.95.table, bf16[64,6656]{1,0:T(8,128)(2,1)S(1)} %bitcast.150, bf16[64,6656]{1,0:T(8,128)(2,1)S(1)} %collective-permute-done.21.refs_1_, ...), custom_call_target="tpu_custom_call" | custom-call | bytes 65536 | tf_op jit(solution)/shard_map/weight_pass/pallas_call | solution.py:124
  295.2 3.7 collective-permute-done.38
  299.5 1.8 collective-permute-start.42
  301.3 10.1 %collective-permute-done.42.refs_4_ = bf16[32,6656]{1,0:T(8,128)(2,1)S(1)} collective-permute-done((bf16[32,6656]{1,0:T(8,128)(2,1)S(1)}, bf16[32,6656]{1,0:T(8,128)(2,1)S(1)}, u32[]{:S(2)}, u32[]{:S(2)}) %collective-permute-start.42) | collective-permute-done | bytes 426016 | tf_op jit(solution)/shard_map/ppermute | solution.py:68
  311.4 24.7 %weight_pass.7 = (bf16[128,6656]{1,0:T(8,128)(2,1)S(1)}, f32[4,16,4096]{2,1,0:T(8,128)S(1)}, bf16[4,16,4096]{2,1,0:T(8,128)(2,1)S(1)}) custom-call(s32[9]{0:T(128)S(1)} %stack.95.table, bf16[32,6656]{1,0:T(8,128)(2,1)S(1)} %bitcast.156, bf16[32,6656]{1,0:T(8,128)(2,1)S(1)} %collective-permute-done.31.refs_1_, ...), custom_call_target="tpu_custom_call" | custom-call | bytes 65536 | tf_op jit(solution)/shard_map/weight_pass/pallas_call | solution.py:124
  336.8 4.2 %factor_gradient.2.refs_8_ = f32[256,6656]{1,0:T(8,128)} custom-call(bf16[256,128]{1,0:T(8,128)(2,1)S(1)} %bitcast.161, bf16[256,384]{1,0:T(8,128)(2,1)S(1)} %bitcast.151, bf16[256,256]{1,0:T(8,128)(2,1)S(1)} %bitcast.157, bf16[256,128]{1,0:T(8,128)(2,1)S(1)} %bitcast.159, bf16[128,6656]{1,0:T(8,128)(2,1)S(1)} %get-tuple-element.147.refs_4_, ...), custom_call_target="tpu_custom_call" | custom-call | bytes 65536 | tf_op jit(solution)/shard_map/factor_gradient/pallas_call | solution.py:159
  341.0 4.2 %factor_gradient.3 = f32[256,6656]{1,0:T(8,128)} custom-call(bf16[256,128]{1,0:T(8,128)(2,1)S(1)} %bitcast.162, bf16[256,384]{1,0:T(8,128)(2,1)S(1)} %bitcast.152, bf16[256,256]{1,0:T(8,128)(2,1)S(1)} %bitcast.158, bf16[256,128]{1,0:T(8,128)(2,1)S(1)} %bitcast.160, bf16[128,6656]{1,0:T(8,128)(2,1)S(1)} %get-tuple-element.147.refs_4_, ...), custom_call_target="tpu_custom_call", output_to_operand_aliasing={{}: (8, {})} | custom-call | bytes 65536 | tf_op jit(solution)/shard_map/factor_gradient/pallas_call | solution.py:159
  351.4 1.9 collective-permute-done.51
  353.3 1.6 collective-permute-start.50
  355.4 2.4 collective-permute-done.44
  358.9 1.6 collective-permute-start.45
  362.0 1.9 collective-permute-done.45
  367.9 2.4 pad_maximum_fusion
  (201 shorter events, 70.7 us)
Async XLA Ops:
  2.6 51.0 %collective-permute-start.2 = (bf16[32,6656]{1,0:T(8,128)(2,1)}, bf16[32,6656]{1,0:T(8,128)(2,1)}, u32[]{:S(2)}, u32[]{:S(2)}) collective-permute-start(bf16[32,6656]{1,0:T(8,128)(2,1)} %bitcast.1.refs_0_), channel_id=1, source_target_pairs={{0,2},{1,3},{2,0},{3,1},{4,6},{5,7},{6,4},{7,5},{8,10},{9,11},{10,... | collective-permute-start | bytes 1277960 | tf_op jit(solution)/shard_map/ppermute | solution.py:36
  6.6 47.0 %collective-permute-start.1 = (bf16[32,6656]{1,0:T(8,128)(2,1)}, bf16[32,6656]{1,0:T(8,128)(2,1)}, u32[]{:S(2)}, u32[]{:S(2)}) collective-permute-start(bf16[32,6656]{1,0:T(8,128)(2,1)} %bitcast.1.refs_0_), channel_id=1, source_target_pairs={{0,1},{1,0},{2,3},{3,2},{4,5},{5,4},{6,7},{7,6},{8,9},{9,8},{10,11... | collective-permute-start | bytes 1277960 | tf_op jit(solution)/shard_map/ppermute | solution.py:36
  8.2 54.6 %collective-permute-start = (bf16[32,6656]{1,0:T(8,128)(2,1)}, bf16[32,6656]{1,0:T(8,128)(2,1)}, u32[]{:S(2)}, u32[]{:S(2)}) collective-permute-start(bf16[32,6656]{1,0:T(8,128)(2,1)} %bitcast.1.refs_0_), channel_id=1, source_target_pairs={{1,2},{2,1},{5,6},{6,5},{9,10},{10,9},{13,14},{14,13},{17,18},{18,... | collective-permute-start | bytes 1277960 | tf_op jit(solution)/shard_map/ppermute | solution.py:67
  12.7 24.8 %collective-permute-start.7 = (f32[56,256]{1,0:T(8,128)}, f32[56,256]{1,0:T(8,128)}, u32[]{:S(2)}, u32[]{:S(2)}) collective-permute-start(f32[56,256]{1,0:T(8,128)} %dynamic-slice_bitcast_fusion.1), channel_id=1, source_target_pairs={{0,2},{1,3},{2,0},{3,1},{4,6},{5,7},{6,4},{7,5},{8,10},{9,11},{10,... | collective-permute-start | bytes 172040 | tf_op jit(solution)/shard_map/ppermute | solution.py:36
  40.0 4.8 %collective-permute-start.3 = (f32[112,256]{1,0:T(8,128)S(1)}, f32[112,256]{1,0:T(8,128)S(1)}, u32[]{:S(2)}, u32[]{:S(2)}) collective-permute-start(f32[112,256]{1,0:T(8,128)S(1)} %dynamic-slice_bitcast_fusion), channel_id=1, source_target_pairs={{0,16},{4,20},{8,24},{12,28},{16,0},{20,4},{24,8},{28,12},{1,17},{... | collective-permute-start | bytes 344072 | tf_op jit(solution)/shard_map/ppermute | solution.py:36
  42.4 4.9 %collective-permute-start.9 = (bf16[28,256]{1,0:T(8,128)(2,1)S(1)}, bf16[28,256]{1,0:T(8,128)(2,1)S(1)}, u32[]{:S(2)}, u32[]{:S(2)}) collective-permute-start(bf16[28,256]{1,0:T(8,128)(2,1)S(1)} %fusion.42), channel_id=1, source_target_pairs={{0,1},{1,0},{2,3},{3,2},{4,5},{5,4},{6,7},{7,6},{8,9},{9,8},{10,11... | collective-permute-start | bytes 43016 | tf_op jit(solution)/shard_map/ppermute | solution.py:36
  50.1 6.0 %collective-permute-start.10 = (bf16[56,256]{1,0:T(8,128)(2,1)S(1)}, bf16[56,256]{1,0:T(8,128)(2,1)S(1)}, u32[]{:S(2)}, u32[]{:S(2)}) collective-permute-start(bf16[56,256]{1,0:T(8,128)(2,1)S(1)} %pad_maximum_fusion.17), channel_id=1, source_target_pairs={{0,2},{1,3},{2,0},{3,1},{4,6},{5,7},{6,4},{7,5},{8,10},{9,11},{10,... | collective-permute-start | bytes 86024 | tf_op jit(solution)/shard_map/ppermute | solution.py:36
  56.2 14.5 %collective-permute-start.6 = (bf16[32,6656]{1,0:T(8,128)(2,1)}, bf16[32,6656]{1,0:T(8,128)(2,1)S(1)}, u32[]{:S(2)}, u32[]{:S(2)}) collective-permute-start(bf16[32,6656]{1,0:T(8,128)(2,1)} %collective-permute-done.2.refs_2_), channel_id=1, source_target_pairs={{1,0},{2,3},{5,4},{6,7},{9,8},{10,11},{13,12},{14,15},{17,16},{18,... | collective-permute-start | bytes 1277960 | tf_op jit(solution)/shard_map/ppermute | solution.py:68
  57.5 5.2 %collective-permute-start.12 = (bf16[2,28,256]{2,1,0:T(8,128)(2,1)S(1)}, bf16[2,28,256]{2,1,0:T(8,128)(2,1)S(1)}, u32[]{:S(2)}, u32[]{:S(2)}) collective-permute-start(bf16[2,28,256]{2,1,0:T(8,128)(2,1)S(1)} %pad_maximum_fusion.16), channel_id=1, source_target_pairs={{0,2},{1,3},{2,0},{3,1},{4,6},{5,7},{6,4},{7,5},{8,10},{9,11},{10,... | collective-permute-start | bytes 86024 | tf_op jit(solution)/shard_map/ppermute | solution.py:36
  72.1 87.8 %collective-permute-start.23 = (bf16[96,6656]{1,0:T(8,128)(2,1)S(1)}, bf16[96,6656]{1,0:T(8,128)(2,1)}, u32[]{:S(2)}, u32[]{:S(2)}) collective-permute-start(bf16[96,6656]{1,0:T(8,128)(2,1)S(1)} %bitcast.143), channel_id=1, source_target_pairs={{1,2},{2,1},{5,6},{6,5},{9,10},{10,9},{13,14},{14,13},{17,18},{18,... | collective-permute-start | bytes 3833864 | tf_op jit(solution)/shard_map/ppermute | solution.py:67
  73.8 83.6 %collective-permute-start.14 = (bf16[96,6656]{1,0:T(8,128)(2,1)S(1)}, bf16[96,6656]{1,0:T(8,128)(2,1)}, u32[]{:S(2)}, u32[]{:S(2)}) collective-permute-start(bf16[96,6656]{1,0:T(8,128)(2,1)S(1)} %bitcast.144), channel_id=1, source_target_pairs={{0,2},{1,3},{2,0},{3,1},{4,6},{5,7},{6,4},{7,5},{8,10},{9,11},{10,... | collective-permute-start | bytes 3833864 | tf_op jit(solution)/shard_map/ppermute | solution.py:36
  75.2 82.2 %collective-permute-start.13 = (bf16[96,6656]{1,0:T(8,128)(2,1)S(1)}, bf16[96,6656]{1,0:T(8,128)(2,1)}, u32[]{:S(2)}, u32[]{:S(2)}) collective-permute-start(bf16[96,6656]{1,0:T(8,128)(2,1)S(1)} %bitcast.145), channel_id=1, source_target_pairs={{0,1},{1,0},{2,3},{3,2},{4,5},{5,4},{6,7},{7,6},{8,9},{9,8},{10,11... | collective-permute-start | bytes 3833864 | tf_op jit(solution)/shard_map/ppermute | solution.py:36
  75.8 37.3 %collective-permute-start.18 = (bf16[1,112,256]{2,1,0:T(8,128)(2,1)}, bf16[1,112,256]{2,1,0:T(8,128)(2,1)}, u32[]{:S(2)}, u32[]{:S(2)}) collective-permute-start(bf16[1,112,256]{2,1,0:T(8,128)(2,1)} %bitcast.21), channel_id=1, source_target_pairs={{0,4},{4,0},{8,12},{12,8},{16,20},{20,16},{24,28},{28,24},{1,5},{5... | collective-permute-start | bytes 172040 | tf_op jit(solution)/shard_map/ppermute | solution.py:36
  75.8 40.2 %collective-permute-start.15 = (bf16[1,4,28,256]{3,2,0,1:T(8,128)(2,1)S(1)}, bf16[1,4,28,256]{3,2,0,1:T(8,128)(2,1)}, u32[]{:S(2)}, u32[]{:S(2)}) collective-permute-start(bf16[1,4,28,256]{3,2,0,1:T(8,128)(2,1)S(1)} %bitcast.179), channel_id=1, source_target_pairs={{0,4},{4,0},{8,12},{12,8},{16,20},{20,16},{24,28},{28,24},{1,5},{5... | collective-permute-start | bytes 172040 | tf_op jit(solution)/shard_map/ppermute | solution.py:36
  83.6 57.6 %all-to-all-start = ((bf16[8,112,512]{2,1,0:T(8,128)(2,1)}), bf16[8,112,512]{2,1,0:T(8,128)(2,1)}, u32[]{:S(2)}, u32[]{:S(2)}) async-start(bf16[8,112,512]{2,1,0:T(8,128)(2,1)} %bitcast_dynamic-update-slice_fusion), calls=%async_computation | async-start | bytes 1835008 | tf_op jit(solution)/shard_map/all_to_all | solution.py:268
  114.1 5.5 %collective-permute-start.19 = (bf16[2,112,256]{2,1,0:T(8,128)(2,1)S(1)}, bf16[2,112,256]{2,1,0:T(8,128)(2,1)S(1)}, u32[]{:S(2)}, u32[]{:S(2)}) collective-permute-start(bf16[2,112,256]{2,1,0:T(8,128)(2,1)S(1)} %pad_maximum_fusion.13), channel_id=1, source_target_pairs={{0,8},{4,12},{8,0},{12,4},{16,24},{20,28},{24,16},{28,20},{1,9},{5... | collective-permute-start | bytes 344072 | tf_op jit(solution)/shard_map/ppermute | solution.py:36
  116.9 5.5 %collective-permute-start.16 = (bf16[2,4,28,256]{3,2,0,1:T(8,128)(2,1)S(1)}, bf16[2,4,28,256]{3,2,0,1:T(8,128)(2,1)S(1)}, u32[]{:S(2)}, u32[]{:S(2)}) collective-permute-start(bf16[2,4,28,256]{3,2,0,1:T(8,128)(2,1)S(1)} %pad_maximum_fusion.9), channel_id=1, source_target_pairs={{0,8},{4,12},{8,0},{12,4},{16,24},{20,28},{24,16},{28,20},{1,9},{5... | collective-permute-start | bytes 344072 | tf_op jit(solution)/shard_map/ppermute | solution.py:36
  119.7 8.5 %collective-permute-start.20 = (bf16[4,112,256]{2,1,0:T(8,128)(2,1)S(1)}, bf16[4,112,256]{2,1,0:T(8,128)(2,1)S(1)}, u32[]{:S(2)}, u32[]{:S(2)}) collective-permute-start(bf16[4,112,256]{2,1,0:T(8,128)(2,1)S(1)} %pad_maximum_fusion.8), channel_id=1, source_target_pairs={{0,16},{4,20},{8,24},{12,28},{16,0},{20,4},{24,8},{28,12},{1,17},{... | collective-permute-start | bytes 688136 | tf_op jit(solution)/shard_map/ppermute | solution.py:36
  123.2 10.5 %collective-permute-start.17 = (bf16[4,4,28,256]{3,2,0,1:T(8,128)(2,1)}, bf16[4,4,28,256]{3,2,0,1:T(8,128)(2,1)}, u32[]{:S(2)}, u32[]{:S(2)}) collective-permute-start(bf16[4,4,28,256]{3,2,0,1:T(8,128)(2,1)} %pad_maximum_fusion.6), channel_id=1, source_target_pairs={{0,16},{4,20},{8,24},{12,28},{16,0},{20,4},{24,8},{28,12},{1,17},{... | collective-permute-start | bytes 688136 | tf_op jit(solution)/shard_map/ppermute | solution.py:36
  157.4 31.0 %collective-permute-start.24 = (bf16[96,6656]{1,0:T(8,128)(2,1)}, bf16[96,6656]{1,0:T(8,128)(2,1)S(1)}, u32[]{:S(2)}, u32[]{:S(2)}) collective-permute-start(bf16[96,6656]{1,0:T(8,128)(2,1)} %collective-permute-done.14.refs_2_), channel_id=1, source_target_pairs={{1,0},{2,3},{5,4},{6,7},{9,8},{10,11},{13,12},{14,15},{17,16},{18,... | collective-permute-start | bytes 3833864 | tf_op jit(solution)/shard_map/ppermute | solution.py:68
  188.4 34.6 %collective-permute-start.26 = (bf16[4,16,4096]{2,1,0:T(8,128)(2,1)S(1)}, bf16[4,16,4096]{2,1,0:T(8,128)(2,1)S(1)}, u32[]{:S(2)}, u32[]{:S(2)}) collective-permute-start(bf16[4,16,4096]{2,1,0:T(8,128)(2,1)S(1)} %copy-done.5), channel_id=1, source_target_pairs={{0,4},{4,0},{8,12},{12,8},{16,20},{20,16},{24,28},{28,24},{1,5},{5... | collective-permute-start | bytes 1572872 | tf_op jit(solution)/shard_map/ppermute | solution.py:36
  188.4 47.0 %collective-permute-start.22 = (bf16[64,6656]{1,0:T(8,128)(2,1)S(1)}, bf16[64,6656]{1,0:T(8,128)(2,1)S(1)}, u32[]{:S(2)}, u32[]{:S(2)}) collective-permute-start(bf16[64,6656]{1,0:T(8,128)(2,1)S(1)} %bitcast.147), channel_id=1, source_target_pairs={{0,2},{1,3},{2,0},{3,1},{4,6},{5,7},{6,4},{7,5},{8,10},{9,11},{10,... | collective-permute-start | bytes 2555912 | tf_op jit(solution)/shard_map/ppermute | solution.py:36
  188.5 46.9 %collective-permute-start.21 = (bf16[64,6656]{1,0:T(8,128)(2,1)S(1)}, bf16[64,6656]{1,0:T(8,128)(2,1)S(1)}, u32[]{:S(2)}, u32[]{:S(2)}) collective-permute-start(bf16[64,6656]{1,0:T(8,128)(2,1)S(1)} %bitcast.148), channel_id=1, source_target_pairs={{0,1},{1,0},{2,3},{3,2},{4,5},{5,4},{6,7},{7,6},{8,9},{9,8},{10,11... | collective-permute-start | bytes 2555912 | tf_op jit(solution)/shard_map/ppermute | solution.py:36
  189.6 35.2 %collective-permute-start.25 = (f32[512,256]{1,0:T(8,128)S(1)}, f32[512,256]{1,0:T(8,128)S(1)}, u32[]{:S(2)}, u32[]{:S(2)}) collective-permute-start(f32[512,256]{1,0:T(8,128)S(1)} %convolution_multiply_fusion.1), channel_id=1, source_target_pairs={{0,16},{4,20},{8,24},{12,28},{16,0},{20,4},{24,8},{28,12},{1,17},{... | collective-permute-start | bytes 1572872 | tf_op jit(solution)/shard_map/ppermute | solution.py:36
  190.9 46.8 %collective-permute-start.33 = (bf16[64,6656]{1,0:T(8,128)(2,1)S(1)}, bf16[64,6656]{1,0:T(8,128)(2,1)S(1)}, u32[]{:S(2)}, u32[]{:S(2)}) collective-permute-start(bf16[64,6656]{1,0:T(8,128)(2,1)S(1)} %bitcast.149), channel_id=1, source_target_pairs={{1,2},{2,1},{5,6},{6,5},{9,10},{10,9},{13,14},{14,13},{17,18},{18,... | collective-permute-start | bytes 2555912 | tf_op jit(solution)/shard_map/ppermute | solution.py:67
  223.3 5.1 %collective-permute-start.27 = (bf16[2,16,2048]{2,1,0:T(8,128)(2,1)S(1)}, bf16[2,16,2048]{2,1,0:T(8,128)(2,1)S(1)}, u32[]{:S(2)}, u32[]{:S(2)}) collective-permute-start(bf16[2,16,2048]{2,1,0:T(8,128)(2,1)S(1)} %pad_maximum_fusion.10), channel_id=1, source_target_pairs={{0,8},{4,12},{8,0},{12,4},{16,24},{20,28},{24,16},{28,20},{1,9},{5... | collective-permute-start | bytes 393224 | tf_op jit(solution)/shard_map/ppermute | solution.py:36
  224.8 5.0 %collective-permute-start.29 = (bf16[2,16,2048]{2,1,0:T(8,128)(2,1)S(1)}, bf16[2,16,2048]{2,1,0:T(8,128)(2,1)S(1)}, u32[]{:S(2)}, u32[]{:S(2)}) collective-permute-start(bf16[2,16,2048]{2,1,0:T(8,128)(2,1)S(1)} %slice.342), channel_id=1, source_target_pairs={{0,16},{4,20},{8,24},{12,28},{16,0},{20,4},{24,8},{28,12},{1,17},{... | collective-permute-start | bytes 393224 | tf_op jit(solution)/shard_map/ppermute | solution.py:36
  235.4 21.4 %collective-permute-start.34 = (bf16[64,6656]{1,0:T(8,128)(2,1)S(1)}, bf16[64,6656]{1,0:T(8,128)(2,1)S(1)}, u32[]{:S(2)}, u32[]{:S(2)}) collective-permute-start(bf16[64,6656]{1,0:T(8,128)(2,1)S(1)} %collective-permute-done.22.refs_2_), channel_id=1, source_target_pairs={{1,0},{2,3},{5,4},{6,7},{9,8},{10,11},{13,12},{14,15},{17,16},{18,... | collective-permute-start | bytes 2555912 | tf_op jit(solution)/shard_map/ppermute | solution.py:68
  256.8 33.7 %collective-permute-start.35 = (f32[1024,256]{1,0:T(8,128)S(1)}, f32[1024,256]{1,0:T(8,128)}, u32[]{:S(2)}, u32[]{:S(2)}) collective-permute-start(f32[1024,256]{1,0:T(8,128)S(1)} %pad_maximum_fusion.2), channel_id=1, source_target_pairs={{0,8},{4,12},{8,0},{12,4},{16,24},{20,28},{24,16},{28,20},{1,9},{5... | collective-permute-start | bytes 3145736 | tf_op jit(solution)/shard_map/ppermute | solution.py:36
  262.5 30.3 %collective-permute-start.37 = (bf16[2,48,2048]{2,1,0:T(8,128)(2,1)S(1)}, bf16[2,48,2048]{2,1,0:T(8,128)(2,1)S(1)}, u32[]{:S(2)}, u32[]{:S(2)}) collective-permute-start(bf16[2,48,2048]{2,1,0:T(8,128)(2,1)S(1)} %pad_maximum_fusion.4), channel_id=1, source_target_pairs={{0,8},{4,12},{8,0},{12,4},{16,24},{20,28},{24,16},{28,20},{1,9},{5... | collective-permute-start | bytes 1179656 | tf_op jit(solution)/shard_map/ppermute | solution.py:36
  263.2 29.6 %collective-permute-start.39 = (bf16[2,48,2048]{2,1,0:T(8,128)(2,1)S(1)}, bf16[2,48,2048]{2,1,0:T(8,128)(2,1)S(1)}, u32[]{:S(2)}, u32[]{:S(2)}) collective-permute-start(bf16[2,48,2048]{2,1,0:T(8,128)(2,1)S(1)} %slice.354), channel_id=1, source_target_pairs={{0,16},{4,20},{8,24},{12,28},{16,0},{20,4},{24,8},{28,12},{1,17},{... | collective-permute-start | bytes 1179656 | tf_op jit(solution)/shard_map/ppermute | solution.py:36
  264.6 34.9 %collective-permute-start.32 = (bf16[32,6656]{1,0:T(8,128)(2,1)S(1)}, bf16[32,6656]{1,0:T(8,128)(2,1)S(1)}, u32[]{:S(2)}, u32[]{:S(2)}) collective-permute-start(bf16[32,6656]{1,0:T(8,128)(2,1)S(1)} %bitcast.153), channel_id=1, source_target_pairs={{0,2},{1,3},{2,0},{3,1},{4,6},{5,7},{6,4},{7,5},{8,10},{9,11},{10,... | collective-permute-start | bytes 1277960 | tf_op jit(solution)/shard_map/ppermute | solution.py:36
  264.6 34.9 %collective-permute-start.31 = (bf16[32,6656]{1,0:T(8,128)(2,1)S(1)}, bf16[32,6656]{1,0:T(8,128)(2,1)S(1)}, u32[]{:S(2)}, u32[]{:S(2)}) collective-permute-start(bf16[32,6656]{1,0:T(8,128)(2,1)S(1)} %bitcast.154), channel_id=1, source_target_pairs={{0,1},{1,0},{2,3},{3,2},{4,5},{5,4},{6,7},{7,6},{8,9},{9,8},{10,11... | collective-permute-start | bytes 1277960 | tf_op jit(solution)/shard_map/ppermute | solution.py:36
  290.5 10.8 %collective-permute-start.41 = (bf16[32,6656]{1,0:T(8,128)(2,1)S(1)}, bf16[32,6656]{1,0:T(8,128)(2,1)S(1)}, u32[]{:S(2)}, u32[]{:S(2)}) collective-permute-start(bf16[32,6656]{1,0:T(8,128)(2,1)S(1)} %bitcast.155), channel_id=1, source_target_pairs={{1,2},{2,1},{5,6},{6,5},{9,10},{10,9},{13,14},{14,13},{17,18},{18,... | collective-permute-start | bytes 1277960 | tf_op jit(solution)/shard_map/ppermute | solution.py:67
  292.9 5.9 %collective-permute-start.38 = (bf16[1,48,2048]{2,1,0:T(8,128)(2,1)S(1)}, bf16[1,48,2048]{2,1,0:T(8,128)(2,1)S(1)}, u32[]{:S(2)}, u32[]{:S(2)}) collective-permute-start(bf16[1,48,2048]{2,1,0:T(8,128)(2,1)S(1)} %get-tuple-element.165), channel_id=1, source_target_pairs={{0,16},{4,20},{8,24},{12,28},{16,0},{20,4},{24,8},{28,12},{1,17},{... | collective-permute-start | bytes 589832 | tf_op jit(solution)/shard_map/ppermute | solution.py:36
  293.6 5.7 %collective-permute-start.40 = (bf16[1,48,2048]{2,1,0:T(8,128)(2,1)S(1)}, bf16[1,48,2048]{2,1,0:T(8,128)(2,1)S(1)}, u32[]{:S(2)}, u32[]{:S(2)}) collective-permute-start(bf16[1,48,2048]{2,1,0:T(8,128)(2,1)S(1)} %get-tuple-element.166), channel_id=1, source_target_pairs={{0,8},{4,12},{8,0},{12,4},{16,24},{20,28},{24,16},{28,20},{1,9},{5... | collective-permute-start | bytes 589832 | tf_op jit(solution)/shard_map/ppermute | solution.py:36
  299.5 11.9 %collective-permute-start.42 = (bf16[32,6656]{1,0:T(8,128)(2,1)S(1)}, bf16[32,6656]{1,0:T(8,128)(2,1)S(1)}, u32[]{:S(2)}, u32[]{:S(2)}) collective-permute-start(bf16[32,6656]{1,0:T(8,128)(2,1)S(1)} %collective-permute-done.32.refs_2_), channel_id=1, source_target_pairs={{1,0},{2,3},{5,4},{6,7},{9,8},{10,11},{13,12},{14,15},{17,16},{18,... | collective-permute-start | bytes 1277960 | tf_op jit(solution)/shard_map/ppermute | solution.py:68
  336.1 9.2 %collective-permute-start.48 = (bf16[4,16,4096]{2,1,0:T(8,128)(2,1)S(1)}, bf16[4,16,4096]{2,1,0:T(8,128)(2,1)S(1)}, u32[]{:S(2)}, u32[]{:S(2)}) collective-permute-start(bf16[4,16,4096]{2,1,0:T(8,128)(2,1)S(1)} %get-tuple-element.141), channel_id=1, source_target_pairs={{0,4},{4,0},{8,12},{12,8},{16,20},{20,16},{24,28},{28,24},{1,5},{5... | collective-permute-start | bytes 1572872 | tf_op jit(solution)/shard_map/ppermute | solution.py:36
  336.2 12.2 %collective-permute-start.43 = (bf16[4,32,4096]{2,1,0:T(8,128)(2,1)S(1)}, bf16[4,32,4096]{2,1,0:T(8,128)(2,1)S(1)}, u32[]{:S(2)}, u32[]{:S(2)}) collective-permute-start(bf16[4,32,4096]{2,1,0:T(8,128)(2,1)S(1)} %get-tuple-element.135), channel_id=1, source_target_pairs={{0,4},{4,0},{8,12},{12,8},{16,20},{20,16},{24,28},{28,24},{1,5},{5... | collective-permute-start | bytes 3145736 | tf_op jit(solution)/shard_map/ppermute | solution.py:36
  336.7 30.9 %collective-permute-start.53 = (f32[2048,256]{1,0:T(8,128)S(1)}, f32[2048,256]{1,0:T(8,128)S(1)}, u32[]{:S(2)}, u32[]{:S(2)}) collective-permute-start(f32[2048,256]{1,0:T(8,128)S(1)} %pad_maximum_fusion.1), channel_id=1, source_target_pairs={{0,4},{4,0},{8,12},{12,8},{16,20},{20,16},{24,28},{28,24},{1,5},{5... | collective-permute-start | bytes 6291464 | tf_op jit(solution)/shard_map/ppermute | solution.py:36
  345.5 5.9 %collective-permute-start.49 = (bf16[2,16,2048]{2,1,0:T(8,128)(2,1)S(1)}, bf16[2,16,2048]{2,1,0:T(8,128)(2,1)S(1)}, u32[]{:S(2)}, u32[]{:S(2)}) collective-permute-start(bf16[2,16,2048]{2,1,0:T(8,128)(2,1)S(1)} %pad_maximum_fusion.12), channel_id=1, source_target_pairs={{0,8},{4,12},{8,0},{12,4},{16,24},{20,28},{24,16},{28,20},{1,9},{5... | collective-permute-start | bytes 393224 | tf_op jit(solution)/shard_map/ppermute | solution.py:36
  346.9 6.3 %collective-permute-start.51 = (bf16[2,16,2048]{2,1,0:T(8,128)(2,1)S(1)}, bf16[2,16,2048]{2,1,0:T(8,128)(2,1)S(1)}, u32[]{:S(2)}, u32[]{:S(2)}) collective-permute-start(bf16[2,16,2048]{2,1,0:T(8,128)(2,1)S(1)} %slice.376), channel_id=1, source_target_pairs={{0,16},{4,20},{8,24},{12,28},{16,0},{20,4},{24,8},{28,12},{1,17},{... | collective-permute-start | bytes 393224 | tf_op jit(solution)/shard_map/ppermute | solution.py:36
  348.9 8.9 %collective-permute-start.44 = (bf16[2,32,2048]{2,1,0:T(8,128)(2,1)S(1)}, bf16[2,32,2048]{2,1,0:T(8,128)(2,1)S(1)}, u32[]{:S(2)}, u32[]{:S(2)}) collective-permute-start(bf16[2,32,2048]{2,1,0:T(8,128)(2,1)S(1)} %pad_maximum_fusion.7), channel_id=1, source_target_pairs={{0,8},{4,12},{8,0},{12,4},{16,24},{20,28},{24,16},{28,20},{1,9},{5... | collective-permute-start | bytes 786440 | tf_op jit(solution)/shard_map/ppermute | solution.py:36
  349.5 9.3 %collective-permute-start.46 = (bf16[2,32,2048]{2,1,0:T(8,128)(2,1)S(1)}, bf16[2,32,2048]{2,1,0:T(8,128)(2,1)S(1)}, u32[]{:S(2)}, u32[]{:S(2)}) collective-permute-start(bf16[2,32,2048]{2,1,0:T(8,128)(2,1)S(1)} %slice.365), channel_id=1, source_target_pairs={{0,16},{4,20},{8,24},{12,28},{16,0},{20,4},{24,8},{28,12},{1,17},{... | collective-permute-start | bytes 786440 | tf_op jit(solution)/shard_map/ppermute | solution.py:36
  353.3 7.7 %collective-permute-start.50 = (bf16[1,16,2048]{2,1,0:T(8,128)(2,1)S(1)}, bf16[1,16,2048]{2,1,0:T(8,128)(2,1)S(1)}, u32[]{:S(2)}, u32[]{:S(2)}) collective-permute-start(bf16[1,16,2048]{2,1,0:T(8,128)(2,1)S(1)} %get-tuple-element.179), channel_id=1, source_target_pairs={{0,16},{4,20},{8,24},{12,28},{16,0},{20,4},{24,8},{28,12},{1,17},{... | collective-permute-start | bytes 196616 | tf_op jit(solution)/shard_map/ppermute | solution.py:36
  354.9 6.1 %collective-permute-start.52 = (bf16[1,16,2048]{2,1,0:T(8,128)(2,1)S(1)}, bf16[1,16,2048]{2,1,0:T(8,128)(2,1)S(1)}, u32[]{:S(2)}, u32[]{:S(2)}) collective-permute-start(bf16[1,16,2048]{2,1,0:T(8,128)(2,1)S(1)} %get-tuple-element.180), channel_id=1, source_target_pairs={{0,8},{4,12},{8,0},{12,4},{16,24},{20,28},{24,16},{28,20},{1,9},{5... | collective-permute-start | bytes 196616 | tf_op jit(solution)/shard_map/ppermute | solution.py:36
  358.9 5.0 %collective-permute-start.45 = (bf16[1,32,2048]{2,1,0:T(8,128)(2,1)S(1)}, bf16[1,32,2048]{2,1,0:T(8,128)(2,1)S(1)}, u32[]{:S(2)}, u32[]{:S(2)}) collective-permute-start(bf16[1,32,2048]{2,1,0:T(8,128)(2,1)S(1)} %get-tuple-element.171), channel_id=1, source_target_pairs={{0,16},{4,20},{8,24},{12,28},{16,0},{20,4},{24,8},{28,12},{1,17},{... | collective-permute-start | bytes 393224 | tf_op jit(solution)/shard_map/ppermute | solution.py:36
  360.4 5.0 %collective-permute-start.47 = (bf16[1,32,2048]{2,1,0:T(8,128)(2,1)S(1)}, bf16[1,32,2048]{2,1,0:T(8,128)(2,1)S(1)}, u32[]{:S(2)}, u32[]{:S(2)}) collective-permute-start(bf16[1,32,2048]{2,1,0:T(8,128)(2,1)S(1)} %get-tuple-element.172), channel_id=1, source_target_pairs={{0,8},{4,12},{8,0},{12,4},{16,24},{20,28},{24,16},{28,20},{1,9},{5... | collective-permute-start | bytes 393224 | tf_op jit(solution)/shard_map/ppermute | solution.py:36
  (26 other events, 323.7 us)

commit v5 on v4

--- a/solution.py
+++ b/solution.py
@@ -8,7 +8,7 @@
 from jax.sharding import PartitionSpec as P
 
 adapter_scale = 2.0
-short_rows = 16
+piece_rows = 32
 weight_rows = 512
 vmem_bytes = 40 * 2**20
 light = pl.CostEstimate(flops=0, bytes_accessed=2**16, transcendentals=0)
@@ -169,19 +169,26 @@
     )(*operands)
 
 
-def scatter_sum(kept, sent, axis):
-    bits = bits_of(axis)
-    live = kept + swap(sent, axis, 1)
+def scatter_begin(live):
     half = live.shape[2] // 2
+    return [
+        {p: live[p, :, side * half : (side + 1) * half] for p in range(live.shape[0])}
+        for side in range(2)
+    ]
+
+
+def scatter_hop(state, hop):
+    if hop == 0:
+        kept, sent = state
+        return scatter_begin(kept + swap(sent, "wide", 1))
+    bits = bits_of("wide")[:-1]
     done = []
-    for side, order in ((0, bits[:-1]), (1, bits[:-1][::-1])):
-        part = {p: live[p, :, side * half : (side + 1) * half] for p in range(live.shape[0])}
-        for bit in order:
-            stay = [p for p in part if not p & bit]
-            away = jnp.stack([part[p ^ bit].astype(jnp.bfloat16) for p in stay])
-            got = swap(away, axis, 2 * bit)
-            part = {p: part[p] + got[i] for i, p in enumerate(stay)}
-        done.append(part[0])
+    for part, order in zip(state, (bits, bits[::-1])):
+        bit = order[hop - 1]
+        stay = [p for p in part if not p & bit]
+        away = jnp.stack([part[p ^ bit].astype(jnp.bfloat16) for p in stay])
+        got = swap(away, "wide", 2 * bit)
+        done.append({p: part[p] + got[i] for i, p in enumerate(stay)})
     return done
 
 
@@ -191,11 +198,10 @@
 
 
 def cut_rows(owner_rows):
-    middle = owner_rows - 2 * short_rows
-    sizes = [owner_rows]
-    if middle >= 2 * short_rows:
-        large = -(-middle * 3 // (5 * short_rows)) * short_rows
-        sizes = [short_rows, large, middle - large, short_rows]
+    sizes = [piece_rows] * (owner_rows // piece_rows)
+    if not sizes:
+        sizes = [owner_rows]
+    sizes[0] += owner_rows - sum(sizes)
     starts = [sum(sizes[:i]) for i in range(len(sizes))]
     return list(zip(starts, sizes))
 
@@ -228,7 +234,6 @@
     blocks, near, far, middle, onward = {}, {}, {}, {}, {}
 
     def begin(i):
-        blocks[i] = block_of(grad_out, i)
         if line:
             near[i], far[i] = phase_a(blocks[i], "narrow")
         else:
@@ -240,95 +245,131 @@
         else:
             middle[i], onward[i] = near[i], far[i]
 
+    blocks[0] = block_of(grad_out, 0)
     begin(0)
 
-    act_part = jnp.dot(inputs, adapter_down_matrix, preferred_element_type=jnp.float32)
-    act_small = scatter_small(act_part, "narrow").astype(jnp.bfloat16)
+    act_sum = jnp.dot(inputs, adapter_down_matrix, preferred_element_type=jnp.float32)
     low_part = contract_trailing_axis(grad_out, b_factor)
     low_small = scatter_small(low_part, "wide").astype(jnp.bfloat16)
-    near[0], far[0], grad_out, low_small = hold(near[0], far[0], grad_out, low_small)
+
+    def exchange(act_sum, low_rows, bit):
+        count, part = low_rows.shape[0], low_rows.shape[1]
+        both = jnp.concatenate([act_sum, low_rows.reshape(-1, rank).astype(jnp.float32)], axis=0)
+        got = swap(both, "narrow", bit)
+        other = got[owner_rows:].reshape(count, part, rank).astype(jnp.bfloat16)
+        upper = (me_narrow & bit) != 0
+        first, second = jnp.where(upper, other, low_rows), jnp.where(upper, low_rows, other)
+        return act_sum + got[:owner_rows], jnp.concatenate([first, second], axis=0)
+
+    low_rows = low_small[None]
+    near[0], far[0], blocks[0], grad_out, low_rows, act_sum, inputs = hold(
+        near[0], far[0], blocks[0], grad_out, low_rows, act_sum, inputs
+    )
     complete(0)
-    act_rows = gather_ordered(act_small, "narrow", narrow_bits)
-    low_rows = gather_ordered(low_small[None], "narrow", narrow_bits)
-    middle[0], onward[0], grad_out, act_rows, low_rows, inputs = hold(
-        middle[0], onward[0], grad_out, act_rows, low_rows, inputs
-    )
-    if count > 1:
-        begin(1)
-
-    low_wide = gather_ordered(low_rows[None], "wide", wide_bits)
-    low_rank_all = jnp.swapaxes(low_wide, 0, 1).reshape(owner_rows * owners, rank)
-    low_rank_own = lax.dynamic_slice_in_dim(low_rank_all, me_wide * owner_rows, owner_rows)
-    low_term = adapter_scale * contract_trailing_axis(low_rank_own, adapter_down_matrix)
-    shares = inputs.reshape(owner_rows, owners, -1)
-    flipped = [
-        sum(bit for i, bit in enumerate(wide_bits) if w & wide_bits[len(wide_bits) - 1 - i])
-        for w in range(owners)
-    ]
-    columns = lax.all_to_all(
-        jnp.stack([shares[:, f] for f in flipped], axis=0), "wide", split_axis=0, concat_axis=0
-    ).reshape(owner_rows * owners, -1)
-    grad_a = adapter_matrix * contract_first(columns, low_rank_all)
-    grad_a_steps = wide_bits[::-1]
-
-    acts = gather_ordered(act_rows[None], "wide", wide_bits).reshape(groups, share, owner_rows, rank)
-    if line:
-        for bit in narrow_bits:
-            pair = acts.reshape(groups // (2 * bit), 2, bit, share, owner_rows, rank)
-            acts = jnp.where((me_narrow & bit) != 0, pair[:, ::-1], pair).reshape(acts.shape)
-    turned = [
-        acts[:, :, start : start + rows].reshape(owners * rows, rank).T for start, rows in pieces
-    ]
-
-    tokens, sums, results = {}, {}, {}
+    blocks[1] = block_of(grad_out, 1)
+    for bit in narrow_bits:
+        act_sum, low_rows = exchange(act_sum, low_rows, bit)
+    act_rows = act_sum.astype(jnp.bfloat16)
+    small = {"rows": jnp.concatenate([act_rows, low_rows.reshape(-1, rank)], axis=0)[None]}
+
+    def first_hop(bit):
+        small["rows"] = gather_ordered(small["rows"], "wide", [bit])
+
+    def regroup():
+        shares = small.pop("inputs").reshape(owner_rows, owners, -1)
+        flipped = [
+            sum(bit for i, bit in enumerate(wide_bits) if w & wide_bits[len(wide_bits) - 1 - i])
+            for w in range(owners)
+        ]
+        shares = jnp.stack([shares[:, f] for f in flipped], axis=0)
+        columns = lax.all_to_all(shares, "wide", split_axis=0, concat_axis=0)
+        small["columns"] = columns.reshape(owner_rows * owners, -1)
+
+    def share_made():
+        rows = small.pop("rows")
+        low_wide = rows[:, owner_rows:].reshape(owners, groups, low_small.shape[0], rank)
+        low_all = jnp.swapaxes(low_wide, 0, 1).reshape(owner_rows * owners, rank)
+        low_own = lax.dynamic_slice_in_dim(low_all, me_wide * owner_rows, owner_rows)
+        small["term"] = adapter_scale * contract_trailing_axis(low_own, adapter_down_matrix)
+        made = adapter_matrix * contract_first(small.pop("columns"), low_all)
+        small["grad_a"] = made.astype(jnp.bfloat16)
+        acts = rows[:, :owner_rows].reshape(groups, share, owner_rows, rank)
+        if line:
+            for bit in narrow_bits:
+                cut = acts.reshape(groups // (2 * bit), 2, bit, share, owner_rows, rank)
+                acts = jnp.where((me_narrow & bit) != 0, cut[:, ::-1], cut).reshape(acts.shape)
+        small["turned"] = [
+            acts[:, :, start : start + rows].reshape(owners * rows, rank).T
+            for start, rows in pieces
+        ]
+
+    def second_hop(bit):
+        if "grad_a" not in small:
+            share_made()
+        small["grad_a"] = gather_ordered(small["grad_a"], "wide", [bit])
+
+    hops = [functools.partial(first_hop, bit) for bit in wide_bits]
+    hops += [functools.partial(second_hop, bit) for bit in wide_bits[::-1]]
+    small["inputs"] = inputs
+    tokens, sums = {}, {}
+    waiting = {}
+
+    def step():
+        if hops:
+            hops.pop(0)()
+        for i in sums:
+            if waiting[i]:
+                sums[i] = scatter_hop(sums[i], waiting[i].pop(0))
 
     def run_pass(i):
         sources = [blocks[i], near[i], far[i], middle[i], onward[i]] if line else [near[i]]
-        tokens[i], *sums[i] = weight_pass(table, sources, w_base, owners)
-
-    def finish(i):
-        start, rows = pieces[i]
-        sides = scatter_sum(*sums.pop(i), "wide")
-        half = sides[0].shape[1]
-        mine = low_term[start : start + rows]
-        results[i] = jnp.concatenate(
-            [
-                (side + mine[:, j * half : (j + 1) * half]).astype(jnp.bfloat16)
-                for j, side in enumerate(sides)
-            ],
-            axis=1,
+        tokens[i], kept, sent = weight_pass(table, sources, w_base, owners)
+        sums[i] = (kept, sent)
+        waiting[i] = list(range(len(wide_bits)))
+
+    for i in range(count):
+        if i:
+            near[i], far[i], blocks, grad_out, small, sums = hold(
+                near[i], far[i], blocks, grad_out, small, sums
+            )
+            complete(i)
+            if i + 1 < count:
+                blocks[i + 1] = block_of(grad_out, i + 1)
+            step()
+        middle[i], onward[i], blocks, grad_out, small, sums = hold(
+            middle[i], onward[i], blocks, grad_out, small, sums
         )
-
-    run_pass(0)
-    for i in range(1, count):
-        near[i], far[i], grad_out, grad_a, turned, sums, low_term, results = hold(
-            near[i], far[i], grad_out, grad_a, turned, sums, low_term, results
-        )
-        complete(i)
         if i + 1 < count:
             begin(i + 1)
-            middle[i], onward[i], grad_a, sums, blocks[i + 1] = hold(
-                middle[i], onward[i], grad_a, sums, blocks[i + 1]
-            )
-        else:
-            middle[i], onward[i], grad_a, sums = hold(middle[i], onward[i], grad_a, sums)
-        finish(i - 1)
-        run_pass(i)
-        if grad_a_steps:
-            grad_a = gather_ordered(grad_a, "wide", grad_a_steps[:1])
-            grad_a_steps = grad_a_steps[1:]
-    grad_a = gather_ordered(grad_a, "wide", grad_a_steps)
-    step = max(128 * c for c in range(1, 14) if depth % (128 * c) == 0)
-    steps = depth // step
-    turned = [turned[i] for i in range(count)]
+            step()
+            if i == 0:
+                regroup()
+            run_pass(i)
+    step()
+    run_pass(count - 1)
+    while hops:
+        hops.pop(0)()
+    sums[count - 1] = scatter_hop(sums[count - 1], waiting[count - 1].pop(0))
+    columns_step = max(128 * c for c in range(1, 14) if depth % (128 * c) == 0)
+    steps = depth // columns_step
+    early = steps // 2 or 1
+    turned = small["turned"]
     tokens = [tokens[i] for i in range(count)]
-    grad_b = factor_gradient(turned, tokens, adapter_matrix, step, 0, steps // 2 or 1)
-    if steps > 1:
+    grad_b = factor_gradient(turned, tokens, adapter_matrix, columns_step, 0, early)
+    sums[count - 1], grad_b = hold(sums[count - 1], grad_b)
+    if steps > early:
         grad_b = factor_gradient(
-            turned, tokens, adapter_matrix, step, steps // 2, steps - steps // 2, grad_b
+            turned, tokens, adapter_matrix, columns_step, early, steps - early, grad_b
         )
-    finish(count - 1)
-    return (jnp.concatenate([results[i] for i in range(count)], axis=0), grad_a, grad_b)
+    results = []
+    for i, (start, rows) in enumerate(pieces):
+        for hop in waiting[i]:
+            sums[i] = scatter_hop(sums[i], hop)
+        mine = small["term"][start : start + rows]
+        summed = jnp.concatenate([part[0] for part in sums[i]], axis=1)
+        results.append((summed + mine).astype(jnp.bfloat16))
+    grad_a = small["grad_a"].astype(jnp.float32)
+    return (jnp.concatenate(results, axis=0), grad_a, grad_b)
 
 
 def solution(mesh):

time: 373 us -> 328 us (0.88)
  Pallas kernels: 113 us -> 87.4 us
  waiting for transfers between devices: 140 us -> 117 us
  starting transfers between devices: 64.8 us -> 47.3 us
  local copies, waits for them, and re-layouts: 22.9 us -> 40.3 us
    ppermute x4 -> x3, waiting for transfers between devices: 65.6 us -> 14 us  [phase_b(): lax.ppermute(far, axis, [(1, 0), (2, 3)])]
    ppermute x46 -> x32, waiting for transfers between devices: 74.7 us -> 103 us  [swap(): return lax.ppermute(value, axis, [(i, i ^ bit) for i in range(size)])]
    pallas_call x4 -> x3, Pallas kernels: 105 us -> 79.6 us  [weight_pass(): pl.pallas_call(functools.partial(pass_kernel, sources=len(sources), owner...]
    ppermute x46 -> x32, starting transfers between devices: 50 us -> 35 us  [swap(): return lax.ppermute(value, axis, [(i, i ^ bit) for i in range(size)])]
    unnamed x46 -> x64, local copies, waits for them, and re-layouts: 6.12 us -> 17.3 us
    add x0 -> x14, other arithmetic: none -> 7.41 us  [the longest x10 6.46 us: scatter_hop(): done.append({p: part[p] + got[i] for i, p in enumerate(stay)})]
  transfers between devices with their start and end apart: 55 -> 39, of which waited for: 27 -> 16; matrix products, arithmetic and copies ran while one was open for 12% -> 16% of each run, Pallas kernels for 24% -> 27%
where the time goes in v5:
time: 328 us; the launch traced here: 326 us
  waiting for transfers between devices  117 us (36%)
  Pallas kernels  87.4 us (27%)
  starting transfers between devices  47.3 us (14%)
  local copies, waits for them, and re-layouts  40.3 us (12%)
  other arithmetic  22.5 us (7%)
  matrix products  10.9 us (3%)
    ppermute x32, waiting for transfers between devices, swap(): return lax.ppermute(value, axis, [(i, i ^ bit) for i in range(size)])  103 us
    pallas_call x3, Pallas kernels, weight_pass(): pl.pallas_call(functools.partial(pass_kernel, sources=len(sources), owner...  79.6 us
    ppermute x32, starting transfers between devices, swap(): return lax.ppermute(value, axis, [(i, i ^ bit) for i in range(size)])  35 us
    unnamed x64, local copies, waits for them, and re-layouts  17.3 us
    ppermute x3, waiting for transfers between devices, phase_b(): lax.ppermute(far, axis, [(1, 0), (2, 3)])  14 us
    pallas_call x2, Pallas kernels, factor_gradient(): pl.pallas_call(functools.partial(factor_kernel, count=len(acts), scale=sc...  7.75 us
  transfers between devices with their start and end apart: 39, of which 16 were waited for; matrix products, arithmetic and copies ran while one was open for 16% of the time, Pallas kernels for 27%

profile of v5, /device:TPU:0, one launch (start us, length us, event | category | flops | bytes accessed | tf_op | source)
XLA Modules:
  0.0 326.3 jit_solution(2561211373755016129)
XLA Ops:
  0.7 1.9 copy-done
  2.6 3.7 %fusion.23 = f32[224,256]{1,0:T(8,128)} fusion(bf16[224,6656]{1,0:T(8,128)(2,1)} %param.6, bf16[256,6656]{1,0:T(8,128)(2,1)S(1)} %copy-done), kind=kOutput, calls=%fused_computation.154 | convolution fusion | flops 763363328 | bytes 6619136 | tf_op jit(solution)/shard_map/dot_general | solution.py:18
  7.3 3.0 collective-permute-start.2
  11.6 1.6 collective-permute-start
  13.3 2.6 collective-permute-start.1
  15.9 1.6 collective-permute-start.3
  17.5 2.7 collective-permute-done.3
  20.3 2.3 fusion.24
  22.7 45.9 %collective-permute-done.refs_1_ = bf16[96,6656]{1,0:T(8,128)(2,1)S(1)} collective-permute-done((bf16[96,6656]{1,0:T(8,128)(2,1)S(1)}, bf16[96,6656]{1,0:T(8,128)(2,1)S(1)}, u32[]{:S(2)}, u32[]{:S(2)}) %collective-permute-start) | collective-permute-done | bytes 1277984 | tf_op jit(solution)/shard_map/ppermute | solution.py:36
  68.5 2.5 collective-permute-done.1.refs_2_
  71.5 1.7 collective-permute-start.5
  74.5 1.7 collective-permute-done.7
  76.9 2.7 collective-permute-start.8
  80.9 28.0 %collective-permute-done.8 = f32[168,256]{1,0:T(8,128)} collective-permute-done((f32[168,256]{1,0:T(8,128)}, f32[168,256]{1,0:T(8,128)}, u32[]{:S(2)}, u32[]{:S(2)}) %collective-permute-start.8) | collective-permute-done | bytes 172064 | tf_op jit(solution)/shard_map/ppermute | solution.py:36
  113.1 1.5 reshape.113
  116.4 2.3 collective-permute-start.10
  118.7 1.5 copy.91
  120.2 1.7 fusion.21
  127.1 4.2 %all-to-all-start = ((bf16[8,112,512]{2,1,0:T(8,128)(2,1)}), bf16[8,112,512]{2,1,0:T(8,128)(2,1)}, u32[]{:S(2)}, u32[]{:S(2)}) async-start(bf16[8,112,512]{2,1,0:T(8,128)(2,1)} %bitcast_dynamic-update-slice_fusion), calls=%async_computation | async-start | bytes 1835008 | tf_op jit(solution)/shard_map/all_to_all | solution.py:285
  131.8 31.3 %weight_pass.3 = (bf16[384,6656]{1,0:T(8,128)(2,1)}, f32[4,48,4096]{2,1,0:T(8,128)S(1)}, bf16[4,48,4096]{2,1,0:T(8,128)(2,1)S(1)}) custom-call(s32[9]{0:T(128)S(1)} %stack.119.table, bf16[96,6656]{1,0:T(8,128)(2,1)S(1)} %bitcast.266, bf16[96,6656]{1,0:T(8,128)(2,1)S(1)} %collective-permute-done.refs_1_, bf16[96,6656]{1,0:T(8,128)(2,1)} %collective-permute-done.1.refs_2_, ...), custom_call_target="tpu_custom_call" | custom-call | bytes 65536 | tf_op jit(solution)/shard_map/weight_pass/pallas_call | solution.py:124
  163.1 1.7 copy-done.4
  167.3 1.8 collective-permute-start.14
  171.1 2.1 slice.252
  173.3 1.8 collective-permute-done.14
  178.6 14.0 %collective-permute-done.13.refs_4_ = bf16[64,6656]{1,0:T(8,128)(2,1)S(1)} collective-permute-done((bf16[64,6656]{1,0:T(8,128)(2,1)}, bf16[64,6656]{1,0:T(8,128)(2,1)S(1)}, u32[]{:S(2)}, u32[]{:S(2)}) %collective-permute-start.13) | collective-permute-done | bytes 852000 | tf_op jit(solution)/shard_map/ppermute | solution.py:68
  194.8 2.6 collective-permute-start.17
  197.5 1.7 collective-permute-start.18
  203.1 23.9 %weight_pass.4 = (bf16[256,6656]{1,0:T(8,128)(2,1)S(1)}, f32[4,32,4096]{2,1,0:T(8,128)S(1)}, bf16[4,32,4096]{2,1,0:T(8,128)(2,1)S(1)}) custom-call(s32[9]{0:T(128)S(1)} %stack.119.table, bf16[64,6656]{1,0:T(8,128)(2,1)S(1)} %bitcast.270, bf16[64,6656]{1,0:T(8,128)(2,1)} %collective-permute-done.9.refs_1_, bf16[64,6656]{1,0:T(8,128)(2,1)} %collective-permute-done.10.refs_2_, ...), custom_call_target="tpu_custom_call" | custom-call | bytes 65536 | tf_op jit(solution)/shard_map/weight_pass/pallas_call | solution.py:124
  227.1 2.1 convert_add_fusion.8
  229.2 1.7 convert_add_fusion.7
  235.7 1.6 collective-permute-start.21
  239.8 1.9 reshape.119
  241.8 2.5 fusion
  244.2 1.7 collective-permute-start.23
  245.9 1.7 copy.80
  248.6 1.7 copy.82
  252.0 2.4 convolution_multiply_fusion
  254.5 1.7 collective-permute-done.24
  261.9 24.4 %weight_pass.5 = (bf16[256,6656]{1,0:T(8,128)(2,1)S(1)}, f32[4,32,4096]{2,1,0:T(8,128)S(1)}, bf16[4,32,4096]{2,1,0:T(8,128)(2,1)S(1)}) custom-call(s32[9]{0:T(128)S(1)} %stack.119.table, bf16[64,6656]{1,0:T(8,128)(2,1)} %bitcast.27.refs_0_, bf16[64,6656]{1,0:T(8,128)(2,1)S(1)} %copy-done.11, bf16[64,6656]{1,0:T(8,128)(2,1)} %collective-permute-done.17.refs_2_, ...), custom_call_target="tpu_custom_call" | custom-call | bytes 65536 | tf_op jit(solution)/shard_map/weight_pass/pallas_call | solution.py:124
  287.5 3.9 %factor_gradient.2.refs_6_ = f32[256,6656]{1,0:T(8,128)} custom-call(bf16[256,384]{1,0:T(8,128)(2,1)S(1)} %bitcast.271, bf16[256,256]{1,0:T(8,128)(2,1)S(1)} %bitcast.273, bf16[256,256]{1,0:T(8,128)(2,1)S(1)} %bitcast.275, bf16[384,6656]{1,0:T(8,128)(2,1)S(1)} %bitcast.262, bf16[256,6656]{1,0:T(8,128)(2,1)S(1)} %get-tuple-element.157.refs_4_, ...), custom_call_target="tpu_custom_call" | custom-call | bytes 65536 | tf_op jit(solution)/shard_map/factor_gradient/pallas_call | solution.py:159
  293.6 1.5 collective-permute-start.28
  295.1 8.5 %collective-permute-done.30 = bf16[1,32,2048]{2,1,0:T(8,128)(2,1)S(1)} collective-permute-done((bf16[1,32,2048]{2,1,0:T(8,128)(2,1)S(1)}, bf16[1,32,2048]{2,1,0:T(8,128)(2,1)S(1)}, u32[]{:S(2)}, u32[]{:S(2)}) %collective-permute-start.30) | collective-permute-done | bytes 131104 | tf_op jit(solution)/shard_map/ppermute | solution.py:36
  305.2 1.5 collective-permute-start.34
  307.9 3.9 %factor_gradient.3 = f32[256,6656]{1,0:T(8,128)} custom-call(bf16[256,384]{1,0:T(8,128)(2,1)S(1)} %bitcast.272, bf16[256,256]{1,0:T(8,128)(2,1)S(1)} %bitcast.274, bf16[256,256]{1,0:T(8,128)(2,1)S(1)} %bitcast.276, bf16[384,6656]{1,0:T(8,128)(2,1)S(1)} %bitcast.262, ...), custom_call_target="tpu_custom_call", output_to_operand_aliasing={{}: (6, {})} | custom-call | bytes 65536 | tf_op jit(solution)/shard_map/factor_gradient/pallas_call | solution.py:159
  314.1 2.0 collective-permute-done.32
  316.5 2.0 collective-permute-done.35
  318.6 2.6 collective-permute-done.33
  322.8 2.5 maximum_convert_fusion
  (186 shorter events, 59.3 us)
Async XLA Ops:
  6.3 9.6 %copy-start.25 = (f32[224,256]{1,0:T(8,128)S(1)}, f32[224,256]{1,0:T(8,128)}, u32[]{:S(2)}) copy-start(f32[224,256]{1,0:T(8,128)} %fusion.23) | copy-start | bytes 688132
  7.3 8.6 %collective-permute-start.2 = (f32[112,256]{1,0:T(8,128)S(1)}, f32[112,256]{1,0:T(8,128)S(1)}, u32[]{:S(2)}, u32[]{:S(2)}) collective-permute-start(f32[112,256]{1,0:T(8,128)S(1)} %dynamic-slice_bitcast_fusion), channel_id=1, source_target_pairs={{0,16},{4,20},{8,24},{12,28},{16,0},{20,4},{24,8},{28,12},{1,17},{... | collective-permute-start | bytes 344072 | tf_op jit(solution)/shard_map/ppermute | solution.py:36
  11.6 56.9 %collective-permute-start = (bf16[96,6656]{1,0:T(8,128)(2,1)S(1)}, bf16[96,6656]{1,0:T(8,128)(2,1)S(1)}, u32[]{:S(2)}, u32[]{:S(2)}) collective-permute-start(bf16[96,6656]{1,0:T(8,128)(2,1)S(1)} %bitcast.263), channel_id=1, source_target_pairs={{0,1},{1,0},{2,3},{3,2},{4,5},{5,4},{6,7},{7,6},{8,9},{9,8},{10,11... | collective-permute-start | bytes 3833864 | tf_op jit(solution)/shard_map/ppermute | solution.py:36
  13.3 57.7 %collective-permute-start.1 = (bf16[96,6656]{1,0:T(8,128)(2,1)S(1)}, bf16[96,6656]{1,0:T(8,128)(2,1)}, u32[]{:S(2)}, u32[]{:S(2)}) collective-permute-start(bf16[96,6656]{1,0:T(8,128)(2,1)S(1)} %bitcast.264), channel_id=1, source_target_pairs={{0,2},{1,3},{2,0},{3,1},{4,6},{5,7},{6,4},{7,5},{8,10},{9,11},{10,... | collective-permute-start | bytes 3833864 | tf_op jit(solution)/shard_map/ppermute | solution.py:36
  15.9 4.2 %collective-permute-start.3 = (f32[56,256]{1,0:T(8,128)S(1)}, f32[56,256]{1,0:T(8,128)S(1)}, u32[]{:S(2)}, u32[]{:S(2)}) collective-permute-start(f32[56,256]{1,0:T(8,128)S(1)} %dynamic-slice_bitcast_fusion.1), channel_id=1, source_target_pairs={{0,8},{4,12},{8,0},{12,4},{16,24},{20,28},{24,16},{28,20},{1,9},{5... | collective-permute-start | bytes 172040 | tf_op jit(solution)/shard_map/ppermute | solution.py:36
  20.2 2.4 collective-permute-start.4
  71.0 5.2 %collective-permute-start.7 = (f32[140,256]{1,0:T(8,128)S(1)}, f32[140,256]{1,0:T(8,128)S(1)}, u32[]{:S(2)}, u32[]{:S(2)}) collective-permute-start(f32[140,256]{1,0:T(8,128)S(1)} %pad_maximum_fusion.13), channel_id=1, source_target_pairs={{0,1},{1,0},{2,3},{3,2},{4,5},{5,4},{6,7},{7,6},{8,9},{9,8},{10,11... | collective-permute-start | bytes 430088 | tf_op jit(solution)/shard_map/ppermute | solution.py:36
  71.5 44.8 %collective-permute-start.5 = (bf16[96,6656]{1,0:T(8,128)(2,1)S(1)}, bf16[96,6656]{1,0:T(8,128)(2,1)}, u32[]{:S(2)}, u32[]{:S(2)}) collective-permute-start(bf16[96,6656]{1,0:T(8,128)(2,1)S(1)} %bitcast.265), channel_id=1, source_target_pairs={{1,2},{2,1},{5,6},{6,5},{9,10},{10,9},{13,14},{14,13},{17,18},{18,... | collective-permute-start | bytes 3833864 | tf_op jit(solution)/shard_map/ppermute | solution.py:67
  73.2 43.1 %collective-permute-start.6 = (bf16[96,6656]{1,0:T(8,128)(2,1)}, bf16[96,6656]{1,0:T(8,128)(2,1)}, u32[]{:S(2)}, u32[]{:S(2)}) collective-permute-start(bf16[96,6656]{1,0:T(8,128)(2,1)} %collective-permute-done.1.refs_2_), channel_id=1, source_target_pairs={{1,0},{2,3},{5,4},{6,7},{9,8},{10,11},{13,12},{14,15},{17,16},{18,... | collective-permute-start | bytes 3833864 | tf_op jit(solution)/shard_map/ppermute | solution.py:68
  76.9 32.0 %collective-permute-start.8 = (f32[168,256]{1,0:T(8,128)}, f32[168,256]{1,0:T(8,128)}, u32[]{:S(2)}, u32[]{:S(2)}) collective-permute-start(f32[168,256]{1,0:T(8,128)} %pad_maximum_fusion.12), channel_id=1, source_target_pairs={{0,2},{1,3},{2,0},{3,1},{4,6},{5,7},{6,4},{7,5},{8,10},{9,11},{10,... | collective-permute-start | bytes 516104 | tf_op jit(solution)/shard_map/ppermute | solution.py:36
  80.9 88.2 %copy-start.2 = (bf16[2,32,6656]{2,1,0:T(8,128)(2,1)}, bf16[2,32,6656]{2,1,0:T(8,128)(2,1)S(1)}, u32[]{:S(2)}) copy-start(bf16[2,32,6656]{2,1,0:T(8,128)(2,1)S(1)} %slice.239) | copy-start | bytes 2555908
  116.3 50.6 %collective-permute-start.9 = (bf16[64,6656]{1,0:T(8,128)(2,1)S(1)}, bf16[64,6656]{1,0:T(8,128)(2,1)}, u32[]{:S(2)}, u32[]{:S(2)}) collective-permute-start(bf16[64,6656]{1,0:T(8,128)(2,1)S(1)} %bitcast.267), channel_id=1, source_target_pairs={{0,1},{1,0},{2,3},{3,2},{4,5},{5,4},{6,7},{7,6},{8,9},{9,8},{10,11... | collective-permute-start | bytes 2555912 | tf_op jit(solution)/shard_map/ppermute | solution.py:36
  116.4 50.5 %collective-permute-start.10 = (bf16[64,6656]{1,0:T(8,128)(2,1)S(1)}, bf16[64,6656]{1,0:T(8,128)(2,1)}, u32[]{:S(2)}, u32[]{:S(2)}) collective-permute-start(bf16[64,6656]{1,0:T(8,128)(2,1)S(1)} %bitcast.268), channel_id=1, source_target_pairs={{0,2},{1,3},{2,0},{3,1},{4,6},{5,7},{6,4},{7,5},{8,10},{9,11},{10,... | collective-permute-start | bytes 2555912 | tf_op jit(solution)/shard_map/ppermute | solution.py:36
  127.1 39.8 %all-to-all-start = ((bf16[8,112,512]{2,1,0:T(8,128)(2,1)}), bf16[8,112,512]{2,1,0:T(8,128)(2,1)}, u32[]{:S(2)}, u32[]{:S(2)}) async-start(bf16[8,112,512]{2,1,0:T(8,128)(2,1)} %bitcast_dynamic-update-slice_fusion), calls=%async_computation | async-start | bytes 1835008 | tf_op jit(solution)/shard_map/all_to_all | solution.py:285
  131.4 34.6 %collective-permute-start.11 = (bf16[1,224,256]{2,1,0:T(8,128)(2,1)S(1)}, bf16[1,224,256]{2,1,0:T(8,128)(2,1)}, u32[]{:S(2)}, u32[]{:S(2)}) collective-permute-start(bf16[1,224,256]{2,1,0:T(8,128)(2,1)S(1)} %maximum_bitcast_fusion), channel_id=1, source_target_pairs={{0,4},{4,0},{8,12},{12,8},{16,20},{20,16},{24,28},{28,24},{1,5},{5... | collective-permute-start | bytes 344072 | tf_op jit(solution)/shard_map/ppermute | solution.py:36
  166.9 9.0 %copy-start.5 = (f32[4,48,4096]{2,1,0:T(8,128)S(1)}, f32[4,48,4096]{2,1,0:T(8,128)}, u32[]{:S(2)}) copy-start(f32[4,48,4096]{2,1,0:T(8,128)} %copy-done.4) | copy-start | bytes 9437188
  167.0 8.9 %collective-permute-start.15 = (bf16[4,48,4096]{2,1,0:T(8,128)(2,1)}, bf16[4,48,4096]{2,1,0:T(8,128)(2,1)S(1)}, u32[]{:S(2)}, u32[]{:S(2)}) collective-permute-start(bf16[4,48,4096]{2,1,0:T(8,128)(2,1)} %copy-done.16), channel_id=1, source_target_pairs={{0,4},{4,0},{8,12},{12,8},{16,20},{20,16},{24,28},{28,24},{1,5},{5... | collective-permute-start | bytes 4718600 | tf_op jit(solution)/shard_map/ppermute | solution.py:36
  167.3 7.8 %collective-permute-start.14 = (bf16[2,224,256]{2,1,0:T(8,128)(2,1)S(1)}, bf16[2,224,256]{2,1,0:T(8,128)(2,1)S(1)}, u32[]{:S(2)}, u32[]{:S(2)}) collective-permute-start(bf16[2,224,256]{2,1,0:T(8,128)(2,1)S(1)} %pad_maximum_fusion.11), channel_id=1, source_target_pairs={{0,8},{4,12},{8,0},{12,4},{16,24},{20,28},{24,16},{28,20},{1,9},{5... | collective-permute-start | bytes 688136 | tf_op jit(solution)/shard_map/ppermute | solution.py:36
  169.1 8.6 %collective-permute-start.12 = (bf16[64,6656]{1,0:T(8,128)(2,1)S(1)}, bf16[64,6656]{1,0:T(8,128)(2,1)S(1)}, u32[]{:S(2)}, u32[]{:S(2)}) collective-permute-start(bf16[64,6656]{1,0:T(8,128)(2,1)S(1)} %bitcast.269), channel_id=1, source_target_pairs={{1,2},{2,1},{5,6},{6,5},{9,10},{10,9},{13,14},{14,13},{17,18},{18,... | collective-permute-start | bytes 2555912 | tf_op jit(solution)/shard_map/ppermute | solution.py:67
  169.8 22.8 %collective-permute-start.13 = (bf16[64,6656]{1,0:T(8,128)(2,1)}, bf16[64,6656]{1,0:T(8,128)(2,1)S(1)}, u32[]{:S(2)}, u32[]{:S(2)}) collective-permute-start(bf16[64,6656]{1,0:T(8,128)(2,1)} %collective-permute-done.10.refs_2_), channel_id=1, source_target_pairs={{1,0},{2,3},{5,4},{6,7},{9,8},{10,11},{13,12},{14,15},{17,16},{18,... | collective-permute-start | bytes 2555912 | tf_op jit(solution)/shard_map/ppermute | solution.py:68
  194.3 32.7 %collective-permute-start.19 = (bf16[2,48,2048]{2,1,0:T(8,128)(2,1)}, bf16[2,48,2048]{2,1,0:T(8,128)(2,1)}, u32[]{:S(2)}, u32[]{:S(2)}) collective-permute-start(bf16[2,48,2048]{2,1,0:T(8,128)(2,1)} %pad_maximum_fusion.5), channel_id=1, source_target_pairs={{0,8},{4,12},{8,0},{12,4},{16,24},{20,28},{24,16},{28,20},{1,9},{5... | collective-permute-start | bytes 1179656 | tf_op jit(solution)/shard_map/ppermute | solution.py:36
  194.8 38.8 %collective-permute-start.16 = (bf16[64,6656]{1,0:T(8,128)(2,1)}, bf16[64,6656]{1,0:T(8,128)(2,1)S(1)}, u32[]{:S(2)}, u32[]{:S(2)}) collective-permute-start(bf16[64,6656]{1,0:T(8,128)(2,1)} %bitcast.27.refs_0_), channel_id=1, source_target_pairs={{0,1},{1,0},{2,3},{3,2},{4,5},{5,4},{6,7},{7,6},{8,9},{9,8},{10,11... | collective-permute-start | bytes 2555912 | tf_op jit(solution)/shard_map/ppermute | solution.py:36
  194.8 39.1 %collective-permute-start.17 = (bf16[64,6656]{1,0:T(8,128)(2,1)}, bf16[64,6656]{1,0:T(8,128)(2,1)}, u32[]{:S(2)}, u32[]{:S(2)}) collective-permute-start(bf16[64,6656]{1,0:T(8,128)(2,1)} %bitcast.27.refs_0_), channel_id=1, source_target_pairs={{0,2},{1,3},{2,0},{3,1},{4,6},{5,7},{6,4},{7,5},{8,10},{9,11},{10,... | collective-permute-start | bytes 2555912 | tf_op jit(solution)/shard_map/ppermute | solution.py:36
  197.5 34.9 %collective-permute-start.18 = (bf16[4,224,256]{2,1,0:T(8,128)(2,1)}, bf16[4,224,256]{2,1,0:T(8,128)(2,1)S(1)}, u32[]{:S(2)}, u32[]{:S(2)}) collective-permute-start(bf16[4,224,256]{2,1,0:T(8,128)(2,1)} %pad_maximum_fusion.4), channel_id=1, source_target_pairs={{0,16},{4,20},{8,24},{12,28},{16,0},{20,4},{24,8},{28,12},{1,17},{... | collective-permute-start | bytes 1376264 | tf_op jit(solution)/shard_map/ppermute | solution.py:36
  199.2 31.6 %collective-permute-start.20 = (bf16[2,48,2048]{2,1,0:T(8,128)(2,1)S(1)}, bf16[2,48,2048]{2,1,0:T(8,128)(2,1)S(1)}, u32[]{:S(2)}, u32[]{:S(2)}) collective-permute-start(bf16[2,48,2048]{2,1,0:T(8,128)(2,1)S(1)} %pad_maximum_fusion.6), channel_id=1, source_target_pairs={{0,16},{4,20},{8,24},{12,28},{16,0},{20,4},{24,8},{28,12},{1,17},{... | collective-permute-start | bytes 1179656 | tf_op jit(solution)/shard_map/ppermute | solution.py:36
  203.1 24.0 %copy-start.22 = (f32[48,2048]{1,0:T(8,128)S(1)}, f32[48,2048]{1,0:T(8,128)}, u32[]{:S(2)}) copy-start(f32[48,2048]{1,0:T(8,128)} %get-tuple-element.113) | copy-start | bytes 1179652
  203.1 26.1 %copy-start.21 = (f32[48,2048]{1,0:T(8,128)S(1)}, f32[48,2048]{1,0:T(8,128)}, u32[]{:S(2)}) copy-start(f32[48,2048]{1,0:T(8,128)} %get-tuple-element.116) | copy-start | bytes 1179652
  203.1 27.7 %copy-start.20 = (f32[48,2048]{1,0:T(8,128)S(1)}, f32[48,2048]{1,0:T(8,128)}, u32[]{:S(2)}) copy-start(f32[48,2048]{1,0:T(8,128)} %get-tuple-element.117) | copy-start | bytes 1179652
  235.7 23.6 %collective-permute-start.21 = (bf16[64,6656]{1,0:T(8,128)(2,1)}, bf16[64,6656]{1,0:T(8,128)(2,1)}, u32[]{:S(2)}, u32[]{:S(2)}) collective-permute-start(bf16[64,6656]{1,0:T(8,128)(2,1)} %bitcast.27.refs_0_), channel_id=1, source_target_pairs={{1,2},{2,1},{5,6},{6,5},{9,10},{10,9},{13,14},{14,13},{17,18},{18,... | collective-permute-start | bytes 2555912 | tf_op jit(solution)/shard_map/ppermute | solution.py:67
  237.3 22.0 %collective-permute-start.22 = (bf16[64,6656]{1,0:T(8,128)(2,1)}, bf16[64,6656]{1,0:T(8,128)(2,1)}, u32[]{:S(2)}, u32[]{:S(2)}) collective-permute-start(bf16[64,6656]{1,0:T(8,128)(2,1)} %collective-permute-done.17.refs_2_), channel_id=1, source_target_pairs={{1,0},{2,3},{5,4},{6,7},{9,8},{10,11},{13,12},{14,15},{17,16},{18,... | collective-permute-start | bytes 2555912 | tf_op jit(solution)/shard_map/ppermute | solution.py:68
  244.2 12.4 %collective-permute-start.23 = (bf16[512,256]{1,0:T(8,128)(2,1)}, bf16[512,256]{1,0:T(8,128)(2,1)}, u32[]{:S(2)}, u32[]{:S(2)}) collective-permute-start(bf16[512,256]{1,0:T(8,128)(2,1)} %fusion), channel_id=1, source_target_pairs={{0,16},{4,20},{8,24},{12,28},{16,0},{20,4},{24,8},{28,12},{1,17},{... | collective-permute-start | bytes 786440 | tf_op jit(solution)/shard_map/ppermute | solution.py:36
  250.3 5.9 %collective-permute-start.24 = (bf16[1,48,2048]{2,1,0:T(8,128)(2,1)}, bf16[1,48,2048]{2,1,0:T(8,128)(2,1)S(1)}, u32[]{:S(2)}, u32[]{:S(2)}) collective-permute-start(bf16[1,48,2048]{2,1,0:T(8,128)(2,1)} %bitcast.306), channel_id=1, source_target_pairs={{0,16},{4,20},{8,24},{12,28},{16,0},{20,4},{24,8},{28,12},{1,17},{... | collective-permute-start | bytes 589832 | tf_op jit(solution)/shard_map/ppermute | solution.py:36
  250.7 5.9 %collective-permute-start.25 = (bf16[1,48,2048]{2,1,0:T(8,128)(2,1)}, bf16[1,48,2048]{2,1,0:T(8,128)(2,1)S(1)}, u32[]{:S(2)}, u32[]{:S(2)}) collective-permute-start(bf16[1,48,2048]{2,1,0:T(8,128)(2,1)} %bitcast.305), channel_id=1, source_target_pairs={{0,8},{4,12},{8,0},{12,4},{16,24},{20,28},{24,16},{28,20},{1,9},{5... | collective-permute-start | bytes 589832 | tf_op jit(solution)/shard_map/ppermute | solution.py:36
  256.2 2.7 collective-permute-start.26
  260.0 31.4 %collective-permute-start.29 = (bf16[2,32,2048]{2,1,0:T(8,128)(2,1)}, bf16[2,32,2048]{2,1,0:T(8,128)(2,1)}, u32[]{:S(2)}, u32[]{:S(2)}) collective-permute-start(bf16[2,32,2048]{2,1,0:T(8,128)(2,1)} %pad_maximum_fusion.8), channel_id=1, source_target_pairs={{0,16},{4,20},{8,24},{12,28},{16,0},{20,4},{24,8},{28,12},{1,17},{... | collective-permute-start | bytes 786440 | tf_op jit(solution)/shard_map/ppermute | solution.py:36
  260.6 26.9 %slice-start = ((s8[5111808]{0:T(1024)(128)(4,1)}), s8[4194304]{0:T(1024)(128)(4,1)S(1)}, s32[]{:S(2)}) async-start(s8[5111808]{0:T(1024)(128)(4,1)} %bitcast.261), calls=%async_computation.1 | async-start | bytes 8388608
  260.6 26.9 %slice-start.1 = ((s8[5111808]{0:T(1024)(128)(4,1)}), s8[917504]{0:T(1024)(128)(4,1)S(1)}, s32[]{:S(2)}) async-start(s8[5111808]{0:T(1024)(128)(4,1)} %bitcast.261), calls=%async_computation.2 | async-start | bytes 1835008
  260.6 26.9 %copy-start.9 = (bf16[256,256]{0,1:T(8,128)(2,1)S(1)}, bf16[256,256]{0,1:T(8,128)(2,1)}, u32[]{:S(2)}) copy-start(bf16[256,256]{0,1:T(8,128)(2,1)} %copy.82) | copy-start | bytes 393220
  260.7 32.9 %collective-permute-start.27 = (bf16[2,32,2048]{2,1,0:T(8,128)(2,1)S(1)}, bf16[2,32,2048]{2,1,0:T(8,128)(2,1)S(1)}, u32[]{:S(2)}, u32[]{:S(2)}) collective-permute-start(bf16[2,32,2048]{2,1,0:T(8,128)(2,1)S(1)} %pad_maximum_fusion.7), channel_id=1, source_target_pairs={{0,8},{4,12},{8,0},{12,4},{16,24},{20,28},{24,16},{28,20},{1,9},{5... | collective-permute-start | bytes 786440 | tf_op jit(solution)/shard_map/ppermute | solution.py:36
  286.4 18.4 %collective-permute-start.31 = (bf16[4,32,4096]{2,1,0:T(8,128)(2,1)S(1)}, bf16[4,32,4096]{2,1,0:T(8,128)(2,1)S(1)}, u32[]{:S(2)}, u32[]{:S(2)}) collective-permute-start(bf16[4,32,4096]{2,1,0:T(8,128)(2,1)S(1)} %get-tuple-element.152), channel_id=1, source_target_pairs={{0,4},{4,0},{8,12},{12,8},{16,20},{20,16},{24,28},{28,24},{1,5},{5... | collective-permute-start | bytes 3145736 | tf_op jit(solution)/shard_map/ppermute | solution.py:36
  286.4 18.2 %collective-permute-start.36 = (bf16[1024,256]{1,0:T(8,128)(2,1)S(1)}, bf16[1024,256]{1,0:T(8,128)(2,1)S(1)}, u32[]{:S(2)}, u32[]{:S(2)}) collective-permute-start(bf16[1024,256]{1,0:T(8,128)(2,1)S(1)} %pad_maximum_fusion.3), channel_id=1, source_target_pairs={{0,8},{4,12},{8,0},{12,4},{16,24},{20,28},{24,16},{28,20},{1,9},{5... | collective-permute-start | bytes 1572872 | tf_op jit(solution)/shard_map/ppermute | solution.py:36
  292.4 11.2 %collective-permute-start.30 = (bf16[1,32,2048]{2,1,0:T(8,128)(2,1)S(1)}, bf16[1,32,2048]{2,1,0:T(8,128)(2,1)S(1)}, u32[]{:S(2)}, u32[]{:S(2)}) collective-permute-start(bf16[1,32,2048]{2,1,0:T(8,128)(2,1)S(1)} %fusion.10), channel_id=1, source_target_pairs={{0,8},{4,12},{8,0},{12,4},{16,24},{20,28},{24,16},{28,20},{1,9},{5... | collective-permute-start | bytes 393224 | tf_op jit(solution)/shard_map/ppermute | solution.py:36
  293.6 11.0 %collective-permute-start.28 = (bf16[1,32,2048]{2,1,0:T(8,128)(2,1)S(1)}, bf16[1,32,2048]{2,1,0:T(8,128)(2,1)S(1)}, u32[]{:S(2)}, u32[]{:S(2)}) collective-permute-start(bf16[1,32,2048]{2,1,0:T(8,128)(2,1)S(1)} %fusion.9), channel_id=1, source_target_pairs={{0,16},{4,20},{8,24},{12,28},{16,0},{20,4},{24,8},{28,12},{1,17},{... | collective-permute-start | bytes 393224 | tf_op jit(solution)/shard_map/ppermute | solution.py:36
  305.2 7.9 %collective-permute-start.34 = (bf16[2,32,2048]{2,1,0:T(8,128)(2,1)S(1)}, bf16[2,32,2048]{2,1,0:T(8,128)(2,1)S(1)}, u32[]{:S(2)}, u32[]{:S(2)}) collective-permute-start(bf16[2,32,2048]{2,1,0:T(8,128)(2,1)S(1)} %pad_maximum_fusion.10), channel_id=1, source_target_pairs={{0,16},{4,20},{8,24},{12,28},{16,0},{20,4},{24,8},{28,12},{1,17},{... | collective-permute-start | bytes 786440 | tf_op jit(solution)/shard_map/ppermute | solution.py:36
  306.8 15.5 %collective-permute-start.37 = (bf16[2048,256]{1,0:T(8,128)(2,1)S(1)}, bf16[2048,256]{1,0:T(8,128)(2,1)S(1)}, u32[]{:S(2)}, u32[]{:S(2)}) collective-permute-start(bf16[2048,256]{1,0:T(8,128)(2,1)S(1)} %pad_maximum_fusion), channel_id=1, source_target_pairs={{0,4},{4,0},{8,12},{12,8},{16,20},{20,16},{24,28},{28,24},{1,5},{5... | collective-permute-start | bytes 3145736 | tf_op jit(solution)/shard_map/ppermute | solution.py:36
  306.9 9.2 %collective-permute-start.32 = (bf16[2,32,2048]{2,1,0:T(8,128)(2,1)S(1)}, bf16[2,32,2048]{2,1,0:T(8,128)(2,1)S(1)}, u32[]{:S(2)}, u32[]{:S(2)}) collective-permute-start(bf16[2,32,2048]{2,1,0:T(8,128)(2,1)S(1)} %pad_maximum_fusion.9), channel_id=1, source_target_pairs={{0,8},{4,12},{8,0},{12,4},{16,24},{20,28},{24,16},{28,20},{1,9},{5... | collective-permute-start | bytes 786440 | tf_op jit(solution)/shard_map/ppermute | solution.py:36
  313.2 5.3 %collective-permute-start.35 = (bf16[1,32,2048]{2,1,0:T(8,128)(2,1)S(1)}, bf16[1,32,2048]{2,1,0:T(8,128)(2,1)S(1)}, u32[]{:S(2)}, u32[]{:S(2)}) collective-permute-start(bf16[1,32,2048]{2,1,0:T(8,128)(2,1)S(1)} %fusion.12), channel_id=1, source_target_pairs={{0,8},{4,12},{8,0},{12,4},{16,24},{20,28},{24,16},{28,20},{1,9},{5... | collective-permute-start | bytes 393224 | tf_op jit(solution)/shard_map/ppermute | solution.py:36
  316.1 5.0 %collective-permute-start.33 = (bf16[1,32,2048]{2,1,0:T(8,128)(2,1)S(1)}, bf16[1,32,2048]{2,1,0:T(8,128)(2,1)S(1)}, u32[]{:S(2)}, u32[]{:S(2)}) collective-permute-start(bf16[1,32,2048]{2,1,0:T(8,128)(2,1)S(1)} %fusion.11), channel_id=1, source_target_pairs={{0,16},{4,20},{8,24},{12,28},{16,0},{20,4},{24,8},{28,12},{1,17},{... | collective-permute-start | bytes 393224 | tf_op jit(solution)/shard_map/ppermute | solution.py:36
  (19 other events, 59.3 us)

commit v6 on v5

--- a/solution.py
+++ b/solution.py
@@ -88,7 +88,7 @@
     else:
         (tokens,) = source_refs
         kept, sent = refs
-    product = contract_trailing_axis(tokens[...], weight[...])
+    product = contract_trailing_axis(weight[...], tokens[...]).T
     for i in range(owners):
         place = table[i]
         part = product[i * rows : (i + 1) * rows]
@@ -169,27 +169,31 @@
     )(*operands)
 
 
-def scatter_begin(live):
-    half = live.shape[2] // 2
-    return [
-        {p: live[p, :, side * half : (side + 1) * half] for p in range(live.shape[0])}
-        for side in range(2)
-    ]
-
-
-def scatter_hop(state, hop):
+def scatter_send(state, hop):
     if hop == 0:
         kept, sent = state
-        return scatter_begin(kept + swap(sent, "wide", 1))
+        half = kept.shape[2] // 2
+        got = [swap(sent[:, :, side * half : (side + 1) * half], "wide", 1) for side in range(2)]
+        return kept, got
     bits = bits_of("wide")[:-1]
-    done = []
+    stay, got = [], []
     for part, order in zip(state, (bits, bits[::-1])):
         bit = order[hop - 1]
-        stay = [p for p in part if not p & bit]
-        away = jnp.stack([part[p ^ bit].astype(jnp.bfloat16) for p in stay])
-        got = swap(away, "wide", 2 * bit)
-        done.append({p: part[p] + got[i] for i, p in enumerate(stay)})
-    return done
+        stay.append({p: part[p] for p in part if not p & bit})
+        away = jnp.stack([part[p | bit].astype(jnp.bfloat16) for p in stay[-1]])
+        got.append(swap(away, "wide", 2 * bit))
+    return stay, got
+
+
+def scatter_take(flight, hop):
+    stay, got = flight
+    if hop == 0:
+        half = stay.shape[2] // 2
+        return [
+            {p: stay[p, :, side * half : (side + 1) * half] + got[side][p] for p in range(stay.shape[0])}
+            for side in range(2)
+        ]
+    return [{p: part[p] + new[i] for i, p in enumerate(part)} for part, new in zip(stay, got)]
 
 
 def hold(*groups):
@@ -248,32 +252,53 @@
     blocks[0] = block_of(grad_out, 0)
     begin(0)
 
-    act_sum = jnp.dot(inputs, adapter_down_matrix, preferred_element_type=jnp.float32)
-    low_part = contract_trailing_axis(grad_out, b_factor)
+    blocks[0], low_source = hold(blocks[0], grad_out)
+    low_part = contract_trailing_axis(low_source, b_factor)
     low_small = scatter_small(low_part, "wide").astype(jnp.bfloat16)
 
     def exchange(act_sum, low_rows, bit):
-        count, part = low_rows.shape[0], low_rows.shape[1]
         both = jnp.concatenate([act_sum, low_rows.reshape(-1, rank).astype(jnp.float32)], axis=0)
-        got = swap(both, "narrow", bit)
-        other = got[owner_rows:].reshape(count, part, rank).astype(jnp.bfloat16)
+        return swap(both, "narrow", bit)
+
+    def exchanged(act_sum, low_rows, got, bit):
+        other = got[owner_rows:].reshape(low_rows.shape).astype(jnp.bfloat16)
         upper = (me_narrow & bit) != 0
         first, second = jnp.where(upper, other, low_rows), jnp.where(upper, low_rows, other)
         return act_sum + got[:owner_rows], jnp.concatenate([first, second], axis=0)
 
     low_rows = low_small[None]
-    near[0], far[0], blocks[0], grad_out, low_rows, act_sum, inputs = hold(
-        near[0], far[0], blocks[0], grad_out, low_rows, act_sum, inputs
-    )
+    near[0], far[0], blocks[0], grad_out, low_rows, inputs = hold(
+        near[0], far[0], blocks[0], grad_out, low_rows, inputs
+    )
+    act_sum = jnp.dot(inputs, adapter_down_matrix, preferred_element_type=jnp.float32)
     complete(0)
     blocks[1] = block_of(grad_out, 1)
-    for bit in narrow_bits:
-        act_sum, low_rows = exchange(act_sum, low_rows, bit)
-    act_rows = act_sum.astype(jnp.bfloat16)
-    small = {"rows": jnp.concatenate([act_rows, low_rows.reshape(-1, rank)], axis=0)[None]}
-
-    def first_hop(bit):
-        small["rows"] = gather_ordered(small["rows"], "wide", [bit])
+    for bit in narrow_bits[:-1]:
+        act_sum, low_rows = exchanged(act_sum, low_rows, exchange(act_sum, low_rows, bit), bit)
+    small = {"inputs": inputs, "act": act_sum, "low": low_rows}
+    small["got"] = exchange(act_sum, low_rows, narrow_bits[-1])
+
+    def take():
+        if "got" in small and "act" in small:
+            act, low = exchanged(small.pop("act"), small.pop("low"), small.pop("got"), narrow_bits[-1])
+            small["rows"] = jnp.concatenate([act.astype(jnp.bfloat16), low.reshape(-1, rank)], axis=0)[None]
+        elif "got" in small:
+            upper = (me_wide & taken.pop(0)) != 0
+            name = "rows" if "rows" in small else "grad_a"
+            mine, other = small[name], small.pop("got")
+            first, second = jnp.where(upper, other, mine), jnp.where(upper, mine, other)
+            small[name] = jnp.concatenate([first, second], axis=0)
+
+    taken = wide_bits + wide_bits[::-1]
+    bits_left = list(taken)
+
+    def small_hop():
+        take()
+        if not bits_left:
+            return
+        if len(bits_left) == len(wide_bits):
+            share_made()
+        small["got"] = swap(small["rows" if "rows" in small else "grad_a"], "wide", bits_left.pop(0))
 
     def regroup():
         shares = small.pop("inputs").reshape(owner_rows, owners, -1)
@@ -303,29 +328,28 @@
             for start, rows in pieces
         ]
 
-    def second_hop(bit):
-        if "grad_a" not in small:
-            share_made()
-        small["grad_a"] = gather_ordered(small["grad_a"], "wide", [bit])
-
-    hops = [functools.partial(first_hop, bit) for bit in wide_bits]
-    hops += [functools.partial(second_hop, bit) for bit in wide_bits[::-1]]
-    small["inputs"] = inputs
     tokens, sums = {}, {}
-    waiting = {}
+    done_hops = {}
+
+    def sum_hop(i):
+        if done_hops[i]:
+            sums[i] = scatter_take(sums[i], done_hops[i] - 1)
+        if done_hops[i] < len(wide_bits):
+            sums[i] = scatter_send(sums[i], done_hops[i])
+        done_hops[i] += 1
 
     def step():
-        if hops:
-            hops.pop(0)()
+        small_hop()
         for i in sums:
-            if waiting[i]:
-                sums[i] = scatter_hop(sums[i], waiting[i].pop(0))
+            if done_hops[i] <= len(wide_bits):
+                sum_hop(i)
 
     def run_pass(i):
         sources = [blocks[i], near[i], far[i], middle[i], onward[i]] if line else [near[i]]
         tokens[i], kept, sent = weight_pass(table, sources, w_base, owners)
         sums[i] = (kept, sent)
-        waiting[i] = list(range(len(wide_bits)))
+        done_hops[i] = 0
+        sum_hop(i)
 
     for i in range(count):
         if i:
@@ -342,20 +366,21 @@
         if i + 1 < count:
             begin(i + 1)
             step()
-            if i == 0:
+            if i + 2 == count:
                 regroup()
             run_pass(i)
     step()
     run_pass(count - 1)
-    while hops:
-        hops.pop(0)()
-    sums[count - 1] = scatter_hop(sums[count - 1], waiting[count - 1].pop(0))
+    small, sums = hold(small, sums)
+    while bits_left or "got" in small:
+        small_hop()
     columns_step = max(128 * c for c in range(1, 14) if depth % (128 * c) == 0)
     steps = depth // columns_step
     early = steps // 2 or 1
     turned = small["turned"]
     tokens = [tokens[i] for i in range(count)]
     grad_b = factor_gradient(turned, tokens, adapter_matrix, columns_step, 0, early)
+    sum_hop(count - 1)
     sums[count - 1], grad_b = hold(sums[count - 1], grad_b)
     if steps > early:
         grad_b = factor_gradient(
@@ -363,8 +388,8 @@
         )
     results = []
     for i, (start, rows) in enumerate(pieces):
-        for hop in waiting[i]:
-            sums[i] = scatter_hop(sums[i], hop)
+        while done_hops[i] <= len(wide_bits):
+            sum_hop(i)
         mine = small["term"][start : start + rows]
         summed = jnp.concatenate([part[0] for part in sums[i]], axis=1)
         results.append((summed + mine).astype(jnp.bfloat16))

time: 328 us -> 333 us (1.015)
  Pallas kernels: 87.4 us -> 96 us
    ppermute x32 -> x35, waiting for transfers between devices: 103 us -> 114 us  [swap(): return lax.ppermute(value, axis, [(i, i ^ bit) for i in range(size)])]
    ppermute x3, waiting for transfers between devices: 14 us -> 2.73 us  [phase_b(): lax.ppermute(far, axis, [(1, 0), (2, 3)])]
    pallas_call x3, Pallas kernels: 79.6 us -> 88.2 us  [weight_pass(): pl.pallas_call(functools.partial(pass_kernel, sources=len(sources), owner...]
    add x14 -> x6, other arithmetic: 7.41 us -> 0.25 us  [the longest x5 0.23 us: scatter_take(): part[p] + new[i]]
    convert_element_type x1 -> x4, other arithmetic: 0.91 us -> 7.18 us  [the longest x3 6.27 us: scatter_send(): away = jnp.stack([part[p | bit].astype(jnp.bfloat16) for p in stay[-1]])]
    ppermute x32 -> x35, starting transfers between devices: 35 us -> 36.1 us  [swap(): return lax.ppermute(value, axis, [(i, i ^ bit) for i in range(size)])]
    unnamed x64 -> x94, local copies, waits for them, and re-layouts: 17.3 us -> 17.3 us
  transfers between devices with their start and end apart: 39 -> 42, of which waited for: 16 -> 18; matrix products, arithmetic and copies ran while one was open for 16% -> 14% of each run, Pallas kernels for 27% -> 29%
where the time goes in v6:
time: 333 us; the launch traced here: 331 us
  waiting for transfers between devices  117 us (35%)
  Pallas kernels  96 us (29%)
  starting transfers between devices  47.4 us (14%)
  local copies, waits for them, and re-layouts  39.3 us (12%)
  other arithmetic  20.3 us (6%)
  matrix products  10.1 us (3%)
    ppermute x35, waiting for transfers between devices, swap(): return lax.ppermute(value, axis, [(i, i ^ bit) for i in range(size)])  114 us
    pallas_call x3, Pallas kernels, weight_pass(): pl.pallas_call(functools.partial(pass_kernel, sources=len(sources), owner...  88.2 us
    ppermute x35, starting transfers between devices, swap(): return lax.ppermute(value, axis, [(i, i ^ bit) for i in range(size)])  36.1 us
    unnamed x94, local copies, waits for them, and re-layouts  17.3 us
    pallas_call x2, Pallas kernels, factor_gradient(): pl.pallas_call(functools.partial(factor_kernel, count=len(acts), scale=sc...  7.74 us
  transfers between devices with their start and end apart: 42, of which 18 were waited for; matrix products, arithmetic and copies ran while one was open for 14% of the time, Pallas kernels for 29%

profile of v6, /device:TPU:0, one launch (start us, length us, event | category | flops | bytes accessed | tf_op | source)
XLA Modules:
  0.0 331.3 jit_solution(10303901719903010207)
XLA Ops:
  0.6 2.6 slice.358
  3.2 3.0 collective-permute-start
  6.3 2.6 collective-permute-start.1
  8.9 3.7 %fusion.29 = f32[224,256]{1,0:T(8,128)} fusion(bf16[224,6656]{1,0:T(8,128)(2,1)} %param.6, bf16[256,6656]{1,0:T(8,128)(2,1)S(1)} %copy-done), kind=kOutput, calls=%fused_computation.133 | convolution fusion | flops 763363328 | bytes 6619136 | tf_op jit(solution)/shard_map/dot_general | solution.py:18
  13.4 1.5 collective-permute-start.2
  15.0 3.3 collective-permute-done.2
  19.2 1.6 collective-permute-start.3
  20.7 2.7 collective-permute-done.3
  24.8 37.1 %collective-permute-done.refs_1_ = bf16[96,6656]{1,0:T(8,128)(2,1)} collective-permute-done((bf16[96,6656]{1,0:T(8,128)(2,1)}, bf16[96,6656]{1,0:T(8,128)(2,1)}, u32[]{:S(2)}, u32[]{:S(2)}) %collective-permute-start) | collective-permute-done | bytes 1277984 | tf_op jit(solution)/shard_map/ppermute | solution.py:36
  61.9 2.6 collective-permute-done.1.refs_2_
  66.5 2.3 fusion.30
  68.9 2.8 collective-permute-start.7
  71.6 27.1 %collective-permute-done.7 = f32[140,256]{1,0:T(8,128)S(1)} collective-permute-done((f32[140,256]{1,0:T(8,128)S(1)}, f32[140,256]{1,0:T(8,128)S(1)}, u32[]{:S(2)}, u32[]{:S(2)}) %collective-permute-start.7) | collective-permute-done | bytes 143392 | tf_op jit(solution)/shard_map/ppermute | solution.py:36
  102.0 6.6 %collective-permute-done.8 = f32[168,256]{1,0:T(8,128)} collective-permute-done((f32[168,256]{1,0:T(8,128)}, f32[168,256]{1,0:T(8,128)}, u32[]{:S(2)}, u32[]{:S(2)}) %collective-permute-start.8) | collective-permute-done | bytes 172064 | tf_op jit(solution)/shard_map/ppermute | solution.py:36
  110.6 2.2 collective-permute-start.10
  115.4 39.2 %weight_pass.3 = (bf16[384,6656]{1,0:T(8,128)(2,1)}, f32[4,48,4096]{2,1,0:T(8,128)S(1)}, bf16[4,48,4096]{2,1,0:T(8,128)(2,1)S(1)}) custom-call(s32[9]{0:T(128)S(1)} %stack.94.table, bf16[96,6656]{1,0:T(8,128)(2,1)} %bitcast.1.refs_0_, bf16[96,6656]{1,0:T(8,128)(2,1)} %collective-permute-done.refs_1_, bf16[96,6656]{1,0:T(8,128)(2,1)} %collective-permute-done.1.refs_2_, ...), custom_call_target="tpu_custom_call" | custom-call | bytes 65536 | tf_op jit(solution)/shard_map/weight_pass/pallas_call | solution.py:124
  154.6 1.7 copy-done.4
  156.3 1.3 fusion.24
  165.9 3.8 %add_convert_fusion.1 = (bf16[1,48,2048]{2,1,0:T(8,128)(2,1)S(1)}, bf16[1,48,2048]{2,1,0:T(8,128)(2,1)S(1)}, f32[48,2048]{1,0:T(8,128)}, f32[48,2048]{1,0:T(8,12...) fusion(f32[4,48,4096]{2,1,0:T(8,128)} %copy-done.4, ...), kind=kLoop, calls=%fused_computation.38 | loop fusion | flops 1966080 | bytes 7077888 | tf_op jit(solution)/shard_map/convert_element_type | solution.py:183
  169.8 1.6 collective-permute-start.17
  171.4 1.6 collective-permute-start.18
  173.6 2.1 slice.363
  175.8 10.2 %collective-permute-done.16 = bf16[2,224,256]{2,1,0:T(8,128)(2,1)S(1)} collective-permute-done((bf16[2,224,256]{2,1,0:T(8,128)(2,1)S(1)}, bf16[2,224,256]{2,1,0:T(8,128)(2,1)S(1)}, u32[]{:S(2)}, u32[]{:S(2)}) %collective-permute-start.16) | collective-permute-done | bytes 229408 | tf_op jit(solution)/shard_map/ppermute | solution.py:36
  186.0 1.7 collective-permute-done.15.refs_4_
  189.4 2.0 collective-permute-start.20
  191.8 1.5 fusion.27
  198.6 4.4 %all-to-all-start = ((bf16[8,112,512]{2,1,0:T(8,128)(2,1)}), bf16[8,112,512]{2,1,0:T(8,128)(2,1)}, u32[]{:S(2)}, u32[]{:S(2)}) async-start(bf16[8,112,512]{2,1,0:T(8,128)(2,1)} %bitcast_dynamic-update-slice_fusion), calls=%async_computation | async-start | bytes 1835008 | tf_op jit(solution)/shard_map/all_to_all | solution.py:310
  203.9 1.7 collective-permute-start.22
  206.5 1.5 collective-permute-start.23
  208.0 24.0 %weight_pass.4 = (bf16[256,6656]{1,0:T(8,128)(2,1)S(1)}, f32[4,32,4096]{2,1,0:T(8,128)S(1)}, bf16[4,32,4096]{2,1,0:T(8,128)(2,1)S(1)}) custom-call(s32[9]{0:T(128)S(1)} %stack.94.table, bf16[64,6656]{1,0:T(8,128)(2,1)S(1)} %bitcast.180, bf16[64,6656]{1,0:T(8,128)(2,1)S(1)} %copy-done.13, bf16[64,6656]{1,0:T(8,128)(2,1)} %collective-permute-done.10.refs_2_, ...), custom_call_target="tpu_custom_call" | custom-call | bytes 65536 | tf_op jit(solution)/shard_map/weight_pass/pallas_call | solution.py:124
  237.2 12.3 %collective-permute-done.21 = bf16[4,224,256]{2,1,0:T(8,128)(2,1)} collective-permute-done((bf16[4,224,256]{2,1,0:T(8,128)(2,1)}, bf16[4,224,256]{2,1,0:T(8,128)(2,1)}, u32[]{:S(2)}, u32[]{:S(2)}) %collective-permute-start.21) | collective-permute-done | bytes 458784 | tf_op jit(solution)/shard_map/ppermute | solution.py:36
  252.5 1.6 collective-permute-start.26
  256.5 1.9 reshape.143
  258.4 2.5 fusion
  261.4 1.7 copy.80
  264.2 1.7 copy.82
  265.8 2.2 add_convert_fusion.9
  268.5 1.8 collective-permute-start.30
  270.4 1.6 convolution_multiply_fusion
  272.0 3.4 %collective-permute-done.29 = bf16[2,32,2048]{2,1,0:T(8,128)(2,1)S(1)} collective-permute-done((bf16[2,32,2048]{2,1,0:T(8,128)(2,1)S(1)}, bf16[2,32,2048]{2,1,0:T(8,128)(2,1)S(1)}, u32[]{:S(2)}, u32[]{:S(2)}) %collective-permute-start.29) | collective-permute-done | bytes 262176 | tf_op jit(solution)/shard_map/ppermute | solution.py:36
  278.5 1.5 collective-permute-start.32
  280.0 25.0 %weight_pass.5 = (bf16[256,6656]{1,0:T(8,128)(2,1)S(1)}, f32[4,32,4096]{2,1,0:T(8,128)S(1)}, bf16[4,32,4096]{2,1,0:T(8,128)(2,1)S(1)}) custom-call(s32[9]{0:T(128)S(1)} %stack.94.table, bf16[64,6656]{1,0:T(8,128)(2,1)} %bitcast.26.refs_0_, bf16[64,6656]{1,0:T(8,128)(2,1)} %collective-permute-done.19.refs_1_, ...), custom_call_target="tpu_custom_call" | custom-call | bytes 65536 | tf_op jit(solution)/shard_map/weight_pass/pallas_call | solution.py:124
  306.4 4.9 %collective-permute-done.33 = bf16[1,32,2048]{2,1,0:T(8,128)(2,1)S(1)} collective-permute-done((bf16[1,32,2048]{2,1,0:T(8,128)(2,1)S(1)}, bf16[1,32,2048]{2,1,0:T(8,128)(2,1)S(1)}, u32[]{:S(2)}, u32[]{:S(2)}) %collective-permute-start.33) | collective-permute-done | bytes 131104 | tf_op jit(solution)/shard_map/ppermute | solution.py:36
  312.3 1.3 collective-permute-start.37
  314.8 3.9 %factor_gradient.2.refs_6_ = f32[256,6656]{1,0:T(8,128)} custom-call(bf16[256,384]{1,0:T(8,128)(2,1)S(1)} %bitcast.181, bf16[256,256]{1,0:T(8,128)(2,1)S(1)} %bitcast.183, bf16[256,256]{1,0:T(8,128)(2,1)S(1)} %bitcast.185, bf16[384,6656]{1,0:T(8,128)(2,1)S(1)} %bitcast.176, bf16[256,6656]{1,0:T(8,128)(2,1)S(1)} %get-tuple-element.194.refs_4_, ...), custom_call_target="tpu_custom_call" | custom-call | bytes 65536 | tf_op jit(solution)/shard_map/factor_gradient/pallas_call | solution.py:159
  319.6 1.5 collective-permute-start.39
  321.8 3.9 %factor_gradient.3 = f32[256,6656]{1,0:T(8,128)} custom-call(bf16[256,384]{1,0:T(8,128)(2,1)S(1)} %bitcast.182, bf16[256,256]{1,0:T(8,128)(2,1)S(1)} %bitcast.184, bf16[256,256]{1,0:T(8,128)(2,1)S(1)} %bitcast.186, bf16[384,6656]{1,0:T(8,128)(2,1)S(1)} %bitcast.176, ...), custom_call_target="tpu_custom_call", output_to_operand_aliasing={{}: (6, {})} | custom-call | bytes 65536 | tf_op jit(solution)/shard_map/factor_gradient/pallas_call | solution.py:159
  327.8 2.5 maximum_convert_fusion
  (215 shorter events, 54.7 us)
Async XLA Ops:
  3.2 58.7 %collective-permute-start = (bf16[96,6656]{1,0:T(8,128)(2,1)}, bf16[96,6656]{1,0:T(8,128)(2,1)}, u32[]{:S(2)}, u32[]{:S(2)}) collective-permute-start(bf16[96,6656]{1,0:T(8,128)(2,1)} %bitcast.1.refs_0_), channel_id=1, source_target_pairs={{0,1},{1,0},{2,3},{3,2},{4,5},{5,4},{6,7},{7,6},{8,9},{9,8},{10,11... | collective-permute-start | bytes 3833864 | tf_op jit(solution)/shard_map/ppermute | solution.py:36
  6.3 58.2 %collective-permute-start.1 = (bf16[96,6656]{1,0:T(8,128)(2,1)}, bf16[96,6656]{1,0:T(8,128)(2,1)}, u32[]{:S(2)}, u32[]{:S(2)}) collective-permute-start(bf16[96,6656]{1,0:T(8,128)(2,1)} %bitcast.1.refs_0_), channel_id=1, source_target_pairs={{0,2},{1,3},{2,0},{3,1},{4,6},{5,7},{6,4},{7,5},{8,10},{9,11},{10,... | collective-permute-start | bytes 3833864 | tf_op jit(solution)/shard_map/ppermute | solution.py:36
  13.4 4.8 %collective-permute-start.2 = (f32[112,256]{1,0:T(8,128)S(1)}, f32[112,256]{1,0:T(8,128)S(1)}, u32[]{:S(2)}, u32[]{:S(2)}) collective-permute-start(f32[112,256]{1,0:T(8,128)S(1)} %dynamic-slice_bitcast_fusion), channel_id=1, source_target_pairs={{0,16},{4,20},{8,24},{12,28},{16,0},{20,4},{24,8},{28,12},{1,17},{... | collective-permute-start | bytes 344072 | tf_op jit(solution)/shard_map/ppermute | solution.py:36
  19.2 4.2 %collective-permute-start.3 = (f32[56,256]{1,0:T(8,128)S(1)}, f32[56,256]{1,0:T(8,128)S(1)}, u32[]{:S(2)}, u32[]{:S(2)}) collective-permute-start(f32[56,256]{1,0:T(8,128)S(1)} %dynamic-slice_bitcast_fusion.1), channel_id=1, source_target_pairs={{0,8},{4,12},{8,0},{12,4},{16,24},{20,28},{24,16},{28,20},{1,9},{5... | collective-permute-start | bytes 172040 | tf_op jit(solution)/shard_map/ppermute | solution.py:36
  23.5 1.3 collective-permute-start.4
  64.5 44.1 %collective-permute-start.5 = (bf16[96,6656]{1,0:T(8,128)(2,1)}, bf16[96,6656]{1,0:T(8,128)(2,1)S(1)}, u32[]{:S(2)}, u32[]{:S(2)}) collective-permute-start(bf16[96,6656]{1,0:T(8,128)(2,1)} %bitcast.1.refs_0_), channel_id=1, source_target_pairs={{1,2},{2,1},{5,6},{6,5},{9,10},{10,9},{13,14},{14,13},{17,18},{18,... | collective-permute-start | bytes 3833864 | tf_op jit(solution)/shard_map/ppermute | solution.py:67
  65.2 44.4 %collective-permute-start.6 = (bf16[96,6656]{1,0:T(8,128)(2,1)}, bf16[96,6656]{1,0:T(8,128)(2,1)S(1)}, u32[]{:S(2)}, u32[]{:S(2)}) collective-permute-start(bf16[96,6656]{1,0:T(8,128)(2,1)} %collective-permute-done.1.refs_2_), channel_id=1, source_target_pairs={{1,0},{2,3},{5,4},{6,7},{9,8},{10,11},{13,12},{14,15},{17,16},{18,... | collective-permute-start | bytes 3833864 | tf_op jit(solution)/shard_map/ppermute | solution.py:68
  68.9 29.9 %collective-permute-start.7 = (f32[140,256]{1,0:T(8,128)S(1)}, f32[140,256]{1,0:T(8,128)S(1)}, u32[]{:S(2)}, u32[]{:S(2)}) collective-permute-start(f32[140,256]{1,0:T(8,128)S(1)} %pad_maximum_fusion.13), channel_id=1, source_target_pairs={{0,1},{1,0},{2,3},{3,2},{4,5},{5,4},{6,7},{7,6},{8,9},{9,8},{10,11... | collective-permute-start | bytes 430088 | tf_op jit(solution)/shard_map/ppermute | solution.py:36
  100.1 8.4 %collective-permute-start.8 = (f32[168,256]{1,0:T(8,128)}, f32[168,256]{1,0:T(8,128)}, u32[]{:S(2)}, u32[]{:S(2)}) collective-permute-start(f32[168,256]{1,0:T(8,128)} %pad_maximum_fusion.12), channel_id=1, source_target_pairs={{0,2},{1,3},{2,0},{3,1},{4,6},{5,7},{6,4},{7,5},{8,10},{9,11},{10,... | collective-permute-start | bytes 516104 | tf_op jit(solution)/shard_map/ppermute | solution.py:36
  101.9 62.0 %copy-start.2 = (bf16[2,32,6656]{2,1,0:T(8,128)(2,1)}, bf16[2,32,6656]{2,1,0:T(8,128)(2,1)S(1)}, u32[]{:S(2)}) copy-start(bf16[2,32,6656]{2,1,0:T(8,128)(2,1)S(1)} %slice.359) | copy-start | bytes 2555908
  110.6 52.2 %collective-permute-start.9 = (bf16[64,6656]{1,0:T(8,128)(2,1)S(1)}, bf16[64,6656]{1,0:T(8,128)(2,1)S(1)}, u32[]{:S(2)}, u32[]{:S(2)}) collective-permute-start(bf16[64,6656]{1,0:T(8,128)(2,1)S(1)} %bitcast.177), channel_id=1, source_target_pairs={{0,1},{1,0},{2,3},{3,2},{4,5},{5,4},{6,7},{7,6},{8,9},{9,8},{10,11... | collective-permute-start | bytes 2555912 | tf_op jit(solution)/shard_map/ppermute | solution.py:36
  110.6 52.2 %collective-permute-start.10 = (bf16[64,6656]{1,0:T(8,128)(2,1)S(1)}, bf16[64,6656]{1,0:T(8,128)(2,1)}, u32[]{:S(2)}, u32[]{:S(2)}) collective-permute-start(bf16[64,6656]{1,0:T(8,128)(2,1)S(1)} %bitcast.178), channel_id=1, source_target_pairs={{0,2},{1,3},{2,0},{3,1},{4,6},{5,7},{6,4},{7,5},{8,10},{9,11},{10,... | collective-permute-start | bytes 2555912 | tf_op jit(solution)/shard_map/ppermute | solution.py:36
  158.5 4.3 %collective-permute-start.12 = (bf16[4,48,2048]{2,1,0:T(8,128)(2,1)}, bf16[4,48,2048]{2,1,0:T(8,128)(2,1)S(1)}, u32[]{:S(2)}, u32[]{:S(2)}) collective-permute-start(bf16[4,48,2048]{2,1,0:T(8,128)(2,1)} %get-tuple-element.246), channel_id=1, source_target_pairs={{0,4},{4,0},{8,12},{12,8},{16,20},{20,16},{24,28},{28,24},{1,5},{5... | collective-permute-start | bytes 2359304 | tf_op jit(solution)/shard_map/ppermute | solution.py:36
  158.5 4.2 %collective-permute-start.13 = (bf16[4,48,2048]{2,1,0:T(8,128)(2,1)}, bf16[4,48,2048]{2,1,0:T(8,128)(2,1)S(1)}, u32[]{:S(2)}, u32[]{:S(2)}) collective-permute-start(bf16[4,48,2048]{2,1,0:T(8,128)(2,1)} %get-tuple-element.245), channel_id=1, source_target_pairs={{0,4},{4,0},{8,12},{12,8},{16,20},{20,16},{24,28},{28,24},{1,5},{5... | collective-permute-start | bytes 2359304 | tf_op jit(solution)/shard_map/ppermute | solution.py:36
  161.4 1.3 collective-permute-start.11
  163.9 22.1 %collective-permute-start.14 = (bf16[64,6656]{1,0:T(8,128)(2,1)S(1)}, bf16[64,6656]{1,0:T(8,128)(2,1)S(1)}, u32[]{:S(2)}, u32[]{:S(2)}) collective-permute-start(bf16[64,6656]{1,0:T(8,128)(2,1)S(1)} %bitcast.179), channel_id=1, source_target_pairs={{1,2},{2,1},{5,6},{6,5},{9,10},{10,9},{13,14},{14,13},{17,18},{18,... | collective-permute-start | bytes 2555912 | tf_op jit(solution)/shard_map/ppermute | solution.py:67
  164.6 23.1 %collective-permute-start.15 = (bf16[64,6656]{1,0:T(8,128)(2,1)}, bf16[64,6656]{1,0:T(8,128)(2,1)S(1)}, u32[]{:S(2)}, u32[]{:S(2)}) collective-permute-start(bf16[64,6656]{1,0:T(8,128)(2,1)} %collective-permute-done.10.refs_2_), channel_id=1, source_target_pairs={{1,0},{2,3},{5,4},{6,7},{9,8},{10,11},{13,12},{14,15},{17,16},{18,... | collective-permute-start | bytes 2555912 | tf_op jit(solution)/shard_map/ppermute | solution.py:68
  169.7 21.7 %copy-start.19 = (bf16[112,4096]{1,0:T(8,128)(2,1)S(1)}, bf16[112,4096]{1,0:T(8,128)(2,1)}, u32[]{:S(2)}) copy-start(bf16[112,4096]{1,0:T(8,128)(2,1)} %param.5) | copy-start | bytes 2752516
  169.8 16.2 %collective-permute-start.17 = (bf16[2,48,2048]{2,1,0:T(8,128)(2,1)S(1)}, bf16[2,48,2048]{2,1,0:T(8,128)(2,1)S(1)}, u32[]{:S(2)}, u32[]{:S(2)}) collective-permute-start(bf16[2,48,2048]{2,1,0:T(8,128)(2,1)S(1)} %pad_maximum_fusion.5), channel_id=1, source_target_pairs={{0,8},{4,12},{8,0},{12,4},{16,24},{20,28},{24,16},{28,20},{1,9},{5... | collective-permute-start | bytes 1179656 | tf_op jit(solution)/shard_map/ppermute | solution.py:36
  171.4 14.6 %collective-permute-start.18 = (bf16[2,48,2048]{2,1,0:T(8,128)(2,1)S(1)}, bf16[2,48,2048]{2,1,0:T(8,128)(2,1)S(1)}, u32[]{:S(2)}, u32[]{:S(2)}) collective-permute-start(bf16[2,48,2048]{2,1,0:T(8,128)(2,1)S(1)} %pad_maximum_fusion.6), channel_id=1, source_target_pairs={{0,16},{4,20},{8,24},{12,28},{16,0},{20,4},{24,8},{28,12},{1,17},{... | collective-permute-start | bytes 1179656 | tf_op jit(solution)/shard_map/ppermute | solution.py:36
  173.0 18.4 %copy-start.26 = (bf16[2,224,256]{2,1,0:T(8,128)(2,1)}, bf16[2,224,256]{2,1,0:T(8,128)(2,1)S(1)}, u32[]{:S(2)}) copy-start(bf16[2,224,256]{2,1,0:T(8,128)(2,1)S(1)} %pad_maximum_fusion.11) | copy-start | bytes 688132
  173.0 12.9 %collective-permute-start.16 = (bf16[2,224,256]{2,1,0:T(8,128)(2,1)S(1)}, bf16[2,224,256]{2,1,0:T(8,128)(2,1)S(1)}, u32[]{:S(2)}, u32[]{:S(2)}) collective-permute-start(bf16[2,224,256]{2,1,0:T(8,128)(2,1)S(1)} %pad_maximum_fusion.11), channel_id=1, source_target_pairs={{0,8},{4,12},{8,0},{12,4},{16,24},{20,28},{24,16},{28,20},{1,9},{5... | collective-permute-start | bytes 688136 | tf_op jit(solution)/shard_map/ppermute | solution.py:36
  188.6 60.9 %collective-permute-start.19 = (bf16[64,6656]{1,0:T(8,128)(2,1)}, bf16[64,6656]{1,0:T(8,128)(2,1)}, u32[]{:S(2)}, u32[]{:S(2)}) collective-permute-start(bf16[64,6656]{1,0:T(8,128)(2,1)} %bitcast.26.refs_0_), channel_id=1, source_target_pairs={{0,1},{1,0},{2,3},{3,2},{4,5},{5,4},{6,7},{7,6},{8,9},{9,8},{10,11... | collective-permute-start | bytes 2555912 | tf_op jit(solution)/shard_map/ppermute | solution.py:36
  189.4 60.2 %collective-permute-start.20 = (bf16[64,6656]{1,0:T(8,128)(2,1)}, bf16[64,6656]{1,0:T(8,128)(2,1)}, u32[]{:S(2)}, u32[]{:S(2)}) collective-permute-start(bf16[64,6656]{1,0:T(8,128)(2,1)} %bitcast.26.refs_0_), channel_id=1, source_target_pairs={{0,2},{1,3},{2,0},{3,1},{4,6},{5,7},{6,4},{7,5},{8,10},{9,11},{10,... | collective-permute-start | bytes 2555912 | tf_op jit(solution)/shard_map/ppermute | solution.py:36
  194.0 9.1 %copy-start.22 = (f32[48,2048]{1,0:T(8,128)S(1)}, f32[48,2048]{1,0:T(8,128)}, u32[]{:S(2)}) copy-start(f32[48,2048]{1,0:T(8,128)} %get-tuple-element.137) | copy-start | bytes 1179652
  194.0 9.1 %copy-start.23 = (f32[48,2048]{1,0:T(8,128)S(1)}, f32[48,2048]{1,0:T(8,128)}, u32[]{:S(2)}) copy-start(f32[48,2048]{1,0:T(8,128)} %get-tuple-element.141) | copy-start | bytes 1179652
  194.0 9.1 %copy-start.33 = (bf16[2,48,2048]{2,1,0:T(8,128)(2,1)S(1)}, bf16[2,48,2048]{2,1,0:T(8,128)(2,1)}, u32[]{:S(2)}) copy-start(bf16[2,48,2048]{2,1,0:T(8,128)(2,1)} %copy-done.32) | copy-start | bytes 1179652
  198.6 51.0 %all-to-all-start = ((bf16[8,112,512]{2,1,0:T(8,128)(2,1)}), bf16[8,112,512]{2,1,0:T(8,128)(2,1)}, u32[]{:S(2)}, u32[]{:S(2)}) async-start(bf16[8,112,512]{2,1,0:T(8,128)(2,1)} %bitcast_dynamic-update-slice_fusion), calls=%async_computation | async-start | bytes 1835008 | tf_op jit(solution)/shard_map/all_to_all | solution.py:310
  203.9 30.7 %collective-permute-start.22 = (bf16[1,48,2048]{2,1,0:T(8,128)(2,1)S(1)}, bf16[1,48,2048]{2,1,0:T(8,128)(2,1)S(1)}, u32[]{:S(2)}, u32[]{:S(2)}) collective-permute-start(bf16[1,48,2048]{2,1,0:T(8,128)(2,1)S(1)} %get-tuple-element.273), channel_id=1, source_target_pairs={{0,16},{4,20},{8,24},{12,28},{16,0},{20,4},{24,8},{28,12},{1,17},{... | collective-permute-start | bytes 589832 | tf_op jit(solution)/shard_map/ppermute | solution.py:36
  206.5 29.5 %collective-permute-start.23 = (bf16[1,48,2048]{2,1,0:T(8,128)(2,1)S(1)}, bf16[1,48,2048]{2,1,0:T(8,128)(2,1)S(1)}, u32[]{:S(2)}, u32[]{:S(2)}) collective-permute-start(bf16[1,48,2048]{2,1,0:T(8,128)(2,1)S(1)} %get-tuple-element.271), channel_id=1, source_target_pairs={{0,8},{4,12},{8,0},{12,4},{16,24},{20,28},{24,16},{28,20},{1,9},{5... | collective-permute-start | bytes 589832 | tf_op jit(solution)/shard_map/ppermute | solution.py:36
  234.5 15.1 %collective-permute-start.24 = (bf16[4,32,2048]{2,1,0:T(8,128)(2,1)}, bf16[4,32,2048]{2,1,0:T(8,128)(2,1)}, u32[]{:S(2)}, u32[]{:S(2)}) collective-permute-start(bf16[4,32,2048]{2,1,0:T(8,128)(2,1)} %get-tuple-element.252), channel_id=1, source_target_pairs={{0,4},{4,0},{8,12},{12,8},{16,20},{20,16},{24,28},{28,24},{1,5},{5... | collective-permute-start | bytes 1572872 | tf_op jit(solution)/shard_map/ppermute | solution.py:36
  234.6 14.9 %collective-permute-start.25 = (bf16[4,32,2048]{2,1,0:T(8,128)(2,1)}, bf16[4,32,2048]{2,1,0:T(8,128)(2,1)}, u32[]{:S(2)}, u32[]{:S(2)}) collective-permute-start(bf16[4,32,2048]{2,1,0:T(8,128)(2,1)} %get-tuple-element.251), channel_id=1, source_target_pairs={{0,4},{4,0},{8,12},{12,8},{16,20},{20,16},{24,28},{28,24},{1,5},{5... | collective-permute-start | bytes 1572872 | tf_op jit(solution)/shard_map/ppermute | solution.py:36
  236.7 12.9 %collective-permute-start.21 = (bf16[4,224,256]{2,1,0:T(8,128)(2,1)}, bf16[4,224,256]{2,1,0:T(8,128)(2,1)}, u32[]{:S(2)}, u32[]{:S(2)}) collective-permute-start(bf16[4,224,256]{2,1,0:T(8,128)(2,1)} %pad_maximum_fusion.4), channel_id=1, source_target_pairs={{0,16},{4,20},{8,24},{12,28},{16,0},{20,4},{24,8},{28,12},{1,17},{... | collective-permute-start | bytes 1376264 | tf_op jit(solution)/shard_map/ppermute | solution.py:36
  252.5 23.0 %collective-permute-start.26 = (bf16[64,6656]{1,0:T(8,128)(2,1)}, bf16[64,6656]{1,0:T(8,128)(2,1)}, u32[]{:S(2)}, u32[]{:S(2)}) collective-permute-start(bf16[64,6656]{1,0:T(8,128)(2,1)} %bitcast.26.refs_0_), channel_id=1, source_target_pairs={{1,2},{2,1},{5,6},{6,5},{9,10},{10,9},{13,14},{14,13},{17,18},{18,... | collective-permute-start | bytes 2555912 | tf_op jit(solution)/shard_map/ppermute | solution.py:67
  254.1 22.4 %collective-permute-start.27 = (bf16[64,6656]{1,0:T(8,128)(2,1)}, bf16[64,6656]{1,0:T(8,128)(2,1)}, u32[]{:S(2)}, u32[]{:S(2)}) collective-permute-start(bf16[64,6656]{1,0:T(8,128)(2,1)} %collective-permute-done.20.refs_2_), channel_id=1, source_target_pairs={{1,0},{2,3},{5,4},{6,7},{9,8},{10,11},{13,12},{14,15},{17,16},{18,... | collective-permute-start | bytes 2555912 | tf_op jit(solution)/shard_map/ppermute | solution.py:68
  260.9 11.2 %collective-permute-start.28 = (bf16[512,256]{1,0:T(8,128)(2,1)}, bf16[512,256]{1,0:T(8,128)(2,1)}, u32[]{:S(2)}, u32[]{:S(2)}) collective-permute-start(bf16[512,256]{1,0:T(8,128)(2,1)} %fusion), channel_id=1, source_target_pairs={{0,16},{4,20},{8,24},{12,28},{16,0},{20,4},{24,8},{28,12},{1,17},{... | collective-permute-start | bytes 786440 | tf_op jit(solution)/shard_map/ppermute | solution.py:36
  268.1 7.3 %collective-permute-start.29 = (bf16[2,32,2048]{2,1,0:T(8,128)(2,1)S(1)}, bf16[2,32,2048]{2,1,0:T(8,128)(2,1)S(1)}, u32[]{:S(2)}, u32[]{:S(2)}) collective-permute-start(bf16[2,32,2048]{2,1,0:T(8,128)(2,1)S(1)} %pad_maximum_fusion.7), channel_id=1, source_target_pairs={{0,8},{4,12},{8,0},{12,4},{16,24},{20,28},{24,16},{28,20},{1,9},{5... | collective-permute-start | bytes 786440 | tf_op jit(solution)/shard_map/ppermute | solution.py:36
  268.5 7.0 %collective-permute-start.30 = (bf16[2,32,2048]{2,1,0:T(8,128)(2,1)S(1)}, bf16[2,32,2048]{2,1,0:T(8,128)(2,1)S(1)}, u32[]{:S(2)}, u32[]{:S(2)}) collective-permute-start(bf16[2,32,2048]{2,1,0:T(8,128)(2,1)S(1)} %pad_maximum_fusion.8), channel_id=1, source_target_pairs={{0,16},{4,20},{8,24},{12,28},{16,0},{20,4},{24,8},{28,12},{1,17},{... | collective-permute-start | bytes 786440 | tf_op jit(solution)/shard_map/ppermute | solution.py:36
  277.6 33.7 %collective-permute-start.31 = (bf16[1024,256]{1,0:T(8,128)(2,1)S(1)}, bf16[1024,256]{1,0:T(8,128)(2,1)S(1)}, u32[]{:S(2)}, u32[]{:S(2)}) collective-permute-start(bf16[1024,256]{1,0:T(8,128)(2,1)S(1)} %pad_maximum_fusion.2), channel_id=1, source_target_pairs={{0,8},{4,12},{8,0},{12,4},{16,24},{20,28},{24,16},{28,20},{1,9},{5... | collective-permute-start | bytes 1572872 | tf_op jit(solution)/shard_map/ppermute | solution.py:36
  278.5 28.0 %collective-permute-start.32 = (bf16[1,32,2048]{2,1,0:T(8,128)(2,1)S(1)}, bf16[1,32,2048]{2,1,0:T(8,128)(2,1)S(1)}, u32[]{:S(2)}, u32[]{:S(2)}) collective-permute-start(bf16[1,32,2048]{2,1,0:T(8,128)(2,1)S(1)} %get-tuple-element.277), channel_id=1, source_target_pairs={{0,16},{4,20},{8,24},{12,28},{16,0},{20,4},{24,8},{28,12},{1,17},{... | collective-permute-start | bytes 393224 | tf_op jit(solution)/shard_map/ppermute | solution.py:36
  305.2 6.2 %collective-permute-start.34 = (bf16[4,32,2048]{2,1,0:T(8,128)(2,1)S(1)}, bf16[4,32,2048]{2,1,0:T(8,128)(2,1)S(1)}, u32[]{:S(2)}, u32[]{:S(2)}) collective-permute-start(bf16[4,32,2048]{2,1,0:T(8,128)(2,1)S(1)} %get-tuple-element.250), channel_id=1, source_target_pairs={{0,4},{4,0},{8,12},{12,8},{16,20},{20,16},{24,28},{28,24},{1,5},{5... | collective-permute-start | bytes 1572872 | tf_op jit(solution)/shard_map/ppermute | solution.py:36
  305.3 6.1 %collective-permute-start.35 = (bf16[4,32,2048]{2,1,0:T(8,128)(2,1)S(1)}, bf16[4,32,2048]{2,1,0:T(8,128)(2,1)S(1)}, u32[]{:S(2)}, u32[]{:S(2)}) collective-permute-start(bf16[4,32,2048]{2,1,0:T(8,128)(2,1)S(1)} %get-tuple-element.249), channel_id=1, source_target_pairs={{0,4},{4,0},{8,12},{12,8},{16,20},{20,16},{24,28},{28,24},{1,5},{5... | collective-permute-start | bytes 1572872 | tf_op jit(solution)/shard_map/ppermute | solution.py:36
  305.8 5.5 %collective-permute-start.33 = (bf16[1,32,2048]{2,1,0:T(8,128)(2,1)S(1)}, bf16[1,32,2048]{2,1,0:T(8,128)(2,1)S(1)}, u32[]{:S(2)}, u32[]{:S(2)}) collective-permute-start(bf16[1,32,2048]{2,1,0:T(8,128)(2,1)S(1)} %get-tuple-element.275), channel_id=1, source_target_pairs={{0,8},{4,12},{8,0},{12,4},{16,24},{20,28},{24,16},{28,20},{1,9},{5... | collective-permute-start | bytes 393224 | tf_op jit(solution)/shard_map/ppermute | solution.py:36
  311.7 7.5 %collective-permute-start.36 = (bf16[2,32,2048]{2,1,0:T(8,128)(2,1)S(1)}, bf16[2,32,2048]{2,1,0:T(8,128)(2,1)S(1)}, u32[]{:S(2)}, u32[]{:S(2)}) collective-permute-start(bf16[2,32,2048]{2,1,0:T(8,128)(2,1)S(1)} %pad_maximum_fusion.9), channel_id=1, source_target_pairs={{0,8},{4,12},{8,0},{12,4},{16,24},{20,28},{24,16},{28,20},{1,9},{5... | collective-permute-start | bytes 786440 | tf_op jit(solution)/shard_map/ppermute | solution.py:36
  312.3 7.2 %collective-permute-start.37 = (bf16[2,32,2048]{2,1,0:T(8,128)(2,1)S(1)}, bf16[2,32,2048]{2,1,0:T(8,128)(2,1)S(1)}, u32[]{:S(2)}, u32[]{:S(2)}) collective-permute-start(bf16[2,32,2048]{2,1,0:T(8,128)(2,1)S(1)} %pad_maximum_fusion.10), channel_id=1, source_target_pairs={{0,16},{4,20},{8,24},{12,28},{16,0},{20,4},{24,8},{28,12},{1,17},{... | collective-permute-start | bytes 786440 | tf_op jit(solution)/shard_map/ppermute | solution.py:36
  313.9 13.5 %collective-permute-start.40 = (bf16[2048,256]{1,0:T(8,128)(2,1)S(1)}, bf16[2048,256]{1,0:T(8,128)(2,1)S(1)}, u32[]{:S(2)}, u32[]{:S(2)}) collective-permute-start(bf16[2048,256]{1,0:T(8,128)(2,1)S(1)} %pad_maximum_fusion), channel_id=1, source_target_pairs={{0,4},{4,0},{8,12},{12,8},{16,20},{20,16},{24,28},{28,24},{1,5},{5... | collective-permute-start | bytes 3145736 | tf_op jit(solution)/shard_map/ppermute | solution.py:36
  319.6 6.1 %collective-permute-start.39 = (bf16[1,32,2048]{2,1,0:T(8,128)(2,1)S(1)}, bf16[1,32,2048]{2,1,0:T(8,128)(2,1)S(1)}, u32[]{:S(2)}, u32[]{:S(2)}) collective-permute-start(bf16[1,32,2048]{2,1,0:T(8,128)(2,1)S(1)} %fusion.17), channel_id=1, source_target_pairs={{0,8},{4,12},{8,0},{12,4},{16,24},{20,28},{24,16},{28,20},{1,9},{5... | collective-permute-start | bytes 393224 | tf_op jit(solution)/shard_map/ppermute | solution.py:36
  321.2 5.0 %collective-permute-start.38 = (bf16[1,32,2048]{2,1,0:T(8,128)(2,1)S(1)}, bf16[1,32,2048]{2,1,0:T(8,128)(2,1)S(1)}, u32[]{:S(2)}, u32[]{:S(2)}) collective-permute-start(bf16[1,32,2048]{2,1,0:T(8,128)(2,1)S(1)} %fusion.16), channel_id=1, source_target_pairs={{0,16},{4,20},{8,24},{12,28},{16,0},{20,4},{24,8},{28,12},{1,17},{... | collective-permute-start | bytes 393224 | tf_op jit(solution)/shard_map/ppermute | solution.py:36
  (37 other events, 138.8 us)

commit v7 on v0

v7 whole, which is shorter than its diff:
```python
import functools

import jax
import jax.numpy as jnp
from jax import lax
from jax.experimental import pallas as pl
from jax.experimental.pallas import tpu as pltpu
from jax.sharding import PartitionSpec as P

adapter_scale = 2.0
last_rows = 32
weight_rows = 512
vmem_bytes = 40 * 2**20
light = pl.CostEstimate(flops=0, bytes_accessed=2**16, transcendentals=0)


def contract_trailing_axis(left, right):
    return lax.dot_general(
        left, right, (((1,), (1,)), ((), ())), preferred_element_type=jnp.float32
    )


def contract_first(left, right):
    return lax.dot_general(
        left, right, (((0,), (0,)), ((), ())), preferred_element_type=jnp.float32
    )


def bits_of(axis):
    size = lax.axis_size(axis)
    return [1 << i for i in range(size.bit_length() - 1)]


def swap(value, axis, bit):
    size = lax.axis_size(axis)
    return lax.ppermute(value, axis, [(i, i ^ bit) for i in range(size)])


def scatter_small(value, axis):
    me = lax.axis_index(axis)
    for bit in reversed(bits_of(axis)):
        pair = value.reshape(2, value.shape[0] // 2, value.shape[1])
        mine = ((me & bit) != 0).astype(jnp.int32)
        kept = lax.dynamic_index_in_dim(pair, mine, 0, keepdims=False)
        sent = lax.dynamic_index_in_dim(pair, 1 - mine, 0, keepdims=False)
        value = kept + swap(sent, axis, bit)
    return value


def gather_ordered(value, axis, order):
    me = lax.axis_index(axis)
    for bit in order:
        other = swap(value, axis, bit)
        upper = (me & bit) != 0
        value = jnp.concatenate(
            [jnp.where(upper, other, value), jnp.where(upper, value, other)], axis=0
        )
    return value


def pass_kernel(table, tokens, weight, kept, sent, *, owners, rows):
    product = contract_trailing_axis(tokens[...], weight[...])
    for i in range(owners):
        place = table[i]
        part = product[i * rows : (i + 1) * rows]

        @pl.when((place & 1) == 0)
        def _():
            kept[place >> 1] = part

        @pl.when((place & 1) == 1)
        def _():
            sent[place >> 1] = part.astype(jnp.bfloat16)


def weight_pass(table, tokens, weight, owners):
    total, depth = tokens.shape
    width = weight.shape[0]
    rows = total // owners
    step = min(weight_rows, width)
    half = (owners // 2, rows, width)
    return pl.pallas_call(
        functools.partial(pass_kernel, owners=owners, rows=rows),
        grid_spec=pltpu.PrefetchScalarGridSpec(
            num_scalar_prefetch=1,
            grid=(width // step,),
            in_specs=[
                pl.BlockSpec((total, depth), lambda i, *_: (0, 0), pipeline_mode=pl.Buffered(1)),
                pl.BlockSpec((step, depth), lambda i, *_: (i, 0)),
            ],
            out_specs=[pl.BlockSpec((owners // 2, rows, step), lambda i, *_: (0, 0, i))] * 2,
        ),
        out_shape=[
            jax.ShapeDtypeStruct(half, jnp.float32),
            jax.ShapeDtypeStruct(half, jnp.bfloat16),
        ],
        compiler_params=pltpu.CompilerParams(vmem_limit_bytes=vmem_bytes),
        cost_estimate=light,
        name="weight_pass",
    )(table, tokens, weight)


def factor_kernel(*refs, count, scale):
    acts, tokens, out = refs[:count], refs[count : 2 * count], refs[-1]
    out[...] = scale * sum(
        jnp.dot(a[...], t[...], preferred_element_type=jnp.float32) for a, t in zip(acts, tokens)
    )


def factor_gradient(acts, tokens, scale, step, first, blocks, into=None):
    rank, depth = acts[0].shape[0], tokens[0].shape[1]
    in_specs = [
        pl.BlockSpec(a.shape, lambda i: (0, 0), pipeline_mode=pl.Buffered(1)) for a in acts
    ]
    in_specs += [pl.BlockSpec((t.shape[0], step), lambda i: (0, first + i)) for t in tokens]
    operands = [*acts, *tokens]
    aliases = {}
    if into is not None:
        aliases = {len(operands): 0}
        operands.append(into)
        in_specs.append(pl.BlockSpec(memory_space=pl.ANY))
    return pl.pallas_call(
        functools.partial(factor_kernel, count=len(acts), scale=scale),
        grid=(blocks,),
        in_specs=in_specs,
        out_specs=pl.BlockSpec((rank, step), lambda i: (0, first + i)),
        out_shape=jax.ShapeDtypeStruct((rank, depth), jnp.float32),
        input_output_aliases=aliases,
        compiler_params=pltpu.CompilerParams(vmem_limit_bytes=vmem_bytes),
        cost_estimate=light,
        name="factor_gradient",
    )(*operands)


def scatter_send(state, hop, strips):
    if hop == 0:
        kept, sent = state
        width = kept.shape[2] // strips
        return kept, [
            swap(sent[:, :, i * width : (i + 1) * width], "wide", 1) for i in range(strips)
        ]
    bits = bits_of("wide")[:-1]
    stay, got = [], []
    for i, part in enumerate(state):
        bit = (bits, bits[::-1])[i % 2][hop - 1]
        stay.append({p: part[p] for p in part if not p & bit})
        away = jnp.stack([part[p | bit].astype(jnp.bfloat16) for p in stay[-1]])
        got.append(swap(away, "wide", 2 * bit))
    return stay, got


def scatter_take(flight, hop):
    stay, got = flight
    if hop == 0:
        width = stay.shape[2] // len(got)
        return [
            {p: stay[p, :, i * width : (i + 1) * width] + new[p] for p in range(stay.shape[0])}
            for i, new in enumerate(got)
        ]
    return [{p: part[p] + new[i] for i, p in enumerate(part)} for part, new in zip(stay, got)]


def hold(*groups):
    leaves, tree = jax.tree.flatten(groups)
    return jax.tree.unflatten(tree, lax.optimization_barrier(leaves))


def cut_rows(owner_rows):
    last = last_rows if owner_rows >= 2 * last_rows else 0
    sizes = [owner_rows - last] + [last] * (last > 0)
    starts = [sum(sizes[:i]) for i in range(len(sizes))]
    return list(zip(starts, sizes))


def shards(inputs, grad_out, w_base, adapter_down_matrix, b_factor):
    owner_rows = inputs.shape[0]
    owners = lax.axis_size("wide")
    groups = lax.axis_size("narrow")
    me_wide = lax.axis_index("wide")
    adapter_matrix = adapter_scale / (owner_rows * owners)
    share = grad_out.shape[0] // owner_rows
    rank = b_factor.shape[0]
    depth = grad_out.shape[1]
    wide_bits = bits_of("wide")
    pieces = cut_rows(owner_rows)
    count = len(pieces)
    table = jnp.arange(owners, dtype=jnp.int32) ^ me_wide.astype(jnp.int32)

    def gather(source, i):
        start, rows = pieces[i]
        own = source.reshape(share, owner_rows, depth)
        block = own[:, start : start + rows].reshape(share * rows, depth)
        return lax.all_gather(block, "narrow", axis=0, tiled=True)

    tokens = [gather(grad_out, 0)]

    low_part = contract_trailing_axis(grad_out, b_factor)
    low_small = scatter_small(low_part, "wide").astype(jnp.bfloat16)
    low_small, grad_out = hold(low_small, grad_out)
    for i in range(1, count):
        tokens.append(gather(grad_out, i))
    low_rows = gather_ordered(low_small[None], "narrow", bits_of("narrow"))
    act_part = jnp.dot(inputs, adapter_down_matrix, preferred_element_type=jnp.float32)
    act_small = scatter_small(act_part, "narrow").astype(jnp.bfloat16)
    act_rows = gather_ordered(act_small, "narrow", bits_of("narrow"))
    both = jnp.concatenate([act_rows, low_rows.reshape(-1, rank)], axis=0)
    both = gather_ordered(both[None], "wide", wide_bits)
    low_wide = both[:, owner_rows:].reshape(owners, groups, low_small.shape[0], rank)
    low_all = jnp.swapaxes(low_wide, 0, 1).reshape(owner_rows * owners, rank)
    low_own = lax.dynamic_slice_in_dim(low_all, me_wide * owner_rows, owner_rows)
    low_term = adapter_scale * contract_trailing_axis(low_own, adapter_down_matrix)
    turned = [
        both[:, start : start + rows].reshape(owners * rows, rank).T for start, rows in pieces
    ]

    shares = inputs.reshape(owner_rows, owners, -1)
    flipped = [
        sum(bit for i, bit in enumerate(wide_bits) if w & wide_bits[len(wide_bits) - 1 - i])
        for w in range(owners)
    ]
    shares = jnp.stack([shares[:, f] for f in flipped], axis=0)
    columns = lax.all_to_all(shares, "wide", split_axis=0, concat_axis=0)
    columns = columns.reshape(owner_rows * owners, -1)
    grad_a = adapter_matrix * contract_first(columns, low_all)
    grad_a = gather_ordered(grad_a, "wide", wide_bits[::-1])

    columns_step = max(128 * c for c in range(1, 14) if depth % (128 * c) == 0)
    steps = depth // columns_step
    early = steps // 2 or 1

    def hops(state, first, end, strips):
        for hop in range(first, end):
            state = scatter_take(scatter_send(state, hop, strips), hop)
        return state

    last = count - 1
    sums, flights = [], []
    for i in range(count):
        tokens[i], grad_a, turned, low_term, sums = hold(tokens[i], grad_a, turned, low_term, sums)
        flights = [scatter_send(state, 1, 4) for state in sums]
        made = weight_pass(table, tokens[i], w_base, owners)
        if i < last:
            sums.append(hops(made, 0, 1, 4))
    made, flights = hold(made, flights)
    state = hops(made, 0, 1, 2)
    grad_b = factor_gradient(turned, tokens, adapter_matrix, columns_step, 0, early)
    state, grad_b = hold(state, grad_b)
    if steps > early:
        grad_b = factor_gradient(
            turned, tokens, adapter_matrix, columns_step, early, steps - early, grad_b
        )
    sums = [hops(scatter_take(flight, 1), 2, len(wide_bits), 4) for flight in flights]
    sums.append(hops(state, 1, len(wide_bits), 2))
    results = []
    for (start, rows), parts in zip(pieces, sums):
        summed = jnp.concatenate([part[0] for part in parts], axis=1)
        results.append((summed + low_term[start : start + rows]).astype(jnp.bfloat16))
    return (jnp.concatenate(results, axis=0), grad_a, grad_b)


def solution(mesh):
    return jax.shard_map(
        shards,
        mesh=mesh,
        in_specs=(
            P("wide", "narrow"),
            P("narrow", "wide"),
            P("narrow", "wide"),
            P("narrow", None),
            P(None, "wide"),
        ),
        out_specs=(P("wide", "narrow"), P("narrow", None), P(None, "wide")),
        check_vma=False,
    )
```

time: 501 us -> 310 us (0.62)
  waiting for transfers between devices: 357 us -> 137 us
  Pallas kernels: 0 us -> 75.6 us
  matrix products: 82.7 us -> 9.44 us
  starting transfers between devices: 0.12 us -> 37.9 us
  blocking collectives: 30.2 us -> 0 us
  local copies, waits for them, and re-layouts: 5.62 us -> 16.8 us
  other arithmetic: 10.6 us -> 17.7 us
    all_gather x1 -> x2, waiting for transfers between devices: 212 us -> 43.3 us  [gather(): return lax.all_gather(block, 'narrow', axis=0, tiled=True)]
    reduce_scatter x1 -> x0, waiting for transfers between devices: 107 us -> none  [shards(): summed = lax.psum_scatter(stacked, 'wide', scatter_dimension=0, tiled=True)]
    ppermute x0 -> x33, waiting for transfers between devices: none -> 89.5 us  [swap(): return lax.ppermute(value, axis, [(i, i ^ bit) for i in range(size)])]
    pallas_call x0 -> x4, Pallas kernels: none -> 75.6 us  [the longest x2 67.8 us: weight_pass(): pl.pallas_call(functools.partial(pass_kernel, owners=owners, rows=rows),...]
    dot_general x3 -> x2, matrix products: 68 us -> 6.64 us  [contract_trailing_axis(): lax.dot_general(left, right, (((1,), (1,)), ((), ())), preferred_element_...]
    psum x1 -> x0, waiting for transfers between devices: 38 us -> none  [shards(): lax.psum(adapter_matrix * contract_first(inputs, low_rank_gradient), 'wide')]
    ppermute x0 -> x33, starting transfers between devices: none -> 33.7 us  [swap(): return lax.ppermute(value, axis, [(i, i ^ bit) for i in range(size)])]
    psum x1 -> x0, blocking collectives: 20.7 us -> none  [shards(): low_act = lax.psum(low_part, 'narrow').astype(jnp.bfloat16)]
  transfers between devices with their start and end apart: 3 -> 36, of which waited for: 3 -> 22; matrix products, arithmetic and copies ran while one was open for 3% -> 11% of each run, Pallas kernels for 0% -> 24%
where the time goes in v7:
time: 310 us; the launch traced here: 309 us
  waiting for transfers between devices  137 us (44%)
  Pallas kernels  75.6 us (24%)
  starting transfers between devices  37.9 us (12%)
  other arithmetic  17.7 us (6%)
  local copies, waits for them, and re-layouts  16.8 us (5%)
  between operations  14.8 us (5%)
  matrix products  9.44 us (3%)
    ppermute x33, waiting for transfers between devices, swap(): return lax.ppermute(value, axis, [(i, i ^ bit) for i in range(size)])  89.5 us
    pallas_call x2, Pallas kernels, weight_pass(): pl.pallas_call(functools.partial(pass_kernel, owners=owners, rows=rows),...  67.8 us
    all_gather x2, waiting for transfers between devices, gather(): return lax.all_gather(block, 'narrow', axis=0, tiled=True)  43.3 us
    ppermute x33, starting transfers between devices, swap(): return lax.ppermute(value, axis, [(i, i ^ bit) for i in range(size)])  33.7 us
    unnamed x50, local copies, waits for them, and re-layouts  8.26 us
    pallas_call x2, Pallas kernels, factor_gradient(): pl.pallas_call(functools.partial(factor_kernel, count=len(acts), scale=sc...  7.75 us
    dot_general x2, matrix products, contract_trailing_axis(): lax.dot_general(left, right, (((1,), (1,)), ((), ())), preferred_element_...  6.64 us
  transfers between devices with their start and end apart: 36, of which 22 were waited for; matrix products, arithmetic and copies ran while one was open for 11% of the time, Pallas kernels for 24%

profile of v7, /device:TPU:0, one launch (start us, length us, event | category | flops | bytes accessed | tf_op | source)
XLA Modules:
  0.0 309.3 jit_solution(12317278833005127147)
XLA Ops:
  7.2 3.2 %slice.325 = bf16[2,80,6656]{2,1,0:T(8,128)(2,1)} slice(bf16[2,112,6656]{2,1,0:T(8,128)(2,1)} %bitcast.241), slice={[0:2], [0:80], [0:6656]} | slice | bytes 4259840 | tf_op jit(solution)/shard_map/slice | solution.py:192
  10.5 3.0 fusion.23
  14.2 3.0 collective-permute-start
  17.2 2.3 fusion.24
  19.6 2.7 collective-permute-start.3
  22.6 1.5 fusion.22
  27.5 5.4 %collective-permute-start.4 = (f32[28,256]{1,0:T(8,128)S(1)}, f32[28,256]{1,0:T(8,128)S(1)}, u32[]{:S(2)}, u32[]{:S(2)}) collective-permute-start(f32[28,256]{1,0:T(8,128)S(1)} %dynamic-slice_bitcast_fusion.3), channel_id=1, source_target_pairs={{0,1},{1,0},{2,3},{3,2},{4,5},{5,4},{6,7},{7,6},{8,9},{9,8},{10,11... | collective-permute-start | bytes 86024 | tf_op jit(solution)/shard_map/ppermute | solution.py:36
  33.0 1.6 collective-permute-start.1
  34.5 6.4 %collective-permute-done.4 = f32[28,256]{1,0:T(8,128)S(1)} collective-permute-done((f32[28,256]{1,0:T(8,128)S(1)}, f32[28,256]{1,0:T(8,128)S(1)}, u32[]{:S(2)}, u32[]{:S(2)}) %collective-permute-start.4) | collective-permute-done | bytes 28704 | tf_op jit(solution)/shard_map/ppermute | solution.py:36
  41.1 3.9 %collective-permute-done.5 = bf16[28,256]{1,0:T(8,128)(2,1)S(1)} collective-permute-done((bf16[28,256]{1,0:T(8,128)(2,1)S(1)}, bf16[28,256]{1,0:T(8,128)(2,1)S(1)}, u32[]{:S(2)}, u32[]{:S(2)}) %collective-permute-start.5) | collective-permute-done | bytes 14368 | tf_op jit(solution)/shard_map/ppermute | solution.py:36
  45.1 1.6 collective-permute-start.6
  46.7 5.7 %collective-permute-done.7 = bf16[1,28,256]{2,1,0:T(8,128)(2,1)S(1)} collective-permute-done((bf16[1,28,256]{2,1,0:T(8,128)(2,1)S(1)}, bf16[1,28,256]{2,1,0:T(8,128)(2,1)S(1)}, u32[]{:S(2)}, u32[]{:S(2)}) %collective-permute-start.7) | collective-permute-done | bytes 14368 | tf_op jit(solution)/shard_map/ppermute | solution.py:36
  52.5 7.5 %collective-permute-done.8 = bf16[2,28,256]{2,1,0:T(8,128)(2,1)S(1)} collective-permute-done((bf16[2,28,256]{2,1,0:T(8,128)(2,1)S(1)}, bf16[2,28,256]{2,1,0:T(8,128)(2,1)S(1)}, u32[]{:S(2)}, u32[]{:S(2)}) %collective-permute-start.8) | collective-permute-done | bytes 28704 | tf_op jit(solution)/shard_map/ppermute | solution.py:36
  61.5 1.5 collective-permute-start.10
  63.7 5.5 %collective-permute-done.10 = bf16[2,224,256]{2,1,0:T(8,128)(2,1)S(1)} collective-permute-done((bf16[2,224,256]{2,1,0:T(8,128)(2,1)S(1)}, bf16[2,224,256]{2,1,0:T(8,128)(2,1)S(1)}, u32[]{:S(2)}, u32[]{:S(2)}) %collective-permute-start.10) | collective-permute-done | bytes 229408 | tf_op jit(solution)/shard_map/ppermute | solution.py:36
  70.1 4.2 %all-to-all-start = ((bf16[8,112,512]{2,1,0:T(8,128)(2,1)}), bf16[8,112,512]{2,1,0:T(8,128)(2,1)S(1)}, u32[]{:S(2)}, u32[]{:S(2)}) async-start(bf16[8,112,512]{2,1,0:T(8,128)(2,1)} %bitcast_dynamic-update-slice_fusion), calls=%async_computation | async-start | bytes 1835008 | tf_op jit(solution)/shard_map/all_to_all | solution.py:222
  74.3 11.1 %collective-permute-done.11 = bf16[4,224,256]{2,1,0:T(8,128)(2,1)} collective-permute-done((bf16[4,224,256]{2,1,0:T(8,128)(2,1)S(1)}, bf16[4,224,256]{2,1,0:T(8,128)(2,1)}, u32[]{:S(2)}, u32[]{:S(2)}) %collective-permute-start.11) | collective-permute-done | bytes 458784 | tf_op jit(solution)/shard_map/ppermute | solution.py:36
  87.0 4.1 %all-to-all-done = bf16[8,112,512]{2,1,0:T(8,128)(2,1)S(1)} async-done(((bf16[8,112,512]{2,1,0:T(8,128)(2,1)}), bf16[8,112,512]{2,1,0:T(8,128)(2,1)S(1)}, u32[]{:S(2)}, u32[]{:S(2)}) %all-to-all-start) | async-done | bytes 917536 | tf_op jit(solution)/shard_map/all_to_all | solution.py:222
  91.9 12.5 %collective-permute-done.12 = f32[512,256]{1,0:T(8,128)S(1)} collective-permute-done((f32[512,256]{1,0:T(8,128)S(1)}, f32[512,256]{1,0:T(8,128)S(1)}, u32[]{:S(2)}, u32[]{:S(2)}) %collective-permute-start.12) | collective-permute-done | bytes 524320 | tf_op jit(solution)/shard_map/ppermute | solution.py:36
  104.6 1.5 collective-permute-start.13
  106.2 2.1 slice.324
  108.3 19.7 %collective-permute-done.13 = f32[1024,256]{1,0:T(8,128)} collective-permute-done((f32[1024,256]{1,0:T(8,128)S(1)}, f32[1024,256]{1,0:T(8,128)}, u32[]{:S(2)}, u32[]{:S(2)}) %collective-permute-start.13) | collective-permute-done | bytes 1048608 | tf_op jit(solution)/shard_map/ppermute | solution.py:36
  128.0 1.7 broadcast_select_fusion.3
  129.7 1.5 pad_maximum_fusion.1
  132.4 3.6 %convolution_multiply_fusion = f32[112,4096]{1,0:T(8,128)} fusion(bf16[4096,256]{1,0:T(8,128)(2,1)} %param.8, bf16[896,256]{1,0:T(8,128)(2,1)} %copy-done.15, s32[]{:T(128)S(6)} %select_n.196), kind=kOutput, calls=%fused_computation | convolution fusion | flops 235339776 | bytes 3989508 | tf_op jit(solution)/shard_map/dot_general | solution.py:18
  136.0 1.9 broadcast_select_fusion.1
  137.9 2.3 pad_maximum_fusion
  140.2 27.5 %all-gather.5.cloned.1.call-done.tokens.refs_2_ = bf16[640,6656]{1,0:T(8,128)(2,1)} async-done(((bf16[160,6656]{1,0:T(8,128)(2,1)}), bf16[640,6656]{1,0:T(8,128)(2,1)}) %all-gather.5.cloned.1.call-update) | async-done | bytes 8519696 | tf_op jit(solution)/shard_map/all_gather | solution.py:193
  167.7 44.5 %weight_pass.2 = (f32[4,80,4096]{2,1,0:T(8,128)S(1)}, bf16[4,80,4096]{2,1,0:T(8,128)(2,1)S(1)}) custom-call(s32[8]{0:T(128)S(1)} %iota_xor_fusion.table, bf16[640,6656]{1,0:T(8,128)(2,1)} %all-gather.5.cloned.1.call-done.tokens.refs_2_, bf16[4096,6656]{1,0:T(8,128)(2,1)} %weight.3), custom_call_target="tpu_custom_call" | custom-call | bytes 65536 | tf_op jit(solution)/shard_map/weight_pass/pallas_call | solution.py:82
  217.5 1.2 add_bitcast_fusion
  218.7 1.5 add_bitcast_fusion.2
  220.2 15.8 %all-gather.3.cloned.1.call-done.tokens.refs_3_ = bf16[256,6656]{1,0:T(8,128)(2,1)} async-done(((bf16[64,6656]{1,0:T(8,128)(2,1)}), bf16[256,6656]{1,0:T(8,128)(2,1)}) %all-gather.3.cloned.1.call-update) | async-done | bytes 3407888 | tf_op jit(solution)/shard_map/all_gather | solution.py:193
  237.0 1.5 collective-permute-start.19
  238.6 1.2 pad_maximum_fusion.6
  239.8 1.5 collective-permute-start.20
  243.6 2.3 copy-done.2
  245.9 23.3 %weight_pass.3 = (f32[4,32,4096]{2,1,0:T(8,128)S(1)}, bf16[4,32,4096]{2,1,0:T(8,128)(2,1)S(1)}) custom-call(s32[8]{0:T(128)S(1)} %iota_xor_fusion.table, bf16[256,6656]{1,0:T(8,128)(2,1)S(1)} %copy-done.2, bf16[4096,6656]{1,0:T(8,128)(2,1)} %weight.3), custom_call_target="tpu_custom_call" | custom-call | bytes 65536 | tf_op jit(solution)/shard_map/weight_pass/pallas_call | solution.py:82
  269.2 3.9 %factor_gradient.2.refs_4_ = f32[256,6656]{1,0:T(8,128)} custom-call(bf16[256,640]{1,0:T(8,128)(2,1)S(1)} %bitcast.233, bf16[256,256]{1,0:T(8,128)(2,1)S(1)} %bitcast.235, bf16[640,6656]{1,0:T(8,128)(2,1)S(1)} %bitcast.232, bf16[256,6656]{1,0:T(8,128)(2,1)S(1)} %copy-done.2), custom_call_target="tpu_custom_call" | custom-call | bytes 65536 | tf_op jit(solution)/shard_map/factor_gradient/pallas_call | solution.py:122
  274.1 1.5 collective-permute-start.26
  275.7 1.2 collective-permute-start.25
  277.7 3.6 %collective-permute-done.26 = bf16[1,80,1024]{2,1,0:T(8,128)(2,1)S(1)} collective-permute-done((bf16[1,80,1024]{2,1,0:T(8,128)(2,1)S(1)}, bf16[1,80,1024]{2,1,0:T(8,128)(2,1)S(1)}, u32[]{:S(2)}, u32[]{:S(2)}) %collective-permute-start.26) | collective-permute-done | bytes 163872 | tf_op jit(solution)/shard_map/ppermute | solution.py:36
  283.7 2.9 collective-permute-done.23
  287.0 1.2 collective-permute-start.31
  288.5 1.5 collective-permute-start.29
  290.0 3.9 %factor_gradient.3 = f32[256,6656]{1,0:T(8,128)} custom-call(bf16[256,640]{1,0:T(8,128)(2,1)S(1)} %bitcast.234, bf16[256,256]{1,0:T(8,128)(2,1)S(1)} %bitcast.236, bf16[640,6656]{1,0:T(8,128)(2,1)S(1)} %bitcast.232, bf16[256,6656]{1,0:T(8,128)(2,1)S(1)} %copy-done.2, f32[256,6656]{1,0:T(8,128)} %factor_gradient.2.refs_4_), custom_call_target="tpu_custom_call", output_to_operand_aliasing={{}: (4, {})} | custom-call | bytes 65536 | tf_op jit(solution)/shard_map/factor_gradient/pallas_call | solution.py:122
  295.0 1.3 collective-permute-done.29
  297.5 1.4 collective-permute-done.32
  299.0 2.4 collective-permute-done.30
  (157 shorter events, 28.1 us)
Async XLA Ops:
  7.2 160.5 %all-gather.5.cloned.1.call-start = ((), (), s32[]{:S(2)}) async-start(), calls=%async_computation.2 | async-start | bytes 10649600 | tf_op jit(solution)/shard_map/all_gather | solution.py:193
  13.5 8.7 %copy-start.7 = (bf16[112,4096]{1,0:T(8,128)(2,1)S(1)}, bf16[112,4096]{1,0:T(8,128)(2,1)}, u32[]{:S(2)}) copy-start(bf16[112,4096]{1,0:T(8,128)(2,1)} %param.5) | copy-start | bytes 2752516
  14.2 18.7 %collective-permute-start = (f32[112,256]{1,0:T(8,128)S(1)}, f32[112,256]{1,0:T(8,128)S(1)}, u32[]{:S(2)}, u32[]{:S(2)}) collective-permute-start(f32[112,256]{1,0:T(8,128)S(1)} %dynamic-slice_bitcast_fusion), channel_id=1, source_target_pairs={{0,16},{4,20},{8,24},{12,28},{16,0},{20,4},{24,8},{28,12},{1,17},{... | collective-permute-start | bytes 344072 | tf_op jit(solution)/shard_map/ppermute | solution.py:36
  19.6 7.8 %collective-permute-start.3 = (f32[56,256]{1,0:T(8,128)S(1)}, f32[56,256]{1,0:T(8,128)S(1)}, u32[]{:S(2)}, u32[]{:S(2)}) collective-permute-start(f32[56,256]{1,0:T(8,128)S(1)} %dynamic-slice_bitcast_fusion.1), channel_id=1, source_target_pairs={{0,2},{1,3},{2,0},{3,1},{4,6},{5,7},{6,4},{7,5},{8,10},{9,11},{10,... | collective-permute-start | bytes 172040 | tf_op jit(solution)/shard_map/ppermute | solution.py:36
  22.6 10.3 %copy-start.17 = (f32[224,256]{1,0:T(8,128)S(1)}, f32[224,256]{1,0:T(8,128)}, u32[]{:S(2)}) copy-start(f32[224,256]{1,0:T(8,128)} %copy-done.16) | copy-start | bytes 688132
  27.5 13.4 %collective-permute-start.4 = (f32[28,256]{1,0:T(8,128)S(1)}, f32[28,256]{1,0:T(8,128)S(1)}, u32[]{:S(2)}, u32[]{:S(2)}) collective-permute-start(f32[28,256]{1,0:T(8,128)S(1)} %dynamic-slice_bitcast_fusion.3), channel_id=1, source_target_pairs={{0,1},{1,0},{2,3},{3,2},{4,5},{5,4},{6,7},{7,6},{8,9},{9,8},{10,11... | collective-permute-start | bytes 86024 | tf_op jit(solution)/shard_map/ppermute | solution.py:36
  33.0 8.0 %collective-permute-start.1 = (f32[56,256]{1,0:T(8,128)S(1)}, f32[56,256]{1,0:T(8,128)S(1)}, u32[]{:S(2)}, u32[]{:S(2)}) collective-permute-start(f32[56,256]{1,0:T(8,128)S(1)} %dynamic-slice_bitcast_fusion.2), channel_id=1, source_target_pairs={{0,8},{4,12},{8,0},{12,4},{16,24},{20,28},{24,16},{28,20},{1,9},{5... | collective-permute-start | bytes 172040 | tf_op jit(solution)/shard_map/ppermute | solution.py:36
  40.9 4.1 %collective-permute-start.5 = (bf16[28,256]{1,0:T(8,128)(2,1)S(1)}, bf16[28,256]{1,0:T(8,128)(2,1)S(1)}, u32[]{:S(2)}, u32[]{:S(2)}) collective-permute-start(bf16[28,256]{1,0:T(8,128)(2,1)S(1)} %fusion.17), channel_id=1, source_target_pairs={{0,1},{1,0},{2,3},{3,2},{4,5},{5,4},{6,7},{7,6},{8,9},{9,8},{10,11... | collective-permute-start | bytes 43016 | tf_op jit(solution)/shard_map/ppermute | solution.py:36
  41.0 4.0 %collective-permute-start.2 = (f32[28,256]{1,0:T(8,128)S(1)}, f32[28,256]{1,0:T(8,128)S(1)}, u32[]{:S(2)}, u32[]{:S(2)}) collective-permute-start(f32[28,256]{1,0:T(8,128)S(1)} %dynamic-slice_bitcast_fusion.4), channel_id=1, source_target_pairs={{0,4},{4,0},{8,12},{12,8},{16,20},{20,16},{24,28},{28,24},{1,5},{5... | collective-permute-start | bytes 86024 | tf_op jit(solution)/shard_map/ppermute | solution.py:36
  45.0 7.4 %collective-permute-start.7 = (bf16[1,28,256]{2,1,0:T(8,128)(2,1)S(1)}, bf16[1,28,256]{2,1,0:T(8,128)(2,1)S(1)}, u32[]{:S(2)}, u32[]{:S(2)}) collective-permute-start(bf16[1,28,256]{2,1,0:T(8,128)(2,1)S(1)} %bitcast.265), channel_id=1, source_target_pairs={{0,1},{1,0},{2,3},{3,2},{4,5},{5,4},{6,7},{7,6},{8,9},{9,8},{10,11... | collective-permute-start | bytes 43016 | tf_op jit(solution)/shard_map/ppermute | solution.py:36
  45.1 7.4 %collective-permute-start.6 = (bf16[56,256]{1,0:T(8,128)(2,1)S(1)}, bf16[56,256]{1,0:T(8,128)(2,1)S(1)}, u32[]{:S(2)}, u32[]{:S(2)}) collective-permute-start(bf16[56,256]{1,0:T(8,128)(2,1)S(1)} %pad_maximum_fusion.15), channel_id=1, source_target_pairs={{0,2},{1,3},{2,0},{3,1},{4,6},{5,7},{6,4},{7,5},{8,10},{9,11},{10,... | collective-permute-start | bytes 86024 | tf_op jit(solution)/shard_map/ppermute | solution.py:36
  52.4 7.6 %collective-permute-start.8 = (bf16[2,28,256]{2,1,0:T(8,128)(2,1)S(1)}, bf16[2,28,256]{2,1,0:T(8,128)(2,1)S(1)}, u32[]{:S(2)}, u32[]{:S(2)}) collective-permute-start(bf16[2,28,256]{2,1,0:T(8,128)(2,1)S(1)} %pad_maximum_fusion.14), channel_id=1, source_target_pairs={{0,2},{1,3},{2,0},{3,1},{4,6},{5,7},{6,4},{7,5},{8,10},{9,11},{10,... | collective-permute-start | bytes 86024 | tf_op jit(solution)/shard_map/ppermute | solution.py:36
  60.1 1.4 collective-permute-start.9
  61.5 7.7 %collective-permute-start.10 = (bf16[2,224,256]{2,1,0:T(8,128)(2,1)S(1)}, bf16[2,224,256]{2,1,0:T(8,128)(2,1)S(1)}, u32[]{:S(2)}, u32[]{:S(2)}) collective-permute-start(bf16[2,224,256]{2,1,0:T(8,128)(2,1)S(1)} %pad_maximum_fusion.11), channel_id=1, source_target_pairs={{0,8},{4,12},{8,0},{12,4},{16,24},{20,28},{24,16},{28,20},{1,9},{5... | collective-permute-start | bytes 688136 | tf_op jit(solution)/shard_map/ppermute | solution.py:36
  69.4 16.1 %collective-permute-start.11 = (bf16[4,224,256]{2,1,0:T(8,128)(2,1)S(1)}, bf16[4,224,256]{2,1,0:T(8,128)(2,1)}, u32[]{:S(2)}, u32[]{:S(2)}) collective-permute-start(bf16[4,224,256]{2,1,0:T(8,128)(2,1)S(1)} %pad_maximum_fusion.4), channel_id=1, source_target_pairs={{0,16},{4,20},{8,24},{12,28},{16,0},{20,4},{24,8},{28,12},{1,17},{... | collective-permute-start | bytes 1376264 | tf_op jit(solution)/shard_map/ppermute | solution.py:36
  70.1 21.0 %all-to-all-start = ((bf16[8,112,512]{2,1,0:T(8,128)(2,1)}), bf16[8,112,512]{2,1,0:T(8,128)(2,1)S(1)}, u32[]{:S(2)}, u32[]{:S(2)}) async-start(bf16[8,112,512]{2,1,0:T(8,128)(2,1)} %bitcast_dynamic-update-slice_fusion), calls=%async_computation | async-start | bytes 1835008 | tf_op jit(solution)/shard_map/all_to_all | solution.py:222
  74.3 161.7 %all-gather.3.cloned.1.call-start = ((), (), s32[]{:S(2)}) async-start(), calls=%async_computation.1 | async-start | bytes 4259840 | tf_op jit(solution)/shard_map/all_gather | solution.py:193
  86.5 44.6 %copy-start.4 = (bf16[4,224,256]{2,1,0:T(8,128)(2,1)}, bf16[4,224,256]{2,1,0:T(8,128)(2,1)S(1)}, u32[]{:S(2)}) copy-start(bf16[4,224,256]{2,1,0:T(8,128)(2,1)S(1)} %get-tuple-element.166) | copy-start | bytes 1376260
  86.9 5.0 %copy-start.15 = (bf16[896,256]{1,0:T(8,128)(2,1)}, bf16[896,256]{1,0:T(8,128)(2,1)S(1)}, u32[]{:S(2)}) copy-start(bf16[896,256]{1,0:T(8,128)(2,1)S(1)} %reshape.151) | copy-start | bytes 1376260
  91.6 12.9 %collective-permute-start.12 = (f32[512,256]{1,0:T(8,128)S(1)}, f32[512,256]{1,0:T(8,128)S(1)}, u32[]{:S(2)}, u32[]{:S(2)}) collective-permute-start(f32[512,256]{1,0:T(8,128)S(1)} %convolution_multiply_fusion.1), channel_id=1, source_target_pairs={{0,16},{4,20},{8,24},{12,28},{16,0},{20,4},{24,8},{28,12},{1,17},{... | collective-permute-start | bytes 1572872 | tf_op jit(solution)/shard_map/ppermute | solution.py:36
  104.6 23.4 %collective-permute-start.13 = (f32[1024,256]{1,0:T(8,128)S(1)}, f32[1024,256]{1,0:T(8,128)}, u32[]{:S(2)}, u32[]{:S(2)}) collective-permute-start(f32[1024,256]{1,0:T(8,128)S(1)} %pad_maximum_fusion.2), channel_id=1, source_target_pairs={{0,8},{4,12},{8,0},{12,4},{16,24},{20,28},{24,16},{28,20},{1,9},{5... | collective-permute-start | bytes 3145736 | tf_op jit(solution)/shard_map/ppermute | solution.py:36
  131.2 4.9 %collective-permute-start.14 = (f32[2048,256]{1,0:T(8,128)}, f32[2048,256]{1,0:T(8,128)}, u32[]{:S(2)}, u32[]{:S(2)}) collective-permute-start(f32[2048,256]{1,0:T(8,128)} %pad_maximum_fusion.1), channel_id=1, source_target_pairs={{0,4},{4,0},{8,12},{12,8},{16,20},{20,16},{24,28},{28,24},{1,5},{5... | collective-permute-start | bytes 6291464 | tf_op jit(solution)/shard_map/ppermute | solution.py:36
  212.5 2.2 collective-permute-start.18
  212.7 2.9 collective-permute-start.17
  213.1 3.5 %collective-permute-start.16 = (bf16[4,80,1024]{2,1,0:T(8,128)(2,1)S(1)}, bf16[4,80,1024]{2,1,0:T(8,128)(2,1)S(1)}, u32[]{:S(2)}, u32[]{:S(2)}) collective-permute-start(bf16[4,80,1024]{2,1,0:T(8,128)(2,1)S(1)} %get-tuple-element.153), channel_id=1, source_target_pairs={{0,4},{4,0},{8,12},{12,8},{16,20},{20,16},{24,28},{28,24},{1,5},{5... | collective-permute-start | bytes 1966088 | tf_op jit(solution)/shard_map/ppermute | solution.py:36
  213.2 4.3 %collective-permute-start.15 = (bf16[4,80,1024]{2,1,0:T(8,128)(2,1)S(1)}, bf16[4,80,1024]{2,1,0:T(8,128)(2,1)S(1)}, u32[]{:S(2)}, u32[]{:S(2)}) collective-permute-start(bf16[4,80,1024]{2,1,0:T(8,128)(2,1)S(1)} %get-tuple-element.154), channel_id=1, source_target_pairs={{0,4},{4,0},{8,12},{12,8},{16,20},{20,16},{24,28},{28,24},{1,5},{5... | collective-permute-start | bytes 1966088 | tf_op jit(solution)/shard_map/ppermute | solution.py:36
  220.2 22.7 %copy-start.14 = (bf16[80,1024]{1,0:T(8,128)(2,1)S(1)}, bf16[80,1024]{1,0:T(8,128)(2,1)}, u32[]{:S(2)}) copy-start(bf16[80,1024]{1,0:T(8,128)(2,1)} %get-tuple-element.84) | copy-start | bytes 491524
  237.0 36.1 %collective-permute-start.19 = (bf16[2,80,1024]{2,1,0:T(8,128)(2,1)S(1)}, bf16[2,80,1024]{2,1,0:T(8,128)(2,1)S(1)}, u32[]{:S(2)}, u32[]{:S(2)}) collective-permute-start(bf16[2,80,1024]{2,1,0:T(8,128)(2,1)S(1)} %pad_maximum_fusion.5), channel_id=1, source_target_pairs={{0,8},{4,12},{8,0},{12,4},{16,24},{20,28},{24,16},{28,20},{1,9},{5... | collective-permute-start | bytes 983048 | tf_op jit(solution)/shard_map/ppermute | solution.py:36
  238.6 30.6 %slice-start = ((s8[8519680]{0:T(1024)(128)(4,1)}), s8[4194304]{0:T(1024)(128)(4,1)S(1)}, s32[]{:S(2)}) async-start(s8[8519680]{0:T(1024)(128)(4,1)} %bitcast.231), calls=%async_computation.3 | async-start | bytes 8388608
  239.8 33.4 %collective-permute-start.20 = (bf16[2,80,1024]{2,1,0:T(8,128)(2,1)S(1)}, bf16[2,80,1024]{2,1,0:T(8,128)(2,1)S(1)}, u32[]{:S(2)}, u32[]{:S(2)}) collective-permute-start(bf16[2,80,1024]{2,1,0:T(8,128)(2,1)S(1)} %pad_maximum_fusion.6), channel_id=1, source_target_pairs={{0,16},{4,20},{8,24},{12,28},{16,0},{20,4},{24,8},{28,12},{1,17},{... | collective-permute-start | bytes 983048 | tf_op jit(solution)/shard_map/ppermute | solution.py:36
  242.3 30.8 %collective-permute-start.21 = (bf16[2,80,1024]{2,1,0:T(8,128)(2,1)S(1)}, bf16[2,80,1024]{2,1,0:T(8,128)(2,1)S(1)}, u32[]{:S(2)}, u32[]{:S(2)}) collective-permute-start(bf16[2,80,1024]{2,1,0:T(8,128)(2,1)S(1)} %pad_maximum_fusion.7), channel_id=1, source_target_pairs={{0,8},{4,12},{8,0},{12,4},{16,24},{20,28},{24,16},{28,20},{1,9},{5... | collective-permute-start | bytes 983048 | tf_op jit(solution)/shard_map/ppermute | solution.py:36
  243.0 26.2 %slice-start.1 = ((s8[8519680]{0:T(1024)(128)(4,1)}), s8[4194304]{0:T(1024)(128)(4,1)S(1)}, s32[]{:S(2)}) async-start(s8[8519680]{0:T(1024)(128)(4,1)} %bitcast.231), calls=%async_computation.4 | async-start | bytes 8388608
  243.0 26.2 %slice-start.2 = ((s8[8519680]{0:T(1024)(128)(4,1)}), s8[131072]{0:T(1024)(128)(4,1)S(1)}, s32[]{:S(2)}) async-start(s8[8519680]{0:T(1024)(128)(4,1)} %bitcast.231), calls=%async_computation.5 | async-start | bytes 262144
  243.0 30.1 %collective-permute-start.22 = (bf16[2,80,1024]{2,1,0:T(8,128)(2,1)S(1)}, bf16[2,80,1024]{2,1,0:T(8,128)(2,1)S(1)}, u32[]{:S(2)}, u32[]{:S(2)}) collective-permute-start(bf16[2,80,1024]{2,1,0:T(8,128)(2,1)S(1)} %pad_maximum_fusion.8), channel_id=1, source_target_pairs={{0,16},{4,20},{8,24},{12,28},{16,0},{20,4},{24,8},{28,12},{1,17},{... | collective-permute-start | bytes 983048 | tf_op jit(solution)/shard_map/ppermute | solution.py:36
  273.1 9.3 %copy-start.13 = (f32[80,1024]{1,0:T(8,128)S(1)}, f32[80,1024]{1,0:T(8,128)}, u32[]{:S(2)}) copy-start(f32[80,1024]{1,0:T(8,128)} %get-tuple-element.95) | copy-start | bytes 983044
  273.2 9.3 %copy-start.12 = (f32[80,1024]{1,0:T(8,128)S(1)}, f32[80,1024]{1,0:T(8,128)}, u32[]{:S(2)}) copy-start(f32[80,1024]{1,0:T(8,128)} %get-tuple-element.92) | copy-start | bytes 983044
  273.2 13.4 %collective-permute-start.28 = (bf16[4,32,2048]{2,1,0:T(8,128)(2,1)S(1)}, bf16[4,32,2048]{2,1,0:T(8,128)(2,1)S(1)}, u32[]{:S(2)}, u32[]{:S(2)}) collective-permute-start(bf16[4,32,2048]{2,1,0:T(8,128)(2,1)S(1)} %get-tuple-element.161), channel_id=1, source_target_pairs={{0,4},{4,0},{8,12},{12,8},{16,20},{20,16},{24,28},{28,24},{1,5},{5... | collective-permute-start | bytes 1572872 | tf_op jit(solution)/shard_map/ppermute | solution.py:36
  273.3 13.4 %collective-permute-start.27 = (bf16[4,32,2048]{2,1,0:T(8,128)(2,1)S(1)}, bf16[4,32,2048]{2,1,0:T(8,128)(2,1)S(1)}, u32[]{:S(2)}, u32[]{:S(2)}) collective-permute-start(bf16[4,32,2048]{2,1,0:T(8,128)(2,1)S(1)} %get-tuple-element.162), channel_id=1, source_target_pairs={{0,4},{4,0},{8,12},{12,8},{16,20},{20,16},{24,28},{28,24},{1,5},{5... | collective-permute-start | bytes 1572872 | tf_op jit(solution)/shard_map/ppermute | solution.py:36
  274.1 9.5 %copy-start.11 = (f32[80,1024]{1,0:T(8,128)S(1)}, f32[80,1024]{1,0:T(8,128)}, u32[]{:S(2)}) copy-start(f32[80,1024]{1,0:T(8,128)} %get-tuple-element.89) | copy-start | bytes 983044
  274.1 7.2 %collective-permute-start.26 = (bf16[1,80,1024]{2,1,0:T(8,128)(2,1)S(1)}, bf16[1,80,1024]{2,1,0:T(8,128)(2,1)S(1)}, u32[]{:S(2)}, u32[]{:S(2)}) collective-permute-start(bf16[1,80,1024]{2,1,0:T(8,128)(2,1)S(1)} %fusion.13), channel_id=1, source_target_pairs={{0,8},{4,12},{8,0},{12,4},{16,24},{20,28},{24,16},{28,20},{1,9},{5... | collective-permute-start | bytes 491528 | tf_op jit(solution)/shard_map/ppermute | solution.py:36
  275.7 10.9 %copy-start.10 = (f32[80,1024]{1,0:T(8,128)S(1)}, f32[80,1024]{1,0:T(8,128)}, u32[]{:S(2)}) copy-start(f32[80,1024]{1,0:T(8,128)} %get-tuple-element.86) | copy-start | bytes 983044
  275.7 6.8 %collective-permute-start.25 = (bf16[1,80,1024]{2,1,0:T(8,128)(2,1)S(1)}, bf16[1,80,1024]{2,1,0:T(8,128)(2,1)S(1)}, u32[]{:S(2)}, u32[]{:S(2)}) collective-permute-start(bf16[1,80,1024]{2,1,0:T(8,128)(2,1)S(1)} %fusion.12), channel_id=1, source_target_pairs={{0,16},{4,20},{8,24},{12,28},{16,0},{20,4},{24,8},{28,12},{1,17},{... | collective-permute-start | bytes 491528 | tf_op jit(solution)/shard_map/ppermute | solution.py:36
  277.0 6.6 %collective-permute-start.24 = (bf16[1,80,1024]{2,1,0:T(8,128)(2,1)S(1)}, bf16[1,80,1024]{2,1,0:T(8,128)(2,1)S(1)}, u32[]{:S(2)}, u32[]{:S(2)}) collective-permute-start(bf16[1,80,1024]{2,1,0:T(8,128)(2,1)S(1)} %fusion.11), channel_id=1, source_target_pairs={{0,8},{4,12},{8,0},{12,4},{16,24},{20,28},{24,16},{28,20},{1,9},{5... | collective-permute-start | bytes 491528 | tf_op jit(solution)/shard_map/ppermute | solution.py:36
  281.3 5.3 %collective-permute-start.23 = (bf16[1,80,1024]{2,1,0:T(8,128)(2,1)S(1)}, bf16[1,80,1024]{2,1,0:T(8,128)(2,1)S(1)}, u32[]{:S(2)}, u32[]{:S(2)}) collective-permute-start(bf16[1,80,1024]{2,1,0:T(8,128)(2,1)S(1)} %fusion.10), channel_id=1, source_target_pairs={{0,16},{4,20},{8,24},{12,28},{16,0},{20,4},{24,8},{28,12},{1,17},{... | collective-permute-start | bytes 491528 | tf_op jit(solution)/shard_map/ppermute | solution.py:36
  287.0 6.8 %collective-permute-start.31 = (bf16[2,32,2048]{2,1,0:T(8,128)(2,1)S(1)}, bf16[2,32,2048]{2,1,0:T(8,128)(2,1)S(1)}, u32[]{:S(2)}, u32[]{:S(2)}) collective-permute-start(bf16[2,32,2048]{2,1,0:T(8,128)(2,1)S(1)} %pad_maximum_fusion.10), channel_id=1, source_target_pairs={{0,16},{4,20},{8,24},{12,28},{16,0},{20,4},{24,8},{28,12},{1,17},{... | collective-permute-start | bytes 786440 | tf_op jit(solution)/shard_map/ppermute | solution.py:36
  288.5 7.8 %collective-permute-start.29 = (bf16[2,32,2048]{2,1,0:T(8,128)(2,1)S(1)}, bf16[2,32,2048]{2,1,0:T(8,128)(2,1)S(1)}, u32[]{:S(2)}, u32[]{:S(2)}) collective-permute-start(bf16[2,32,2048]{2,1,0:T(8,128)(2,1)S(1)} %pad_maximum_fusion.9), channel_id=1, source_target_pairs={{0,8},{4,12},{8,0},{12,4},{16,24},{20,28},{24,16},{28,20},{1,9},{5... | collective-permute-start | bytes 786440 | tf_op jit(solution)/shard_map/ppermute | solution.py:36
  293.9 5.0 %collective-permute-start.32 = (bf16[1,32,2048]{2,1,0:T(8,128)(2,1)S(1)}, bf16[1,32,2048]{2,1,0:T(8,128)(2,1)S(1)}, u32[]{:S(2)}, u32[]{:S(2)}) collective-permute-start(bf16[1,32,2048]{2,1,0:T(8,128)(2,1)S(1)} %fusion.15), channel_id=1, source_target_pairs={{0,8},{4,12},{8,0},{12,4},{16,24},{20,28},{24,16},{28,20},{1,9},{5... | collective-permute-start | bytes 393224 | tf_op jit(solution)/shard_map/ppermute | solution.py:36
  296.3 5.0 %collective-permute-start.30 = (bf16[1,32,2048]{2,1,0:T(8,128)(2,1)S(1)}, bf16[1,32,2048]{2,1,0:T(8,128)(2,1)S(1)}, u32[]{:S(2)}, u32[]{:S(2)}) collective-permute-start(bf16[1,32,2048]{2,1,0:T(8,128)(2,1)S(1)} %fusion.14), channel_id=1, source_target_pairs={{0,16},{4,20},{8,24},{12,28},{16,0},{20,4},{24,8},{28,12},{1,17},{... | collective-permute-start | bytes 393224 | tf_op jit(solution)/shard_map/ppermute | solution.py:36
  (9 other events, 22.5 us)
Sparse Core Ops, SparseCore 0:
  10.6 157.0 all-gather.4
  169.8 66.1 all-gather.2

commit v8 on v6

--- a/solution.py
+++ b/solution.py
@@ -88,7 +88,7 @@
     else:
         (tokens,) = source_refs
         kept, sent = refs
-    product = contract_trailing_axis(weight[...], tokens[...]).T
+    product = contract_trailing_axis(tokens[...], weight[...])
     for i in range(owners):
         place = table[i]
         part = product[i * rows : (i + 1) * rows]
@@ -256,32 +256,26 @@
     low_part = contract_trailing_axis(low_source, b_factor)
     low_small = scatter_small(low_part, "wide").astype(jnp.bfloat16)
 
-    def exchange(act_sum, low_rows, bit):
-        both = jnp.concatenate([act_sum, low_rows.reshape(-1, rank).astype(jnp.float32)], axis=0)
-        return swap(both, "narrow", bit)
-
-    def exchanged(act_sum, low_rows, got, bit):
-        other = got[owner_rows:].reshape(low_rows.shape).astype(jnp.bfloat16)
-        upper = (me_narrow & bit) != 0
-        first, second = jnp.where(upper, other, low_rows), jnp.where(upper, low_rows, other)
-        return act_sum + got[:owner_rows], jnp.concatenate([first, second], axis=0)
-
-    low_rows = low_small[None]
+    low_rows = low_small
     near[0], far[0], blocks[0], grad_out, low_rows, inputs = hold(
         near[0], far[0], blocks[0], grad_out, low_rows, inputs
     )
-    act_sum = jnp.dot(inputs, adapter_down_matrix, preferred_element_type=jnp.float32)
     complete(0)
     blocks[1] = block_of(grad_out, 1)
-    for bit in narrow_bits[:-1]:
-        act_sum, low_rows = exchanged(act_sum, low_rows, exchange(act_sum, low_rows, bit), bit)
-    small = {"inputs": inputs, "act": act_sum, "low": low_rows}
-    small["got"] = exchange(act_sum, low_rows, narrow_bits[-1])
+    act_part = jnp.dot(inputs, adapter_down_matrix, preferred_element_type=jnp.float32)
+    both = jnp.concatenate([act_part.astype(jnp.bfloat16), low_rows], axis=0)
+    small = {"inputs": inputs, "both": both}
+    small["got"] = [swap(both, "narrow", p) for p in range(1, groups)]
 
     def take():
-        if "got" in small and "act" in small:
-            act, low = exchanged(small.pop("act"), small.pop("low"), small.pop("got"), narrow_bits[-1])
-            small["rows"] = jnp.concatenate([act.astype(jnp.bfloat16), low.reshape(-1, rank)], axis=0)[None]
+        if "both" in small:
+            value = jnp.stack([small.pop("both"), *small.pop("got")])
+            for bit in narrow_bits:
+                cut = value.reshape(groups // (2 * bit), 2, bit, *value.shape[1:])
+                value = jnp.where((me_narrow & bit) != 0, cut[:, ::-1], cut).reshape(value.shape)
+            act = jnp.sum(value[:, :owner_rows].astype(jnp.float32), axis=0).astype(jnp.bfloat16)
+            low = value[:, owner_rows:].reshape(-1, rank)
+            small["rows"] = jnp.concatenate([act, low], axis=0)[None]
         elif "got" in small:
             upper = (me_wide & taken.pop(0)) != 0
             name = "rows" if "rows" in small else "grad_a"
@@ -349,8 +343,8 @@
         tokens[i], kept, sent = weight_pass(table, sources, w_base, owners)
         sums[i] = (kept, sent)
         done_hops[i] = 0
-        sum_hop(i)
-
+
+    regroup()
     for i in range(count):
         if i:
             near[i], far[i], blocks, grad_out, small, sums = hold(
@@ -366,8 +360,6 @@
         if i + 1 < count:
             begin(i + 1)
             step()
-            if i + 2 == count:
-                regroup()
             run_pass(i)
     step()
     run_pass(count - 1)
@@ -379,6 +371,7 @@
     early = steps // 2 or 1
     turned = small["turned"]
     tokens = [tokens[i] for i in range(count)]
+    sum_hop(count - 1)
     grad_b = factor_gradient(turned, tokens, adapter_matrix, columns_step, 0, early)
     sum_hop(count - 1)
     sums[count - 1], grad_b = hold(sums[count - 1], grad_b)

time: 333 us -> 300 us (0.901)
  waiting for transfers between devices: 117 us -> 94.5 us
  Pallas kernels: 96 us -> 87.6 us
  local copies, waits for them, and re-layouts: 39.3 us -> 31 us
  other arithmetic: 20.3 us -> 24.3 us
  starting transfers between devices: 47.4 us -> 51.3 us
    ppermute x35 -> x36, waiting for transfers between devices: 114 us -> 81.7 us  [swap(): return lax.ppermute(value, axis, [(i, i ^ bit) for i in range(size)])]
    ppermute x3, waiting for transfers between devices: 2.73 us -> 12.7 us  [phase_b(): lax.ppermute(far, axis, [(1, 0), (2, 3)])]
    pallas_call x3, Pallas kernels: 88.2 us -> 79.8 us  [weight_pass(): pl.pallas_call(functools.partial(pass_kernel, sources=len(sources), owner...]
    another operation x12, other arithmetic: 2.01 us -> 7.77 us  [scatter_send(): away = jnp.stack([part[p | bit].astype(jnp.bfloat16) for p in stay[-1]])]
    unnamed x94 -> x50, local copies, waits for them, and re-layouts: 17.3 us -> 12.1 us
    convert_element_type x3, other arithmetic: 6.27 us -> 2.15 us  [scatter_send(): away = jnp.stack([part[p | bit].astype(jnp.bfloat16) for p in stay[-1]])]
    ppermute x35 -> x36, starting transfers between devices: 36.1 us -> 40 us  [swap(): return lax.ppermute(value, axis, [(i, i ^ bit) for i in range(size)])]
  transfers between devices with their start and end apart: 42 -> 43, of which waited for: 18 -> 17; matrix products, arithmetic and copies ran while one was open for 14% -> 16% of each run, Pallas kernels for 29% -> 29%
where the time goes in v8:
time: 300 us; the launch traced here: 299 us
  waiting for transfers between devices  94.5 us (32%)
  Pallas kernels  87.6 us (29%)
  starting transfers between devices  51.3 us (17%)
  local copies, waits for them, and re-layouts  31 us (10%)
  other arithmetic  24.3 us (8%)
  matrix products  8.53 us (3%)
    ppermute x36, waiting for transfers between devices, swap(): return lax.ppermute(value, axis, [(i, i ^ bit) for i in range(size)])  81.7 us
    pallas_call x3, Pallas kernels, weight_pass(): pl.pallas_call(functools.partial(pass_kernel, sources=len(sources), owner...  79.8 us
    ppermute x36, starting transfers between devices, swap(): return lax.ppermute(value, axis, [(i, i ^ bit) for i in range(size)])  40 us
    ppermute x3, waiting for transfers between devices, phase_b(): lax.ppermute(far, axis, [(1, 0), (2, 3)])  12.7 us
    unnamed x50, local copies, waits for them, and re-layouts  12.1 us
    another operation x12, other arithmetic, scatter_send(): away = jnp.stack([part[p | bit].astype(jnp.bfloat16) for p in stay[-1]])  7.77 us
    pallas_call x2, Pallas kernels, factor_gradient(): pl.pallas_call(functools.partial(factor_kernel, count=len(acts), scale=sc...  7.75 us
  transfers between devices with their start and end apart: 43, of which 17 were waited for; matrix products, arithmetic and copies ran while one was open for 16% of the time, Pallas kernels for 29%

profile of v8, /device:TPU:0, one launch (start us, length us, event | category | flops | bytes accessed | tf_op | source)
XLA Modules:
  0.0 298.5 jit_solution(8049362356198397551)
XLA Ops:
  0.6 2.6 slice.348
  3.2 3.0 %collective-permute-start = (bf16[96,6656]{1,0:T(8,128)(2,1)}, bf16[96,6656]{1,0:T(8,128)(2,1)}, u32[]{:S(2)}, u32[]{:S(2)}) collective-permute-start(bf16[96,6656]{1,0:T(8,128)(2,1)} %bitcast.1.refs_0_), channel_id=1, source_target_pairs={{0,1},{1,0},{2,3},{3,2},{4,5},{5,4},{6,7},{7,6},{8,9},{9,8},{10,11... | collective-permute-start | bytes 3833864 | tf_op jit(solution)/shard_map/ppermute | solution.py:36
  6.3 2.6 collective-permute-start.1
  8.9 3.7 %fusion.27 = f32[224,256]{1,0:T(8,128)} fusion(bf16[224,6656]{1,0:T(8,128)(2,1)} %param.6, bf16[256,6656]{1,0:T(8,128)(2,1)S(1)} %copy-done), kind=kOutput, calls=%fused_computation.124 | convolution fusion | flops 763363328 | bytes 6619136 | tf_op jit(solution)/shard_map/dot_general | solution.py:18
  13.4 1.5 collective-permute-start.2
  15.0 3.3 %collective-permute-done.2 = f32[112,256]{1,0:T(8,128)S(1)} collective-permute-done((f32[112,256]{1,0:T(8,128)S(1)}, f32[112,256]{1,0:T(8,128)S(1)}, u32[]{:S(2)}, u32[]{:S(2)}) %collective-permute-start.2) | collective-permute-done | bytes 114720 | tf_op jit(solution)/shard_map/ppermute | solution.py:36
  19.2 1.6 collective-permute-start.3
  20.7 2.7 collective-permute-done.3
  24.8 37.1 %collective-permute-done.refs_1_ = bf16[96,6656]{1,0:T(8,128)(2,1)} collective-permute-done((bf16[96,6656]{1,0:T(8,128)(2,1)}, bf16[96,6656]{1,0:T(8,128)(2,1)}, u32[]{:S(2)}, u32[]{:S(2)}) %collective-permute-start) | collective-permute-done | bytes 1277984 | tf_op jit(solution)/shard_map/ppermute | solution.py:36
  61.9 2.6 collective-permute-done.1.refs_2_
  66.5 1.5 copy.91
  68.0 1.5 fusion.25
  74.8 4.2 %all-to-all-start = ((bf16[8,112,512]{2,1,0:T(8,128)(2,1)}), bf16[8,112,512]{2,1,0:T(8,128)(2,1)}, u32[]{:S(2)}, u32[]{:S(2)}) async-start(bf16[8,112,512]{2,1,0:T(8,128)(2,1)} %bitcast_dynamic-update-slice_fusion), calls=%async_computation | async-start | bytes 1835008 | tf_op jit(solution)/shard_map/all_to_all | solution.py:304
  79.1 2.3 convolution_convert_fusion
  81.4 2.8 collective-permute-start.7
  87.9 11.6 %collective-permute-done.7 = bf16[140,256]{1,0:T(8,128)(2,1)S(1)} collective-permute-done((bf16[140,256]{1,0:T(8,128)(2,1)S(1)}, bf16[140,256]{1,0:T(8,128)(2,1)S(1)}, u32[]{:S(2)}, u32[]{:S(2)}) %collective-permute-start.7) | collective-permute-done | bytes 71712 | tf_op jit(solution)/shard_map/ppermute | solution.py:36
  108.1 31.2 %weight_pass.3 = (bf16[384,6656]{1,0:T(8,128)(2,1)}, f32[4,48,4096]{2,1,0:T(8,128)S(1)}, bf16[4,48,4096]{2,1,0:T(8,128)(2,1)S(1)}) custom-call(s32[9]{0:T(128)S(1)} %stack.115.table, bf16[96,6656]{1,0:T(8,128)(2,1)} %bitcast.1.refs_0_, bf16[96,6656]{1,0:T(8,128)(2,1)} %collective-permute-done.refs_1_, bf16[96,6656]{1,0:T(8,128)(2,1)} %collective-permute-done.1.refs_2_, ...), custom_call_target="tpu_custom_call" | custom-call | bytes 65536 | tf_op jit(solution)/shard_map/weight_pass/pallas_call | solution.py:124
  143.9 1.6 collective-permute-start.15
  145.4 2.1 slice.360
  147.6 4.0 %collective-permute-done.15 = bf16[2,224,256]{2,1,0:T(8,128)(2,1)S(1)} collective-permute-done((bf16[2,224,256]{2,1,0:T(8,128)(2,1)S(1)}, bf16[2,224,256]{2,1,0:T(8,128)(2,1)S(1)}, u32[]{:S(2)}, u32[]{:S(2)}) %collective-permute-start.15) | collective-permute-done | bytes 229408 | tf_op jit(solution)/shard_map/ppermute | solution.py:36
  151.5 12.7 %collective-permute-done.14.refs_4_ = bf16[64,6656]{1,0:T(8,128)(2,1)S(1)} collective-permute-done((bf16[64,6656]{1,0:T(8,128)(2,1)}, bf16[64,6656]{1,0:T(8,128)(2,1)S(1)}, u32[]{:S(2)}, u32[]{:S(2)}) %collective-permute-start.14) | collective-permute-done | bytes 852000 | tf_op jit(solution)/shard_map/ppermute | solution.py:68
  164.3 1.9 collective-permute-start.19
  167.0 1.5 collective-permute-start.20
  168.5 1.6 add_convert_fusion.1
  170.9 1.5 collective-permute-start.21
  177.2 23.9 %weight_pass.4 = (bf16[256,6656]{1,0:T(8,128)(2,1)S(1)}, f32[4,32,4096]{2,1,0:T(8,128)S(1)}, bf16[4,32,4096]{2,1,0:T(8,128)(2,1)S(1)}) custom-call(s32[9]{0:T(128)S(1)} %stack.115.table, bf16[64,6656]{1,0:T(8,128)(2,1)S(1)} %bitcast.175, bf16[64,6656]{1,0:T(8,128)(2,1)} %collective-permute-done.10.refs_1_, bf16[64,6656]{1,0:T(8,128)(2,1)} %collective-permute-done.11.refs_2_, ...), custom_call_target="tpu_custom_call" | custom-call | bytes 65536 | tf_op jit(solution)/shard_map/weight_pass/pallas_call | solution.py:124
  202.1 2.2 collective-permute-done.19.refs_2_
  207.2 1.6 collective-permute-start.23
  208.8 1.5 collective-permute-start.24
  211.3 1.9 reshape.141
  213.3 1.8 copy.80
  216.0 1.7 copy.82
  217.7 1.4 fusion.13
  219.1 1.6 collective-permute-start.26
  222.1 1.6 collective-permute-start.27
  224.9 1.7 fusion
  229.1 6.2 %collective-permute-done.25 = bf16[512,256]{1,0:T(8,128)(2,1)S(1)} collective-permute-done((bf16[512,256]{1,0:T(8,128)(2,1)S(1)}, bf16[512,256]{1,0:T(8,128)(2,1)S(1)}, u32[]{:S(2)}, u32[]{:S(2)}) %collective-permute-start.25) | collective-permute-done | bytes 262176 | tf_op jit(solution)/shard_map/ppermute | solution.py:36
  235.5 1.6 collective-permute-start.30
  239.3 1.5 collective-permute-start.32
  240.9 24.7 %weight_pass.5 = (bf16[256,6656]{1,0:T(8,128)(2,1)S(1)}, f32[4,32,4096]{2,1,0:T(8,128)S(1)}, bf16[4,32,4096]{2,1,0:T(8,128)(2,1)S(1)}) custom-call(s32[9]{0:T(128)S(1)} %stack.115.table, bf16[64,6656]{1,0:T(8,128)(2,1)} %bitcast.31.refs_0_, bf16[64,6656]{1,0:T(8,128)(2,1)} %collective-permute-done.18.refs_1_, ...), custom_call_target="tpu_custom_call" | custom-call | bytes 65536 | tf_op jit(solution)/shard_map/weight_pass/pallas_call | solution.py:124
  267.6 1.6 collective-permute-start.34
  272.5 3.9 %factor_gradient.2.refs_6_ = f32[256,6656]{1,0:T(8,128)} custom-call(bf16[256,384]{1,0:T(8,128)(2,1)S(1)} %bitcast.176, bf16[256,256]{1,0:T(8,128)(2,1)S(1)} %bitcast.178, bf16[256,256]{1,0:T(8,128)(2,1)S(1)} %bitcast.180, bf16[384,6656]{1,0:T(8,128)(2,1)S(1)} %bitcast.171, bf16[256,6656]{1,0:T(8,128)(2,1)S(1)} %get-tuple-element.190.refs_4_, ...), custom_call_target="tpu_custom_call" | custom-call | bytes 65536 | tf_op jit(solution)/shard_map/factor_gradient/pallas_call | solution.py:159
  278.2 1.6 collective-permute-start.38
  280.8 5.2 %collective-permute-done.37 = bf16[2,32,2048]{2,1,0:T(8,128)(2,1)S(1)} collective-permute-done((bf16[2,32,2048]{2,1,0:T(8,128)(2,1)S(1)}, bf16[2,32,2048]{2,1,0:T(8,128)(2,1)S(1)}, u32[]{:S(2)}, u32[]{:S(2)}) %collective-permute-start.37) | collective-permute-done | bytes 262176 | tf_op jit(solution)/shard_map/ppermute | solution.py:36
  286.4 1.6 collective-permute-start.40
  288.0 1.6 collective-permute-start.39
  289.6 3.9 %factor_gradient.3 = f32[256,6656]{1,0:T(8,128)} custom-call(bf16[256,384]{1,0:T(8,128)(2,1)S(1)} %bitcast.177, bf16[256,256]{1,0:T(8,128)(2,1)S(1)} %bitcast.179, bf16[256,256]{1,0:T(8,128)(2,1)S(1)} %bitcast.181, bf16[384,6656]{1,0:T(8,128)(2,1)S(1)} %bitcast.171, ...), custom_call_target="tpu_custom_call", output_to_operand_aliasing={{}: (6, {})} | custom-call | bytes 65536 | tf_op jit(solution)/shard_map/factor_gradient/pallas_call | solution.py:159
  295.0 2.5 maximum_convert_fusion
  (167 shorter events, 57.7 us)
Async XLA Ops:
  3.2 58.7 %collective-permute-start = (bf16[96,6656]{1,0:T(8,128)(2,1)}, bf16[96,6656]{1,0:T(8,128)(2,1)}, u32[]{:S(2)}, u32[]{:S(2)}) collective-permute-start(bf16[96,6656]{1,0:T(8,128)(2,1)} %bitcast.1.refs_0_), channel_id=1, source_target_pairs={{0,1},{1,0},{2,3},{3,2},{4,5},{5,4},{6,7},{7,6},{8,9},{9,8},{10,11... | collective-permute-start | bytes 3833864 | tf_op jit(solution)/shard_map/ppermute | solution.py:36
  6.3 58.2 %collective-permute-start.1 = (bf16[96,6656]{1,0:T(8,128)(2,1)}, bf16[96,6656]{1,0:T(8,128)(2,1)}, u32[]{:S(2)}, u32[]{:S(2)}) collective-permute-start(bf16[96,6656]{1,0:T(8,128)(2,1)} %bitcast.1.refs_0_), channel_id=1, source_target_pairs={{0,2},{1,3},{2,0},{3,1},{4,6},{5,7},{6,4},{7,5},{8,10},{9,11},{10,... | collective-permute-start | bytes 3833864 | tf_op jit(solution)/shard_map/ppermute | solution.py:36
  13.4 4.8 %collective-permute-start.2 = (f32[112,256]{1,0:T(8,128)S(1)}, f32[112,256]{1,0:T(8,128)S(1)}, u32[]{:S(2)}, u32[]{:S(2)}) collective-permute-start(f32[112,256]{1,0:T(8,128)S(1)} %dynamic-slice_bitcast_fusion), channel_id=1, source_target_pairs={{0,16},{4,20},{8,24},{12,28},{16,0},{20,4},{24,8},{28,12},{1,17},{... | collective-permute-start | bytes 344072 | tf_op jit(solution)/shard_map/ppermute | solution.py:36
  19.2 4.2 %collective-permute-start.3 = (f32[56,256]{1,0:T(8,128)S(1)}, f32[56,256]{1,0:T(8,128)S(1)}, u32[]{:S(2)}, u32[]{:S(2)}) collective-permute-start(f32[56,256]{1,0:T(8,128)S(1)} %dynamic-slice_bitcast_fusion.1), channel_id=1, source_target_pairs={{0,8},{4,12},{8,0},{12,4},{16,24},{20,28},{24,16},{28,20},{1,9},{5... | collective-permute-start | bytes 172040 | tf_op jit(solution)/shard_map/ppermute | solution.py:36
  23.5 1.3 collective-permute-start.4
  64.5 36.5 %collective-permute-start.5 = (bf16[96,6656]{1,0:T(8,128)(2,1)}, bf16[96,6656]{1,0:T(8,128)(2,1)S(1)}, u32[]{:S(2)}, u32[]{:S(2)}) collective-permute-start(bf16[96,6656]{1,0:T(8,128)(2,1)} %bitcast.1.refs_0_), channel_id=1, source_target_pairs={{1,2},{2,1},{5,6},{6,5},{9,10},{10,9},{13,14},{14,13},{17,18},{18,... | collective-permute-start | bytes 3833864 | tf_op jit(solution)/shard_map/ppermute | solution.py:67
  65.2 35.8 %collective-permute-start.6 = (bf16[96,6656]{1,0:T(8,128)(2,1)}, bf16[96,6656]{1,0:T(8,128)(2,1)S(1)}, u32[]{:S(2)}, u32[]{:S(2)}) collective-permute-start(bf16[96,6656]{1,0:T(8,128)(2,1)} %collective-permute-done.1.refs_2_), channel_id=1, source_target_pairs={{1,0},{2,3},{5,4},{6,7},{9,8},{10,11},{13,12},{14,15},{17,16},{18,... | collective-permute-start | bytes 3833864 | tf_op jit(solution)/shard_map/ppermute | solution.py:68
  74.8 26.1 %all-to-all-start = ((bf16[8,112,512]{2,1,0:T(8,128)(2,1)}), bf16[8,112,512]{2,1,0:T(8,128)(2,1)}, u32[]{:S(2)}, u32[]{:S(2)}) async-start(bf16[8,112,512]{2,1,0:T(8,128)(2,1)} %bitcast_dynamic-update-slice_fusion), calls=%async_computation | async-start | bytes 1835008 | tf_op jit(solution)/shard_map/all_to_all | solution.py:304
  81.4 18.1 %collective-permute-start.7 = (bf16[140,256]{1,0:T(8,128)(2,1)S(1)}, bf16[140,256]{1,0:T(8,128)(2,1)S(1)}, u32[]{:S(2)}, u32[]{:S(2)}) collective-permute-start(bf16[140,256]{1,0:T(8,128)(2,1)S(1)} %pad_maximum_fusion.13), channel_id=1, source_target_pairs={{0,1},{1,0},{2,3},{3,2},{4,5},{5,4},{6,7},{7,6},{8,9},{9,8},{10,11... | collective-permute-start | bytes 215048 | tf_op jit(solution)/shard_map/ppermute | solution.py:36
  84.2 16.7 %collective-permute-start.8 = (bf16[140,256]{1,0:T(8,128)(2,1)S(1)}, bf16[140,256]{1,0:T(8,128)(2,1)}, u32[]{:S(2)}, u32[]{:S(2)}) collective-permute-start(bf16[140,256]{1,0:T(8,128)(2,1)S(1)} %pad_maximum_fusion.13), channel_id=1, source_target_pairs={{0,2},{1,3},{2,0},{3,1},{4,6},{5,7},{6,4},{7,5},{8,10},{9,11},{10,... | collective-permute-start | bytes 215048 | tf_op jit(solution)/shard_map/ppermute | solution.py:36
  85.3 15.7 %collective-permute-start.9 = (bf16[140,256]{1,0:T(8,128)(2,1)S(1)}, bf16[140,256]{1,0:T(8,128)(2,1)}, u32[]{:S(2)}, u32[]{:S(2)}) collective-permute-start(bf16[140,256]{1,0:T(8,128)(2,1)S(1)} %pad_maximum_fusion.13), channel_id=1, source_target_pairs={{0,3},{1,2},{2,1},{3,0},{4,7},{5,6},{6,5},{7,4},{8,11},{9,10},{10,... | collective-permute-start | bytes 215048 | tf_op jit(solution)/shard_map/ppermute | solution.py:36
  87.9 52.2 %copy-start.2 = (bf16[2,32,6656]{2,1,0:T(8,128)(2,1)}, bf16[2,32,6656]{2,1,0:T(8,128)(2,1)S(1)}, u32[]{:S(2)}) copy-start(bf16[2,32,6656]{2,1,0:T(8,128)(2,1)S(1)} %slice.349) | copy-start | bytes 2555908
  101.0 38.4 %collective-permute-start.10 = (bf16[64,6656]{1,0:T(8,128)(2,1)S(1)}, bf16[64,6656]{1,0:T(8,128)(2,1)}, u32[]{:S(2)}, u32[]{:S(2)}) collective-permute-start(bf16[64,6656]{1,0:T(8,128)(2,1)S(1)} %bitcast.172), channel_id=1, source_target_pairs={{0,1},{1,0},{2,3},{3,2},{4,5},{5,4},{6,7},{7,6},{8,9},{9,8},{10,11... | collective-permute-start | bytes 2555912 | tf_op jit(solution)/shard_map/ppermute | solution.py:36
  102.4 37.8 %collective-permute-start.11 = (bf16[64,6656]{1,0:T(8,128)(2,1)S(1)}, bf16[64,6656]{1,0:T(8,128)(2,1)}, u32[]{:S(2)}, u32[]{:S(2)}) collective-permute-start(bf16[64,6656]{1,0:T(8,128)(2,1)S(1)} %bitcast.173), channel_id=1, source_target_pairs={{0,2},{1,3},{2,0},{3,1},{4,6},{5,7},{6,4},{7,5},{8,10},{9,11},{10,... | collective-permute-start | bytes 2555912 | tf_op jit(solution)/shard_map/ppermute | solution.py:36
  108.0 31.4 %collective-permute-start.12 = (bf16[1,224,256]{2,1,0:T(8,128)(2,1)S(1)}, bf16[1,224,256]{2,1,0:T(8,128)(2,1)}, u32[]{:S(2)}, u32[]{:S(2)}) collective-permute-start(bf16[1,224,256]{2,1,0:T(8,128)(2,1)S(1)} %maximum_bitcast_fusion), channel_id=1, source_target_pairs={{0,4},{4,0},{8,12},{12,8},{16,20},{20,16},{24,28},{28,24},{1,5},{5... | collective-permute-start | bytes 344072 | tf_op jit(solution)/shard_map/ppermute | solution.py:36
  140.1 11.4 %collective-permute-start.13 = (bf16[64,6656]{1,0:T(8,128)(2,1)S(1)}, bf16[64,6656]{1,0:T(8,128)(2,1)S(1)}, u32[]{:S(2)}, u32[]{:S(2)}) collective-permute-start(bf16[64,6656]{1,0:T(8,128)(2,1)S(1)} %bitcast.174), channel_id=1, source_target_pairs={{1,2},{2,1},{5,6},{6,5},{9,10},{10,9},{13,14},{14,13},{17,18},{18,... | collective-permute-start | bytes 2555912 | tf_op jit(solution)/shard_map/ppermute | solution.py:67
  140.8 23.4 %collective-permute-start.14 = (bf16[64,6656]{1,0:T(8,128)(2,1)}, bf16[64,6656]{1,0:T(8,128)(2,1)S(1)}, u32[]{:S(2)}, u32[]{:S(2)}) collective-permute-start(bf16[64,6656]{1,0:T(8,128)(2,1)} %collective-permute-done.11.refs_2_), channel_id=1, source_target_pairs={{1,0},{2,3},{5,4},{6,7},{9,8},{10,11},{13,12},{14,15},{17,16},{18,... | collective-permute-start | bytes 2555912 | tf_op jit(solution)/shard_map/ppermute | solution.py:68
  142.3 9.2 %collective-permute-start.16 = (bf16[4,48,2048]{2,1,0:T(8,128)(2,1)S(1)}, bf16[4,48,2048]{2,1,0:T(8,128)(2,1)S(1)}, u32[]{:S(2)}, u32[]{:S(2)}) collective-permute-start(bf16[4,48,2048]{2,1,0:T(8,128)(2,1)S(1)} %get-tuple-element.242), channel_id=1, source_target_pairs={{0,4},{4,0},{8,12},{12,8},{16,20},{20,16},{24,28},{28,24},{1,5},{5... | collective-permute-start | bytes 2359304 | tf_op jit(solution)/shard_map/ppermute | solution.py:36
  142.4 9.1 %collective-permute-start.17 = (bf16[4,48,2048]{2,1,0:T(8,128)(2,1)S(1)}, bf16[4,48,2048]{2,1,0:T(8,128)(2,1)S(1)}, u32[]{:S(2)}, u32[]{:S(2)}) collective-permute-start(bf16[4,48,2048]{2,1,0:T(8,128)(2,1)S(1)} %get-tuple-element.241), channel_id=1, source_target_pairs={{0,4},{4,0},{8,12},{12,8},{16,20},{20,16},{24,28},{28,24},{1,5},{5... | collective-permute-start | bytes 2359304 | tf_op jit(solution)/shard_map/ppermute | solution.py:36
  143.9 7.7 %collective-permute-start.15 = (bf16[2,224,256]{2,1,0:T(8,128)(2,1)S(1)}, bf16[2,224,256]{2,1,0:T(8,128)(2,1)S(1)}, u32[]{:S(2)}, u32[]{:S(2)}) collective-permute-start(bf16[2,224,256]{2,1,0:T(8,128)(2,1)S(1)} %pad_maximum_fusion.12), channel_id=1, source_target_pairs={{0,8},{4,12},{8,0},{12,4},{16,24},{20,28},{24,16},{28,20},{1,9},{5... | collective-permute-start | bytes 688136 | tf_op jit(solution)/shard_map/ppermute | solution.py:36
  151.5 18.6 %copy-start.10 = (bf16[64,6656]{1,0:T(8,128)(2,1)}, bf16[64,6656]{1,0:T(8,128)(2,1)S(1)}, u32[]{:S(2)}) copy-start(bf16[64,6656]{1,0:T(8,128)(2,1)S(1)} %collective-permute-done.13.refs_3_) | copy-start | bytes 2555908
  164.3 37.8 %collective-permute-start.18 = (bf16[64,6656]{1,0:T(8,128)(2,1)}, bf16[64,6656]{1,0:T(8,128)(2,1)}, u32[]{:S(2)}, u32[]{:S(2)}) collective-permute-start(bf16[64,6656]{1,0:T(8,128)(2,1)} %bitcast.31.refs_0_), channel_id=1, source_target_pairs={{0,1},{1,0},{2,3},{3,2},{4,5},{5,4},{6,7},{7,6},{8,9},{9,8},{10,11... | collective-permute-start | bytes 2555912 | tf_op jit(solution)/shard_map/ppermute | solution.py:36
  164.3 40.0 %collective-permute-start.19 = (bf16[64,6656]{1,0:T(8,128)(2,1)}, bf16[64,6656]{1,0:T(8,128)(2,1)}, u32[]{:S(2)}, u32[]{:S(2)}) collective-permute-start(bf16[64,6656]{1,0:T(8,128)(2,1)} %bitcast.31.refs_0_), channel_id=1, source_target_pairs={{0,2},{1,3},{2,0},{3,1},{4,6},{5,7},{6,4},{7,5},{8,10},{9,11},{10,... | collective-permute-start | bytes 2555912 | tf_op jit(solution)/shard_map/ppermute | solution.py:36
  167.0 34.1 %collective-permute-start.20 = (bf16[4,224,256]{2,1,0:T(8,128)(2,1)}, bf16[4,224,256]{2,1,0:T(8,128)(2,1)}, u32[]{:S(2)}, u32[]{:S(2)}) collective-permute-start(bf16[4,224,256]{2,1,0:T(8,128)(2,1)} %pad_maximum_fusion.4), channel_id=1, source_target_pairs={{0,16},{4,20},{8,24},{12,28},{16,0},{20,4},{24,8},{28,12},{1,17},{... | collective-permute-start | bytes 1376264 | tf_op jit(solution)/shard_map/ppermute | solution.py:36
  170.9 30.2 %collective-permute-start.21 = (bf16[2,48,2048]{2,1,0:T(8,128)(2,1)}, bf16[2,48,2048]{2,1,0:T(8,128)(2,1)}, u32[]{:S(2)}, u32[]{:S(2)}) collective-permute-start(bf16[2,48,2048]{2,1,0:T(8,128)(2,1)} %pad_maximum_fusion.5), channel_id=1, source_target_pairs={{0,8},{4,12},{8,0},{12,4},{16,24},{20,28},{24,16},{28,20},{1,9},{5... | collective-permute-start | bytes 1179656 | tf_op jit(solution)/shard_map/ppermute | solution.py:36
  173.2 27.9 %collective-permute-start.22 = (bf16[2,48,2048]{2,1,0:T(8,128)(2,1)}, bf16[2,48,2048]{2,1,0:T(8,128)(2,1)}, u32[]{:S(2)}, u32[]{:S(2)}) collective-permute-start(bf16[2,48,2048]{2,1,0:T(8,128)(2,1)} %pad_maximum_fusion.6), channel_id=1, source_target_pairs={{0,16},{4,20},{8,24},{12,28},{16,0},{20,4},{24,8},{28,12},{1,17},{... | collective-permute-start | bytes 1179656 | tf_op jit(solution)/shard_map/ppermute | solution.py:36
  207.2 28.1 %collective-permute-start.23 = (bf16[64,6656]{1,0:T(8,128)(2,1)}, bf16[64,6656]{1,0:T(8,128)(2,1)}, u32[]{:S(2)}, u32[]{:S(2)}) collective-permute-start(bf16[64,6656]{1,0:T(8,128)(2,1)} %bitcast.31.refs_0_), channel_id=1, source_target_pairs={{1,2},{2,1},{5,6},{6,5},{9,10},{10,9},{13,14},{14,13},{17,18},{18,... | collective-permute-start | bytes 2555912 | tf_op jit(solution)/shard_map/ppermute | solution.py:67
  208.8 26.6 %collective-permute-start.24 = (bf16[64,6656]{1,0:T(8,128)(2,1)}, bf16[64,6656]{1,0:T(8,128)(2,1)}, u32[]{:S(2)}, u32[]{:S(2)}) collective-permute-start(bf16[64,6656]{1,0:T(8,128)(2,1)} %collective-permute-done.19.refs_2_), channel_id=1, source_target_pairs={{1,0},{2,3},{5,4},{6,7},{9,8},{10,11},{13,12},{14,15},{17,16},{18,... | collective-permute-start | bytes 2555912 | tf_op jit(solution)/shard_map/ppermute | solution.py:68
  219.1 5.7 %collective-permute-start.26 = (bf16[1,48,2048]{2,1,0:T(8,128)(2,1)S(1)}, bf16[1,48,2048]{2,1,0:T(8,128)(2,1)S(1)}, u32[]{:S(2)}, u32[]{:S(2)}) collective-permute-start(bf16[1,48,2048]{2,1,0:T(8,128)(2,1)S(1)} %get-tuple-element.269), channel_id=1, source_target_pairs={{0,16},{4,20},{8,24},{12,28},{16,0},{20,4},{24,8},{28,12},{1,17},{... | collective-permute-start | bytes 589832 | tf_op jit(solution)/shard_map/ppermute | solution.py:36
  222.1 5.7 %collective-permute-start.27 = (bf16[1,48,2048]{2,1,0:T(8,128)(2,1)S(1)}, bf16[1,48,2048]{2,1,0:T(8,128)(2,1)S(1)}, u32[]{:S(2)}, u32[]{:S(2)}) collective-permute-start(bf16[1,48,2048]{2,1,0:T(8,128)(2,1)S(1)} %get-tuple-element.267), channel_id=1, source_target_pairs={{0,8},{4,12},{8,0},{12,4},{16,24},{20,28},{24,16},{28,20},{1,9},{5... | collective-permute-start | bytes 589832 | tf_op jit(solution)/shard_map/ppermute | solution.py:36
  223.8 11.6 %collective-permute-start.28 = (bf16[4,32,2048]{2,1,0:T(8,128)(2,1)S(1)}, bf16[4,32,2048]{2,1,0:T(8,128)(2,1)S(1)}, u32[]{:S(2)}, u32[]{:S(2)}) collective-permute-start(bf16[4,32,2048]{2,1,0:T(8,128)(2,1)S(1)} %get-tuple-element.248), channel_id=1, source_target_pairs={{0,4},{4,0},{8,12},{12,8},{16,20},{20,16},{24,28},{28,24},{1,5},{5... | collective-permute-start | bytes 1572872 | tf_op jit(solution)/shard_map/ppermute | solution.py:36
  224.9 10.5 %collective-permute-start.29 = (bf16[4,32,2048]{2,1,0:T(8,128)(2,1)S(1)}, bf16[4,32,2048]{2,1,0:T(8,128)(2,1)S(1)}, u32[]{:S(2)}, u32[]{:S(2)}) collective-permute-start(bf16[4,32,2048]{2,1,0:T(8,128)(2,1)S(1)} %get-tuple-element.247), channel_id=1, source_target_pairs={{0,4},{4,0},{8,12},{12,8},{16,20},{20,16},{24,28},{28,24},{1,5},{5... | collective-permute-start | bytes 1572872 | tf_op jit(solution)/shard_map/ppermute | solution.py:36
  226.6 10.5 %copy-start.5 = (f32[4,32,4096]{2,1,0:T(8,128)S(1)}, f32[4,32,4096]{2,1,0:T(8,128)}, u32[]{:S(2)}) copy-start(f32[4,32,4096]{2,1,0:T(8,128)} %copy-done.4) | copy-start | bytes 6291460
  227.8 7.5 %collective-permute-start.25 = (bf16[512,256]{1,0:T(8,128)(2,1)S(1)}, bf16[512,256]{1,0:T(8,128)(2,1)S(1)}, u32[]{:S(2)}, u32[]{:S(2)}) collective-permute-start(bf16[512,256]{1,0:T(8,128)(2,1)S(1)} %fusion), channel_id=1, source_target_pairs={{0,16},{4,20},{8,24},{12,28},{16,0},{20,4},{24,8},{28,12},{1,17},{... | collective-permute-start | bytes 786440 | tf_op jit(solution)/shard_map/ppermute | solution.py:36
  235.5 31.2 %collective-permute-start.30 = (bf16[1024,256]{1,0:T(8,128)(2,1)S(1)}, bf16[1024,256]{1,0:T(8,128)(2,1)S(1)}, u32[]{:S(2)}, u32[]{:S(2)}) collective-permute-start(bf16[1024,256]{1,0:T(8,128)(2,1)S(1)} %pad_maximum_fusion.2), channel_id=1, source_target_pairs={{0,8},{4,12},{8,0},{12,4},{16,24},{20,28},{24,16},{28,20},{1,9},{5... | collective-permute-start | bytes 1572872 | tf_op jit(solution)/shard_map/ppermute | solution.py:36
  237.1 34.7 %slice-start = ((s8[5111808]{0:T(1024)(128)(4,1)}), s8[4194304]{0:T(1024)(128)(4,1)S(1)}, s32[]{:S(2)}) async-start(s8[5111808]{0:T(1024)(128)(4,1)} %bitcast.170), calls=%async_computation.1 | async-start | bytes 8388608
  238.1 28.5 %collective-permute-start.31 = (bf16[2,32,2048]{2,1,0:T(8,128)(2,1)}, bf16[2,32,2048]{2,1,0:T(8,128)(2,1)}, u32[]{:S(2)}, u32[]{:S(2)}) collective-permute-start(bf16[2,32,2048]{2,1,0:T(8,128)(2,1)} %pad_maximum_fusion.8), channel_id=1, source_target_pairs={{0,8},{4,12},{8,0},{12,4},{16,24},{20,28},{24,16},{28,20},{1,9},{5... | collective-permute-start | bytes 786440 | tf_op jit(solution)/shard_map/ppermute | solution.py:36
  239.3 32.5 %slice-start.1 = ((s8[5111808]{0:T(1024)(128)(4,1)}), s8[917504]{0:T(1024)(128)(4,1)S(1)}, s32[]{:S(2)}) async-start(s8[5111808]{0:T(1024)(128)(4,1)} %bitcast.170), calls=%async_computation.2 | async-start | bytes 1835008
  239.3 27.3 %collective-permute-start.32 = (bf16[2,32,2048]{2,1,0:T(8,128)(2,1)}, bf16[2,32,2048]{2,1,0:T(8,128)(2,1)}, u32[]{:S(2)}, u32[]{:S(2)}) collective-permute-start(bf16[2,32,2048]{2,1,0:T(8,128)(2,1)} %pad_maximum_fusion.9), channel_id=1, source_target_pairs={{0,16},{4,20},{8,24},{12,28},{16,0},{20,4},{24,8},{28,12},{1,17},{... | collective-permute-start | bytes 786440 | tf_op jit(solution)/shard_map/ppermute | solution.py:36
  267.6 8.7 %collective-permute-start.34 = (bf16[1,32,2048]{2,1,0:T(8,128)(2,1)S(1)}, bf16[1,32,2048]{2,1,0:T(8,128)(2,1)S(1)}, u32[]{:S(2)}, u32[]{:S(2)}) collective-permute-start(bf16[1,32,2048]{2,1,0:T(8,128)(2,1)S(1)} %fusion.16), channel_id=1, source_target_pairs={{0,8},{4,12},{8,0},{12,4},{16,24},{20,28},{24,16},{28,20},{1,9},{5... | collective-permute-start | bytes 393224 | tf_op jit(solution)/shard_map/ppermute | solution.py:36
  270.1 9.7 %collective-permute-start.33 = (bf16[1,32,2048]{2,1,0:T(8,128)(2,1)S(1)}, bf16[1,32,2048]{2,1,0:T(8,128)(2,1)S(1)}, u32[]{:S(2)}, u32[]{:S(2)}) collective-permute-start(bf16[1,32,2048]{2,1,0:T(8,128)(2,1)S(1)} %fusion.15), channel_id=1, source_target_pairs={{0,16},{4,20},{8,24},{12,28},{16,0},{20,4},{24,8},{28,12},{1,17},{... | collective-permute-start | bytes 393224 | tf_op jit(solution)/shard_map/ppermute | solution.py:36
  270.8 6.5 %collective-permute-start.36 = (bf16[4,32,2048]{2,1,0:T(8,128)(2,1)S(1)}, bf16[4,32,2048]{2,1,0:T(8,128)(2,1)S(1)}, u32[]{:S(2)}, u32[]{:S(2)}) collective-permute-start(bf16[4,32,2048]{2,1,0:T(8,128)(2,1)S(1)} %get-tuple-element.245), channel_id=1, source_target_pairs={{0,4},{4,0},{8,12},{12,8},{16,20},{20,16},{24,28},{28,24},{1,5},{5... | collective-permute-start | bytes 1572872 | tf_op jit(solution)/shard_map/ppermute | solution.py:36
  270.9 6.4 %collective-permute-start.35 = (bf16[4,32,2048]{2,1,0:T(8,128)(2,1)S(1)}, bf16[4,32,2048]{2,1,0:T(8,128)(2,1)S(1)}, u32[]{:S(2)}, u32[]{:S(2)}) collective-permute-start(bf16[4,32,2048]{2,1,0:T(8,128)(2,1)S(1)} %get-tuple-element.246), channel_id=1, source_target_pairs={{0,4},{4,0},{8,12},{12,8},{16,20},{20,16},{24,28},{28,24},{1,5},{5... | collective-permute-start | bytes 1572872 | tf_op jit(solution)/shard_map/ppermute | solution.py:36
  271.6 23.1 %collective-permute-start.41 = (bf16[2048,256]{1,0:T(8,128)(2,1)S(1)}, bf16[2048,256]{1,0:T(8,128)(2,1)S(1)}, u32[]{:S(2)}, u32[]{:S(2)}) collective-permute-start(bf16[2048,256]{1,0:T(8,128)(2,1)S(1)} %pad_maximum_fusion), channel_id=1, source_target_pairs={{0,4},{4,0},{8,12},{12,8},{16,20},{20,16},{24,28},{28,24},{1,5},{5... | collective-permute-start | bytes 3145736 | tf_op jit(solution)/shard_map/ppermute | solution.py:36
  277.7 8.4 %collective-permute-start.37 = (bf16[2,32,2048]{2,1,0:T(8,128)(2,1)S(1)}, bf16[2,32,2048]{2,1,0:T(8,128)(2,1)S(1)}, u32[]{:S(2)}, u32[]{:S(2)}) collective-permute-start(bf16[2,32,2048]{2,1,0:T(8,128)(2,1)S(1)} %pad_maximum_fusion.10), channel_id=1, source_target_pairs={{0,8},{4,12},{8,0},{12,4},{16,24},{20,28},{24,16},{28,20},{1,9},{5... | collective-permute-start | bytes 786440 | tf_op jit(solution)/shard_map/ppermute | solution.py:36
  278.2 8.1 %collective-permute-start.38 = (bf16[2,32,2048]{2,1,0:T(8,128)(2,1)S(1)}, bf16[2,32,2048]{2,1,0:T(8,128)(2,1)S(1)}, u32[]{:S(2)}, u32[]{:S(2)}) collective-permute-start(bf16[2,32,2048]{2,1,0:T(8,128)(2,1)S(1)} %pad_maximum_fusion.11), channel_id=1, source_target_pairs={{0,16},{4,20},{8,24},{12,28},{16,0},{20,4},{24,8},{28,12},{1,17},{... | collective-permute-start | bytes 786440 | tf_op jit(solution)/shard_map/ppermute | solution.py:36
  286.4 7.1 %collective-permute-start.40 = (bf16[1,32,2048]{2,1,0:T(8,128)(2,1)S(1)}, bf16[1,32,2048]{2,1,0:T(8,128)(2,1)S(1)}, u32[]{:S(2)}, u32[]{:S(2)}) collective-permute-start(bf16[1,32,2048]{2,1,0:T(8,128)(2,1)S(1)} %fusion.18), channel_id=1, source_target_pairs={{0,8},{4,12},{8,0},{12,4},{16,24},{20,28},{24,16},{28,20},{1,9},{5... | collective-permute-start | bytes 393224 | tf_op jit(solution)/shard_map/ppermute | solution.py:36
  288.0 5.5 %collective-permute-start.39 = (bf16[1,32,2048]{2,1,0:T(8,128)(2,1)S(1)}, bf16[1,32,2048]{2,1,0:T(8,128)(2,1)S(1)}, u32[]{:S(2)}, u32[]{:S(2)}) collective-permute-start(bf16[1,32,2048]{2,1,0:T(8,128)(2,1)S(1)} %fusion.17), channel_id=1, source_target_pairs={{0,16},{4,20},{8,24},{12,28},{16,0},{20,4},{24,8},{28,12},{1,17},{... | collective-permute-start | bytes 393224 | tf_op jit(solution)/shard_map/ppermute | solution.py:36
  (16 other events, 62.7 us)

commit v9 on v8

--- a/solution.py
+++ b/solution.py
@@ -137,36 +137,54 @@
     return outs if len(sources) > 1 else [sources[0], *outs]
 
 
-def factor_kernel(*refs, count, scale):
-    acts, tokens, out = refs[:count], refs[count : 2 * count], refs[-1]
-    out[...] = scale * sum(
-        jnp.dot(a[...], t[...], preferred_element_type=jnp.float32) for a, t in zip(acts, tokens)
-    )
-
-
-def factor_gradient(acts, tokens, scale, step, first, blocks, into=None):
-    rank, depth = acts[0].shape[0], tokens[0].shape[1]
+def factor_kernel(order, acts, *refs, pieces, scale):
+    tokens, out, lined = refs[: len(pieces)], refs[-2], refs[-1]
+    owners = acts.shape[0]
+
+    @pl.when(pl.program_id(0) == 0)
+    def _():
+        base = 0
+        for start, rows in pieces:
+            for i in range(owners):
+                lined[base : base + rows] = acts[order[i], start : start + rows, :]
+                base += rows
+
+    base, total = 0, None
+    for token in tokens:
+        size = token.shape[0]
+        part = contract_first(lined[base : base + size], token[...])
+        total = part if total is None else total + part
+        base += size
+    out[...] = scale * total
+
+
+def factor_gradient(order, acts, tokens, pieces, scale, step, first, blocks, into=None):
+    rank, depth = acts.shape[2], tokens[0].shape[1]
     in_specs = [
-        pl.BlockSpec(a.shape, lambda i: (0, 0), pipeline_mode=pl.Buffered(1)) for a in acts
+        pl.BlockSpec(acts.shape, lambda i, *_: (0, 0, 0), pipeline_mode=pl.Buffered(1))
     ]
-    in_specs += [pl.BlockSpec((t.shape[0], step), lambda i: (0, first + i)) for t in tokens]
-    operands = [*acts, *tokens]
+    in_specs += [pl.BlockSpec((t.shape[0], step), lambda i, *_: (0, first + i)) for t in tokens]
+    operands = [acts, *tokens]
     aliases = {}
     if into is not None:
-        aliases = {len(operands): 0}
+        aliases = {1 + len(operands): 0}
         operands.append(into)
         in_specs.append(pl.BlockSpec(memory_space=pl.ANY))
     return pl.pallas_call(
-        functools.partial(factor_kernel, count=len(acts), scale=scale),
-        grid=(blocks,),
-        in_specs=in_specs,
-        out_specs=pl.BlockSpec((rank, step), lambda i: (0, first + i)),
+        functools.partial(factor_kernel, pieces=pieces, scale=scale),
+        grid_spec=pltpu.PrefetchScalarGridSpec(
+            num_scalar_prefetch=1,
+            grid=(blocks,),
+            in_specs=in_specs,
+            out_specs=pl.BlockSpec((rank, step), lambda i, *_: (0, first + i)),
+            scratch_shapes=[pltpu.VMEM((sum(t.shape[0] for t in tokens), rank), jnp.bfloat16)],
+        ),
         out_shape=jax.ShapeDtypeStruct((rank, depth), jnp.float32),
         input_output_aliases=aliases,
         compiler_params=pltpu.CompilerParams(vmem_limit_bytes=vmem_bytes),
         cost_estimate=light,
         name="factor_gradient",
-    )(*operands)
+    )(order, *operands)
 
 
 def scatter_send(state, hop):
@@ -227,6 +245,7 @@
 
     held = [me_narrow ^ i if line else jnp.int32(i) for i in range(groups)]
     table = [(block * share + h) ^ me_wide for block in held for h in range(share)]
+    order = jnp.stack([block * share + h for block in held for h in range(share)]).astype(jnp.int32)
     table.append(((me_narrow == 0) | (me_narrow == groups - 1)).astype(jnp.int32))
     table = jnp.stack([entry.astype(jnp.int32) for entry in table])
 
@@ -312,15 +331,7 @@
         small["term"] = adapter_scale * contract_trailing_axis(low_own, adapter_down_matrix)
         made = adapter_matrix * contract_first(small.pop("columns"), low_all)
         small["grad_a"] = made.astype(jnp.bfloat16)
-        acts = rows[:, :owner_rows].reshape(groups, share, owner_rows, rank)
-        if line:
-            for bit in narrow_bits:
-                cut = acts.reshape(groups // (2 * bit), 2, bit, share, owner_rows, rank)
-                acts = jnp.where((me_narrow & bit) != 0, cut[:, ::-1], cut).reshape(acts.shape)
-        small["turned"] = [
-            acts[:, :, start : start + rows].reshape(owners * rows, rank).T
-            for start, rows in pieces
-        ]
+        small["acts"] = rows[:, :owner_rows]
 
     tokens, sums = {}, {}
     done_hops = {}
@@ -332,8 +343,9 @@
             sums[i] = scatter_send(sums[i], done_hops[i])
         done_hops[i] += 1
 
-    def step():
-        small_hop()
+    def step(small_hops=1):
+        for _ in range(small_hops):
+            small_hop()
         for i in sums:
             if done_hops[i] <= len(wide_bits):
                 sum_hop(i)
@@ -343,6 +355,9 @@
         tokens[i], kept, sent = weight_pass(table, sources, w_base, owners)
         sums[i] = (kept, sent)
         done_hops[i] = 0
+        if i + 2 == count:
+            sums.update(hold(sums)[0])
+            sum_hop(i)
 
     regroup()
     for i in range(count):
@@ -353,32 +368,37 @@
             complete(i)
             if i + 1 < count:
                 blocks[i + 1] = block_of(grad_out, i + 1)
-            step()
+            step(2 if i == 1 else 1)
         middle[i], onward[i], blocks, grad_out, small, sums = hold(
             middle[i], onward[i], blocks, grad_out, small, sums
         )
         if i + 1 < count:
             begin(i + 1)
-            step()
+            step(1 if i == 0 else 0)
             run_pass(i)
     step()
     run_pass(count - 1)
     small, sums = hold(small, sums)
-    while bits_left or "got" in small:
-        small_hop()
     columns_step = max(128 * c for c in range(1, 14) if depth % (128 * c) == 0)
     steps = depth // columns_step
     early = steps // 2 or 1
-    turned = small["turned"]
     tokens = [tokens[i] for i in range(count)]
-    sum_hop(count - 1)
-    grad_b = factor_gradient(turned, tokens, adapter_matrix, columns_step, 0, early)
-    sum_hop(count - 1)
-    sums[count - 1], grad_b = hold(sums[count - 1], grad_b)
+    last = count - 1
+
+    def factor(first, blocks, into=None):
+        return factor_gradient(
+            order, small["acts"], tokens, pieces, adapter_matrix, columns_step, first, blocks, into
+        )
+
+    sum_hop(last)
+    while bits_left or "got" in small:
+        small_hop()
+    grad_a = small["grad_a"].astype(jnp.float32)
+    grad_b = factor(0, early)
+    sum_hop(last)
+    sums[last], grad_a, grad_b = hold(sums[last], grad_a, grad_b)
     if steps > early:
-        grad_b = factor_gradient(
-            turned, tokens, adapter_matrix, columns_step, early, steps - early, grad_b
-        )
+        grad_b = factor(early, steps - early, grad_b)
     results = []
     for i, (start, rows) in enumerate(pieces):
         while done_hops[i] <= len(wide_bits):
@@ -386,7 +406,6 @@
         mine = small["term"][start : start + rows]
         summed = jnp.concatenate([part[0] for part in sums[i]], axis=1)
         results.append((summed + mine).astype(jnp.bfloat16))
-    grad_a = small["grad_a"].astype(jnp.float32)
     return (jnp.concatenate(results, axis=0), grad_a, grad_b)
 
 

time: 300 us -> 293 us (0.977)
  other arithmetic: 24.3 us -> 16.1 us
  local copies, waits for them, and re-layouts: 31 us -> 24.4 us
  waiting for transfers between devices: 94.5 us -> 101 us
    ppermute x36, waiting for transfers between devices: 81.7 us -> 98.7 us  [swap(): return lax.ppermute(value, axis, [(i, i ^ bit) for i in range(size)])]
    ppermute x3, waiting for transfers between devices: 12.7 us -> 2.24 us  [phase_b(): lax.ppermute(far, axis, [(1, 0), (2, 3)])]
    another operation x12, other arithmetic: 7.77 us -> 1.51 us  [scatter_send(): away = jnp.stack([part[p | bit].astype(jnp.bfloat16) for p in stay[-1]])]
    reshape x3 -> x0, local copies, waits for them, and re-layouts: 4.44 us -> none  [share_made(): acts[:, :, start:start + rows].reshape(owners * rows, rank)]
    unnamed x50 -> x52, local copies, waits for them, and re-layouts: 12.1 us -> 10.1 us
  transfers between devices with their start and end apart: 43 -> 43, of which waited for: 17 -> 17; matrix products, arithmetic and copies ran while one was open for 16% -> 14% of each run, Pallas kernels for 29% -> 31%
where the time goes in v9:
time: 293 us; the launch traced here: 291 us
  waiting for transfers between devices  101 us (34%)
  Pallas kernels  89.2 us (30%)
  starting transfers between devices  49.5 us (17%)
  local copies, waits for them, and re-layouts  24.4 us (8%)
  other arithmetic  16.1 us (5%)
  matrix products  9.53 us (3%)
    ppermute x36, waiting for transfers between devices, swap(): return lax.ppermute(value, axis, [(i, i ^ bit) for i in range(size)])  98.7 us
    pallas_call x3, Pallas kernels, weight_pass(): pl.pallas_call(functools.partial(pass_kernel, sources=len(sources), owner...  80.2 us
    ppermute x36, starting transfers between devices, swap(): return lax.ppermute(value, axis, [(i, i ^ bit) for i in range(size)])  38.2 us
    unnamed x52, local copies, waits for them, and re-layouts  10.1 us
    pallas_call x2, Pallas kernels, factor_gradient(): pl.pallas_call(functools.partial(factor_kernel, pieces=pieces, scale=scal...  9.02 us
    slice x3, local copies, waits for them, and re-layouts, block_of(): return own[:, start:start + rows].reshape(share * rows, depth)  5.91 us
  transfers between devices with their start and end apart: 43, of which 17 were waited for; matrix products, arithmetic and copies ran while one was open for 14% of the time, Pallas kernels for 31%

profile of v9, /device:TPU:0, one launch (start us, length us, event | category | flops | bytes accessed | tf_op | source)
XLA Modules:
  0.0 290.9 jit_solution(16543084133276847449)
XLA Ops:
  0.6 2.6 slice.336
  3.2 3.0 %collective-permute-start = (bf16[96,6656]{1,0:T(8,128)(2,1)}, bf16[96,6656]{1,0:T(8,128)(2,1)}, u32[]{:S(2)}, u32[]{:S(2)}) collective-permute-start(bf16[96,6656]{1,0:T(8,128)(2,1)} %bitcast.1.refs_0_), channel_id=1, source_target_pairs={{0,1},{1,0},{2,3},{3,2},{4,5},{5,4},{6,7},{7,6},{8,9},{9,8},{10,11... | collective-permute-start | bytes 3833864 | tf_op jit(solution)/shard_map/ppermute | solution.py:36
  6.3 2.6 collective-permute-start.1
  8.9 3.7 %fusion.25 = f32[224,256]{1,0:T(8,128)} fusion(bf16[224,6656]{1,0:T(8,128)(2,1)} %param.6, bf16[256,6656]{1,0:T(8,128)(2,1)S(1)} %copy-done), kind=kOutput, calls=%fused_computation.120 | convolution fusion | flops 763363328 | bytes 6619136 | tf_op jit(solution)/shard_map/dot_general | solution.py:18
  13.4 1.5 collective-permute-start.2
  15.0 3.3 %collective-permute-done.2 = f32[112,256]{1,0:T(8,128)S(1)} collective-permute-done((f32[112,256]{1,0:T(8,128)S(1)}, f32[112,256]{1,0:T(8,128)S(1)}, u32[]{:S(2)}, u32[]{:S(2)}) %collective-permute-start.2) | collective-permute-done | bytes 114720 | tf_op jit(solution)/shard_map/ppermute | solution.py:36
  19.2 1.6 collective-permute-start.3
  20.7 2.7 collective-permute-done.3
  24.8 37.1 %collective-permute-done.refs_1_ = bf16[96,6656]{1,0:T(8,128)(2,1)} collective-permute-done((bf16[96,6656]{1,0:T(8,128)(2,1)}, bf16[96,6656]{1,0:T(8,128)(2,1)}, u32[]{:S(2)}, u32[]{:S(2)}) %collective-permute-start) | collective-permute-done | bytes 1277984 | tf_op jit(solution)/shard_map/ppermute | solution.py:36
  61.9 2.6 collective-permute-done.1.refs_2_
  66.5 1.5 copy.63
  68.0 1.5 fusion.24
  74.8 4.2 %all-to-all-start = ((bf16[8,112,512]{2,1,0:T(8,128)(2,1)}), bf16[8,112,512]{2,1,0:T(8,128)(2,1)}, u32[]{:S(2)}, u32[]{:S(2)}) async-start(bf16[8,112,512]{2,1,0:T(8,128)(2,1)} %bitcast_dynamic-update-slice_fusion), calls=%async_computation | async-start | bytes 1835008 | tf_op jit(solution)/shard_map/all_to_all | solution.py:323
  79.1 2.3 convolution_convert_fusion
  81.4 2.8 collective-permute-start.7
  87.9 11.6 %collective-permute-done.7 = bf16[140,256]{1,0:T(8,128)(2,1)S(1)} collective-permute-done((bf16[140,256]{1,0:T(8,128)(2,1)S(1)}, bf16[140,256]{1,0:T(8,128)(2,1)S(1)}, u32[]{:S(2)}, u32[]{:S(2)}) %collective-permute-start.7) | collective-permute-done | bytes 71712 | tf_op jit(solution)/shard_map/ppermute | solution.py:36
  101.0 1.4 collective-permute-start.10
  108.1 31.2 %weight_pass.3 = (bf16[384,6656]{1,0:T(8,128)(2,1)}, f32[4,48,4096]{2,1,0:T(8,128)S(1)}, bf16[4,48,4096]{2,1,0:T(8,128)(2,1)S(1)}) custom-call(s32[9]{0:T(128)S(1)} %stack.142.table, bf16[96,6656]{1,0:T(8,128)(2,1)} %bitcast.1.refs_0_, bf16[96,6656]{1,0:T(8,128)(2,1)} %collective-permute-done.refs_1_, bf16[96,6656]{1,0:T(8,128)(2,1)} %collective-permute-done.1.refs_2_, ...), custom_call_target="tpu_custom_call" | custom-call | bytes 65536 | tf_op jit(solution)/shard_map/weight_pass/pallas_call | solution.py:124
  143.1 1.6 collective-permute-start.15
  145.4 5.1 %collective-permute-done.15 = bf16[2,224,256]{2,1,0:T(8,128)(2,1)S(1)} collective-permute-done((bf16[2,224,256]{2,1,0:T(8,128)(2,1)S(1)}, bf16[2,224,256]{2,1,0:T(8,128)(2,1)S(1)}, u32[]{:S(2)}, u32[]{:S(2)}) %collective-permute-start.15) | collective-permute-done | bytes 229408 | tf_op jit(solution)/shard_map/ppermute | solution.py:36
  150.6 1.6 collective-permute-start.16
  152.2 2.1 slice.348
  154.3 7.7 %collective-permute-done.16 = bf16[4,224,256]{2,1,0:T(8,128)(2,1)S(1)} collective-permute-done((bf16[4,224,256]{2,1,0:T(8,128)(2,1)S(1)}, bf16[4,224,256]{2,1,0:T(8,128)(2,1)S(1)}, u32[]{:S(2)}, u32[]{:S(2)}) %collective-permute-start.16) | collective-permute-done | bytes 458784 | tf_op jit(solution)/shard_map/ppermute | solution.py:36
  162.0 2.2 collective-permute-done.14.refs_4_
  164.3 1.5 add_convert_fusion.1
  165.9 1.6 collective-permute-start.21
  167.5 1.6 collective-permute-start.22
  171.0 23.9 %weight_pass.4 = (bf16[256,6656]{1,0:T(8,128)(2,1)S(1)}, f32[4,32,4096]{2,1,0:T(8,128)S(1)}, bf16[4,32,4096]{2,1,0:T(8,128)(2,1)S(1)}) custom-call(s32[9]{0:T(128)S(1)} %stack.142.table, bf16[64,6656]{1,0:T(8,128)(2,1)S(1)} %bitcast.173, bf16[64,6656]{1,0:T(8,128)(2,1)} %collective-permute-done.10.refs_1_, bf16[64,6656]{1,0:T(8,128)(2,1)} %collective-permute-done.11.refs_2_, ...), custom_call_target="tpu_custom_call" | custom-call | bytes 65536 | tf_op jit(solution)/shard_map/weight_pass/pallas_call | solution.py:124
  198.1 8.3 %collective-permute-done.19.refs_1_ = bf16[64,6656]{1,0:T(8,128)(2,1)} collective-permute-done((bf16[64,6656]{1,0:T(8,128)(2,1)}, bf16[64,6656]{1,0:T(8,128)(2,1)}, u32[]{:S(2)}, u32[]{:S(2)}) %collective-permute-start.19) | collective-permute-done | bytes 852000 | tf_op jit(solution)/shard_map/ppermute | solution.py:36
  206.3 2.2 collective-permute-done.20.refs_2_
  208.6 1.6 collective-permute-start.25
  210.1 1.5 collective-permute-start.26
  214.7 1.9 reshape.129
  216.6 1.9 fusion
  220.3 1.5 collective-permute-start.28
  222.5 1.6 add_convert_fusion.9
  224.2 4.8 %collective-permute-done.28 = bf16[1,48,2048]{2,1,0:T(8,128)(2,1)S(1)} collective-permute-done((bf16[1,48,2048]{2,1,0:T(8,128)(2,1)S(1)}, bf16[1,48,2048]{2,1,0:T(8,128)(2,1)S(1)}, u32[]{:S(2)}, u32[]{:S(2)}) %collective-permute-start.28) | collective-permute-done | bytes 196640 | tf_op jit(solution)/shard_map/ppermute | solution.py:36
  229.5 1.6 convolution_multiply_fusion
  231.1 6.3 %collective-permute-done.30 = bf16[2,32,2048]{2,1,0:T(8,128)(2,1)S(1)} collective-permute-done((bf16[2,32,2048]{2,1,0:T(8,128)(2,1)S(1)}, bf16[2,32,2048]{2,1,0:T(8,128)(2,1)S(1)}, u32[]{:S(2)}, u32[]{:S(2)}) %collective-permute-start.30) | collective-permute-done | bytes 262176 | tf_op jit(solution)/shard_map/ppermute | solution.py:36
  237.5 1.4 collective-permute-start.32
  240.2 25.0 %weight_pass.5 = (bf16[256,6656]{1,0:T(8,128)(2,1)S(1)}, f32[4,32,4096]{2,1,0:T(8,128)S(1)}, bf16[4,32,4096]{2,1,0:T(8,128)(2,1)S(1)}) custom-call(s32[9]{0:T(128)S(1)} %stack.142.table, bf16[64,6656]{1,0:T(8,128)(2,1)} %bitcast.31.refs_0_, bf16[64,6656]{1,0:T(8,128)(2,1)} %collective-permute-done.19.refs_1_, ...), custom_call_target="tpu_custom_call" | custom-call | bytes 65536 | tf_op jit(solution)/shard_map/weight_pass/pallas_call | solution.py:124
  267.1 4.5 %factor_gradient.2.refs_3_ = f32[256,6656]{1,0:T(8,128)} custom-call(s32[8]{0:T(128)S(1)} %stack.161.order, bf16[8,112,256]{2,1,0:T(8,128)(2,1)S(1)} %copy-done.2, bf16[384,6656]{1,0:T(8,128)(2,1)S(1)} %bitcast.169, bf16[256,6656]{1,0:T(8,128)(2,1)S(1)} %get-tuple-element.205.refs_1_, bf16[256,6656]{1,0:T(8,128)(2,1)S(1)} %get-tuple-element.206.refs_2_), custom_call_target="tpu_custom_call" | custom-call | bytes 65536 | tf_op jit(solution)/shard_map/factor_gradient/pallas_call | solution.py:173
  272.0 1.5 collective-permute-start.37
  273.5 1.7 collective-permute-start.38
  275.6 2.3 maximum_convert_fusion
  277.9 2.4 collective-permute-done.37
  282.3 1.8 collective-permute-start.40
  284.1 4.5 %factor_gradient.3 = f32[256,6656]{1,0:T(8,128)} custom-call(s32[8]{0:T(128)S(1)} %stack.161.order, bf16[8,112,256]{2,1,0:T(8,128)(2,1)S(1)} %copy-done.2, bf16[384,6656]{1,0:T(8,128)(2,1)S(1)} %bitcast.169, bf16[256,6656]{1,0:T(8,128)(2,1)S(1)} %get-tuple-element.205.refs_1_, ...), custom_call_target="tpu_custom_call", output_to_operand_aliasing={{}: (5, {})} | custom-call | bytes 65536 | tf_op jit(solution)/shard_map/factor_gradient/pallas_call | solution.py:173
  (163 shorter events, 45.2 us)
Async XLA Ops:
  0.6 8.2 %copy-start = (bf16[256,6656]{1,0:T(8,128)(2,1)S(1)}, bf16[256,6656]{1,0:T(8,128)(2,1)}, u32[]{:S(2)}) copy-start(bf16[256,6656]{1,0:T(8,128)(2,1)} %param.9) | copy-start | bytes 10223620
  3.2 58.7 %collective-permute-start = (bf16[96,6656]{1,0:T(8,128)(2,1)}, bf16[96,6656]{1,0:T(8,128)(2,1)}, u32[]{:S(2)}, u32[]{:S(2)}) collective-permute-start(bf16[96,6656]{1,0:T(8,128)(2,1)} %bitcast.1.refs_0_), channel_id=1, source_target_pairs={{0,1},{1,0},{2,3},{3,2},{4,5},{5,4},{6,7},{7,6},{8,9},{9,8},{10,11... | collective-permute-start | bytes 3833864 | tf_op jit(solution)/shard_map/ppermute | solution.py:36
  6.3 58.2 %collective-permute-start.1 = (bf16[96,6656]{1,0:T(8,128)(2,1)}, bf16[96,6656]{1,0:T(8,128)(2,1)}, u32[]{:S(2)}, u32[]{:S(2)}) collective-permute-start(bf16[96,6656]{1,0:T(8,128)(2,1)} %bitcast.1.refs_0_), channel_id=1, source_target_pairs={{0,2},{1,3},{2,0},{3,1},{4,6},{5,7},{6,4},{7,5},{8,10},{9,11},{10,... | collective-permute-start | bytes 3833864 | tf_op jit(solution)/shard_map/ppermute | solution.py:36
  13.4 4.8 %collective-permute-start.2 = (f32[112,256]{1,0:T(8,128)S(1)}, f32[112,256]{1,0:T(8,128)S(1)}, u32[]{:S(2)}, u32[]{:S(2)}) collective-permute-start(f32[112,256]{1,0:T(8,128)S(1)} %dynamic-slice_bitcast_fusion), channel_id=1, source_target_pairs={{0,16},{4,20},{8,24},{12,28},{16,0},{20,4},{24,8},{28,12},{1,17},{... | collective-permute-start | bytes 344072 | tf_op jit(solution)/shard_map/ppermute | solution.py:36
  19.2 4.2 %collective-permute-start.3 = (f32[56,256]{1,0:T(8,128)S(1)}, f32[56,256]{1,0:T(8,128)S(1)}, u32[]{:S(2)}, u32[]{:S(2)}) collective-permute-start(f32[56,256]{1,0:T(8,128)S(1)} %dynamic-slice_bitcast_fusion.1), channel_id=1, source_target_pairs={{0,8},{4,12},{8,0},{12,4},{16,24},{20,28},{24,16},{28,20},{1,9},{5... | collective-permute-start | bytes 172040 | tf_op jit(solution)/shard_map/ppermute | solution.py:36
  23.5 1.3 collective-permute-start.4
  64.5 36.5 %collective-permute-start.5 = (bf16[96,6656]{1,0:T(8,128)(2,1)}, bf16[96,6656]{1,0:T(8,128)(2,1)S(1)}, u32[]{:S(2)}, u32[]{:S(2)}) collective-permute-start(bf16[96,6656]{1,0:T(8,128)(2,1)} %bitcast.1.refs_0_), channel_id=1, source_target_pairs={{1,2},{2,1},{5,6},{6,5},{9,10},{10,9},{13,14},{14,13},{17,18},{18,... | collective-permute-start | bytes 3833864 | tf_op jit(solution)/shard_map/ppermute | solution.py:67
  65.2 35.8 %collective-permute-start.6 = (bf16[96,6656]{1,0:T(8,128)(2,1)}, bf16[96,6656]{1,0:T(8,128)(2,1)S(1)}, u32[]{:S(2)}, u32[]{:S(2)}) collective-permute-start(bf16[96,6656]{1,0:T(8,128)(2,1)} %collective-permute-done.1.refs_2_), channel_id=1, source_target_pairs={{1,0},{2,3},{5,4},{6,7},{9,8},{10,11},{13,12},{14,15},{17,16},{18,... | collective-permute-start | bytes 3833864 | tf_op jit(solution)/shard_map/ppermute | solution.py:68
  74.8 26.1 %all-to-all-start = ((bf16[8,112,512]{2,1,0:T(8,128)(2,1)}), bf16[8,112,512]{2,1,0:T(8,128)(2,1)}, u32[]{:S(2)}, u32[]{:S(2)}) async-start(bf16[8,112,512]{2,1,0:T(8,128)(2,1)} %bitcast_dynamic-update-slice_fusion), calls=%async_computation | async-start | bytes 1835008 | tf_op jit(solution)/shard_map/all_to_all | solution.py:323
  81.4 18.1 %collective-permute-start.7 = (bf16[140,256]{1,0:T(8,128)(2,1)S(1)}, bf16[140,256]{1,0:T(8,128)(2,1)S(1)}, u32[]{:S(2)}, u32[]{:S(2)}) collective-permute-start(bf16[140,256]{1,0:T(8,128)(2,1)S(1)} %pad_maximum_fusion.13), channel_id=1, source_target_pairs={{0,1},{1,0},{2,3},{3,2},{4,5},{5,4},{6,7},{7,6},{8,9},{9,8},{10,11... | collective-permute-start | bytes 215048 | tf_op jit(solution)/shard_map/ppermute | solution.py:36
  84.2 16.7 %collective-permute-start.8 = (bf16[140,256]{1,0:T(8,128)(2,1)S(1)}, bf16[140,256]{1,0:T(8,128)(2,1)}, u32[]{:S(2)}, u32[]{:S(2)}) collective-permute-start(bf16[140,256]{1,0:T(8,128)(2,1)S(1)} %pad_maximum_fusion.13), channel_id=1, source_target_pairs={{0,2},{1,3},{2,0},{3,1},{4,6},{5,7},{6,4},{7,5},{8,10},{9,11},{10,... | collective-permute-start | bytes 215048 | tf_op jit(solution)/shard_map/ppermute | solution.py:36
  85.3 15.6 %collective-permute-start.9 = (bf16[140,256]{1,0:T(8,128)(2,1)S(1)}, bf16[140,256]{1,0:T(8,128)(2,1)}, u32[]{:S(2)}, u32[]{:S(2)}) collective-permute-start(bf16[140,256]{1,0:T(8,128)(2,1)S(1)} %pad_maximum_fusion.13), channel_id=1, source_target_pairs={{0,3},{1,2},{2,1},{3,0},{4,7},{5,6},{6,5},{7,4},{8,11},{9,10},{10,... | collective-permute-start | bytes 215048 | tf_op jit(solution)/shard_map/ppermute | solution.py:36
  87.9 52.2 %copy-start.3 = (bf16[2,32,6656]{2,1,0:T(8,128)(2,1)}, bf16[2,32,6656]{2,1,0:T(8,128)(2,1)S(1)}, u32[]{:S(2)}) copy-start(bf16[2,32,6656]{2,1,0:T(8,128)(2,1)S(1)} %slice.337) | copy-start | bytes 2555908
  101.0 38.4 %collective-permute-start.10 = (bf16[64,6656]{1,0:T(8,128)(2,1)S(1)}, bf16[64,6656]{1,0:T(8,128)(2,1)}, u32[]{:S(2)}, u32[]{:S(2)}) collective-permute-start(bf16[64,6656]{1,0:T(8,128)(2,1)S(1)} %bitcast.170), channel_id=1, source_target_pairs={{0,1},{1,0},{2,3},{3,2},{4,5},{5,4},{6,7},{7,6},{8,9},{9,8},{10,11... | collective-permute-start | bytes 2555912 | tf_op jit(solution)/shard_map/ppermute | solution.py:36
  102.4 37.8 %collective-permute-start.11 = (bf16[64,6656]{1,0:T(8,128)(2,1)S(1)}, bf16[64,6656]{1,0:T(8,128)(2,1)}, u32[]{:S(2)}, u32[]{:S(2)}) collective-permute-start(bf16[64,6656]{1,0:T(8,128)(2,1)S(1)} %bitcast.171), channel_id=1, source_target_pairs={{0,2},{1,3},{2,0},{3,1},{4,6},{5,7},{6,4},{7,5},{8,10},{9,11},{10,... | collective-permute-start | bytes 2555912 | tf_op jit(solution)/shard_map/ppermute | solution.py:36
  108.0 31.4 %collective-permute-start.12 = (bf16[1,224,256]{2,1,0:T(8,128)(2,1)S(1)}, bf16[1,224,256]{2,1,0:T(8,128)(2,1)}, u32[]{:S(2)}, u32[]{:S(2)}) collective-permute-start(bf16[1,224,256]{2,1,0:T(8,128)(2,1)S(1)} %maximum_bitcast_fusion), channel_id=1, source_target_pairs={{0,4},{4,0},{8,12},{12,8},{16,20},{20,16},{24,28},{28,24},{1,5},{5... | collective-permute-start | bytes 344072 | tf_op jit(solution)/shard_map/ppermute | solution.py:36
  140.1 21.9 %collective-permute-start.13 = (bf16[64,6656]{1,0:T(8,128)(2,1)S(1)}, bf16[64,6656]{1,0:T(8,128)(2,1)S(1)}, u32[]{:S(2)}, u32[]{:S(2)}) collective-permute-start(bf16[64,6656]{1,0:T(8,128)(2,1)S(1)} %bitcast.172), channel_id=1, source_target_pairs={{1,2},{2,1},{5,6},{6,5},{9,10},{10,9},{13,14},{14,13},{17,18},{18,... | collective-permute-start | bytes 2555912 | tf_op jit(solution)/shard_map/ppermute | solution.py:67
  140.8 23.4 %collective-permute-start.14 = (bf16[64,6656]{1,0:T(8,128)(2,1)}, bf16[64,6656]{1,0:T(8,128)(2,1)S(1)}, u32[]{:S(2)}, u32[]{:S(2)}) collective-permute-start(bf16[64,6656]{1,0:T(8,128)(2,1)} %collective-permute-done.11.refs_2_), channel_id=1, source_target_pairs={{1,0},{2,3},{5,4},{6,7},{9,8},{10,11},{13,12},{14,15},{17,16},{18,... | collective-permute-start | bytes 2555912 | tf_op jit(solution)/shard_map/ppermute | solution.py:68
  143.1 7.4 %collective-permute-start.15 = (bf16[2,224,256]{2,1,0:T(8,128)(2,1)S(1)}, bf16[2,224,256]{2,1,0:T(8,128)(2,1)S(1)}, u32[]{:S(2)}, u32[]{:S(2)}) collective-permute-start(bf16[2,224,256]{2,1,0:T(8,128)(2,1)S(1)} %pad_maximum_fusion.12), channel_id=1, source_target_pairs={{0,8},{4,12},{8,0},{12,4},{16,24},{20,28},{24,16},{28,20},{1,9},{5... | collective-permute-start | bytes 688136 | tf_op jit(solution)/shard_map/ppermute | solution.py:36
  144.8 17.2 %collective-permute-start.17 = (bf16[4,48,2048]{2,1,0:T(8,128)(2,1)S(1)}, bf16[4,48,2048]{2,1,0:T(8,128)(2,1)S(1)}, u32[]{:S(2)}, u32[]{:S(2)}) collective-permute-start(bf16[4,48,2048]{2,1,0:T(8,128)(2,1)S(1)} %get-tuple-element.256), channel_id=1, source_target_pairs={{0,4},{4,0},{8,12},{12,8},{16,20},{20,16},{24,28},{28,24},{1,5},{5... | collective-permute-start | bytes 2359304 | tf_op jit(solution)/shard_map/ppermute | solution.py:36
  144.9 17.1 %collective-permute-start.18 = (bf16[4,48,2048]{2,1,0:T(8,128)(2,1)S(1)}, bf16[4,48,2048]{2,1,0:T(8,128)(2,1)S(1)}, u32[]{:S(2)}, u32[]{:S(2)}) collective-permute-start(bf16[4,48,2048]{2,1,0:T(8,128)(2,1)S(1)} %get-tuple-element.255), channel_id=1, source_target_pairs={{0,4},{4,0},{8,12},{12,8},{16,20},{20,16},{24,28},{28,24},{1,5},{5... | collective-permute-start | bytes 2359304 | tf_op jit(solution)/shard_map/ppermute | solution.py:36
  150.6 15.2 %copy-start.8 = (bf16[4,224,256]{2,1,0:T(8,128)(2,1)}, bf16[4,224,256]{2,1,0:T(8,128)(2,1)S(1)}, u32[]{:S(2)}) copy-start(bf16[4,224,256]{2,1,0:T(8,128)(2,1)S(1)} %pad_maximum_fusion.4) | copy-start | bytes 1376260
  150.6 11.4 %collective-permute-start.16 = (bf16[4,224,256]{2,1,0:T(8,128)(2,1)S(1)}, bf16[4,224,256]{2,1,0:T(8,128)(2,1)S(1)}, u32[]{:S(2)}, u32[]{:S(2)}) collective-permute-start(bf16[4,224,256]{2,1,0:T(8,128)(2,1)S(1)} %pad_maximum_fusion.4), channel_id=1, source_target_pairs={{0,16},{4,20},{8,24},{12,28},{16,0},{20,4},{24,8},{28,12},{1,17},{... | collective-permute-start | bytes 1376264 | tf_op jit(solution)/shard_map/ppermute | solution.py:36
  165.9 30.4 %collective-permute-start.21 = (bf16[2,48,2048]{2,1,0:T(8,128)(2,1)S(1)}, bf16[2,48,2048]{2,1,0:T(8,128)(2,1)S(1)}, u32[]{:S(2)}, u32[]{:S(2)}) collective-permute-start(bf16[2,48,2048]{2,1,0:T(8,128)(2,1)S(1)} %pad_maximum_fusion.5), channel_id=1, source_target_pairs={{0,8},{4,12},{8,0},{12,4},{16,24},{20,28},{24,16},{28,20},{1,9},{5... | collective-permute-start | bytes 1179656 | tf_op jit(solution)/shard_map/ppermute | solution.py:36
  167.5 28.7 %collective-permute-start.22 = (bf16[2,48,2048]{2,1,0:T(8,128)(2,1)S(1)}, bf16[2,48,2048]{2,1,0:T(8,128)(2,1)S(1)}, u32[]{:S(2)}, u32[]{:S(2)}) collective-permute-start(bf16[2,48,2048]{2,1,0:T(8,128)(2,1)S(1)} %pad_maximum_fusion.6), channel_id=1, source_target_pairs={{0,16},{4,20},{8,24},{12,28},{16,0},{20,4},{24,8},{28,12},{1,17},{... | collective-permute-start | bytes 1179656 | tf_op jit(solution)/shard_map/ppermute | solution.py:36
  169.0 37.3 %collective-permute-start.19 = (bf16[64,6656]{1,0:T(8,128)(2,1)}, bf16[64,6656]{1,0:T(8,128)(2,1)}, u32[]{:S(2)}, u32[]{:S(2)}) collective-permute-start(bf16[64,6656]{1,0:T(8,128)(2,1)} %bitcast.31.refs_0_), channel_id=1, source_target_pairs={{0,1},{1,0},{2,3},{3,2},{4,5},{5,4},{6,7},{7,6},{8,9},{9,8},{10,11... | collective-permute-start | bytes 2555912 | tf_op jit(solution)/shard_map/ppermute | solution.py:36
  170.3 38.2 %collective-permute-start.20 = (bf16[64,6656]{1,0:T(8,128)(2,1)}, bf16[64,6656]{1,0:T(8,128)(2,1)}, u32[]{:S(2)}, u32[]{:S(2)}) collective-permute-start(bf16[64,6656]{1,0:T(8,128)(2,1)} %bitcast.31.refs_0_), channel_id=1, source_target_pairs={{0,2},{1,3},{2,0},{3,1},{4,6},{5,7},{6,4},{7,5},{8,10},{9,11},{10,... | collective-permute-start | bytes 2555912 | tf_op jit(solution)/shard_map/ppermute | solution.py:36
  197.5 11.1 %collective-permute-start.23 = (bf16[4,32,2048]{2,1,0:T(8,128)(2,1)}, bf16[4,32,2048]{2,1,0:T(8,128)(2,1)}, u32[]{:S(2)}, u32[]{:S(2)}) collective-permute-start(bf16[4,32,2048]{2,1,0:T(8,128)(2,1)} %get-tuple-element.262), channel_id=1, source_target_pairs={{0,4},{4,0},{8,12},{12,8},{16,20},{20,16},{24,28},{28,24},{1,5},{5... | collective-permute-start | bytes 1572872 | tf_op jit(solution)/shard_map/ppermute | solution.py:36
  197.5 11.1 %collective-permute-start.24 = (bf16[4,32,2048]{2,1,0:T(8,128)(2,1)}, bf16[4,32,2048]{2,1,0:T(8,128)(2,1)}, u32[]{:S(2)}, u32[]{:S(2)}) collective-permute-start(bf16[4,32,2048]{2,1,0:T(8,128)(2,1)} %get-tuple-element.261), channel_id=1, source_target_pairs={{0,4},{4,0},{8,12},{12,8},{16,20},{20,16},{24,28},{28,24},{1,5},{5... | collective-permute-start | bytes 1572872 | tf_op jit(solution)/shard_map/ppermute | solution.py:36
  208.6 28.8 %collective-permute-start.25 = (bf16[64,6656]{1,0:T(8,128)(2,1)}, bf16[64,6656]{1,0:T(8,128)(2,1)}, u32[]{:S(2)}, u32[]{:S(2)}) collective-permute-start(bf16[64,6656]{1,0:T(8,128)(2,1)} %bitcast.31.refs_0_), channel_id=1, source_target_pairs={{1,2},{2,1},{5,6},{6,5},{9,10},{10,9},{13,14},{14,13},{17,18},{18,... | collective-permute-start | bytes 2555912 | tf_op jit(solution)/shard_map/ppermute | solution.py:67
  210.1 27.3 %collective-permute-start.26 = (bf16[64,6656]{1,0:T(8,128)(2,1)}, bf16[64,6656]{1,0:T(8,128)(2,1)}, u32[]{:S(2)}, u32[]{:S(2)}) collective-permute-start(bf16[64,6656]{1,0:T(8,128)(2,1)} %collective-permute-done.20.refs_2_), channel_id=1, source_target_pairs={{1,0},{2,3},{5,4},{6,7},{9,8},{10,11},{13,12},{14,15},{17,16},{18,... | collective-permute-start | bytes 2555912 | tf_op jit(solution)/shard_map/ppermute | solution.py:68
  218.6 12.5 %collective-permute-start.27 = (bf16[512,256]{1,0:T(8,128)(2,1)S(1)}, bf16[512,256]{1,0:T(8,128)(2,1)S(1)}, u32[]{:S(2)}, u32[]{:S(2)}) collective-permute-start(bf16[512,256]{1,0:T(8,128)(2,1)S(1)} %fusion), channel_id=1, source_target_pairs={{0,16},{4,20},{8,24},{12,28},{16,0},{20,4},{24,8},{28,12},{1,17},{... | collective-permute-start | bytes 786440 | tf_op jit(solution)/shard_map/ppermute | solution.py:36
  220.3 8.7 %collective-permute-start.28 = (bf16[1,48,2048]{2,1,0:T(8,128)(2,1)S(1)}, bf16[1,48,2048]{2,1,0:T(8,128)(2,1)S(1)}, u32[]{:S(2)}, u32[]{:S(2)}) collective-permute-start(bf16[1,48,2048]{2,1,0:T(8,128)(2,1)S(1)} %get-tuple-element.281), channel_id=1, source_target_pairs={{0,16},{4,20},{8,24},{12,28},{16,0},{20,4},{24,8},{28,12},{1,17},{... | collective-permute-start | bytes 589832 | tf_op jit(solution)/shard_map/ppermute | solution.py:36
  221.9 7.0 %collective-permute-start.29 = (bf16[1,48,2048]{2,1,0:T(8,128)(2,1)S(1)}, bf16[1,48,2048]{2,1,0:T(8,128)(2,1)S(1)}, u32[]{:S(2)}, u32[]{:S(2)}) collective-permute-start(bf16[1,48,2048]{2,1,0:T(8,128)(2,1)S(1)} %get-tuple-element.279), channel_id=1, source_target_pairs={{0,8},{4,12},{8,0},{12,4},{16,24},{20,28},{24,16},{28,20},{1,9},{5... | collective-permute-start | bytes 589832 | tf_op jit(solution)/shard_map/ppermute | solution.py:36
  229.0 8.4 %collective-permute-start.30 = (bf16[2,32,2048]{2,1,0:T(8,128)(2,1)S(1)}, bf16[2,32,2048]{2,1,0:T(8,128)(2,1)S(1)}, u32[]{:S(2)}, u32[]{:S(2)}) collective-permute-start(bf16[2,32,2048]{2,1,0:T(8,128)(2,1)S(1)} %pad_maximum_fusion.8), channel_id=1, source_target_pairs={{0,8},{4,12},{8,0},{12,4},{16,24},{20,28},{24,16},{28,20},{1,9},{5... | collective-permute-start | bytes 786440 | tf_op jit(solution)/shard_map/ppermute | solution.py:36
  229.0 8.4 %collective-permute-start.31 = (bf16[2,32,2048]{2,1,0:T(8,128)(2,1)S(1)}, bf16[2,32,2048]{2,1,0:T(8,128)(2,1)S(1)}, u32[]{:S(2)}, u32[]{:S(2)}) collective-permute-start(bf16[2,32,2048]{2,1,0:T(8,128)(2,1)S(1)} %pad_maximum_fusion.9), channel_id=1, source_target_pairs={{0,16},{4,20},{8,24},{12,28},{16,0},{20,4},{24,8},{28,12},{1,17},{... | collective-permute-start | bytes 786440 | tf_op jit(solution)/shard_map/ppermute | solution.py:36
  237.5 27.7 %collective-permute-start.32 = (bf16[1024,256]{1,0:T(8,128)(2,1)S(1)}, bf16[1024,256]{1,0:T(8,128)(2,1)S(1)}, u32[]{:S(2)}, u32[]{:S(2)}) collective-permute-start(bf16[1024,256]{1,0:T(8,128)(2,1)S(1)} %pad_maximum_fusion.2), channel_id=1, source_target_pairs={{0,8},{4,12},{8,0},{12,4},{16,24},{20,28},{24,16},{28,20},{1,9},{5... | collective-permute-start | bytes 1572872 | tf_op jit(solution)/shard_map/ppermute | solution.py:36
  239.0 26.2 %collective-permute-start.33 = (bf16[1,32,2048]{2,1,0:T(8,128)(2,1)S(1)}, bf16[1,32,2048]{2,1,0:T(8,128)(2,1)S(1)}, u32[]{:S(2)}, u32[]{:S(2)}) collective-permute-start(bf16[1,32,2048]{2,1,0:T(8,128)(2,1)S(1)} %get-tuple-element.285), channel_id=1, source_target_pairs={{0,16},{4,20},{8,24},{12,28},{16,0},{20,4},{24,8},{28,12},{1,17},{... | collective-permute-start | bytes 393224 | tf_op jit(solution)/shard_map/ppermute | solution.py:36
  239.5 25.7 %collective-permute-start.34 = (bf16[1,32,2048]{2,1,0:T(8,128)(2,1)S(1)}, bf16[1,32,2048]{2,1,0:T(8,128)(2,1)S(1)}, u32[]{:S(2)}, u32[]{:S(2)}) collective-permute-start(bf16[1,32,2048]{2,1,0:T(8,128)(2,1)S(1)} %get-tuple-element.283), channel_id=1, source_target_pairs={{0,8},{4,12},{8,0},{12,4},{16,24},{20,28},{24,16},{28,20},{1,9},{5... | collective-permute-start | bytes 393224 | tf_op jit(solution)/shard_map/ppermute | solution.py:36
  240.1 26.9 %slice-start = ((s8[5111808]{0:T(1024)(128)(4,1)}), s8[4194304]{0:T(1024)(128)(4,1)S(1)}, s32[]{:S(2)}) async-start(s8[5111808]{0:T(1024)(128)(4,1)} %bitcast.168), calls=%async_computation.1 | async-start | bytes 8388608
  240.2 26.8 %slice-start.1 = ((s8[5111808]{0:T(1024)(128)(4,1)}), s8[917504]{0:T(1024)(128)(4,1)S(1)}, s32[]{:S(2)}) async-start(s8[5111808]{0:T(1024)(128)(4,1)} %bitcast.168), calls=%async_computation.2 | async-start | bytes 1835008
  265.3 6.3 %collective-permute-start.36 = (bf16[4,32,2048]{2,1,0:T(8,128)(2,1)S(1)}, bf16[4,32,2048]{2,1,0:T(8,128)(2,1)S(1)}, u32[]{:S(2)}, u32[]{:S(2)}) collective-permute-start(bf16[4,32,2048]{2,1,0:T(8,128)(2,1)S(1)} %get-tuple-element.259), channel_id=1, source_target_pairs={{0,4},{4,0},{8,12},{12,8},{16,20},{20,16},{24,28},{28,24},{1,5},{5... | collective-permute-start | bytes 1572872 | tf_op jit(solution)/shard_map/ppermute | solution.py:36
  265.4 6.2 %collective-permute-start.35 = (bf16[4,32,2048]{2,1,0:T(8,128)(2,1)S(1)}, bf16[4,32,2048]{2,1,0:T(8,128)(2,1)S(1)}, u32[]{:S(2)}, u32[]{:S(2)}) collective-permute-start(bf16[4,32,2048]{2,1,0:T(8,128)(2,1)S(1)} %get-tuple-element.260), channel_id=1, source_target_pairs={{0,4},{4,0},{8,12},{12,8},{16,20},{20,16},{24,28},{28,24},{1,5},{5... | collective-permute-start | bytes 1572872 | tf_op jit(solution)/shard_map/ppermute | solution.py:36
  266.1 9.1 %collective-permute-start.39 = (bf16[2048,256]{1,0:T(8,128)(2,1)S(1)}, bf16[2048,256]{1,0:T(8,128)(2,1)S(1)}, u32[]{:S(2)}, u32[]{:S(2)}) collective-permute-start(bf16[2048,256]{1,0:T(8,128)(2,1)S(1)} %pad_maximum_fusion), channel_id=1, source_target_pairs={{0,4},{4,0},{8,12},{12,8},{16,20},{20,16},{24,28},{28,24},{1,5},{5... | collective-permute-start | bytes 3145736 | tf_op jit(solution)/shard_map/ppermute | solution.py:36
  272.0 8.4 %collective-permute-start.37 = (bf16[2,32,2048]{2,1,0:T(8,128)(2,1)S(1)}, bf16[2,32,2048]{2,1,0:T(8,128)(2,1)S(1)}, u32[]{:S(2)}, u32[]{:S(2)}) collective-permute-start(bf16[2,32,2048]{2,1,0:T(8,128)(2,1)S(1)} %pad_maximum_fusion.10), channel_id=1, source_target_pairs={{0,8},{4,12},{8,0},{12,4},{16,24},{20,28},{24,16},{28,20},{1,9},{5... | collective-permute-start | bytes 786440 | tf_op jit(solution)/shard_map/ppermute | solution.py:36
  273.5 8.1 %collective-permute-start.38 = (bf16[2,32,2048]{2,1,0:T(8,128)(2,1)S(1)}, bf16[2,32,2048]{2,1,0:T(8,128)(2,1)S(1)}, u32[]{:S(2)}, u32[]{:S(2)}) collective-permute-start(bf16[2,32,2048]{2,1,0:T(8,128)(2,1)S(1)} %pad_maximum_fusion.11), channel_id=1, source_target_pairs={{0,16},{4,20},{8,24},{12,28},{16,0},{20,4},{24,8},{28,12},{1,17},{... | collective-permute-start | bytes 786440 | tf_op jit(solution)/shard_map/ppermute | solution.py:36
  281.6 7.0 %collective-permute-start.41 = (bf16[1,32,2048]{2,1,0:T(8,128)(2,1)S(1)}, bf16[1,32,2048]{2,1,0:T(8,128)(2,1)S(1)}, u32[]{:S(2)}, u32[]{:S(2)}) collective-permute-start(bf16[1,32,2048]{2,1,0:T(8,128)(2,1)S(1)} %fusion.17), channel_id=1, source_target_pairs={{0,8},{4,12},{8,0},{12,4},{16,24},{20,28},{24,16},{28,20},{1,9},{5... | collective-permute-start | bytes 393224 | tf_op jit(solution)/shard_map/ppermute | solution.py:36
  282.3 6.4 %collective-permute-start.40 = (bf16[1,32,2048]{2,1,0:T(8,128)(2,1)S(1)}, bf16[1,32,2048]{2,1,0:T(8,128)(2,1)S(1)}, u32[]{:S(2)}, u32[]{:S(2)}) collective-permute-start(bf16[1,32,2048]{2,1,0:T(8,128)(2,1)S(1)} %fusion.16), channel_id=1, source_target_pairs={{0,16},{4,20},{8,24},{12,28},{16,0},{20,4},{24,8},{28,12},{1,17},{... | collective-permute-start | bytes 393224 | tf_op jit(solution)/shard_map/ppermute | solution.py:36
  (17 other events, 50.8 us)

commit v10 on v9

--- a/solution.py
+++ b/solution.py
@@ -309,9 +309,13 @@
         take()
         if not bits_left:
             return
-        if len(bits_left) == len(wide_bits):
+        prepare()
+        small["got"] = swap(small["rows" if "rows" in small else "grad_a"], "wide", bits_left.pop(0))
+
+    def prepare():
+        if len(bits_left) <= len(wide_bits) and "rows" in small:
+            take()
             share_made()
-        small["got"] = swap(small["rows" if "rows" in small else "grad_a"], "wide", bits_left.pop(0))
 
     def regroup():
         shares = small.pop("inputs").reshape(owner_rows, owners, -1)
@@ -375,11 +379,12 @@
         if i + 1 < count:
             begin(i + 1)
             step(1 if i == 0 else 0)
+            prepare()
             run_pass(i)
     step()
     run_pass(count - 1)
     small, sums = hold(small, sums)
-    columns_step = max(128 * c for c in range(1, 14) if depth % (128 * c) == 0)
+    columns_step = max(128 * c for c in range(1, 5) if depth % (128 * c) == 0)
     steps = depth // columns_step
     early = steps // 2 or 1
     tokens = [tokens[i] for i in range(count)]

time: 293 us -> 297 us (1.014)
  other arithmetic: 16.1 us -> 27.2 us
  waiting for transfers between devices: 101 us -> 90.7 us
    ppermute x36, waiting for transfers between devices: 98.7 us -> 87.3 us  [swap(): return lax.ppermute(value, axis, [(i, i ^ bit) for i in range(size)])]
    another operation x12, other arithmetic: 1.51 us -> 8.92 us  [scatter_send(): away = jnp.stack([part[p | bit].astype(jnp.bfloat16) for p in stay[-1]])]
    unnamed x52 -> x66, local copies, waits for them, and re-layouts: 10.1 us -> 12 us
  transfers between devices with their start and end apart: 43 -> 43, of which waited for: 17 -> 16; matrix products, arithmetic and copies ran while one was open for 14% -> 18% of each run, Pallas kernels for 31% -> 31%
where the time goes in v10:
time: 297 us; the launch traced here: 296 us
  Pallas kernels  91.2 us (31%)
  waiting for transfers between devices  90.7 us (31%)
  starting transfers between devices  49.7 us (17%)
  other arithmetic  27.2 us (9%)
  local copies, waits for them, and re-layouts  25.4 us (9%)
  matrix products  10.4 us (4%)
    ppermute x36, waiting for transfers between devices, swap(): return lax.ppermute(value, axis, [(i, i ^ bit) for i in range(size)])  87.3 us
    pallas_call x3, Pallas kernels, weight_pass(): pl.pallas_call(functools.partial(pass_kernel, sources=len(sources), owner...  80.2 us
    ppermute x36, starting transfers between devices, swap(): return lax.ppermute(value, axis, [(i, i ^ bit) for i in range(size)])  38.4 us
    unnamed x66, local copies, waits for them, and re-layouts  12 us
    pallas_call x2, Pallas kernels, factor_gradient(): pl.pallas_call(functools.partial(factor_kernel, pieces=pieces, scale=scal...  11.1 us
    another operation x12, other arithmetic, scatter_send(): away = jnp.stack([part[p | bit].astype(jnp.bfloat16) for p in stay[-1]])  8.92 us
  transfers between devices with their start and end apart: 43, of which 16 were waited for; matrix products, arithmetic and copies ran while one was open for 18% of the time, Pallas kernels for 31%

profile of v10, /device:TPU:0, one launch (start us, length us, event | category | flops | bytes accessed | tf_op | source)
XLA Modules:
  0.0 296.0 jit_solution(15694458630821095378)
XLA Ops:
  0.6 2.6 slice.336
  3.2 3.0 %collective-permute-start = (bf16[96,6656]{1,0:T(8,128)(2,1)}, bf16[96,6656]{1,0:T(8,128)(2,1)}, u32[]{:S(2)}, u32[]{:S(2)}) collective-permute-start(bf16[96,6656]{1,0:T(8,128)(2,1)} %bitcast.1.refs_0_), channel_id=1, source_target_pairs={{0,1},{1,0},{2,3},{3,2},{4,5},{5,4},{6,7},{7,6},{8,9},{9,8},{10,11... | collective-permute-start | bytes 3833864 | tf_op jit(solution)/shard_map/ppermute | solution.py:36
  6.3 2.6 collective-permute-start.1
  8.9 3.7 %fusion.25 = f32[224,256]{1,0:T(8,128)} fusion(bf16[224,6656]{1,0:T(8,128)(2,1)} %param.6, bf16[256,6656]{1,0:T(8,128)(2,1)S(1)} %copy-done), kind=kOutput, calls=%fused_computation.120 | convolution fusion | flops 763363328 | bytes 6619136 | tf_op jit(solution)/shard_map/dot_general | solution.py:18
  13.4 1.5 collective-permute-start.2
  15.0 3.3 %collective-permute-done.2 = f32[112,256]{1,0:T(8,128)S(1)} collective-permute-done((f32[112,256]{1,0:T(8,128)S(1)}, f32[112,256]{1,0:T(8,128)S(1)}, u32[]{:S(2)}, u32[]{:S(2)}) %collective-permute-start.2) | collective-permute-done | bytes 114720 | tf_op jit(solution)/shard_map/ppermute | solution.py:36
  19.2 1.6 collective-permute-start.3
  20.7 2.7 collective-permute-done.3
  24.8 37.1 %collective-permute-done.refs_1_ = bf16[96,6656]{1,0:T(8,128)(2,1)} collective-permute-done((bf16[96,6656]{1,0:T(8,128)(2,1)}, bf16[96,6656]{1,0:T(8,128)(2,1)}, u32[]{:S(2)}, u32[]{:S(2)}) %collective-permute-start) | collective-permute-done | bytes 1277984 | tf_op jit(solution)/shard_map/ppermute | solution.py:36
  61.9 2.6 collective-permute-done.1.refs_2_
  66.5 1.5 copy.63
  68.0 1.7 fusion.24
  75.0 4.2 %all-to-all-start = ((bf16[8,112,512]{2,1,0:T(8,128)(2,1)}), bf16[8,112,512]{2,1,0:T(8,128)(2,1)}, u32[]{:S(2)}, u32[]{:S(2)}) async-start(bf16[8,112,512]{2,1,0:T(8,128)(2,1)} %bitcast_dynamic-update-slice_fusion), calls=%async_computation | async-start | bytes 1835008 | tf_op jit(solution)/shard_map/all_to_all | solution.py:327
  79.2 2.3 convolution_convert_fusion
  81.5 2.8 collective-permute-start.7
  88.0 11.5 %collective-permute-done.7 = bf16[140,256]{1,0:T(8,128)(2,1)S(1)} collective-permute-done((bf16[140,256]{1,0:T(8,128)(2,1)S(1)}, bf16[140,256]{1,0:T(8,128)(2,1)S(1)}, u32[]{:S(2)}, u32[]{:S(2)}) %collective-permute-start.7) | collective-permute-done | bytes 71712 | tf_op jit(solution)/shard_map/ppermute | solution.py:36
  99.5 1.4 collective-permute-done.8
  101.0 1.4 collective-permute-start.10
  109.0 31.3 %weight_pass.3 = (bf16[384,6656]{1,0:T(8,128)(2,1)}, f32[4,48,4096]{2,1,0:T(8,128)S(1)}, bf16[4,48,4096]{2,1,0:T(8,128)(2,1)S(1)}) custom-call(s32[9]{0:T(128)S(1)} %stack.142.table, bf16[96,6656]{1,0:T(8,128)(2,1)} %bitcast.1.refs_0_, bf16[96,6656]{1,0:T(8,128)(2,1)} %collective-permute-done.refs_1_, bf16[96,6656]{1,0:T(8,128)(2,1)} %collective-permute-done.1.refs_2_, ...), custom_call_target="tpu_custom_call" | custom-call | bytes 65536 | tf_op jit(solution)/shard_map/weight_pass/pallas_call | solution.py:124
  141.0 1.5 collective-permute-start.14
  143.4 1.6 collective-permute-start.15
  146.8 4.7 %collective-permute-done.15 = bf16[2,224,256]{2,1,0:T(8,128)(2,1)S(1)} collective-permute-done((bf16[2,224,256]{2,1,0:T(8,128)(2,1)S(1)}, bf16[2,224,256]{2,1,0:T(8,128)(2,1)S(1)}, u32[]{:S(2)}, u32[]{:S(2)}) %collective-permute-start.15) | collective-permute-done | bytes 229408 | tf_op jit(solution)/shard_map/ppermute | solution.py:36
  151.6 1.6 collective-permute-start.16
  153.2 2.1 slice.348
  155.3 8.6 %collective-permute-done.16 = bf16[4,224,256]{2,1,0:T(8,128)(2,1)} collective-permute-done((bf16[4,224,256]{2,1,0:T(8,128)(2,1)S(1)}, bf16[4,224,256]{2,1,0:T(8,128)(2,1)}, u32[]{:S(2)}, u32[]{:S(2)}) %collective-permute-start.16) | collective-permute-done | bytes 458784 | tf_op jit(solution)/shard_map/ppermute | solution.py:36
  165.1 1.7 collective-permute-start.19
  167.0 3.9 %add_convert_fusion.1 = (bf16[1,48,2048]{2,1,0:T(8,128)(2,1)S(1)}, bf16[1,48,2048]{2,1,0:T(8,128)(2,1)S(1)}, f32[48,2048]{1,0:T(8,128)}, f32[48,2048]{1,0:T(8,12...) fusion(f32[4,48,4096]{2,1,0:T(8,128)} %copy-done.5, ...), kind=kLoop, calls=%fused_computation.38 | loop fusion | flops 1966080 | bytes 7077888 | tf_op jit(solution)/shard_map/convert_element_type | solution.py:201
  171.7 1.5 collective-permute-start.21
  174.0 1.5 collective-permute-start.22
  182.0 23.9 %weight_pass.4 = (bf16[256,6656]{1,0:T(8,128)(2,1)S(1)}, f32[4,32,4096]{2,1,0:T(8,128)S(1)}, bf16[4,32,4096]{2,1,0:T(8,128)(2,1)S(1)}) custom-call(s32[9]{0:T(128)S(1)} %stack.142.table, bf16[64,6656]{1,0:T(8,128)(2,1)S(1)} %bitcast.173, bf16[64,6656]{1,0:T(8,128)(2,1)} %collective-permute-done.10.refs_1_, bf16[64,6656]{1,0:T(8,128)(2,1)} %collective-permute-done.11.refs_2_, ...), custom_call_target="tpu_custom_call" | custom-call | bytes 65536 | tf_op jit(solution)/shard_map/weight_pass/pallas_call | solution.py:124
  206.9 2.4 fusion
  209.3 2.0 convolution_multiply_fusion
  211.4 1.6 collective-permute-start.25
  214.8 1.9 fusion.12
  216.7 1.5 collective-permute-start.28
  218.2 1.9 fusion.13
  223.2 3.5 %collective-permute-done.28 = bf16[1,48,2048]{2,1,0:T(8,128)(2,1)S(1)} collective-permute-done((bf16[1,48,2048]{2,1,0:T(8,128)(2,1)S(1)}, bf16[1,48,2048]{2,1,0:T(8,128)(2,1)S(1)}, u32[]{:S(2)}, u32[]{:S(2)}) %collective-permute-start.28) | collective-permute-done | bytes 196640 | tf_op jit(solution)/shard_map/ppermute | solution.py:36
  228.1 6.2 %collective-permute-done.30 = bf16[2,32,2048]{2,1,0:T(8,128)(2,1)} collective-permute-done((bf16[2,32,2048]{2,1,0:T(8,128)(2,1)}, bf16[2,32,2048]{2,1,0:T(8,128)(2,1)}, u32[]{:S(2)}, u32[]{:S(2)}) %collective-permute-start.30) | collective-permute-done | bytes 262176 | tf_op jit(solution)/shard_map/ppermute | solution.py:36
  234.6 2.3 collective-permute-done.26.refs_4_
  241.3 1.5 collective-permute-start.34
  242.9 25.0 %weight_pass.5 = (bf16[256,6656]{1,0:T(8,128)(2,1)S(1)}, f32[4,32,4096]{2,1,0:T(8,128)S(1)}, bf16[4,32,4096]{2,1,0:T(8,128)(2,1)S(1)}) custom-call(s32[9]{0:T(128)S(1)} %stack.142.table, bf16[64,6656]{1,0:T(8,128)(2,1)} %bitcast.31.refs_0_, bf16[64,6656]{1,0:T(8,128)(2,1)} %collective-permute-done.19.refs_1_, ...), custom_call_target="tpu_custom_call" | custom-call | bytes 65536 | tf_op jit(solution)/shard_map/weight_pass/pallas_call | solution.py:124
  269.8 5.1 %factor_gradient.2.refs_3_ = f32[256,6656]{1,0:T(8,128)} custom-call(s32[8]{0:T(128)S(1)} %stack.161.order, bf16[8,112,256]{2,1,0:T(8,128)(2,1)S(1)} %copy-done.2, bf16[384,6656]{1,0:T(8,128)(2,1)S(1)} %bitcast.169, bf16[256,6656]{1,0:T(8,128)(2,1)S(1)} %get-tuple-element.205.refs_1_, bf16[256,6656]{1,0:T(8,128)(2,1)S(1)} %get-tuple-element.206.refs_2_), custom_call_target="tpu_custom_call" | custom-call | bytes 65536 | tf_op jit(solution)/shard_map/factor_gradient/pallas_call | solution.py:173
  275.9 1.6 collective-permute-start.38
  277.9 2.3 maximum_convert_fusion
  280.3 3.8 %collective-permute-done.37 = bf16[2,32,2048]{2,1,0:T(8,128)(2,1)S(1)} collective-permute-done((bf16[2,32,2048]{2,1,0:T(8,128)(2,1)S(1)}, bf16[2,32,2048]{2,1,0:T(8,128)(2,1)S(1)}, u32[]{:S(2)}, u32[]{:S(2)}) %collective-permute-start.37) | collective-permute-done | bytes 262176 | tf_op jit(solution)/shard_map/ppermute | solution.py:36
  284.5 1.6 collective-permute-start.41
  286.1 1.6 collective-permute-start.40
  287.7 5.9 %factor_gradient.3 = f32[256,6656]{1,0:T(8,128)} custom-call(s32[8]{0:T(128)S(1)} %stack.161.order, bf16[8,112,256]{2,1,0:T(8,128)(2,1)S(1)} %copy-done.2, bf16[384,6656]{1,0:T(8,128)(2,1)S(1)} %bitcast.169, bf16[256,6656]{1,0:T(8,128)(2,1)S(1)} %get-tuple-element.205.refs_1_, ...), custom_call_target="tpu_custom_call", output_to_operand_aliasing={{}: (5, {})} | custom-call | bytes 65536 | tf_op jit(solution)/shard_map/factor_gradient/pallas_call | solution.py:173
  (177 shorter events, 51.7 us)
Async XLA Ops:
  3.2 58.7 %collective-permute-start = (bf16[96,6656]{1,0:T(8,128)(2,1)}, bf16[96,6656]{1,0:T(8,128)(2,1)}, u32[]{:S(2)}, u32[]{:S(2)}) collective-permute-start(bf16[96,6656]{1,0:T(8,128)(2,1)} %bitcast.1.refs_0_), channel_id=1, source_target_pairs={{0,1},{1,0},{2,3},{3,2},{4,5},{5,4},{6,7},{7,6},{8,9},{9,8},{10,11... | collective-permute-start | bytes 3833864 | tf_op jit(solution)/shard_map/ppermute | solution.py:36
  6.3 58.2 %collective-permute-start.1 = (bf16[96,6656]{1,0:T(8,128)(2,1)}, bf16[96,6656]{1,0:T(8,128)(2,1)}, u32[]{:S(2)}, u32[]{:S(2)}) collective-permute-start(bf16[96,6656]{1,0:T(8,128)(2,1)} %bitcast.1.refs_0_), channel_id=1, source_target_pairs={{0,2},{1,3},{2,0},{3,1},{4,6},{5,7},{6,4},{7,5},{8,10},{9,11},{10,... | collective-permute-start | bytes 3833864 | tf_op jit(solution)/shard_map/ppermute | solution.py:36
  13.4 4.8 %collective-permute-start.2 = (f32[112,256]{1,0:T(8,128)S(1)}, f32[112,256]{1,0:T(8,128)S(1)}, u32[]{:S(2)}, u32[]{:S(2)}) collective-permute-start(f32[112,256]{1,0:T(8,128)S(1)} %dynamic-slice_bitcast_fusion), channel_id=1, source_target_pairs={{0,16},{4,20},{8,24},{12,28},{16,0},{20,4},{24,8},{28,12},{1,17},{... | collective-permute-start | bytes 344072 | tf_op jit(solution)/shard_map/ppermute | solution.py:36
  19.2 4.2 %collective-permute-start.3 = (f32[56,256]{1,0:T(8,128)S(1)}, f32[56,256]{1,0:T(8,128)S(1)}, u32[]{:S(2)}, u32[]{:S(2)}) collective-permute-start(f32[56,256]{1,0:T(8,128)S(1)} %dynamic-slice_bitcast_fusion.1), channel_id=1, source_target_pairs={{0,8},{4,12},{8,0},{12,4},{16,24},{20,28},{24,16},{28,20},{1,9},{5... | collective-permute-start | bytes 172040 | tf_op jit(solution)/shard_map/ppermute | solution.py:36
  23.5 1.3 collective-permute-start.4
  64.5 36.5 %collective-permute-start.5 = (bf16[96,6656]{1,0:T(8,128)(2,1)}, bf16[96,6656]{1,0:T(8,128)(2,1)S(1)}, u32[]{:S(2)}, u32[]{:S(2)}) collective-permute-start(bf16[96,6656]{1,0:T(8,128)(2,1)} %bitcast.1.refs_0_), channel_id=1, source_target_pairs={{1,2},{2,1},{5,6},{6,5},{9,10},{10,9},{13,14},{14,13},{17,18},{18,... | collective-permute-start | bytes 3833864 | tf_op jit(solution)/shard_map/ppermute | solution.py:67
  65.2 35.8 %collective-permute-start.6 = (bf16[96,6656]{1,0:T(8,128)(2,1)}, bf16[96,6656]{1,0:T(8,128)(2,1)S(1)}, u32[]{:S(2)}, u32[]{:S(2)}) collective-permute-start(bf16[96,6656]{1,0:T(8,128)(2,1)} %collective-permute-done.1.refs_2_), channel_id=1, source_target_pairs={{1,0},{2,3},{5,4},{6,7},{9,8},{10,11},{13,12},{14,15},{17,16},{18,... | collective-permute-start | bytes 3833864 | tf_op jit(solution)/shard_map/ppermute | solution.py:68
  75.0 26.0 %all-to-all-start = ((bf16[8,112,512]{2,1,0:T(8,128)(2,1)}), bf16[8,112,512]{2,1,0:T(8,128)(2,1)}, u32[]{:S(2)}, u32[]{:S(2)}) async-start(bf16[8,112,512]{2,1,0:T(8,128)(2,1)} %bitcast_dynamic-update-slice_fusion), calls=%async_computation | async-start | bytes 1835008 | tf_op jit(solution)/shard_map/all_to_all | solution.py:327
  81.5 18.0 %collective-permute-start.7 = (bf16[140,256]{1,0:T(8,128)(2,1)S(1)}, bf16[140,256]{1,0:T(8,128)(2,1)S(1)}, u32[]{:S(2)}, u32[]{:S(2)}) collective-permute-start(bf16[140,256]{1,0:T(8,128)(2,1)S(1)} %pad_maximum_fusion.13), channel_id=1, source_target_pairs={{0,1},{1,0},{2,3},{3,2},{4,5},{5,4},{6,7},{7,6},{8,9},{9,8},{10,11... | collective-permute-start | bytes 215048 | tf_op jit(solution)/shard_map/ppermute | solution.py:36
  84.3 16.6 %collective-permute-start.8 = (bf16[140,256]{1,0:T(8,128)(2,1)S(1)}, bf16[140,256]{1,0:T(8,128)(2,1)}, u32[]{:S(2)}, u32[]{:S(2)}) collective-permute-start(bf16[140,256]{1,0:T(8,128)(2,1)S(1)} %pad_maximum_fusion.13), channel_id=1, source_target_pairs={{0,2},{1,3},{2,0},{3,1},{4,6},{5,7},{6,4},{7,5},{8,10},{9,11},{10,... | collective-permute-start | bytes 215048 | tf_op jit(solution)/shard_map/ppermute | solution.py:36
  85.4 15.5 %collective-permute-start.9 = (bf16[140,256]{1,0:T(8,128)(2,1)S(1)}, bf16[140,256]{1,0:T(8,128)(2,1)}, u32[]{:S(2)}, u32[]{:S(2)}) collective-permute-start(bf16[140,256]{1,0:T(8,128)(2,1)S(1)} %pad_maximum_fusion.13), channel_id=1, source_target_pairs={{0,3},{1,2},{2,1},{3,0},{4,7},{5,6},{6,5},{7,4},{8,11},{9,10},{10,... | collective-permute-start | bytes 215048 | tf_op jit(solution)/shard_map/ppermute | solution.py:36
  88.0 52.2 %copy-start.3 = (bf16[2,32,6656]{2,1,0:T(8,128)(2,1)}, bf16[2,32,6656]{2,1,0:T(8,128)(2,1)S(1)}, u32[]{:S(2)}) copy-start(bf16[2,32,6656]{2,1,0:T(8,128)(2,1)S(1)} %slice.337) | copy-start | bytes 2555908
  101.0 39.3 %collective-permute-start.10 = (bf16[64,6656]{1,0:T(8,128)(2,1)S(1)}, bf16[64,6656]{1,0:T(8,128)(2,1)}, u32[]{:S(2)}, u32[]{:S(2)}) collective-permute-start(bf16[64,6656]{1,0:T(8,128)(2,1)S(1)} %bitcast.170), channel_id=1, source_target_pairs={{0,1},{1,0},{2,3},{3,2},{4,5},{5,4},{6,7},{7,6},{8,9},{9,8},{10,11... | collective-permute-start | bytes 2555912 | tf_op jit(solution)/shard_map/ppermute | solution.py:36
  102.4 37.9 %collective-permute-start.11 = (bf16[64,6656]{1,0:T(8,128)(2,1)S(1)}, bf16[64,6656]{1,0:T(8,128)(2,1)}, u32[]{:S(2)}, u32[]{:S(2)}) collective-permute-start(bf16[64,6656]{1,0:T(8,128)(2,1)S(1)} %bitcast.171), channel_id=1, source_target_pairs={{0,2},{1,3},{2,0},{3,1},{4,6},{5,7},{6,4},{7,5},{8,10},{9,11},{10,... | collective-permute-start | bytes 2555912 | tf_op jit(solution)/shard_map/ppermute | solution.py:36
  108.8 31.4 %collective-permute-start.12 = (bf16[1,224,256]{2,1,0:T(8,128)(2,1)S(1)}, bf16[1,224,256]{2,1,0:T(8,128)(2,1)}, u32[]{:S(2)}, u32[]{:S(2)}) collective-permute-start(bf16[1,224,256]{2,1,0:T(8,128)(2,1)S(1)} %maximum_bitcast_fusion), channel_id=1, source_target_pairs={{0,4},{4,0},{8,12},{12,8},{16,20},{20,16},{24,28},{28,24},{1,5},{5... | collective-permute-start | bytes 344072 | tf_op jit(solution)/shard_map/ppermute | solution.py:36
  140.3 23.7 %collective-permute-start.13 = (bf16[64,6656]{1,0:T(8,128)(2,1)S(1)}, bf16[64,6656]{1,0:T(8,128)(2,1)S(1)}, u32[]{:S(2)}, u32[]{:S(2)}) collective-permute-start(bf16[64,6656]{1,0:T(8,128)(2,1)S(1)} %bitcast.172), channel_id=1, source_target_pairs={{1,2},{2,1},{5,6},{6,5},{9,10},{10,9},{13,14},{14,13},{17,18},{18,... | collective-permute-start | bytes 2555912 | tf_op jit(solution)/shard_map/ppermute | solution.py:67
  141.0 24.1 %collective-permute-start.14 = (bf16[64,6656]{1,0:T(8,128)(2,1)}, bf16[64,6656]{1,0:T(8,128)(2,1)S(1)}, u32[]{:S(2)}, u32[]{:S(2)}) collective-permute-start(bf16[64,6656]{1,0:T(8,128)(2,1)} %collective-permute-done.11.refs_2_), channel_id=1, source_target_pairs={{1,0},{2,3},{5,4},{6,7},{9,8},{10,11},{13,12},{14,15},{17,16},{18,... | collective-permute-start | bytes 2555912 | tf_op jit(solution)/shard_map/ppermute | solution.py:68
  143.4 8.1 %collective-permute-start.15 = (bf16[2,224,256]{2,1,0:T(8,128)(2,1)S(1)}, bf16[2,224,256]{2,1,0:T(8,128)(2,1)S(1)}, u32[]{:S(2)}, u32[]{:S(2)}) collective-permute-start(bf16[2,224,256]{2,1,0:T(8,128)(2,1)S(1)} %pad_maximum_fusion.12), channel_id=1, source_target_pairs={{0,8},{4,12},{8,0},{12,4},{16,24},{20,28},{24,16},{28,20},{1,9},{5... | collective-permute-start | bytes 688136 | tf_op jit(solution)/shard_map/ppermute | solution.py:36
  146.3 17.7 %collective-permute-start.17 = (bf16[4,48,2048]{2,1,0:T(8,128)(2,1)}, bf16[4,48,2048]{2,1,0:T(8,128)(2,1)}, u32[]{:S(2)}, u32[]{:S(2)}) collective-permute-start(bf16[4,48,2048]{2,1,0:T(8,128)(2,1)} %get-tuple-element.256), channel_id=1, source_target_pairs={{0,4},{4,0},{8,12},{12,8},{16,20},{20,16},{24,28},{28,24},{1,5},{5... | collective-permute-start | bytes 2359304 | tf_op jit(solution)/shard_map/ppermute | solution.py:36
  146.6 17.4 %collective-permute-start.18 = (bf16[4,48,2048]{2,1,0:T(8,128)(2,1)}, bf16[4,48,2048]{2,1,0:T(8,128)(2,1)}, u32[]{:S(2)}, u32[]{:S(2)}) collective-permute-start(bf16[4,48,2048]{2,1,0:T(8,128)(2,1)} %get-tuple-element.255), channel_id=1, source_target_pairs={{0,4},{4,0},{8,12},{12,8},{16,20},{20,16},{24,28},{28,24},{1,5},{5... | collective-permute-start | bytes 2359304 | tf_op jit(solution)/shard_map/ppermute | solution.py:36
  151.6 12.3 %collective-permute-start.16 = (bf16[4,224,256]{2,1,0:T(8,128)(2,1)S(1)}, bf16[4,224,256]{2,1,0:T(8,128)(2,1)}, u32[]{:S(2)}, u32[]{:S(2)}) collective-permute-start(bf16[4,224,256]{2,1,0:T(8,128)(2,1)S(1)} %pad_maximum_fusion.4), channel_id=1, source_target_pairs={{0,16},{4,20},{8,24},{12,28},{16,0},{20,4},{24,8},{28,12},{1,17},{... | collective-permute-start | bytes 1376264 | tf_op jit(solution)/shard_map/ppermute | solution.py:36
  165.1 46.2 %collective-permute-start.19 = (bf16[64,6656]{1,0:T(8,128)(2,1)}, bf16[64,6656]{1,0:T(8,128)(2,1)}, u32[]{:S(2)}, u32[]{:S(2)}) collective-permute-start(bf16[64,6656]{1,0:T(8,128)(2,1)} %bitcast.31.refs_0_), channel_id=1, source_target_pairs={{0,1},{1,0},{2,3},{3,2},{4,5},{5,4},{6,7},{7,6},{8,9},{9,8},{10,11... | collective-permute-start | bytes 2555912 | tf_op jit(solution)/shard_map/ppermute | solution.py:36
  166.8 44.5 %collective-permute-start.20 = (bf16[64,6656]{1,0:T(8,128)(2,1)}, bf16[64,6656]{1,0:T(8,128)(2,1)}, u32[]{:S(2)}, u32[]{:S(2)}) collective-permute-start(bf16[64,6656]{1,0:T(8,128)(2,1)} %bitcast.31.refs_0_), channel_id=1, source_target_pairs={{0,2},{1,3},{2,0},{3,1},{4,6},{5,7},{6,4},{7,5},{8,10},{9,11},{10,... | collective-permute-start | bytes 2555912 | tf_op jit(solution)/shard_map/ppermute | solution.py:36
  171.7 34.2 %collective-permute-start.21 = (bf16[2,48,2048]{2,1,0:T(8,128)(2,1)}, bf16[2,48,2048]{2,1,0:T(8,128)(2,1)}, u32[]{:S(2)}, u32[]{:S(2)}) collective-permute-start(bf16[2,48,2048]{2,1,0:T(8,128)(2,1)} %pad_maximum_fusion.5), channel_id=1, source_target_pairs={{0,8},{4,12},{8,0},{12,4},{16,24},{20,28},{24,16},{28,20},{1,9},{5... | collective-permute-start | bytes 1179656 | tf_op jit(solution)/shard_map/ppermute | solution.py:36
  174.0 32.0 %collective-permute-start.22 = (bf16[2,48,2048]{2,1,0:T(8,128)(2,1)}, bf16[2,48,2048]{2,1,0:T(8,128)(2,1)}, u32[]{:S(2)}, u32[]{:S(2)}) collective-permute-start(bf16[2,48,2048]{2,1,0:T(8,128)(2,1)} %pad_maximum_fusion.6), channel_id=1, source_target_pairs={{0,16},{4,20},{8,24},{12,28},{16,0},{20,4},{24,8},{28,12},{1,17},{... | collective-permute-start | bytes 1179656 | tf_op jit(solution)/shard_map/ppermute | solution.py:36
  206.1 5.3 %collective-permute-start.23 = (bf16[4,32,2048]{2,1,0:T(8,128)(2,1)S(1)}, bf16[4,32,2048]{2,1,0:T(8,128)(2,1)S(1)}, u32[]{:S(2)}, u32[]{:S(2)}) collective-permute-start(bf16[4,32,2048]{2,1,0:T(8,128)(2,1)S(1)} %get-tuple-element.262), channel_id=1, source_target_pairs={{0,4},{4,0},{8,12},{12,8},{16,20},{20,16},{24,28},{28,24},{1,5},{5... | collective-permute-start | bytes 1572872 | tf_op jit(solution)/shard_map/ppermute | solution.py:36
  206.1 5.2 %collective-permute-start.24 = (bf16[4,32,2048]{2,1,0:T(8,128)(2,1)S(1)}, bf16[4,32,2048]{2,1,0:T(8,128)(2,1)S(1)}, u32[]{:S(2)}, u32[]{:S(2)}) collective-permute-start(bf16[4,32,2048]{2,1,0:T(8,128)(2,1)S(1)} %get-tuple-element.261), channel_id=1, source_target_pairs={{0,4},{4,0},{8,12},{12,8},{16,20},{20,16},{24,28},{28,24},{1,5},{5... | collective-permute-start | bytes 1572872 | tf_op jit(solution)/shard_map/ppermute | solution.py:36
  211.4 23.2 %collective-permute-start.25 = (bf16[64,6656]{1,0:T(8,128)(2,1)}, bf16[64,6656]{1,0:T(8,128)(2,1)}, u32[]{:S(2)}, u32[]{:S(2)}) collective-permute-start(bf16[64,6656]{1,0:T(8,128)(2,1)} %bitcast.31.refs_0_), channel_id=1, source_target_pairs={{1,2},{2,1},{5,6},{6,5},{9,10},{10,9},{13,14},{14,13},{17,18},{18,... | collective-permute-start | bytes 2555912 | tf_op jit(solution)/shard_map/ppermute | solution.py:67
  213.0 23.9 %collective-permute-start.26 = (bf16[64,6656]{1,0:T(8,128)(2,1)}, bf16[64,6656]{1,0:T(8,128)(2,1)}, u32[]{:S(2)}, u32[]{:S(2)}) collective-permute-start(bf16[64,6656]{1,0:T(8,128)(2,1)} %collective-permute-done.20.refs_2_), channel_id=1, source_target_pairs={{1,0},{2,3},{5,4},{6,7},{9,8},{10,11},{13,12},{14,15},{17,16},{18,... | collective-permute-start | bytes 2555912 | tf_op jit(solution)/shard_map/ppermute | solution.py:68
  214.2 13.8 %collective-permute-start.27 = (bf16[512,256]{1,0:T(8,128)(2,1)}, bf16[512,256]{1,0:T(8,128)(2,1)}, u32[]{:S(2)}, u32[]{:S(2)}) collective-permute-start(bf16[512,256]{1,0:T(8,128)(2,1)} %fusion), channel_id=1, source_target_pairs={{0,16},{4,20},{8,24},{12,28},{16,0},{20,4},{24,8},{28,12},{1,17},{... | collective-permute-start | bytes 786440 | tf_op jit(solution)/shard_map/ppermute | solution.py:36
  216.7 10.0 %collective-permute-start.28 = (bf16[1,48,2048]{2,1,0:T(8,128)(2,1)S(1)}, bf16[1,48,2048]{2,1,0:T(8,128)(2,1)S(1)}, u32[]{:S(2)}, u32[]{:S(2)}) collective-permute-start(bf16[1,48,2048]{2,1,0:T(8,128)(2,1)S(1)} %get-tuple-element.281), channel_id=1, source_target_pairs={{0,16},{4,20},{8,24},{12,28},{16,0},{20,4},{24,8},{28,12},{1,17},{... | collective-permute-start | bytes 589832 | tf_op jit(solution)/shard_map/ppermute | solution.py:36
  220.1 7.2 %collective-permute-start.29 = (bf16[1,48,2048]{2,1,0:T(8,128)(2,1)S(1)}, bf16[1,48,2048]{2,1,0:T(8,128)(2,1)S(1)}, u32[]{:S(2)}, u32[]{:S(2)}) collective-permute-start(bf16[1,48,2048]{2,1,0:T(8,128)(2,1)S(1)} %get-tuple-element.279), channel_id=1, source_target_pairs={{0,8},{4,12},{8,0},{12,4},{16,24},{20,28},{24,16},{28,20},{1,9},{5... | collective-permute-start | bytes 589832 | tf_op jit(solution)/shard_map/ppermute | solution.py:36
  226.7 7.5 %collective-permute-start.30 = (bf16[2,32,2048]{2,1,0:T(8,128)(2,1)}, bf16[2,32,2048]{2,1,0:T(8,128)(2,1)}, u32[]{:S(2)}, u32[]{:S(2)}) collective-permute-start(bf16[2,32,2048]{2,1,0:T(8,128)(2,1)} %pad_maximum_fusion.8), channel_id=1, source_target_pairs={{0,8},{4,12},{8,0},{12,4},{16,24},{20,28},{24,16},{28,20},{1,9},{5... | collective-permute-start | bytes 786440 | tf_op jit(solution)/shard_map/ppermute | solution.py:36
  227.3 7.3 %collective-permute-start.31 = (bf16[2,32,2048]{2,1,0:T(8,128)(2,1)}, bf16[2,32,2048]{2,1,0:T(8,128)(2,1)}, u32[]{:S(2)}, u32[]{:S(2)}) collective-permute-start(bf16[2,32,2048]{2,1,0:T(8,128)(2,1)} %pad_maximum_fusion.9), channel_id=1, source_target_pairs={{0,16},{4,20},{8,24},{12,28},{16,0},{20,4},{24,8},{28,12},{1,17},{... | collective-permute-start | bytes 786440 | tf_op jit(solution)/shard_map/ppermute | solution.py:36
  228.1 12.2 %copy-start.18 = (f32[32,2048]{1,0:T(8,128)S(1)}, f32[32,2048]{1,0:T(8,128)}, u32[]{:S(2)}) copy-start(f32[32,2048]{1,0:T(8,128)} %get-tuple-element.185) | copy-start | bytes 786436
  228.1 12.1 %copy-start.19 = (f32[32,2048]{1,0:T(8,128)S(1)}, f32[32,2048]{1,0:T(8,128)}, u32[]{:S(2)}) copy-start(f32[32,2048]{1,0:T(8,128)} %get-tuple-element.182) | copy-start | bytes 786436
  238.1 29.9 %collective-permute-start.32 = (bf16[1024,256]{1,0:T(8,128)(2,1)S(1)}, bf16[1024,256]{1,0:T(8,128)(2,1)S(1)}, u32[]{:S(2)}, u32[]{:S(2)}) collective-permute-start(bf16[1024,256]{1,0:T(8,128)(2,1)S(1)} %pad_maximum_fusion.2), channel_id=1, source_target_pairs={{0,8},{4,12},{8,0},{12,4},{16,24},{20,28},{24,16},{28,20},{1,9},{5... | collective-permute-start | bytes 1572872 | tf_op jit(solution)/shard_map/ppermute | solution.py:36
  239.6 28.3 %collective-permute-start.33 = (bf16[1,32,2048]{2,1,0:T(8,128)(2,1)S(1)}, bf16[1,32,2048]{2,1,0:T(8,128)(2,1)S(1)}, u32[]{:S(2)}, u32[]{:S(2)}) collective-permute-start(bf16[1,32,2048]{2,1,0:T(8,128)(2,1)S(1)} %get-tuple-element.285), channel_id=1, source_target_pairs={{0,16},{4,20},{8,24},{12,28},{16,0},{20,4},{24,8},{28,12},{1,17},{... | collective-permute-start | bytes 393224 | tf_op jit(solution)/shard_map/ppermute | solution.py:36
  241.3 26.7 %collective-permute-start.34 = (bf16[1,32,2048]{2,1,0:T(8,128)(2,1)S(1)}, bf16[1,32,2048]{2,1,0:T(8,128)(2,1)S(1)}, u32[]{:S(2)}, u32[]{:S(2)}) collective-permute-start(bf16[1,32,2048]{2,1,0:T(8,128)(2,1)S(1)} %get-tuple-element.283), channel_id=1, source_target_pairs={{0,8},{4,12},{8,0},{12,4},{16,24},{20,28},{24,16},{28,20},{1,9},{5... | collective-permute-start | bytes 393224 | tf_op jit(solution)/shard_map/ppermute | solution.py:36
  242.8 27.0 %slice-start = ((s8[5111808]{0:T(1024)(128)(4,1)}), s8[4194304]{0:T(1024)(128)(4,1)S(1)}, s32[]{:S(2)}) async-start(s8[5111808]{0:T(1024)(128)(4,1)} %bitcast.168), calls=%async_computation.1 | async-start | bytes 8388608
  242.9 26.9 %slice-start.1 = ((s8[5111808]{0:T(1024)(128)(4,1)}), s8[917504]{0:T(1024)(128)(4,1)S(1)}, s32[]{:S(2)}) async-start(s8[5111808]{0:T(1024)(128)(4,1)} %bitcast.168), calls=%async_computation.2 | async-start | bytes 1835008
  268.1 6.9 %collective-permute-start.36 = (bf16[4,32,2048]{2,1,0:T(8,128)(2,1)S(1)}, bf16[4,32,2048]{2,1,0:T(8,128)(2,1)S(1)}, u32[]{:S(2)}, u32[]{:S(2)}) collective-permute-start(bf16[4,32,2048]{2,1,0:T(8,128)(2,1)S(1)} %get-tuple-element.259), channel_id=1, source_target_pairs={{0,4},{4,0},{8,12},{12,8},{16,20},{20,16},{24,28},{28,24},{1,5},{5... | collective-permute-start | bytes 1572872 | tf_op jit(solution)/shard_map/ppermute | solution.py:36
  268.2 6.8 %collective-permute-start.35 = (bf16[4,32,2048]{2,1,0:T(8,128)(2,1)S(1)}, bf16[4,32,2048]{2,1,0:T(8,128)(2,1)S(1)}, u32[]{:S(2)}, u32[]{:S(2)}) collective-permute-start(bf16[4,32,2048]{2,1,0:T(8,128)(2,1)S(1)} %get-tuple-element.260), channel_id=1, source_target_pairs={{0,4},{4,0},{8,12},{12,8},{16,20},{20,16},{24,28},{28,24},{1,5},{5... | collective-permute-start | bytes 1572872 | tf_op jit(solution)/shard_map/ppermute | solution.py:36
  268.8 8.7 %collective-permute-start.39 = (bf16[2048,256]{1,0:T(8,128)(2,1)S(1)}, bf16[2048,256]{1,0:T(8,128)(2,1)S(1)}, u32[]{:S(2)}, u32[]{:S(2)}) collective-permute-start(bf16[2048,256]{1,0:T(8,128)(2,1)S(1)} %pad_maximum_fusion), channel_id=1, source_target_pairs={{0,4},{4,0},{8,12},{12,8},{16,20},{20,16},{24,28},{28,24},{1,5},{5... | collective-permute-start | bytes 3145736 | tf_op jit(solution)/shard_map/ppermute | solution.py:36
  275.3 8.8 %collective-permute-start.37 = (bf16[2,32,2048]{2,1,0:T(8,128)(2,1)S(1)}, bf16[2,32,2048]{2,1,0:T(8,128)(2,1)S(1)}, u32[]{:S(2)}, u32[]{:S(2)}) collective-permute-start(bf16[2,32,2048]{2,1,0:T(8,128)(2,1)S(1)} %pad_maximum_fusion.10), channel_id=1, source_target_pairs={{0,8},{4,12},{8,0},{12,4},{16,24},{20,28},{24,16},{28,20},{1,9},{5... | collective-permute-start | bytes 786440 | tf_op jit(solution)/shard_map/ppermute | solution.py:36
  275.9 8.5 %collective-permute-start.38 = (bf16[2,32,2048]{2,1,0:T(8,128)(2,1)S(1)}, bf16[2,32,2048]{2,1,0:T(8,128)(2,1)S(1)}, u32[]{:S(2)}, u32[]{:S(2)}) collective-permute-start(bf16[2,32,2048]{2,1,0:T(8,128)(2,1)S(1)} %pad_maximum_fusion.11), channel_id=1, source_target_pairs={{0,16},{4,20},{8,24},{12,28},{16,0},{20,4},{24,8},{28,12},{1,17},{... | collective-permute-start | bytes 786440 | tf_op jit(solution)/shard_map/ppermute | solution.py:36
  284.5 9.2 %collective-permute-start.41 = (bf16[1,32,2048]{2,1,0:T(8,128)(2,1)S(1)}, bf16[1,32,2048]{2,1,0:T(8,128)(2,1)S(1)}, u32[]{:S(2)}, u32[]{:S(2)}) collective-permute-start(bf16[1,32,2048]{2,1,0:T(8,128)(2,1)S(1)} %fusion.17), channel_id=1, source_target_pairs={{0,8},{4,12},{8,0},{12,4},{16,24},{20,28},{24,16},{28,20},{1,9},{5... | collective-permute-start | bytes 393224 | tf_op jit(solution)/shard_map/ppermute | solution.py:36
  286.1 7.6 %collective-permute-start.40 = (bf16[1,32,2048]{2,1,0:T(8,128)(2,1)S(1)}, bf16[1,32,2048]{2,1,0:T(8,128)(2,1)S(1)}, u32[]{:S(2)}, u32[]{:S(2)}) collective-permute-start(bf16[1,32,2048]{2,1,0:T(8,128)(2,1)S(1)} %fusion.16), channel_id=1, source_target_pairs={{0,16},{4,20},{8,24},{12,28},{16,0},{20,4},{24,8},{28,12},{1,17},{... | collective-permute-start | bytes 393224 | tf_op jit(solution)/shard_map/ppermute | solution.py:36
  (24 other events, 120.5 us)

commit v11 on v10

--- a/solution.py
+++ b/solution.py
@@ -310,12 +310,14 @@
         if not bits_left:
             return
         prepare()
+        if "low_all" in small:
+            share_made()
         small["got"] = swap(small["rows" if "rows" in small else "grad_a"], "wide", bits_left.pop(0))
 
     def prepare():
         if len(bits_left) <= len(wide_bits) and "rows" in small:
             take()
-            share_made()
+            rows_made()
 
     def regroup():
         shares = small.pop("inputs").reshape(owner_rows, owners, -1)
@@ -327,15 +329,18 @@
         columns = lax.all_to_all(shares, "wide", split_axis=0, concat_axis=0)
         small["columns"] = columns.reshape(owner_rows * owners, -1)
 
-    def share_made():
+    def rows_made():
         rows = small.pop("rows")
         low_wide = rows[:, owner_rows:].reshape(owners, groups, low_small.shape[0], rank)
-        low_all = jnp.swapaxes(low_wide, 0, 1).reshape(owner_rows * owners, rank)
+        small["low_all"] = jnp.swapaxes(low_wide, 0, 1).reshape(owner_rows * owners, rank)
+        small["acts"] = rows[:, :owner_rows]
+
+    def share_made():
+        low_all = small.pop("low_all")
         low_own = lax.dynamic_slice_in_dim(low_all, me_wide * owner_rows, owner_rows)
         small["term"] = adapter_scale * contract_trailing_axis(low_own, adapter_down_matrix)
         made = adapter_matrix * contract_first(small.pop("columns"), low_all)
         small["grad_a"] = made.astype(jnp.bfloat16)
-        small["acts"] = rows[:, :owner_rows]
 
     tokens, sums = {}, {}
     done_hops = {}
@@ -360,7 +365,6 @@
         sums[i] = (kept, sent)
         done_hops[i] = 0
         if i + 2 == count:
-            sums.update(hold(sums)[0])
             sum_hop(i)
 
     regroup()
@@ -373,6 +377,8 @@
             if i + 1 < count:
                 blocks[i + 1] = block_of(grad_out, i + 1)
             step(2 if i == 1 else 1)
+            if i == 1 and count > 2:
+                sum_hop(0)
         middle[i], onward[i], blocks, grad_out, small, sums = hold(
             middle[i], onward[i], blocks, grad_out, small, sums
         )
@@ -384,7 +390,7 @@
     step()
     run_pass(count - 1)
     small, sums = hold(small, sums)
-    columns_step = max(128 * c for c in range(1, 5) if depth % (128 * c) == 0)
+    columns_step = max(128 * c for c in range(1, 14) if depth % (128 * c) == 0)
     steps = depth // columns_step
     early = steps // 2 or 1
     tokens = [tokens[i] for i in range(count)]

time: 297 us -> 294 us (0.990)
    ppermute x3, waiting for transfers between devices: 3.41 us -> 9.85 us  [phase_b(): lax.ppermute(far, axis, [(1, 0), (2, 3)])]
    ppermute x36, waiting for transfers between devices: 87.3 us -> 82 us  [swap(): return lax.ppermute(value, axis, [(i, i ^ bit) for i in range(size)])]
    unnamed x66 -> x64, local copies, waits for them, and re-layouts: 12 us -> 13.1 us
  transfers between devices with their start and end apart: 43 -> 43, of which waited for: 16 -> 17; matrix products, arithmetic and copies ran while one was open for 18% -> 17% of each run, Pallas kernels for 31% -> 30%
where the time goes in v11:
time: 294 us; the launch traced here: 293 us
  waiting for transfers between devices  91.8 us (31%)
  Pallas kernels  88.4 us (30%)
  starting transfers between devices  50.6 us (17%)
  other arithmetic  25.2 us (9%)
  local copies, waits for them, and re-layouts  24.6 us (8%)
  matrix products  10.6 us (4%)
    ppermute x36, waiting for transfers between devices, swap(): return lax.ppermute(value, axis, [(i, i ^ bit) for i in range(size)])  82 us
    pallas_call x3, Pallas kernels, weight_pass(): pl.pallas_call(functools.partial(pass_kernel, sources=len(sources), owner...  79.4 us
    ppermute x36, starting transfers between devices, swap(): return lax.ppermute(value, axis, [(i, i ^ bit) for i in range(size)])  40.2 us
    unnamed x64, local copies, waits for them, and re-layouts  13.1 us
    ppermute x3, waiting for transfers between devices, phase_b(): lax.ppermute(far, axis, [(1, 0), (2, 3)])  9.85 us
    pallas_call x2, Pallas kernels, factor_gradient(): pl.pallas_call(functools.partial(factor_kernel, pieces=pieces, scale=scal...  9.02 us
    another operation x12, other arithmetic, scatter_send(): away = jnp.stack([part[p | bit].astype(jnp.bfloat16) for p in stay[-1]])  7.76 us
    dot_general x2, matrix products, contract_trailing_axis(): lax.dot_general(left, right, (((1,), (1,)), ((), ())), preferred_element_...  6.51 us
  transfers between devices with their start and end apart: 43, of which 17 were waited for; matrix products, arithmetic and copies ran while one was open for 17% of the time, Pallas kernels for 30%

profile of v11, /device:TPU:0, one launch (start us, length us, event | category | flops | bytes accessed | tf_op | source)
XLA Modules:
  0.0 292.6 jit_solution(11580900943282309158)
XLA Ops:
  0.6 2.6 slice.336
  3.2 3.0 %collective-permute-start = (bf16[96,6656]{1,0:T(8,128)(2,1)}, bf16[96,6656]{1,0:T(8,128)(2,1)}, u32[]{:S(2)}, u32[]{:S(2)}) collective-permute-start(bf16[96,6656]{1,0:T(8,128)(2,1)} %bitcast.1.refs_0_), channel_id=1, source_target_pairs={{0,1},{1,0},{2,3},{3,2},{4,5},{5,4},{6,7},{7,6},{8,9},{9,8},{10,11... | collective-permute-start | bytes 3833864 | tf_op jit(solution)/shard_map/ppermute | solution.py:36
  6.3 2.6 collective-permute-start.1
  8.9 3.7 %fusion.25 = f32[224,256]{1,0:T(8,128)} fusion(bf16[224,6656]{1,0:T(8,128)(2,1)} %param.6, bf16[256,6656]{1,0:T(8,128)(2,1)S(1)} %copy-done), kind=kOutput, calls=%fused_computation.120 | convolution fusion | flops 763363328 | bytes 6619136 | tf_op jit(solution)/shard_map/dot_general | solution.py:18
  13.4 1.5 collective-permute-start.2
  15.0 3.3 %collective-permute-done.2 = f32[112,256]{1,0:T(8,128)S(1)} collective-permute-done((f32[112,256]{1,0:T(8,128)S(1)}, f32[112,256]{1,0:T(8,128)S(1)}, u32[]{:S(2)}, u32[]{:S(2)}) %collective-permute-start.2) | collective-permute-done | bytes 114720 | tf_op jit(solution)/shard_map/ppermute | solution.py:36
  19.2 1.6 collective-permute-start.3
  20.7 2.7 collective-permute-done.3
  24.8 37.1 %collective-permute-done.refs_1_ = bf16[96,6656]{1,0:T(8,128)(2,1)} collective-permute-done((bf16[96,6656]{1,0:T(8,128)(2,1)}, bf16[96,6656]{1,0:T(8,128)(2,1)}, u32[]{:S(2)}, u32[]{:S(2)}) %collective-permute-start) | collective-permute-done | bytes 1277984 | tf_op jit(solution)/shard_map/ppermute | solution.py:36
  61.9 2.6 collective-permute-done.1.refs_2_
  66.5 1.5 copy.63
  68.0 1.7 fusion.24
  75.0 4.2 %all-to-all-start = ((bf16[8,112,512]{2,1,0:T(8,128)(2,1)}), bf16[8,112,512]{2,1,0:T(8,128)(2,1)}, u32[]{:S(2)}, u32[]{:S(2)}) async-start(bf16[8,112,512]{2,1,0:T(8,128)(2,1)} %bitcast_dynamic-update-slice_fusion), calls=%async_computation | async-start | bytes 1835008 | tf_op jit(solution)/shard_map/all_to_all | solution.py:329
  79.2 2.3 convolution_convert_fusion
  81.5 2.8 collective-permute-start.7
  88.0 11.5 %collective-permute-done.7 = bf16[140,256]{1,0:T(8,128)(2,1)S(1)} collective-permute-done((bf16[140,256]{1,0:T(8,128)(2,1)S(1)}, bf16[140,256]{1,0:T(8,128)(2,1)S(1)}, u32[]{:S(2)}, u32[]{:S(2)}) %collective-permute-start.7) | collective-permute-done | bytes 71712 | tf_op jit(solution)/shard_map/ppermute | solution.py:36
  108.1 31.2 %weight_pass.3 = (bf16[384,6656]{1,0:T(8,128)(2,1)}, f32[4,48,4096]{2,1,0:T(8,128)S(1)}, bf16[4,48,4096]{2,1,0:T(8,128)(2,1)S(1)}) custom-call(s32[9]{0:T(128)S(1)} %stack.142.table, bf16[96,6656]{1,0:T(8,128)(2,1)} %bitcast.1.refs_0_, bf16[96,6656]{1,0:T(8,128)(2,1)} %collective-permute-done.refs_1_, bf16[96,6656]{1,0:T(8,128)(2,1)} %collective-permute-done.1.refs_2_, ...), custom_call_target="tpu_custom_call" | custom-call | bytes 65536 | tf_op jit(solution)/shard_map/weight_pass/pallas_call | solution.py:124
  141.8 1.6 collective-permute-start.15
  145.4 4.1 %collective-permute-done.15 = bf16[2,224,256]{2,1,0:T(8,128)(2,1)S(1)} collective-permute-done((bf16[2,224,256]{2,1,0:T(8,128)(2,1)S(1)}, bf16[2,224,256]{2,1,0:T(8,128)(2,1)S(1)}, u32[]{:S(2)}, u32[]{:S(2)}) %collective-permute-start.15) | collective-permute-done | bytes 229408 | tf_op jit(solution)/shard_map/ppermute | solution.py:36
  149.6 1.6 collective-permute-start.16
  151.2 1.5 add_convert_fusion.1
  153.4 1.5 collective-permute-start.19
  157.4 5.8 %collective-permute-done.16 = bf16[4,224,256]{2,1,0:T(8,128)(2,1)} collective-permute-done((bf16[4,224,256]{2,1,0:T(8,128)(2,1)S(1)}, bf16[4,224,256]{2,1,0:T(8,128)(2,1)}, u32[]{:S(2)}, u32[]{:S(2)}) %collective-permute-start.16) | collective-permute-done | bytes 458784 | tf_op jit(solution)/shard_map/ppermute | solution.py:36
  164.1 3.3 %collective-permute-done.14.refs_4_ = bf16[64,6656]{1,0:T(8,128)(2,1)} collective-permute-done((bf16[64,6656]{1,0:T(8,128)(2,1)}, bf16[64,6656]{1,0:T(8,128)(2,1)}, u32[]{:S(2)}, u32[]{:S(2)}) %collective-permute-start.14) | collective-permute-done | bytes 852000 | tf_op jit(solution)/shard_map/ppermute | solution.py:68
  167.4 2.5 collective-permute-done.20
  171.8 2.1 fusion.12
  173.9 1.5 collective-permute-start.23
  175.4 24.2 %weight_pass.4 = (bf16[256,6656]{1,0:T(8,128)(2,1)S(1)}, f32[4,32,4096]{2,1,0:T(8,128)S(1)}, bf16[4,32,4096]{2,1,0:T(8,128)(2,1)S(1)}) custom-call(s32[9]{0:T(128)S(1)} %stack.142.table, bf16[64,6656]{1,0:T(8,128)(2,1)S(1)} %bitcast.173, bf16[64,6656]{1,0:T(8,128)(2,1)} %collective-permute-done.10.refs_1_, bf16[64,6656]{1,0:T(8,128)(2,1)} %collective-permute-done.11.refs_2_, ...), custom_call_target="tpu_custom_call" | custom-call | bytes 65536 | tf_op jit(solution)/shard_map/weight_pass/pallas_call | solution.py:124
  201.3 2.3 fusion.13
  203.7 1.5 collective-permute-start.24
  207.5 2.5 collective-permute-done.24
  212.2 1.8 fusion
  214.6 2.1 add_convert_fusion.9
  216.8 1.6 collective-permute-start.30
  218.4 1.6 collective-permute-start.31
  220.9 2.8 convolution_multiply_fusion
  223.8 2.8 collective-permute-done.31
  226.6 6.6 %collective-permute-done.28.refs_4_ = bf16[64,6656]{1,0:T(8,128)(2,1)S(1)} collective-permute-done((bf16[64,6656]{1,0:T(8,128)(2,1)}, bf16[64,6656]{1,0:T(8,128)(2,1)S(1)}, u32[]{:S(2)}, u32[]{:S(2)}) %collective-permute-start.28) | collective-permute-done | bytes 852000 | tf_op jit(solution)/shard_map/ppermute | solution.py:68
  234.1 1.5 collective-permute-start.32
  240.8 23.9 %weight_pass.5 = (bf16[256,6656]{1,0:T(8,128)(2,1)S(1)}, f32[4,32,4096]{2,1,0:T(8,128)S(1)}, bf16[4,32,4096]{2,1,0:T(8,128)(2,1)S(1)}) custom-call(s32[9]{0:T(128)S(1)} %stack.142.table, bf16[64,6656]{1,0:T(8,128)(2,1)S(1)} %bitcast.177, bf16[64,6656]{1,0:T(8,128)(2,1)S(1)} %collective-permute-done.21.refs_1_, ...), custom_call_target="tpu_custom_call" | custom-call | bytes 65536 | tf_op jit(solution)/shard_map/weight_pass/pallas_call | solution.py:124
  265.5 1.5 broadcast_select_fusion.3
  269.1 4.5 %factor_gradient.2.refs_3_ = f32[256,6656]{1,0:T(8,128)} custom-call(s32[8]{0:T(128)S(1)} %stack.161.order, bf16[8,112,256]{2,1,0:T(8,128)(2,1)S(1)} %get-tuple-element.185.acts, bf16[384,6656]{1,0:T(8,128)(2,1)S(1)} %bitcast.169, bf16[256,6656]{1,0:T(8,128)(2,1)S(1)} %copy-done.3, bf16[256,6656]{1,0:T(8,128)(2,1)S(1)} %get-tuple-element.188.refs_2_), custom_call_target="tpu_custom_call" | custom-call | bytes 65536 | tf_op jit(solution)/shard_map/factor_gradient/pallas_call | solution.py:173
  273.9 1.5 collective-permute-start.37
  275.5 1.5 collective-permute-start.38
  277.4 2.3 maximum_convert_fusion
  279.8 2.5 collective-permute-done.37
  284.3 1.5 collective-permute-start.40
  285.7 4.5 %factor_gradient.3 = f32[256,6656]{1,0:T(8,128)} custom-call(s32[8]{0:T(128)S(1)} %stack.161.order, bf16[8,112,256]{2,1,0:T(8,128)(2,1)S(1)} %get-tuple-element.185.acts, bf16[384,6656]{1,0:T(8,128)(2,1)S(1)} %bitcast.169, bf16[256,6656]{1,0:T(8,128)(2,1)S(1)} %copy-done.3, ...), custom_call_target="tpu_custom_call", output_to_operand_aliasing={{}: (5, {})} | custom-call | bytes 65536 | tf_op jit(solution)/shard_map/factor_gradient/pallas_call | solution.py:173
  (175 shorter events, 55.0 us)
Async XLA Ops:
  0.6 8.2 %copy-start = (bf16[256,6656]{1,0:T(8,128)(2,1)S(1)}, bf16[256,6656]{1,0:T(8,128)(2,1)}, u32[]{:S(2)}) copy-start(bf16[256,6656]{1,0:T(8,128)(2,1)} %param.9) | copy-start | bytes 10223620
  3.2 58.7 %collective-permute-start = (bf16[96,6656]{1,0:T(8,128)(2,1)}, bf16[96,6656]{1,0:T(8,128)(2,1)}, u32[]{:S(2)}, u32[]{:S(2)}) collective-permute-start(bf16[96,6656]{1,0:T(8,128)(2,1)} %bitcast.1.refs_0_), channel_id=1, source_target_pairs={{0,1},{1,0},{2,3},{3,2},{4,5},{5,4},{6,7},{7,6},{8,9},{9,8},{10,11... | collective-permute-start | bytes 3833864 | tf_op jit(solution)/shard_map/ppermute | solution.py:36
  6.3 58.2 %collective-permute-start.1 = (bf16[96,6656]{1,0:T(8,128)(2,1)}, bf16[96,6656]{1,0:T(8,128)(2,1)}, u32[]{:S(2)}, u32[]{:S(2)}) collective-permute-start(bf16[96,6656]{1,0:T(8,128)(2,1)} %bitcast.1.refs_0_), channel_id=1, source_target_pairs={{0,2},{1,3},{2,0},{3,1},{4,6},{5,7},{6,4},{7,5},{8,10},{9,11},{10,... | collective-permute-start | bytes 3833864 | tf_op jit(solution)/shard_map/ppermute | solution.py:36
  13.4 4.8 %collective-permute-start.2 = (f32[112,256]{1,0:T(8,128)S(1)}, f32[112,256]{1,0:T(8,128)S(1)}, u32[]{:S(2)}, u32[]{:S(2)}) collective-permute-start(f32[112,256]{1,0:T(8,128)S(1)} %dynamic-slice_bitcast_fusion), channel_id=1, source_target_pairs={{0,16},{4,20},{8,24},{12,28},{16,0},{20,4},{24,8},{28,12},{1,17},{... | collective-permute-start | bytes 344072 | tf_op jit(solution)/shard_map/ppermute | solution.py:36
  19.2 4.2 %collective-permute-start.3 = (f32[56,256]{1,0:T(8,128)S(1)}, f32[56,256]{1,0:T(8,128)S(1)}, u32[]{:S(2)}, u32[]{:S(2)}) collective-permute-start(f32[56,256]{1,0:T(8,128)S(1)} %dynamic-slice_bitcast_fusion.1), channel_id=1, source_target_pairs={{0,8},{4,12},{8,0},{12,4},{16,24},{20,28},{24,16},{28,20},{1,9},{5... | collective-permute-start | bytes 172040 | tf_op jit(solution)/shard_map/ppermute | solution.py:36
  23.5 1.3 collective-permute-start.4
  64.5 36.5 %collective-permute-start.5 = (bf16[96,6656]{1,0:T(8,128)(2,1)}, bf16[96,6656]{1,0:T(8,128)(2,1)S(1)}, u32[]{:S(2)}, u32[]{:S(2)}) collective-permute-start(bf16[96,6656]{1,0:T(8,128)(2,1)} %bitcast.1.refs_0_), channel_id=1, source_target_pairs={{1,2},{2,1},{5,6},{6,5},{9,10},{10,9},{13,14},{14,13},{17,18},{18,... | collective-permute-start | bytes 3833864 | tf_op jit(solution)/shard_map/ppermute | solution.py:67
  65.2 35.8 %collective-permute-start.6 = (bf16[96,6656]{1,0:T(8,128)(2,1)}, bf16[96,6656]{1,0:T(8,128)(2,1)S(1)}, u32[]{:S(2)}, u32[]{:S(2)}) collective-permute-start(bf16[96,6656]{1,0:T(8,128)(2,1)} %collective-permute-done.1.refs_2_), channel_id=1, source_target_pairs={{1,0},{2,3},{5,4},{6,7},{9,8},{10,11},{13,12},{14,15},{17,16},{18,... | collective-permute-start | bytes 3833864 | tf_op jit(solution)/shard_map/ppermute | solution.py:68
  75.0 26.0 %all-to-all-start = ((bf16[8,112,512]{2,1,0:T(8,128)(2,1)}), bf16[8,112,512]{2,1,0:T(8,128)(2,1)}, u32[]{:S(2)}, u32[]{:S(2)}) async-start(bf16[8,112,512]{2,1,0:T(8,128)(2,1)} %bitcast_dynamic-update-slice_fusion), calls=%async_computation | async-start | bytes 1835008 | tf_op jit(solution)/shard_map/all_to_all | solution.py:329
  81.5 18.0 %collective-permute-start.7 = (bf16[140,256]{1,0:T(8,128)(2,1)S(1)}, bf16[140,256]{1,0:T(8,128)(2,1)S(1)}, u32[]{:S(2)}, u32[]{:S(2)}) collective-permute-start(bf16[140,256]{1,0:T(8,128)(2,1)S(1)} %pad_maximum_fusion.13), channel_id=1, source_target_pairs={{0,1},{1,0},{2,3},{3,2},{4,5},{5,4},{6,7},{7,6},{8,9},{9,8},{10,11... | collective-permute-start | bytes 215048 | tf_op jit(solution)/shard_map/ppermute | solution.py:36
  84.3 16.6 %collective-permute-start.8 = (bf16[140,256]{1,0:T(8,128)(2,1)S(1)}, bf16[140,256]{1,0:T(8,128)(2,1)}, u32[]{:S(2)}, u32[]{:S(2)}) collective-permute-start(bf16[140,256]{1,0:T(8,128)(2,1)S(1)} %pad_maximum_fusion.13), channel_id=1, source_target_pairs={{0,2},{1,3},{2,0},{3,1},{4,6},{5,7},{6,4},{7,5},{8,10},{9,11},{10,... | collective-permute-start | bytes 215048 | tf_op jit(solution)/shard_map/ppermute | solution.py:36
  85.4 15.5 %collective-permute-start.9 = (bf16[140,256]{1,0:T(8,128)(2,1)S(1)}, bf16[140,256]{1,0:T(8,128)(2,1)}, u32[]{:S(2)}, u32[]{:S(2)}) collective-permute-start(bf16[140,256]{1,0:T(8,128)(2,1)S(1)} %pad_maximum_fusion.13), channel_id=1, source_target_pairs={{0,3},{1,2},{2,1},{3,0},{4,7},{5,6},{6,5},{7,4},{8,11},{9,10},{10,... | collective-permute-start | bytes 215048 | tf_op jit(solution)/shard_map/ppermute | solution.py:36
  101.0 38.4 %collective-permute-start.10 = (bf16[64,6656]{1,0:T(8,128)(2,1)S(1)}, bf16[64,6656]{1,0:T(8,128)(2,1)}, u32[]{:S(2)}, u32[]{:S(2)}) collective-permute-start(bf16[64,6656]{1,0:T(8,128)(2,1)S(1)} %bitcast.170), channel_id=1, source_target_pairs={{0,1},{1,0},{2,3},{3,2},{4,5},{5,4},{6,7},{7,6},{8,9},{9,8},{10,11... | collective-permute-start | bytes 2555912 | tf_op jit(solution)/shard_map/ppermute | solution.py:36
  102.4 37.8 %collective-permute-start.11 = (bf16[64,6656]{1,0:T(8,128)(2,1)S(1)}, bf16[64,6656]{1,0:T(8,128)(2,1)}, u32[]{:S(2)}, u32[]{:S(2)}) collective-permute-start(bf16[64,6656]{1,0:T(8,128)(2,1)S(1)} %bitcast.171), channel_id=1, source_target_pairs={{0,2},{1,3},{2,0},{3,1},{4,6},{5,7},{6,4},{7,5},{8,10},{9,11},{10,... | collective-permute-start | bytes 2555912 | tf_op jit(solution)/shard_map/ppermute | solution.py:36
  108.0 31.4 %collective-permute-start.12 = (bf16[1,224,256]{2,1,0:T(8,128)(2,1)S(1)}, bf16[1,224,256]{2,1,0:T(8,128)(2,1)}, u32[]{:S(2)}, u32[]{:S(2)}) collective-permute-start(bf16[1,224,256]{2,1,0:T(8,128)(2,1)S(1)} %maximum_bitcast_fusion), channel_id=1, source_target_pairs={{0,4},{4,0},{8,12},{12,8},{16,20},{20,16},{24,28},{28,24},{1,5},{5... | collective-permute-start | bytes 344072 | tf_op jit(solution)/shard_map/ppermute | solution.py:36
  140.3 10.9 %collective-permute-start.18 = (bf16[4,48,2048]{2,1,0:T(8,128)(2,1)S(1)}, bf16[4,48,2048]{2,1,0:T(8,128)(2,1)S(1)}, u32[]{:S(2)}, u32[]{:S(2)}) collective-permute-start(bf16[4,48,2048]{2,1,0:T(8,128)(2,1)S(1)} %get-tuple-element.237), channel_id=1, source_target_pairs={{0,4},{4,0},{8,12},{12,8},{16,20},{20,16},{24,28},{28,24},{1,5},{5... | collective-permute-start | bytes 2359304 | tf_op jit(solution)/shard_map/ppermute | solution.py:36
  140.4 10.8 %collective-permute-start.17 = (bf16[4,48,2048]{2,1,0:T(8,128)(2,1)S(1)}, bf16[4,48,2048]{2,1,0:T(8,128)(2,1)S(1)}, u32[]{:S(2)}, u32[]{:S(2)}) collective-permute-start(bf16[4,48,2048]{2,1,0:T(8,128)(2,1)S(1)} %get-tuple-element.238), channel_id=1, source_target_pairs={{0,4},{4,0},{8,12},{12,8},{16,20},{20,16},{24,28},{28,24},{1,5},{5... | collective-permute-start | bytes 2359304 | tf_op jit(solution)/shard_map/ppermute | solution.py:36
  141.8 7.7 %collective-permute-start.15 = (bf16[2,224,256]{2,1,0:T(8,128)(2,1)S(1)}, bf16[2,224,256]{2,1,0:T(8,128)(2,1)S(1)}, u32[]{:S(2)}, u32[]{:S(2)}) collective-permute-start(bf16[2,224,256]{2,1,0:T(8,128)(2,1)S(1)} %pad_maximum_fusion.12), channel_id=1, source_target_pairs={{0,8},{4,12},{8,0},{12,4},{16,24},{20,28},{24,16},{28,20},{1,9},{5... | collective-permute-start | bytes 688136 | tf_op jit(solution)/shard_map/ppermute | solution.py:36
  143.4 19.8 %collective-permute-start.13 = (bf16[64,6656]{1,0:T(8,128)(2,1)S(1)}, bf16[64,6656]{1,0:T(8,128)(2,1)S(1)}, u32[]{:S(2)}, u32[]{:S(2)}) collective-permute-start(bf16[64,6656]{1,0:T(8,128)(2,1)S(1)} %bitcast.172), channel_id=1, source_target_pairs={{1,2},{2,1},{5,6},{6,5},{9,10},{10,9},{13,14},{14,13},{17,18},{18,... | collective-permute-start | bytes 2555912 | tf_op jit(solution)/shard_map/ppermute | solution.py:67
  144.1 23.3 %collective-permute-start.14 = (bf16[64,6656]{1,0:T(8,128)(2,1)}, bf16[64,6656]{1,0:T(8,128)(2,1)}, u32[]{:S(2)}, u32[]{:S(2)}) collective-permute-start(bf16[64,6656]{1,0:T(8,128)(2,1)} %collective-permute-done.11.refs_2_), channel_id=1, source_target_pairs={{1,0},{2,3},{5,4},{6,7},{9,8},{10,11},{13,12},{14,15},{17,16},{18,... | collective-permute-start | bytes 2555912 | tf_op jit(solution)/shard_map/ppermute | solution.py:68
  149.6 13.6 %collective-permute-start.16 = (bf16[4,224,256]{2,1,0:T(8,128)(2,1)S(1)}, bf16[4,224,256]{2,1,0:T(8,128)(2,1)}, u32[]{:S(2)}, u32[]{:S(2)}) collective-permute-start(bf16[4,224,256]{2,1,0:T(8,128)(2,1)S(1)} %pad_maximum_fusion.4), channel_id=1, source_target_pairs={{0,16},{4,20},{8,24},{12,28},{16,0},{20,4},{24,8},{28,12},{1,17},{... | collective-permute-start | bytes 1376264 | tf_op jit(solution)/shard_map/ppermute | solution.py:36
  153.4 14.0 %collective-permute-start.19 = (bf16[2,48,2048]{2,1,0:T(8,128)(2,1)}, bf16[2,48,2048]{2,1,0:T(8,128)(2,1)}, u32[]{:S(2)}, u32[]{:S(2)}) collective-permute-start(bf16[2,48,2048]{2,1,0:T(8,128)(2,1)} %pad_maximum_fusion.5), channel_id=1, source_target_pairs={{0,8},{4,12},{8,0},{12,4},{16,24},{20,28},{24,16},{28,20},{1,9},{5... | collective-permute-start | bytes 1179656 | tf_op jit(solution)/shard_map/ppermute | solution.py:36
  155.7 14.2 %collective-permute-start.20 = (bf16[2,48,2048]{2,1,0:T(8,128)(2,1)}, bf16[2,48,2048]{2,1,0:T(8,128)(2,1)}, u32[]{:S(2)}, u32[]{:S(2)}) collective-permute-start(bf16[2,48,2048]{2,1,0:T(8,128)(2,1)} %pad_maximum_fusion.6), channel_id=1, source_target_pairs={{0,16},{4,20},{8,24},{12,28},{16,0},{20,4},{24,8},{28,12},{1,17},{... | collective-permute-start | bytes 1179656 | tf_op jit(solution)/shard_map/ppermute | solution.py:36
  167.4 8.0 %copy-start.10 = (bf16[64,6656]{1,0:T(8,128)(2,1)S(1)}, bf16[64,6656]{1,0:T(8,128)(2,1)}, u32[]{:S(2)}) copy-start(bf16[64,6656]{1,0:T(8,128)(2,1)} %copy-done.9) | copy-start | bytes 2555908
  169.8 40.1 %collective-permute-start.21 = (bf16[64,6656]{1,0:T(8,128)(2,1)S(1)}, bf16[64,6656]{1,0:T(8,128)(2,1)S(1)}, u32[]{:S(2)}, u32[]{:S(2)}) collective-permute-start(bf16[64,6656]{1,0:T(8,128)(2,1)S(1)} %bitcast.174), channel_id=1, source_target_pairs={{0,1},{1,0},{2,3},{3,2},{4,5},{5,4},{6,7},{7,6},{8,9},{9,8},{10,11... | collective-permute-start | bytes 2555912 | tf_op jit(solution)/shard_map/ppermute | solution.py:36
  170.5 39.4 %collective-permute-start.22 = (bf16[64,6656]{1,0:T(8,128)(2,1)S(1)}, bf16[64,6656]{1,0:T(8,128)(2,1)}, u32[]{:S(2)}, u32[]{:S(2)}) collective-permute-start(bf16[64,6656]{1,0:T(8,128)(2,1)S(1)} %bitcast.175), channel_id=1, source_target_pairs={{0,2},{1,3},{2,0},{3,1},{4,6},{5,7},{6,4},{7,5},{8,10},{9,11},{10,... | collective-permute-start | bytes 2555912 | tf_op jit(solution)/shard_map/ppermute | solution.py:36
  173.9 29.7 %collective-permute-start.23 = (bf16[1,48,2048]{2,1,0:T(8,128)(2,1)S(1)}, bf16[1,48,2048]{2,1,0:T(8,128)(2,1)S(1)}, u32[]{:S(2)}, u32[]{:S(2)}) collective-permute-start(bf16[1,48,2048]{2,1,0:T(8,128)(2,1)S(1)} %get-tuple-element.263), channel_id=1, source_target_pairs={{0,16},{4,20},{8,24},{12,28},{16,0},{20,4},{24,8},{28,12},{1,17},{... | collective-permute-start | bytes 589832 | tf_op jit(solution)/shard_map/ppermute | solution.py:36
  200.7 9.2 %collective-permute-start.25 = (bf16[4,32,2048]{2,1,0:T(8,128)(2,1)}, bf16[4,32,2048]{2,1,0:T(8,128)(2,1)}, u32[]{:S(2)}, u32[]{:S(2)}) collective-permute-start(bf16[4,32,2048]{2,1,0:T(8,128)(2,1)} %get-tuple-element.244), channel_id=1, source_target_pairs={{0,4},{4,0},{8,12},{12,8},{16,20},{20,16},{24,28},{28,24},{1,5},{5... | collective-permute-start | bytes 1572872 | tf_op jit(solution)/shard_map/ppermute | solution.py:36
  200.7 9.2 %collective-permute-start.26 = (bf16[4,32,2048]{2,1,0:T(8,128)(2,1)}, bf16[4,32,2048]{2,1,0:T(8,128)(2,1)}, u32[]{:S(2)}, u32[]{:S(2)}) collective-permute-start(bf16[4,32,2048]{2,1,0:T(8,128)(2,1)} %get-tuple-element.243), channel_id=1, source_target_pairs={{0,4},{4,0},{8,12},{12,8},{16,20},{20,16},{24,28},{28,24},{1,5},{5... | collective-permute-start | bytes 1572872 | tf_op jit(solution)/shard_map/ppermute | solution.py:36
  203.7 6.3 %collective-permute-start.24 = (bf16[1,48,2048]{2,1,0:T(8,128)(2,1)S(1)}, bf16[1,48,2048]{2,1,0:T(8,128)(2,1)S(1)}, u32[]{:S(2)}, u32[]{:S(2)}) collective-permute-start(bf16[1,48,2048]{2,1,0:T(8,128)(2,1)S(1)} %get-tuple-element.261), channel_id=1, source_target_pairs={{0,8},{4,12},{8,0},{12,4},{16,24},{20,28},{24,16},{28,20},{1,9},{5... | collective-permute-start | bytes 589832 | tf_op jit(solution)/shard_map/ppermute | solution.py:36
  210.0 16.6 %collective-permute-start.27 = (bf16[64,6656]{1,0:T(8,128)(2,1)S(1)}, bf16[64,6656]{1,0:T(8,128)(2,1)S(1)}, u32[]{:S(2)}, u32[]{:S(2)}) collective-permute-start(bf16[64,6656]{1,0:T(8,128)(2,1)S(1)} %bitcast.176), channel_id=1, source_target_pairs={{1,2},{2,1},{5,6},{6,5},{9,10},{10,9},{13,14},{14,13},{17,18},{18,... | collective-permute-start | bytes 2555912 | tf_op jit(solution)/shard_map/ppermute | solution.py:67
  210.9 22.3 %collective-permute-start.28 = (bf16[64,6656]{1,0:T(8,128)(2,1)}, bf16[64,6656]{1,0:T(8,128)(2,1)S(1)}, u32[]{:S(2)}, u32[]{:S(2)}) collective-permute-start(bf16[64,6656]{1,0:T(8,128)(2,1)} %collective-permute-done.22.refs_2_), channel_id=1, source_target_pairs={{1,0},{2,3},{5,4},{6,7},{9,8},{10,11},{13,12},{14,15},{17,16},{18,... | collective-permute-start | bytes 2555912 | tf_op jit(solution)/shard_map/ppermute | solution.py:68
  214.0 9.7 %collective-permute-start.29 = (bf16[512,256]{1,0:T(8,128)(2,1)S(1)}, bf16[512,256]{1,0:T(8,128)(2,1)S(1)}, u32[]{:S(2)}, u32[]{:S(2)}) collective-permute-start(bf16[512,256]{1,0:T(8,128)(2,1)S(1)} %fusion), channel_id=1, source_target_pairs={{0,16},{4,20},{8,24},{12,28},{16,0},{20,4},{24,8},{28,12},{1,17},{... | collective-permute-start | bytes 786440 | tf_op jit(solution)/shard_map/ppermute | solution.py:36
  216.8 7.0 %collective-permute-start.30 = (bf16[2,32,2048]{2,1,0:T(8,128)(2,1)S(1)}, bf16[2,32,2048]{2,1,0:T(8,128)(2,1)S(1)}, u32[]{:S(2)}, u32[]{:S(2)}) collective-permute-start(bf16[2,32,2048]{2,1,0:T(8,128)(2,1)S(1)} %pad_maximum_fusion.8), channel_id=1, source_target_pairs={{0,8},{4,12},{8,0},{12,4},{16,24},{20,28},{24,16},{28,20},{1,9},{5... | collective-permute-start | bytes 786440 | tf_op jit(solution)/shard_map/ppermute | solution.py:36
  218.4 8.2 %collective-permute-start.31 = (bf16[2,32,2048]{2,1,0:T(8,128)(2,1)S(1)}, bf16[2,32,2048]{2,1,0:T(8,128)(2,1)S(1)}, u32[]{:S(2)}, u32[]{:S(2)}) collective-permute-start(bf16[2,32,2048]{2,1,0:T(8,128)(2,1)S(1)} %pad_maximum_fusion.9), channel_id=1, source_target_pairs={{0,16},{4,20},{8,24},{12,28},{16,0},{20,4},{24,8},{28,12},{1,17},{... | collective-permute-start | bytes 786440 | tf_op jit(solution)/shard_map/ppermute | solution.py:36
  226.6 11.3 %copy-start.5 = (bf16[64,6656]{1,0:T(8,128)(2,1)}, bf16[64,6656]{1,0:T(8,128)(2,1)S(1)}, u32[]{:S(2)}) copy-start(bf16[64,6656]{1,0:T(8,128)(2,1)S(1)} %collective-permute-done.27.refs_3_) | copy-start | bytes 2555908
  234.1 30.7 %collective-permute-start.32 = (bf16[1024,256]{1,0:T(8,128)(2,1)}, bf16[1024,256]{1,0:T(8,128)(2,1)}, u32[]{:S(2)}, u32[]{:S(2)}) collective-permute-start(bf16[1024,256]{1,0:T(8,128)(2,1)} %pad_maximum_fusion.2), channel_id=1, source_target_pairs={{0,8},{4,12},{8,0},{12,4},{16,24},{20,28},{24,16},{28,20},{1,9},{5... | collective-permute-start | bytes 1572872 | tf_op jit(solution)/shard_map/ppermute | solution.py:36
  235.6 32.4 %slice-start = ((s8[5111808]{0:T(1024)(128)(4,1)}), s8[917504]{0:T(1024)(128)(4,1)S(1)}, s32[]{:S(2)}) async-start(s8[5111808]{0:T(1024)(128)(4,1)} %bitcast.168), calls=%async_computation.1 | async-start | bytes 1835008
  236.4 28.3 %collective-permute-start.33 = (bf16[1,32,2048]{2,1,0:T(8,128)(2,1)}, bf16[1,32,2048]{2,1,0:T(8,128)(2,1)S(1)}, u32[]{:S(2)}, u32[]{:S(2)}) collective-permute-start(bf16[1,32,2048]{2,1,0:T(8,128)(2,1)} %get-tuple-element.267), channel_id=1, source_target_pairs={{0,16},{4,20},{8,24},{12,28},{16,0},{20,4},{24,8},{28,12},{1,17},{... | collective-permute-start | bytes 393224 | tf_op jit(solution)/shard_map/ppermute | solution.py:36
  237.8 26.9 %collective-permute-start.34 = (bf16[1,32,2048]{2,1,0:T(8,128)(2,1)}, bf16[1,32,2048]{2,1,0:T(8,128)(2,1)S(1)}, u32[]{:S(2)}, u32[]{:S(2)}) collective-permute-start(bf16[1,32,2048]{2,1,0:T(8,128)(2,1)} %get-tuple-element.265), channel_id=1, source_target_pairs={{0,8},{4,12},{8,0},{12,4},{16,24},{20,28},{24,16},{28,20},{1,9},{5... | collective-permute-start | bytes 393224 | tf_op jit(solution)/shard_map/ppermute | solution.py:36
  240.8 27.2 %slice-start.1 = ((s8[5111808]{0:T(1024)(128)(4,1)}), s8[4194304]{0:T(1024)(128)(4,1)S(1)}, s32[]{:S(2)}) async-start(s8[5111808]{0:T(1024)(128)(4,1)} %bitcast.168), calls=%async_computation.2 | async-start | bytes 8388608
  264.9 8.7 %collective-permute-start.36 = (bf16[4,32,2048]{2,1,0:T(8,128)(2,1)S(1)}, bf16[4,32,2048]{2,1,0:T(8,128)(2,1)S(1)}, u32[]{:S(2)}, u32[]{:S(2)}) collective-permute-start(bf16[4,32,2048]{2,1,0:T(8,128)(2,1)S(1)} %get-tuple-element.241), channel_id=1, source_target_pairs={{0,4},{4,0},{8,12},{12,8},{16,20},{20,16},{24,28},{28,24},{1,5},{5... | collective-permute-start | bytes 1572872 | tf_op jit(solution)/shard_map/ppermute | solution.py:36
  265.0 8.6 %collective-permute-start.35 = (bf16[4,32,2048]{2,1,0:T(8,128)(2,1)S(1)}, bf16[4,32,2048]{2,1,0:T(8,128)(2,1)S(1)}, u32[]{:S(2)}, u32[]{:S(2)}) collective-permute-start(bf16[4,32,2048]{2,1,0:T(8,128)(2,1)S(1)} %get-tuple-element.242), channel_id=1, source_target_pairs={{0,4},{4,0},{8,12},{12,8},{16,20},{20,16},{24,28},{28,24},{1,5},{5... | collective-permute-start | bytes 1572872 | tf_op jit(solution)/shard_map/ppermute | solution.py:36
  267.1 9.9 %collective-permute-start.39 = (bf16[2048,256]{1,0:T(8,128)(2,1)S(1)}, bf16[2048,256]{1,0:T(8,128)(2,1)S(1)}, u32[]{:S(2)}, u32[]{:S(2)}) collective-permute-start(bf16[2048,256]{1,0:T(8,128)(2,1)S(1)} %pad_maximum_fusion), channel_id=1, source_target_pairs={{0,4},{4,0},{8,12},{12,8},{16,20},{20,16},{24,28},{28,24},{1,5},{5... | collective-permute-start | bytes 3145736 | tf_op jit(solution)/shard_map/ppermute | solution.py:36
  273.9 8.3 %collective-permute-start.37 = (bf16[2,32,2048]{2,1,0:T(8,128)(2,1)S(1)}, bf16[2,32,2048]{2,1,0:T(8,128)(2,1)S(1)}, u32[]{:S(2)}, u32[]{:S(2)}) collective-permute-start(bf16[2,32,2048]{2,1,0:T(8,128)(2,1)S(1)} %pad_maximum_fusion.10), channel_id=1, source_target_pairs={{0,8},{4,12},{8,0},{12,4},{16,24},{20,28},{24,16},{28,20},{1,9},{5... | collective-permute-start | bytes 786440 | tf_op jit(solution)/shard_map/ppermute | solution.py:36
  275.5 8.1 %collective-permute-start.38 = (bf16[2,32,2048]{2,1,0:T(8,128)(2,1)S(1)}, bf16[2,32,2048]{2,1,0:T(8,128)(2,1)S(1)}, u32[]{:S(2)}, u32[]{:S(2)}) collective-permute-start(bf16[2,32,2048]{2,1,0:T(8,128)(2,1)S(1)} %pad_maximum_fusion.11), channel_id=1, source_target_pairs={{0,16},{4,20},{8,24},{12,28},{16,0},{20,4},{24,8},{28,12},{1,17},{... | collective-permute-start | bytes 786440 | tf_op jit(solution)/shard_map/ppermute | solution.py:36
  283.6 6.6 %collective-permute-start.41 = (bf16[1,32,2048]{2,1,0:T(8,128)(2,1)S(1)}, bf16[1,32,2048]{2,1,0:T(8,128)(2,1)S(1)}, u32[]{:S(2)}, u32[]{:S(2)}) collective-permute-start(bf16[1,32,2048]{2,1,0:T(8,128)(2,1)S(1)} %fusion.17), channel_id=1, source_target_pairs={{0,8},{4,12},{8,0},{12,4},{16,24},{20,28},{24,16},{28,20},{1,9},{5... | collective-permute-start | bytes 393224 | tf_op jit(solution)/shard_map/ppermute | solution.py:36
  284.3 6.0 %collective-permute-start.40 = (bf16[1,32,2048]{2,1,0:T(8,128)(2,1)S(1)}, bf16[1,32,2048]{2,1,0:T(8,128)(2,1)S(1)}, u32[]{:S(2)}, u32[]{:S(2)}) collective-permute-start(bf16[1,32,2048]{2,1,0:T(8,128)(2,1)S(1)} %fusion.16), channel_id=1, source_target_pairs={{0,16},{4,20},{8,24},{12,28},{16,0},{20,4},{24,8},{28,12},{1,17},{... | collective-permute-start | bytes 393224 | tf_op jit(solution)/shard_map/ppermute | solution.py:36
  (23 other events, 72.6 us)

commit v12 on v11

--- a/solution.py
+++ b/solution.py
@@ -379,6 +379,8 @@
             step(2 if i == 1 else 1)
             if i == 1 and count > 2:
                 sum_hop(0)
+            if i + 1 == count:
+                step()
         middle[i], onward[i], blocks, grad_out, small, sums = hold(
             middle[i], onward[i], blocks, grad_out, small, sums
         )
@@ -387,7 +389,6 @@
             step(1 if i == 0 else 0)
             prepare()
             run_pass(i)
-    step()
     run_pass(count - 1)
     small, sums = hold(small, sums)
     columns_step = max(128 * c for c in range(1, 14) if depth % (128 * c) == 0)

time: 294 us -> 292 us (level)
    ppermute x36, waiting for transfers between devices: 82 us -> 88.6 us  [swap(): return lax.ppermute(value, axis, [(i, i ^ bit) for i in range(size)])]
    ppermute x3, waiting for transfers between devices: 9.85 us -> 4.01 us  [phase_b(): lax.ppermute(far, axis, [(1, 0), (2, 3)])]
    another operation x12 -> x10, other arithmetic: 7.76 us -> 5.63 us  [scatter_send(): away = jnp.stack([part[p | bit].astype(jnp.bfloat16) for p in stay[-1]])]
    unnamed x64 -> x56, local copies, waits for them, and re-layouts: 13.1 us -> 12.3 us
  transfers between devices with their start and end apart: 43 -> 43, of which waited for: 17 -> 19; matrix products, arithmetic and copies ran while one was open for 17% -> 17% of each run, Pallas kernels for 30% -> 22%
where the time goes in v12:
time: 292 us; the launch traced here: 290 us
  waiting for transfers between devices  92.6 us (32%)
  Pallas kernels  88.3 us (30%)
  starting transfers between devices  49.5 us (17%)
  local copies, waits for them, and re-layouts  26.6 us (9%)
  other arithmetic  22.6 us (8%)
  matrix products  9.54 us (3%)
    ppermute x36, waiting for transfers between devices, swap(): return lax.ppermute(value, axis, [(i, i ^ bit) for i in range(size)])  88.6 us
    pallas_call x3, Pallas kernels, weight_pass(): pl.pallas_call(functools.partial(pass_kernel, sources=len(sources), owner...  79.3 us
    ppermute x36, starting transfers between devices, swap(): return lax.ppermute(value, axis, [(i, i ^ bit) for i in range(size)])  39 us
    unnamed x56, local copies, waits for them, and re-layouts  12.3 us
    pallas_call x2, Pallas kernels, factor_gradient(): pl.pallas_call(functools.partial(factor_kernel, pieces=pieces, scale=scal...  9.02 us
    slice x3, local copies, waits for them, and re-layouts, block_of(): return own[:, start:start + rows].reshape(share * rows, depth)  5.95 us
  transfers between devices with their start and end apart: 43, of which 19 were waited for; matrix products, arithmetic and copies ran while one was open for 17% of the time, Pallas kernels for 22%

profile of v12, /device:TPU:0, one launch (start us, length us, event | category | flops | bytes accessed | tf_op | source)
XLA Modules:
  0.0 290.4 jit_solution(7277193315531433803)
XLA Ops:
  0.6 2.6 slice.336
  3.2 3.0 %collective-permute-start = (bf16[96,6656]{1,0:T(8,128)(2,1)}, bf16[96,6656]{1,0:T(8,128)(2,1)}, u32[]{:S(2)}, u32[]{:S(2)}) collective-permute-start(bf16[96,6656]{1,0:T(8,128)(2,1)} %bitcast.1.refs_0_), channel_id=1, source_target_pairs={{0,1},{1,0},{2,3},{3,2},{4,5},{5,4},{6,7},{7,6},{8,9},{9,8},{10,11... | collective-permute-start | bytes 3833864 | tf_op jit(solution)/shard_map/ppermute | solution.py:36
  6.3 2.6 collective-permute-start.1
  8.9 3.7 %fusion.21 = f32[224,256]{1,0:T(8,128)} fusion(bf16[224,6656]{1,0:T(8,128)(2,1)} %param.6, bf16[256,6656]{1,0:T(8,128)(2,1)S(1)} %copy-done), kind=kOutput, calls=%fused_computation.112 | convolution fusion | flops 763363328 | bytes 6619136 | tf_op jit(solution)/shard_map/dot_general | solution.py:18
  13.4 1.5 collective-permute-start.2
  15.0 3.3 %collective-permute-done.2 = f32[112,256]{1,0:T(8,128)S(1)} collective-permute-done((f32[112,256]{1,0:T(8,128)S(1)}, f32[112,256]{1,0:T(8,128)S(1)}, u32[]{:S(2)}, u32[]{:S(2)}) %collective-permute-start.2) | collective-permute-done | bytes 114720 | tf_op jit(solution)/shard_map/ppermute | solution.py:36
  19.2 1.6 collective-permute-start.3
  20.7 2.7 collective-permute-done.3
  24.8 37.1 %collective-permute-done.refs_1_ = bf16[96,6656]{1,0:T(8,128)(2,1)} collective-permute-done((bf16[96,6656]{1,0:T(8,128)(2,1)}, bf16[96,6656]{1,0:T(8,128)(2,1)}, u32[]{:S(2)}, u32[]{:S(2)}) %collective-permute-start) | collective-permute-done | bytes 1277984 | tf_op jit(solution)/shard_map/ppermute | solution.py:36
  61.9 2.6 collective-permute-done.1.refs_2_
  66.5 1.5 copy.63
  68.0 1.7 fusion.20
  75.0 4.2 %all-to-all-start = ((bf16[8,112,512]{2,1,0:T(8,128)(2,1)}), bf16[8,112,512]{2,1,0:T(8,128)(2,1)}, u32[]{:S(2)}, u32[]{:S(2)}) async-start(bf16[8,112,512]{2,1,0:T(8,128)(2,1)} %bitcast_dynamic-update-slice_fusion), calls=%async_computation | async-start | bytes 1835008 | tf_op jit(solution)/shard_map/all_to_all | solution.py:329
  79.2 2.3 convolution_convert_fusion
  81.6 2.8 collective-permute-start.7
  88.0 11.5 %collective-permute-done.7 = bf16[140,256]{1,0:T(8,128)(2,1)S(1)} collective-permute-done((bf16[140,256]{1,0:T(8,128)(2,1)S(1)}, bf16[140,256]{1,0:T(8,128)(2,1)S(1)}, u32[]{:S(2)}, u32[]{:S(2)}) %collective-permute-start.7) | collective-permute-done | bytes 71712 | tf_op jit(solution)/shard_map/ppermute | solution.py:36
  99.5 1.4 collective-permute-done.8
  101.0 1.4 collective-permute-start.10
  108.1 31.2 %weight_pass.3 = (bf16[384,6656]{1,0:T(8,128)(2,1)}, f32[4,48,4096]{2,1,0:T(8,128)S(1)}, bf16[4,48,4096]{2,1,0:T(8,128)(2,1)S(1)}) custom-call(s32[9]{0:T(128)S(1)} %stack.138.table, bf16[96,6656]{1,0:T(8,128)(2,1)} %bitcast.1.refs_0_, bf16[96,6656]{1,0:T(8,128)(2,1)} %collective-permute-done.refs_1_, bf16[96,6656]{1,0:T(8,128)(2,1)} %collective-permute-done.1.refs_2_, ...), custom_call_target="tpu_custom_call" | custom-call | bytes 65536 | tf_op jit(solution)/shard_map/weight_pass/pallas_call | solution.py:124
  141.8 1.6 collective-permute-start.15
  144.1 1.5 collective-permute-start.14
  145.6 3.9 %collective-permute-done.15 = bf16[2,224,256]{2,1,0:T(8,128)(2,1)S(1)} collective-permute-done((bf16[2,224,256]{2,1,0:T(8,128)(2,1)S(1)}, bf16[2,224,256]{2,1,0:T(8,128)(2,1)S(1)}, u32[]{:S(2)}, u32[]{:S(2)}) %collective-permute-start.15) | collective-permute-done | bytes 229408 | tf_op jit(solution)/shard_map/ppermute | solution.py:36
  149.6 1.6 collective-permute-start.16
  153.3 1.5 collective-permute-start.19
  156.2 2.2 slice.348
  158.4 4.9 %collective-permute-done.16 = bf16[4,224,256]{2,1,0:T(8,128)(2,1)} collective-permute-done((bf16[4,224,256]{2,1,0:T(8,128)(2,1)S(1)}, bf16[4,224,256]{2,1,0:T(8,128)(2,1)}, u32[]{:S(2)}, u32[]{:S(2)}) %collective-permute-start.16) | collective-permute-done | bytes 458784 | tf_op jit(solution)/shard_map/ppermute | solution.py:36
  163.2 4.0 %collective-permute-done.14.refs_4_ = bf16[64,6656]{1,0:T(8,128)(2,1)S(1)} collective-permute-done((bf16[64,6656]{1,0:T(8,128)(2,1)}, bf16[64,6656]{1,0:T(8,128)(2,1)S(1)}, u32[]{:S(2)}, u32[]{:S(2)}) %collective-permute-start.14) | collective-permute-done | bytes 852000 | tf_op jit(solution)/shard_map/ppermute | solution.py:68
  167.2 2.6 collective-permute-done.20
  171.8 2.0 fusion.10
  173.8 1.5 collective-permute-start.23
  178.8 23.9 %weight_pass.4 = (bf16[256,6656]{1,0:T(8,128)(2,1)S(1)}, f32[4,32,4096]{2,1,0:T(8,128)S(1)}, bf16[4,32,4096]{2,1,0:T(8,128)(2,1)S(1)}) custom-call(s32[9]{0:T(128)S(1)} %stack.138.table, bf16[64,6656]{1,0:T(8,128)(2,1)S(1)} %bitcast.153, bf16[64,6656]{1,0:T(8,128)(2,1)} %collective-permute-done.10.refs_1_, bf16[64,6656]{1,0:T(8,128)(2,1)} %collective-permute-done.11.refs_2_, ...), custom_call_target="tpu_custom_call" | custom-call | bytes 65536 | tf_op jit(solution)/shard_map/weight_pass/pallas_call | solution.py:124
  204.4 1.9 fusion.11
  206.3 1.5 collective-permute-start.24
  210.8 1.9 reshape.121
  215.5 1.8 fusion
  219.1 1.6 collective-permute-start.32
  220.8 1.5 collective-permute-start.31
  223.3 3.3 %collective-permute-done.29 = bf16[512,256]{1,0:T(8,128)(2,1)S(1)} collective-permute-done((bf16[512,256]{1,0:T(8,128)(2,1)S(1)}, bf16[512,256]{1,0:T(8,128)(2,1)S(1)}, u32[]{:S(2)}, u32[]{:S(2)}) %collective-permute-start.29) | collective-permute-done | bytes 262176 | tf_op jit(solution)/shard_map/ppermute | solution.py:36
  226.7 1.5 collective-permute-start.30
  228.3 2.2 collective-permute-done.32
  230.5 2.0 add_convert_fusion.8
  234.3 1.7 convolution_multiply_fusion
  237.4 4.3 %collective-permute-done.34 = bf16[1,32,2048]{2,1,0:T(8,128)(2,1)S(1)} collective-permute-done((bf16[1,32,2048]{2,1,0:T(8,128)(2,1)S(1)}, bf16[1,32,2048]{2,1,0:T(8,128)(2,1)S(1)}, u32[]{:S(2)}, u32[]{:S(2)}) %collective-permute-start.34) | collective-permute-done | bytes 131104 | tf_op jit(solution)/shard_map/ppermute | solution.py:36
  241.8 24.2 %weight_pass.5 = (bf16[256,6656]{1,0:T(8,128)(2,1)S(1)}, f32[4,32,4096]{2,1,0:T(8,128)S(1)}, bf16[4,32,4096]{2,1,0:T(8,128)(2,1)S(1)}) custom-call(s32[9]{0:T(128)S(1)} %stack.138.table, bf16[64,6656]{1,0:T(8,128)(2,1)} %bitcast.31.refs_0_, bf16[64,6656]{1,0:T(8,128)(2,1)} %collective-permute-done.21.refs_1_, ...), custom_call_target="tpu_custom_call" | custom-call | bytes 65536 | tf_op jit(solution)/shard_map/weight_pass/pallas_call | solution.py:124
  267.8 4.5 %factor_gradient.2.refs_3_ = f32[256,6656]{1,0:T(8,128)} custom-call(s32[8]{0:T(128)S(1)} %stack.155.order, bf16[8,112,256]{2,1,0:T(8,128)(2,1)S(1)} %copy-done.2, bf16[384,6656]{1,0:T(8,128)(2,1)S(1)} %bitcast.149, bf16[256,6656]{1,0:T(8,128)(2,1)S(1)} %get-tuple-element.183.refs_1_, bf16[256,6656]{1,0:T(8,128)(2,1)S(1)} %get-tuple-element.184.refs_2_), custom_call_target="tpu_custom_call" | custom-call | bytes 65536 | tf_op jit(solution)/shard_map/factor_gradient/pallas_call | solution.py:173
  275.1 2.3 maximum_convert_fusion
  277.4 3.6 %collective-permute-done.37 = bf16[2,32,2048]{2,1,0:T(8,128)(2,1)S(1)} collective-permute-done((bf16[2,32,2048]{2,1,0:T(8,128)(2,1)S(1)}, bf16[2,32,2048]{2,1,0:T(8,128)(2,1)S(1)}, u32[]{:S(2)}, u32[]{:S(2)}) %collective-permute-start.37) | collective-permute-done | bytes 262176 | tf_op jit(solution)/shard_map/ppermute | solution.py:36
  283.5 4.5 %factor_gradient.3 = f32[256,6656]{1,0:T(8,128)} custom-call(s32[8]{0:T(128)S(1)} %stack.155.order, bf16[8,112,256]{2,1,0:T(8,128)(2,1)S(1)} %copy-done.2, bf16[384,6656]{1,0:T(8,128)(2,1)S(1)} %bitcast.149, bf16[256,6656]{1,0:T(8,128)(2,1)S(1)} %get-tuple-element.183.refs_1_, ...), custom_call_target="tpu_custom_call", output_to_operand_aliasing={{}: (5, {})} | custom-call | bytes 65536 | tf_op jit(solution)/shard_map/factor_gradient/pallas_call | solution.py:173
  (166 shorter events, 54.9 us)
Async XLA Ops:
  0.6 8.2 %copy-start = (bf16[256,6656]{1,0:T(8,128)(2,1)S(1)}, bf16[256,6656]{1,0:T(8,128)(2,1)}, u32[]{:S(2)}) copy-start(bf16[256,6656]{1,0:T(8,128)(2,1)} %param.9) | copy-start | bytes 10223620
  3.2 58.7 %collective-permute-start = (bf16[96,6656]{1,0:T(8,128)(2,1)}, bf16[96,6656]{1,0:T(8,128)(2,1)}, u32[]{:S(2)}, u32[]{:S(2)}) collective-permute-start(bf16[96,6656]{1,0:T(8,128)(2,1)} %bitcast.1.refs_0_), channel_id=1, source_target_pairs={{0,1},{1,0},{2,3},{3,2},{4,5},{5,4},{6,7},{7,6},{8,9},{9,8},{10,11... | collective-permute-start | bytes 3833864 | tf_op jit(solution)/shard_map/ppermute | solution.py:36
  6.3 58.2 %collective-permute-start.1 = (bf16[96,6656]{1,0:T(8,128)(2,1)}, bf16[96,6656]{1,0:T(8,128)(2,1)}, u32[]{:S(2)}, u32[]{:S(2)}) collective-permute-start(bf16[96,6656]{1,0:T(8,128)(2,1)} %bitcast.1.refs_0_), channel_id=1, source_target_pairs={{0,2},{1,3},{2,0},{3,1},{4,6},{5,7},{6,4},{7,5},{8,10},{9,11},{10,... | collective-permute-start | bytes 3833864 | tf_op jit(solution)/shard_map/ppermute | solution.py:36
  13.4 4.8 %collective-permute-start.2 = (f32[112,256]{1,0:T(8,128)S(1)}, f32[112,256]{1,0:T(8,128)S(1)}, u32[]{:S(2)}, u32[]{:S(2)}) collective-permute-start(f32[112,256]{1,0:T(8,128)S(1)} %dynamic-slice_bitcast_fusion), channel_id=1, source_target_pairs={{0,16},{4,20},{8,24},{12,28},{16,0},{20,4},{24,8},{28,12},{1,17},{... | collective-permute-start | bytes 344072 | tf_op jit(solution)/shard_map/ppermute | solution.py:36
  19.2 4.2 %collective-permute-start.3 = (f32[56,256]{1,0:T(8,128)S(1)}, f32[56,256]{1,0:T(8,128)S(1)}, u32[]{:S(2)}, u32[]{:S(2)}) collective-permute-start(f32[56,256]{1,0:T(8,128)S(1)} %dynamic-slice_bitcast_fusion.1), channel_id=1, source_target_pairs={{0,8},{4,12},{8,0},{12,4},{16,24},{20,28},{24,16},{28,20},{1,9},{5... | collective-permute-start | bytes 172040 | tf_op jit(solution)/shard_map/ppermute | solution.py:36
  23.5 1.3 collective-permute-start.4
  64.5 36.5 %collective-permute-start.5 = (bf16[96,6656]{1,0:T(8,128)(2,1)}, bf16[96,6656]{1,0:T(8,128)(2,1)S(1)}, u32[]{:S(2)}, u32[]{:S(2)}) collective-permute-start(bf16[96,6656]{1,0:T(8,128)(2,1)} %bitcast.1.refs_0_), channel_id=1, source_target_pairs={{1,2},{2,1},{5,6},{6,5},{9,10},{10,9},{13,14},{14,13},{17,18},{18,... | collective-permute-start | bytes 3833864 | tf_op jit(solution)/shard_map/ppermute | solution.py:67
  65.2 35.8 %collective-permute-start.6 = (bf16[96,6656]{1,0:T(8,128)(2,1)}, bf16[96,6656]{1,0:T(8,128)(2,1)S(1)}, u32[]{:S(2)}, u32[]{:S(2)}) collective-permute-start(bf16[96,6656]{1,0:T(8,128)(2,1)} %collective-permute-done.1.refs_2_), channel_id=1, source_target_pairs={{1,0},{2,3},{5,4},{6,7},{9,8},{10,11},{13,12},{14,15},{17,16},{18,... | collective-permute-start | bytes 3833864 | tf_op jit(solution)/shard_map/ppermute | solution.py:68
  75.0 26.0 %all-to-all-start = ((bf16[8,112,512]{2,1,0:T(8,128)(2,1)}), bf16[8,112,512]{2,1,0:T(8,128)(2,1)}, u32[]{:S(2)}, u32[]{:S(2)}) async-start(bf16[8,112,512]{2,1,0:T(8,128)(2,1)} %bitcast_dynamic-update-slice_fusion), calls=%async_computation | async-start | bytes 1835008 | tf_op jit(solution)/shard_map/all_to_all | solution.py:329
  81.6 18.0 %collective-permute-start.7 = (bf16[140,256]{1,0:T(8,128)(2,1)S(1)}, bf16[140,256]{1,0:T(8,128)(2,1)S(1)}, u32[]{:S(2)}, u32[]{:S(2)}) collective-permute-start(bf16[140,256]{1,0:T(8,128)(2,1)S(1)} %pad_maximum_fusion.13), channel_id=1, source_target_pairs={{0,1},{1,0},{2,3},{3,2},{4,5},{5,4},{6,7},{7,6},{8,9},{9,8},{10,11... | collective-permute-start | bytes 215048 | tf_op jit(solution)/shard_map/ppermute | solution.py:36
  84.4 16.6 %collective-permute-start.8 = (bf16[140,256]{1,0:T(8,128)(2,1)S(1)}, bf16[140,256]{1,0:T(8,128)(2,1)}, u32[]{:S(2)}, u32[]{:S(2)}) collective-permute-start(bf16[140,256]{1,0:T(8,128)(2,1)S(1)} %pad_maximum_fusion.13), channel_id=1, source_target_pairs={{0,2},{1,3},{2,0},{3,1},{4,6},{5,7},{6,4},{7,5},{8,10},{9,11},{10,... | collective-permute-start | bytes 215048 | tf_op jit(solution)/shard_map/ppermute | solution.py:36
  85.4 15.5 %collective-permute-start.9 = (bf16[140,256]{1,0:T(8,128)(2,1)S(1)}, bf16[140,256]{1,0:T(8,128)(2,1)}, u32[]{:S(2)}, u32[]{:S(2)}) collective-permute-start(bf16[140,256]{1,0:T(8,128)(2,1)S(1)} %pad_maximum_fusion.13), channel_id=1, source_target_pairs={{0,3},{1,2},{2,1},{3,0},{4,7},{5,6},{6,5},{7,4},{8,11},{9,10},{10,... | collective-permute-start | bytes 215048 | tf_op jit(solution)/shard_map/ppermute | solution.py:36
  88.0 55.4 %copy-start.3 = (bf16[2,32,6656]{2,1,0:T(8,128)(2,1)}, bf16[2,32,6656]{2,1,0:T(8,128)(2,1)S(1)}, u32[]{:S(2)}) copy-start(bf16[2,32,6656]{2,1,0:T(8,128)(2,1)S(1)} %slice.337) | copy-start | bytes 2555908
  101.0 38.4 %collective-permute-start.10 = (bf16[64,6656]{1,0:T(8,128)(2,1)S(1)}, bf16[64,6656]{1,0:T(8,128)(2,1)}, u32[]{:S(2)}, u32[]{:S(2)}) collective-permute-start(bf16[64,6656]{1,0:T(8,128)(2,1)S(1)} %bitcast.150), channel_id=1, source_target_pairs={{0,1},{1,0},{2,3},{3,2},{4,5},{5,4},{6,7},{7,6},{8,9},{9,8},{10,11... | collective-permute-start | bytes 2555912 | tf_op jit(solution)/shard_map/ppermute | solution.py:36
  102.4 37.8 %collective-permute-start.11 = (bf16[64,6656]{1,0:T(8,128)(2,1)S(1)}, bf16[64,6656]{1,0:T(8,128)(2,1)}, u32[]{:S(2)}, u32[]{:S(2)}) collective-permute-start(bf16[64,6656]{1,0:T(8,128)(2,1)S(1)} %bitcast.151), channel_id=1, source_target_pairs={{0,2},{1,3},{2,0},{3,1},{4,6},{5,7},{6,4},{7,5},{8,10},{9,11},{10,... | collective-permute-start | bytes 2555912 | tf_op jit(solution)/shard_map/ppermute | solution.py:36
  108.0 31.3 %collective-permute-start.12 = (bf16[1,224,256]{2,1,0:T(8,128)(2,1)S(1)}, bf16[1,224,256]{2,1,0:T(8,128)(2,1)}, u32[]{:S(2)}, u32[]{:S(2)}) collective-permute-start(bf16[1,224,256]{2,1,0:T(8,128)(2,1)S(1)} %maximum_bitcast_fusion), channel_id=1, source_target_pairs={{0,4},{4,0},{8,12},{12,8},{16,20},{20,16},{24,28},{28,24},{1,5},{5... | collective-permute-start | bytes 344072 | tf_op jit(solution)/shard_map/ppermute | solution.py:36
  140.3 10.9 %collective-permute-start.18 = (bf16[4,48,2048]{2,1,0:T(8,128)(2,1)S(1)}, bf16[4,48,2048]{2,1,0:T(8,128)(2,1)S(1)}, u32[]{:S(2)}, u32[]{:S(2)}) collective-permute-start(bf16[4,48,2048]{2,1,0:T(8,128)(2,1)S(1)} %get-tuple-element.233), channel_id=1, source_target_pairs={{0,4},{4,0},{8,12},{12,8},{16,20},{20,16},{24,28},{28,24},{1,5},{5... | collective-permute-start | bytes 2359304 | tf_op jit(solution)/shard_map/ppermute | solution.py:36
  140.4 10.8 %collective-permute-start.17 = (bf16[4,48,2048]{2,1,0:T(8,128)(2,1)S(1)}, bf16[4,48,2048]{2,1,0:T(8,128)(2,1)S(1)}, u32[]{:S(2)}, u32[]{:S(2)}) collective-permute-start(bf16[4,48,2048]{2,1,0:T(8,128)(2,1)S(1)} %get-tuple-element.234), channel_id=1, source_target_pairs={{0,4},{4,0},{8,12},{12,8},{16,20},{20,16},{24,28},{28,24},{1,5},{5... | collective-permute-start | bytes 2359304 | tf_op jit(solution)/shard_map/ppermute | solution.py:36
  141.8 7.7 %collective-permute-start.15 = (bf16[2,224,256]{2,1,0:T(8,128)(2,1)S(1)}, bf16[2,224,256]{2,1,0:T(8,128)(2,1)S(1)}, u32[]{:S(2)}, u32[]{:S(2)}) collective-permute-start(bf16[2,224,256]{2,1,0:T(8,128)(2,1)S(1)} %pad_maximum_fusion.12), channel_id=1, source_target_pairs={{0,8},{4,12},{8,0},{12,4},{16,24},{20,28},{24,16},{28,20},{1,9},{5... | collective-permute-start | bytes 688136 | tf_op jit(solution)/shard_map/ppermute | solution.py:36
  143.4 19.8 %collective-permute-start.13 = (bf16[64,6656]{1,0:T(8,128)(2,1)S(1)}, bf16[64,6656]{1,0:T(8,128)(2,1)S(1)}, u32[]{:S(2)}, u32[]{:S(2)}) collective-permute-start(bf16[64,6656]{1,0:T(8,128)(2,1)S(1)} %bitcast.152), channel_id=1, source_target_pairs={{1,2},{2,1},{5,6},{6,5},{9,10},{10,9},{13,14},{14,13},{17,18},{18,... | collective-permute-start | bytes 2555912 | tf_op jit(solution)/shard_map/ppermute | solution.py:67
  144.1 23.1 %collective-permute-start.14 = (bf16[64,6656]{1,0:T(8,128)(2,1)}, bf16[64,6656]{1,0:T(8,128)(2,1)S(1)}, u32[]{:S(2)}, u32[]{:S(2)}) collective-permute-start(bf16[64,6656]{1,0:T(8,128)(2,1)} %collective-permute-done.11.refs_2_), channel_id=1, source_target_pairs={{1,0},{2,3},{5,4},{6,7},{9,8},{10,11},{13,12},{14,15},{17,16},{18,... | collective-permute-start | bytes 2555912 | tf_op jit(solution)/shard_map/ppermute | solution.py:68
  149.6 13.6 %collective-permute-start.16 = (bf16[4,224,256]{2,1,0:T(8,128)(2,1)S(1)}, bf16[4,224,256]{2,1,0:T(8,128)(2,1)}, u32[]{:S(2)}, u32[]{:S(2)}) collective-permute-start(bf16[4,224,256]{2,1,0:T(8,128)(2,1)S(1)} %pad_maximum_fusion.4), channel_id=1, source_target_pairs={{0,16},{4,20},{8,24},{12,28},{16,0},{20,4},{24,8},{28,12},{1,17},{... | collective-permute-start | bytes 1376264 | tf_op jit(solution)/shard_map/ppermute | solution.py:36
  153.3 13.9 %collective-permute-start.19 = (bf16[2,48,2048]{2,1,0:T(8,128)(2,1)}, bf16[2,48,2048]{2,1,0:T(8,128)(2,1)}, u32[]{:S(2)}, u32[]{:S(2)}) collective-permute-start(bf16[2,48,2048]{2,1,0:T(8,128)(2,1)} %pad_maximum_fusion.5), channel_id=1, source_target_pairs={{0,8},{4,12},{8,0},{12,4},{16,24},{20,28},{24,16},{28,20},{1,9},{5... | collective-permute-start | bytes 1179656 | tf_op jit(solution)/shard_map/ppermute | solution.py:36
  155.6 14.2 %collective-permute-start.20 = (bf16[2,48,2048]{2,1,0:T(8,128)(2,1)}, bf16[2,48,2048]{2,1,0:T(8,128)(2,1)}, u32[]{:S(2)}, u32[]{:S(2)}) collective-permute-start(bf16[2,48,2048]{2,1,0:T(8,128)(2,1)} %pad_maximum_fusion.6), channel_id=1, source_target_pairs={{0,16},{4,20},{8,24},{12,28},{16,0},{20,4},{24,8},{28,12},{1,17},{... | collective-permute-start | bytes 1179656 | tf_op jit(solution)/shard_map/ppermute | solution.py:36
  163.2 10.5 %copy-start.7 = (bf16[64,6656]{1,0:T(8,128)(2,1)}, bf16[64,6656]{1,0:T(8,128)(2,1)S(1)}, u32[]{:S(2)}) copy-start(bf16[64,6656]{1,0:T(8,128)(2,1)S(1)} %collective-permute-done.13.refs_3_) | copy-start | bytes 2555908
  169.9 43.6 %collective-permute-start.21 = (bf16[64,6656]{1,0:T(8,128)(2,1)}, bf16[64,6656]{1,0:T(8,128)(2,1)}, u32[]{:S(2)}, u32[]{:S(2)}) collective-permute-start(bf16[64,6656]{1,0:T(8,128)(2,1)} %bitcast.31.refs_0_), channel_id=1, source_target_pairs={{0,1},{1,0},{2,3},{3,2},{4,5},{5,4},{6,7},{7,6},{8,9},{9,8},{10,11... | collective-permute-start | bytes 2555912 | tf_op jit(solution)/shard_map/ppermute | solution.py:36
  170.5 43.0 %collective-permute-start.22 = (bf16[64,6656]{1,0:T(8,128)(2,1)}, bf16[64,6656]{1,0:T(8,128)(2,1)}, u32[]{:S(2)}, u32[]{:S(2)}) collective-permute-start(bf16[64,6656]{1,0:T(8,128)(2,1)} %bitcast.31.refs_0_), channel_id=1, source_target_pairs={{0,2},{1,3},{2,0},{3,1},{4,6},{5,7},{6,4},{7,5},{8,10},{9,11},{10,... | collective-permute-start | bytes 2555912 | tf_op jit(solution)/shard_map/ppermute | solution.py:36
  173.8 32.6 %collective-permute-start.23 = (bf16[1,48,2048]{2,1,0:T(8,128)(2,1)S(1)}, bf16[1,48,2048]{2,1,0:T(8,128)(2,1)S(1)}, u32[]{:S(2)}, u32[]{:S(2)}) collective-permute-start(bf16[1,48,2048]{2,1,0:T(8,128)(2,1)S(1)} %get-tuple-element.259), channel_id=1, source_target_pairs={{0,16},{4,20},{8,24},{12,28},{16,0},{20,4},{24,8},{28,12},{1,17},{... | collective-permute-start | bytes 589832 | tf_op jit(solution)/shard_map/ppermute | solution.py:36
  203.8 9.7 %collective-permute-start.25 = (bf16[4,32,2048]{2,1,0:T(8,128)(2,1)}, bf16[4,32,2048]{2,1,0:T(8,128)(2,1)}, u32[]{:S(2)}, u32[]{:S(2)}) collective-permute-start(bf16[4,32,2048]{2,1,0:T(8,128)(2,1)} %get-tuple-element.240), channel_id=1, source_target_pairs={{0,4},{4,0},{8,12},{12,8},{16,20},{20,16},{24,28},{28,24},{1,5},{5... | collective-permute-start | bytes 1572872 | tf_op jit(solution)/shard_map/ppermute | solution.py:36
  203.8 9.7 %collective-permute-start.26 = (bf16[4,32,2048]{2,1,0:T(8,128)(2,1)}, bf16[4,32,2048]{2,1,0:T(8,128)(2,1)}, u32[]{:S(2)}, u32[]{:S(2)}) collective-permute-start(bf16[4,32,2048]{2,1,0:T(8,128)(2,1)} %get-tuple-element.239), channel_id=1, source_target_pairs={{0,4},{4,0},{8,12},{12,8},{16,20},{20,16},{24,28},{28,24},{1,5},{5... | collective-permute-start | bytes 1572872 | tf_op jit(solution)/shard_map/ppermute | solution.py:36
  206.3 7.1 %collective-permute-start.24 = (bf16[1,48,2048]{2,1,0:T(8,128)(2,1)}, bf16[1,48,2048]{2,1,0:T(8,128)(2,1)}, u32[]{:S(2)}, u32[]{:S(2)}) collective-permute-start(bf16[1,48,2048]{2,1,0:T(8,128)(2,1)} %get-tuple-element.257), channel_id=1, source_target_pairs={{0,8},{4,12},{8,0},{12,4},{16,24},{20,28},{24,16},{28,20},{1,9},{5... | collective-permute-start | bytes 589832 | tf_op jit(solution)/shard_map/ppermute | solution.py:36
  213.5 28.3 %collective-permute-start.27 = (bf16[64,6656]{1,0:T(8,128)(2,1)}, bf16[64,6656]{1,0:T(8,128)(2,1)S(1)}, u32[]{:S(2)}, u32[]{:S(2)}) collective-permute-start(bf16[64,6656]{1,0:T(8,128)(2,1)} %bitcast.31.refs_0_), channel_id=1, source_target_pairs={{1,2},{2,1},{5,6},{6,5},{9,10},{10,9},{13,14},{14,13},{17,18},{18,... | collective-permute-start | bytes 2555912 | tf_op jit(solution)/shard_map/ppermute | solution.py:67
  214.2 27.5 %collective-permute-start.28 = (bf16[64,6656]{1,0:T(8,128)(2,1)}, bf16[64,6656]{1,0:T(8,128)(2,1)S(1)}, u32[]{:S(2)}, u32[]{:S(2)}) collective-permute-start(bf16[64,6656]{1,0:T(8,128)(2,1)} %collective-permute-done.22.refs_2_), channel_id=1, source_target_pairs={{1,0},{2,3},{5,4},{6,7},{9,8},{10,11},{13,12},{14,15},{17,16},{18,... | collective-permute-start | bytes 2555912 | tf_op jit(solution)/shard_map/ppermute | solution.py:68
  217.3 9.3 %collective-permute-start.29 = (bf16[512,256]{1,0:T(8,128)(2,1)S(1)}, bf16[512,256]{1,0:T(8,128)(2,1)S(1)}, u32[]{:S(2)}, u32[]{:S(2)}) collective-permute-start(bf16[512,256]{1,0:T(8,128)(2,1)S(1)} %fusion), channel_id=1, source_target_pairs={{0,16},{4,20},{8,24},{12,28},{16,0},{20,4},{24,8},{28,12},{1,17},{... | collective-permute-start | bytes 786440 | tf_op jit(solution)/shard_map/ppermute | solution.py:36
  219.1 11.3 %collective-permute-start.32 = (bf16[2,32,2048]{2,1,0:T(8,128)(2,1)S(1)}, bf16[2,32,2048]{2,1,0:T(8,128)(2,1)S(1)}, u32[]{:S(2)}, u32[]{:S(2)}) collective-permute-start(bf16[2,32,2048]{2,1,0:T(8,128)(2,1)S(1)} %pad_maximum_fusion.9), channel_id=1, source_target_pairs={{0,16},{4,20},{8,24},{12,28},{16,0},{20,4},{24,8},{28,12},{1,17},{... | collective-permute-start | bytes 786440 | tf_op jit(solution)/shard_map/ppermute | solution.py:36
  220.8 9.7 %collective-permute-start.31 = (bf16[2,32,2048]{2,1,0:T(8,128)(2,1)S(1)}, bf16[2,32,2048]{2,1,0:T(8,128)(2,1)S(1)}, u32[]{:S(2)}, u32[]{:S(2)}) collective-permute-start(bf16[2,32,2048]{2,1,0:T(8,128)(2,1)S(1)} %pad_maximum_fusion.8), channel_id=1, source_target_pairs={{0,8},{4,12},{8,0},{12,4},{16,24},{20,28},{24,16},{28,20},{1,9},{5... | collective-permute-start | bytes 786440 | tf_op jit(solution)/shard_map/ppermute | solution.py:36
  226.7 15.0 %collective-permute-start.30 = (bf16[1024,256]{1,0:T(8,128)(2,1)S(1)}, bf16[1024,256]{1,0:T(8,128)(2,1)S(1)}, u32[]{:S(2)}, u32[]{:S(2)}) collective-permute-start(bf16[1024,256]{1,0:T(8,128)(2,1)S(1)} %pad_maximum_fusion.2), channel_id=1, source_target_pairs={{0,8},{4,12},{8,0},{12,4},{16,24},{20,28},{24,16},{28,20},{1,9},{5... | collective-permute-start | bytes 1572872 | tf_op jit(solution)/shard_map/ppermute | solution.py:36
  232.4 5.0 %collective-permute-start.33 = (bf16[1,32,2048]{2,1,0:T(8,128)(2,1)S(1)}, bf16[1,32,2048]{2,1,0:T(8,128)(2,1)S(1)}, u32[]{:S(2)}, u32[]{:S(2)}) collective-permute-start(bf16[1,32,2048]{2,1,0:T(8,128)(2,1)S(1)} %get-tuple-element.228), channel_id=1, source_target_pairs={{0,16},{4,20},{8,24},{12,28},{16,0},{20,4},{24,8},{28,12},{1,17},{... | collective-permute-start | bytes 393224 | tf_op jit(solution)/shard_map/ppermute | solution.py:36
  232.9 8.8 %collective-permute-start.34 = (bf16[1,32,2048]{2,1,0:T(8,128)(2,1)S(1)}, bf16[1,32,2048]{2,1,0:T(8,128)(2,1)S(1)}, u32[]{:S(2)}, u32[]{:S(2)}) collective-permute-start(bf16[1,32,2048]{2,1,0:T(8,128)(2,1)S(1)} %get-tuple-element.205), channel_id=1, source_target_pairs={{0,8},{4,12},{8,0},{12,4},{16,24},{20,28},{24,16},{28,20},{1,9},{5... | collective-permute-start | bytes 393224 | tf_op jit(solution)/shard_map/ppermute | solution.py:36
  234.3 33.5 %slice-start = ((s8[5111808]{0:T(1024)(128)(4,1)}), s8[4194304]{0:T(1024)(128)(4,1)S(1)}, s32[]{:S(2)}) async-start(s8[5111808]{0:T(1024)(128)(4,1)} %bitcast.148), calls=%async_computation.1 | async-start | bytes 8388608
  241.8 26.0 %slice-start.1 = ((s8[5111808]{0:T(1024)(128)(4,1)}), s8[917504]{0:T(1024)(128)(4,1)S(1)}, s32[]{:S(2)}) async-start(s8[5111808]{0:T(1024)(128)(4,1)} %bitcast.148), calls=%async_computation.2 | async-start | bytes 1835008
  266.1 6.3 %collective-permute-start.36 = (bf16[4,32,2048]{2,1,0:T(8,128)(2,1)S(1)}, bf16[4,32,2048]{2,1,0:T(8,128)(2,1)S(1)}, u32[]{:S(2)}, u32[]{:S(2)}) collective-permute-start(bf16[4,32,2048]{2,1,0:T(8,128)(2,1)S(1)} %get-tuple-element.237), channel_id=1, source_target_pairs={{0,4},{4,0},{8,12},{12,8},{16,20},{20,16},{24,28},{28,24},{1,5},{5... | collective-permute-start | bytes 1572872 | tf_op jit(solution)/shard_map/ppermute | solution.py:36
  266.1 6.2 %collective-permute-start.35 = (bf16[4,32,2048]{2,1,0:T(8,128)(2,1)S(1)}, bf16[4,32,2048]{2,1,0:T(8,128)(2,1)S(1)}, u32[]{:S(2)}, u32[]{:S(2)}) collective-permute-start(bf16[4,32,2048]{2,1,0:T(8,128)(2,1)S(1)} %get-tuple-element.238), channel_id=1, source_target_pairs={{0,4},{4,0},{8,12},{12,8},{16,20},{20,16},{24,28},{28,24},{1,5},{5... | collective-permute-start | bytes 1572872 | tf_op jit(solution)/shard_map/ppermute | solution.py:36
  266.8 7.8 %collective-permute-start.39 = (bf16[2048,256]{1,0:T(8,128)(2,1)S(1)}, bf16[2048,256]{1,0:T(8,128)(2,1)S(1)}, u32[]{:S(2)}, u32[]{:S(2)}) collective-permute-start(bf16[2048,256]{1,0:T(8,128)(2,1)S(1)} %pad_maximum_fusion), channel_id=1, source_target_pairs={{0,4},{4,0},{8,12},{12,8},{16,20},{20,16},{24,28},{28,24},{1,5},{5... | collective-permute-start | bytes 3145736 | tf_op jit(solution)/shard_map/ppermute | solution.py:36
  272.7 8.4 %collective-permute-start.37 = (bf16[2,32,2048]{2,1,0:T(8,128)(2,1)S(1)}, bf16[2,32,2048]{2,1,0:T(8,128)(2,1)S(1)}, u32[]{:S(2)}, u32[]{:S(2)}) collective-permute-start(bf16[2,32,2048]{2,1,0:T(8,128)(2,1)S(1)} %pad_maximum_fusion.10), channel_id=1, source_target_pairs={{0,8},{4,12},{8,0},{12,4},{16,24},{20,28},{24,16},{28,20},{1,9},{5... | collective-permute-start | bytes 786440 | tf_op jit(solution)/shard_map/ppermute | solution.py:36
  274.1 8.1 %collective-permute-start.38 = (bf16[2,32,2048]{2,1,0:T(8,128)(2,1)S(1)}, bf16[2,32,2048]{2,1,0:T(8,128)(2,1)S(1)}, u32[]{:S(2)}, u32[]{:S(2)}) collective-permute-start(bf16[2,32,2048]{2,1,0:T(8,128)(2,1)S(1)} %pad_maximum_fusion.11), channel_id=1, source_target_pairs={{0,16},{4,20},{8,24},{12,28},{16,0},{20,4},{24,8},{28,12},{1,17},{... | collective-permute-start | bytes 786440 | tf_op jit(solution)/shard_map/ppermute | solution.py:36
  282.2 5.9 %collective-permute-start.41 = (bf16[1,32,2048]{2,1,0:T(8,128)(2,1)S(1)}, bf16[1,32,2048]{2,1,0:T(8,128)(2,1)S(1)}, u32[]{:S(2)}, u32[]{:S(2)}) collective-permute-start(bf16[1,32,2048]{2,1,0:T(8,128)(2,1)S(1)} %fusion.13), channel_id=1, source_target_pairs={{0,8},{4,12},{8,0},{12,4},{16,24},{20,28},{24,16},{28,20},{1,9},{5... | collective-permute-start | bytes 393224 | tf_op jit(solution)/shard_map/ppermute | solution.py:36
  283.0 5.1 %collective-permute-start.40 = (bf16[1,32,2048]{2,1,0:T(8,128)(2,1)S(1)}, bf16[1,32,2048]{2,1,0:T(8,128)(2,1)S(1)}, u32[]{:S(2)}, u32[]{:S(2)}) collective-permute-start(bf16[1,32,2048]{2,1,0:T(8,128)(2,1)S(1)} %fusion.12), channel_id=1, source_target_pairs={{0,16},{4,20},{8,24},{12,28},{16,0},{20,4},{24,8},{28,12},{1,17},{... | collective-permute-start | bytes 393224 | tf_op jit(solution)/shard_map/ppermute | solution.py:36
  (19 other events, 63.8 us)

commit v13 on v9

--- a/solution.py
+++ b/solution.py
@@ -381,7 +381,7 @@
     small, sums = hold(small, sums)
     columns_step = max(128 * c for c in range(1, 14) if depth % (128 * c) == 0)
     steps = depth // columns_step
-    early = steps // 2 or 1
+    early = steps // 4 or 1
     tokens = [tokens[i] for i in range(count)]
     last = count - 1
 
@@ -395,10 +395,14 @@
         small_hop()
     grad_a = small["grad_a"].astype(jnp.float32)
     grad_b = factor(0, early)
+    sums[last], grad_b = hold(sums[last], grad_b)
     sum_hop(last)
+    half = min(steps // 2, steps - early)
+    if half:
+        grad_b = factor(early, half, grad_b)
     sums[last], grad_a, grad_b = hold(sums[last], grad_a, grad_b)
-    if steps > early:
-        grad_b = factor(early, steps - early, grad_b)
+    if steps > early + half:
+        grad_b = factor(early + half, steps - early - half, grad_b)
     results = []
     for i, (start, rows) in enumerate(pieces):
         while done_hops[i] <= len(wide_bits):

time: 293 us -> 303 us (1.034)
  waiting for transfers between devices: 101 us -> 110 us
    ppermute x3, waiting for transfers between devices: 2.24 us -> 11.7 us  [phase_b(): lax.ppermute(far, axis, [(1, 0), (2, 3)])]
    pallas_call x2 -> x3, Pallas kernels: 9.02 us -> 10.2 us  [factor_gradient(): pl.pallas_call(functools.partial(factor_kernel, pieces=pieces, scale=scal...]
    unnamed x52 -> x48, local copies, waits for them, and re-layouts: 10.1 us -> 10.1 us
  transfers between devices with their start and end apart: 43 -> 43, of which waited for: 17 -> 16; matrix products, arithmetic and copies ran while one was open for 14% -> 10% of each run, Pallas kernels for 31% -> 30%
where the time goes in v13:
time: 303 us; the launch traced here: 301 us
  waiting for transfers between devices  110 us (36%)
  Pallas kernels  89.9 us (30%)
  starting transfers between devices  49.8 us (16%)
  local copies, waits for them, and re-layouts  24.5 us (8%)
  other arithmetic  16.1 us (5%)
  matrix products  9.53 us (3%)
    ppermute x36, waiting for transfers between devices, swap(): return lax.ppermute(value, axis, [(i, i ^ bit) for i in range(size)])  98.5 us
    pallas_call x3, Pallas kernels, weight_pass(): pl.pallas_call(functools.partial(pass_kernel, sources=len(sources), owner...  79.6 us
    ppermute x36, starting transfers between devices, swap(): return lax.ppermute(value, axis, [(i, i ^ bit) for i in range(size)])  39.2 us
    ppermute x3, waiting for transfers between devices, phase_b(): lax.ppermute(far, axis, [(1, 0), (2, 3)])  11.7 us
    pallas_call x3, Pallas kernels, factor_gradient(): pl.pallas_call(functools.partial(factor_kernel, pieces=pieces, scale=scal...  10.2 us
    unnamed x48, local copies, waits for them, and re-layouts  10.1 us
  transfers between devices with their start and end apart: 43, of which 16 were waited for; matrix products, arithmetic and copies ran while one was open for 10% of the time, Pallas kernels for 30%

profile of v13, /device:TPU:0, one launch (start us, length us, event | category | flops | bytes accessed | tf_op | source)
XLA Modules:
  0.0 301.3 jit_solution(4540778254084411361)
XLA Ops:
  0.6 2.6 slice.336
  3.2 4.0 %collective-permute-start.1 = (bf16[96,6656]{1,0:T(8,128)(2,1)}, bf16[96,6656]{1,0:T(8,128)(2,1)}, u32[]{:S(2)}, u32[]{:S(2)}) collective-permute-start(bf16[96,6656]{1,0:T(8,128)(2,1)} %bitcast.1.refs_0_), channel_id=1, source_target_pairs={{0,2},{1,3},{2,0},{3,1},{4,6},{5,7},{6,4},{7,5},{8,10},{9,11},{10,... | collective-permute-start | bytes 3833864 | tf_op jit(solution)/shard_map/ppermute | solution.py:36
  7.3 1.6 collective-permute-start
  8.9 3.7 %fusion.25 = f32[224,256]{1,0:T(8,128)} fusion(bf16[224,6656]{1,0:T(8,128)(2,1)} %param.6, bf16[256,6656]{1,0:T(8,128)(2,1)S(1)} %copy-done), kind=kOutput, calls=%fused_computation.120 | convolution fusion | flops 763363328 | bytes 6619136 | tf_op jit(solution)/shard_map/dot_general | solution.py:18
  13.4 1.5 collective-permute-start.2
  15.0 3.3 %collective-permute-done.2 = f32[112,256]{1,0:T(8,128)S(1)} collective-permute-done((f32[112,256]{1,0:T(8,128)S(1)}, f32[112,256]{1,0:T(8,128)S(1)}, u32[]{:S(2)}, u32[]{:S(2)}) %collective-permute-start.2) | collective-permute-done | bytes 114720 | tf_op jit(solution)/shard_map/ppermute | solution.py:36
  19.2 1.6 collective-permute-start.3
  20.7 2.7 collective-permute-done.3
  24.8 38.4 %collective-permute-done.1.refs_2_ = bf16[96,6656]{1,0:T(8,128)(2,1)} collective-permute-done((bf16[96,6656]{1,0:T(8,128)(2,1)}, bf16[96,6656]{1,0:T(8,128)(2,1)}, u32[]{:S(2)}, u32[]{:S(2)}) %collective-permute-start.1) | collective-permute-done | bytes 1277984 | tf_op jit(solution)/shard_map/ppermute | solution.py:36
  63.3 1.5 copy.64
  64.8 1.5 fusion.24
  73.7 4.2 %all-to-all-start = ((bf16[8,112,512]{2,1,0:T(8,128)(2,1)}), bf16[8,112,512]{2,1,0:T(8,128)(2,1)}, u32[]{:S(2)}, u32[]{:S(2)}) async-start(bf16[8,112,512]{2,1,0:T(8,128)(2,1)} %bitcast_dynamic-update-slice_fusion), calls=%async_computation | async-start | bytes 1835008 | tf_op jit(solution)/shard_map/all_to_all | solution.py:323
  77.9 2.3 convolution_convert_fusion
  80.3 3.3 %collective-permute-start.9 = (bf16[140,256]{1,0:T(8,128)(2,1)S(1)}, bf16[140,256]{1,0:T(8,128)(2,1)S(1)}, u32[]{:S(2)}, u32[]{:S(2)}) collective-permute-start(bf16[140,256]{1,0:T(8,128)(2,1)S(1)} %pad_maximum_fusion.13), channel_id=1, source_target_pairs={{0,3},{1,2},{2,1},{3,0},{4,7},{5,6},{6,5},{7,4},{8,11},{9,10},{10,... | collective-permute-start | bytes 215048 | tf_op jit(solution)/shard_map/ppermute | solution.py:36
  86.9 18.5 %collective-permute-done.8 = bf16[140,256]{1,0:T(8,128)(2,1)} collective-permute-done((bf16[140,256]{1,0:T(8,128)(2,1)S(1)}, bf16[140,256]{1,0:T(8,128)(2,1)}, u32[]{:S(2)}, u32[]{:S(2)}) %collective-permute-start.8) | collective-permute-done | bytes 71712 | tf_op jit(solution)/shard_map/ppermute | solution.py:36
  106.0 2.6 collective-permute-start.10
  113.0 31.2 %weight_pass.3 = (bf16[384,6656]{1,0:T(8,128)(2,1)}, f32[4,48,4096]{2,1,0:T(8,128)S(1)}, bf16[4,48,4096]{2,1,0:T(8,128)(2,1)S(1)}) custom-call(s32[9]{0:T(128)S(1)} %stack.142.table, bf16[96,6656]{1,0:T(8,128)(2,1)} %bitcast.1.refs_0_, bf16[96,6656]{1,0:T(8,128)(2,1)} %collective-permute-done.refs_1_, bf16[96,6656]{1,0:T(8,128)(2,1)} %collective-permute-done.1.refs_2_, ...), custom_call_target="tpu_custom_call" | custom-call | bytes 65536 | tf_op jit(solution)/shard_map/weight_pass/pallas_call | solution.py:124
  145.2 1.6 collective-permute-start.15
  147.5 1.5 collective-permute-start.14
  149.7 3.6 %collective-permute-done.15 = bf16[2,224,256]{2,1,0:T(8,128)(2,1)S(1)} collective-permute-done((bf16[2,224,256]{2,1,0:T(8,128)(2,1)S(1)}, bf16[2,224,256]{2,1,0:T(8,128)(2,1)S(1)}, u32[]{:S(2)}, u32[]{:S(2)}) %collective-permute-start.15) | collective-permute-done | bytes 229408 | tf_op jit(solution)/shard_map/ppermute | solution.py:36
  153.4 1.6 collective-permute-start.16
  155.0 2.1 slice.348
  157.1 8.5 %collective-permute-done.16 = bf16[4,224,256]{2,1,0:T(8,128)(2,1)S(1)} collective-permute-done((bf16[4,224,256]{2,1,0:T(8,128)(2,1)S(1)}, bf16[4,224,256]{2,1,0:T(8,128)(2,1)S(1)}, u32[]{:S(2)}, u32[]{:S(2)}) %collective-permute-start.16) | collective-permute-done | bytes 458784 | tf_op jit(solution)/shard_map/ppermute | solution.py:36
  165.6 5.0 %collective-permute-done.14.refs_4_ = bf16[64,6656]{1,0:T(8,128)(2,1)S(1)} collective-permute-done((bf16[64,6656]{1,0:T(8,128)(2,1)}, bf16[64,6656]{1,0:T(8,128)(2,1)S(1)}, u32[]{:S(2)}, u32[]{:S(2)}) %collective-permute-start.14) | collective-permute-done | bytes 852000 | tf_op jit(solution)/shard_map/ppermute | solution.py:68
  170.7 1.5 add_convert_fusion.1
  172.9 1.6 collective-permute-start.22
  174.5 2.0 collective-permute-start.19
  176.5 23.9 %weight_pass.4 = (bf16[256,6656]{1,0:T(8,128)(2,1)S(1)}, f32[4,32,4096]{2,1,0:T(8,128)S(1)}, bf16[4,32,4096]{2,1,0:T(8,128)(2,1)S(1)}) custom-call(s32[9]{0:T(128)S(1)} %stack.142.table, bf16[64,6656]{1,0:T(8,128)(2,1)S(1)} %bitcast.173, bf16[64,6656]{1,0:T(8,128)(2,1)} %collective-permute-done.10.refs_1_, bf16[64,6656]{1,0:T(8,128)(2,1)} %collective-permute-done.11.refs_2_, ...), custom_call_target="tpu_custom_call" | custom-call | bytes 65536 | tf_op jit(solution)/shard_map/weight_pass/pallas_call | solution.py:124
  203.6 9.0 %collective-permute-done.20.refs_2_ = bf16[64,6656]{1,0:T(8,128)(2,1)} collective-permute-done((bf16[64,6656]{1,0:T(8,128)(2,1)}, bf16[64,6656]{1,0:T(8,128)(2,1)}, u32[]{:S(2)}, u32[]{:S(2)}) %collective-permute-start.20) | collective-permute-done | bytes 852000 | tf_op jit(solution)/shard_map/ppermute | solution.py:36
  215.8 1.9 reshape.129
  217.8 1.9 fusion
  221.5 1.5 collective-permute-start.28
  223.1 1.6 collective-permute-start.29
  225.4 1.5 collective-permute-start.26
  226.9 1.6 add_convert_fusion.9
  228.6 3.7 %collective-permute-done.28 = bf16[1,48,2048]{2,1,0:T(8,128)(2,1)S(1)} collective-permute-done((bf16[1,48,2048]{2,1,0:T(8,128)(2,1)S(1)}, bf16[1,48,2048]{2,1,0:T(8,128)(2,1)S(1)}, u32[]{:S(2)}, u32[]{:S(2)}) %collective-permute-start.28) | collective-permute-done | bytes 196640 | tf_op jit(solution)/shard_map/ppermute | solution.py:36
  232.2 1.5 collective-permute-start.30
  234.2 1.6 convolution_multiply_fusion
  235.8 3.7 %collective-permute-done.30 = bf16[2,32,2048]{2,1,0:T(8,128)(2,1)S(1)} collective-permute-done((bf16[2,32,2048]{2,1,0:T(8,128)(2,1)S(1)}, bf16[2,32,2048]{2,1,0:T(8,128)(2,1)S(1)}, u32[]{:S(2)}, u32[]{:S(2)}) %collective-permute-start.30) | collective-permute-done | bytes 262176 | tf_op jit(solution)/shard_map/ppermute | solution.py:36
  240.8 6.7 %collective-permute-done.26.refs_4_ = bf16[64,6656]{1,0:T(8,128)(2,1)S(1)} collective-permute-done((bf16[64,6656]{1,0:T(8,128)(2,1)}, bf16[64,6656]{1,0:T(8,128)(2,1)S(1)}, u32[]{:S(2)}, u32[]{:S(2)}) %collective-permute-start.26) | collective-permute-done | bytes 852000 | tf_op jit(solution)/shard_map/ppermute | solution.py:68
  250.6 24.5 %weight_pass.5 = (bf16[256,6656]{1,0:T(8,128)(2,1)S(1)}, f32[4,32,4096]{2,1,0:T(8,128)S(1)}, bf16[4,32,4096]{2,1,0:T(8,128)(2,1)S(1)}) custom-call(s32[9]{0:T(128)S(1)} %stack.142.table, bf16[64,6656]{1,0:T(8,128)(2,1)} %bitcast.31.refs_0_, bf16[64,6656]{1,0:T(8,128)(2,1)} %collective-permute-done.19.refs_1_, ...), custom_call_target="tpu_custom_call" | custom-call | bytes 65536 | tf_op jit(solution)/shard_map/weight_pass/pallas_call | solution.py:124
  277.0 2.9 factor_gradient.3.refs_3_
  281.0 1.4 collective-permute-start.38
  282.4 4.5 %factor_gradient.4.refs_3_ = f32[256,6656]{1,0:T(8,128)} custom-call(s32[8]{0:T(128)S(1)} %stack.159.order, bf16[8,112,256]{2,1,0:T(8,128)(2,1)S(1)} %copy-done.2, bf16[384,6656]{1,0:T(8,128)(2,1)S(1)} %bitcast.169, bf16[256,6656]{1,0:T(8,128)(2,1)S(1)} %get-tuple-element.207.refs_1_, ...), custom_call_target="tpu_custom_call", output_to_operand_aliasing={{}: (5, {})} | custom-call | bytes 65536 | tf_op jit(solution)/shard_map/factor_gradient/pallas_call | solution.py:173
  287.3 2.3 maximum_convert_fusion
  289.7 1.5 collective-permute-start.41
  291.2 2.9 factor_gradient.5
  294.9 4.2 %collective-permute-done.40 = bf16[1,32,2048]{2,1,0:T(8,128)(2,1)S(1)} collective-permute-done((bf16[1,32,2048]{2,1,0:T(8,128)(2,1)S(1)}, bf16[1,32,2048]{2,1,0:T(8,128)(2,1)S(1)}, u32[]{:S(2)}, u32[]{:S(2)}) %collective-permute-start.40) | collective-permute-done | bytes 131104 | tf_op jit(solution)/shard_map/ppermute | solution.py:36
  (160 shorter events, 42.1 us)
Async XLA Ops:
  3.2 59.9 %collective-permute-start.1 = (bf16[96,6656]{1,0:T(8,128)(2,1)}, bf16[96,6656]{1,0:T(8,128)(2,1)}, u32[]{:S(2)}, u32[]{:S(2)}) collective-permute-start(bf16[96,6656]{1,0:T(8,128)(2,1)} %bitcast.1.refs_0_), channel_id=1, source_target_pairs={{0,2},{1,3},{2,0},{3,1},{4,6},{5,7},{6,4},{7,5},{8,10},{9,11},{10,... | collective-permute-start | bytes 3833864 | tf_op jit(solution)/shard_map/ppermute | solution.py:36
  7.3 56.1 %collective-permute-start = (bf16[96,6656]{1,0:T(8,128)(2,1)}, bf16[96,6656]{1,0:T(8,128)(2,1)}, u32[]{:S(2)}, u32[]{:S(2)}) collective-permute-start(bf16[96,6656]{1,0:T(8,128)(2,1)} %bitcast.1.refs_0_), channel_id=1, source_target_pairs={{0,1},{1,0},{2,3},{3,2},{4,5},{5,4},{6,7},{7,6},{8,9},{9,8},{10,11... | collective-permute-start | bytes 3833864 | tf_op jit(solution)/shard_map/ppermute | solution.py:36
  13.4 4.8 %collective-permute-start.2 = (f32[112,256]{1,0:T(8,128)S(1)}, f32[112,256]{1,0:T(8,128)S(1)}, u32[]{:S(2)}, u32[]{:S(2)}) collective-permute-start(f32[112,256]{1,0:T(8,128)S(1)} %dynamic-slice_bitcast_fusion), channel_id=1, source_target_pairs={{0,16},{4,20},{8,24},{12,28},{16,0},{20,4},{24,8},{28,12},{1,17},{... | collective-permute-start | bytes 344072 | tf_op jit(solution)/shard_map/ppermute | solution.py:36
  19.2 4.2 %collective-permute-start.3 = (f32[56,256]{1,0:T(8,128)S(1)}, f32[56,256]{1,0:T(8,128)S(1)}, u32[]{:S(2)}, u32[]{:S(2)}) collective-permute-start(f32[56,256]{1,0:T(8,128)S(1)} %dynamic-slice_bitcast_fusion.1), channel_id=1, source_target_pairs={{0,8},{4,12},{8,0},{12,4},{16,24},{20,28},{24,16},{28,20},{1,9},{5... | collective-permute-start | bytes 172040 | tf_op jit(solution)/shard_map/ppermute | solution.py:36
  23.5 1.3 collective-permute-start.4
  67.0 38.4 %collective-permute-start.5 = (bf16[96,6656]{1,0:T(8,128)(2,1)}, bf16[96,6656]{1,0:T(8,128)(2,1)S(1)}, u32[]{:S(2)}, u32[]{:S(2)}) collective-permute-start(bf16[96,6656]{1,0:T(8,128)(2,1)} %bitcast.1.refs_0_), channel_id=1, source_target_pairs={{1,2},{2,1},{5,6},{6,5},{9,10},{10,9},{13,14},{14,13},{17,18},{18,... | collective-permute-start | bytes 3833864 | tf_op jit(solution)/shard_map/ppermute | solution.py:67
  67.8 37.7 %collective-permute-start.6 = (bf16[96,6656]{1,0:T(8,128)(2,1)}, bf16[96,6656]{1,0:T(8,128)(2,1)S(1)}, u32[]{:S(2)}, u32[]{:S(2)}) collective-permute-start(bf16[96,6656]{1,0:T(8,128)(2,1)} %collective-permute-done.1.refs_2_), channel_id=1, source_target_pairs={{1,0},{2,3},{5,4},{6,7},{9,8},{10,11},{13,12},{14,15},{17,16},{18,... | collective-permute-start | bytes 3833864 | tf_op jit(solution)/shard_map/ppermute | solution.py:68
  73.7 31.7 %all-to-all-start = ((bf16[8,112,512]{2,1,0:T(8,128)(2,1)}), bf16[8,112,512]{2,1,0:T(8,128)(2,1)}, u32[]{:S(2)}, u32[]{:S(2)}) async-start(bf16[8,112,512]{2,1,0:T(8,128)(2,1)} %bitcast_dynamic-update-slice_fusion), calls=%async_computation | async-start | bytes 1835008 | tf_op jit(solution)/shard_map/all_to_all | solution.py:323
  80.3 6.6 %collective-permute-start.9 = (bf16[140,256]{1,0:T(8,128)(2,1)S(1)}, bf16[140,256]{1,0:T(8,128)(2,1)S(1)}, u32[]{:S(2)}, u32[]{:S(2)}) collective-permute-start(bf16[140,256]{1,0:T(8,128)(2,1)S(1)} %pad_maximum_fusion.13), channel_id=1, source_target_pairs={{0,3},{1,2},{2,1},{3,0},{4,7},{5,6},{6,5},{7,4},{8,11},{9,10},{10,... | collective-permute-start | bytes 215048 | tf_op jit(solution)/shard_map/ppermute | solution.py:36
  83.6 21.8 %collective-permute-start.8 = (bf16[140,256]{1,0:T(8,128)(2,1)S(1)}, bf16[140,256]{1,0:T(8,128)(2,1)}, u32[]{:S(2)}, u32[]{:S(2)}) collective-permute-start(bf16[140,256]{1,0:T(8,128)(2,1)S(1)} %pad_maximum_fusion.13), channel_id=1, source_target_pairs={{0,2},{1,3},{2,0},{3,1},{4,6},{5,7},{6,4},{7,5},{8,10},{9,11},{10,... | collective-permute-start | bytes 215048 | tf_op jit(solution)/shard_map/ppermute | solution.py:36
  85.0 20.4 %collective-permute-start.7 = (bf16[140,256]{1,0:T(8,128)(2,1)S(1)}, bf16[140,256]{1,0:T(8,128)(2,1)}, u32[]{:S(2)}, u32[]{:S(2)}) collective-permute-start(bf16[140,256]{1,0:T(8,128)(2,1)S(1)} %pad_maximum_fusion.13), channel_id=1, source_target_pairs={{0,1},{1,0},{2,3},{3,2},{4,5},{5,4},{6,7},{7,6},{8,9},{9,8},{10,11... | collective-permute-start | bytes 215048 | tf_op jit(solution)/shard_map/ppermute | solution.py:36
  86.7 60.1 %copy-start.3 = (bf16[2,32,6656]{2,1,0:T(8,128)(2,1)}, bf16[2,32,6656]{2,1,0:T(8,128)(2,1)S(1)}, u32[]{:S(2)}) copy-start(bf16[2,32,6656]{2,1,0:T(8,128)(2,1)S(1)} %slice.337) | copy-start | bytes 2555908
  105.4 38.8 %collective-permute-start.11 = (bf16[64,6656]{1,0:T(8,128)(2,1)S(1)}, bf16[64,6656]{1,0:T(8,128)(2,1)}, u32[]{:S(2)}, u32[]{:S(2)}) collective-permute-start(bf16[64,6656]{1,0:T(8,128)(2,1)S(1)} %bitcast.170), channel_id=1, source_target_pairs={{0,2},{1,3},{2,0},{3,1},{4,6},{5,7},{6,4},{7,5},{8,10},{9,11},{10,... | collective-permute-start | bytes 2555912 | tf_op jit(solution)/shard_map/ppermute | solution.py:36
  106.0 38.2 %collective-permute-start.10 = (bf16[64,6656]{1,0:T(8,128)(2,1)S(1)}, bf16[64,6656]{1,0:T(8,128)(2,1)}, u32[]{:S(2)}, u32[]{:S(2)}) collective-permute-start(bf16[64,6656]{1,0:T(8,128)(2,1)S(1)} %bitcast.171), channel_id=1, source_target_pairs={{0,1},{1,0},{2,3},{3,2},{4,5},{5,4},{6,7},{7,6},{8,9},{9,8},{10,11... | collective-permute-start | bytes 2555912 | tf_op jit(solution)/shard_map/ppermute | solution.py:36
  112.9 31.3 %collective-permute-start.12 = (bf16[1,224,256]{2,1,0:T(8,128)(2,1)S(1)}, bf16[1,224,256]{2,1,0:T(8,128)(2,1)}, u32[]{:S(2)}, u32[]{:S(2)}) collective-permute-start(bf16[1,224,256]{2,1,0:T(8,128)(2,1)S(1)} %maximum_bitcast_fusion), channel_id=1, source_target_pairs={{0,4},{4,0},{8,12},{12,8},{16,20},{20,16},{24,28},{28,24},{1,5},{5... | collective-permute-start | bytes 344072 | tf_op jit(solution)/shard_map/ppermute | solution.py:36
  145.2 8.1 %collective-permute-start.15 = (bf16[2,224,256]{2,1,0:T(8,128)(2,1)S(1)}, bf16[2,224,256]{2,1,0:T(8,128)(2,1)S(1)}, u32[]{:S(2)}, u32[]{:S(2)}) collective-permute-start(bf16[2,224,256]{2,1,0:T(8,128)(2,1)S(1)} %pad_maximum_fusion.12), channel_id=1, source_target_pairs={{0,8},{4,12},{8,0},{12,4},{16,24},{20,28},{24,16},{28,20},{1,9},{5... | collective-permute-start | bytes 688136 | tf_op jit(solution)/shard_map/ppermute | solution.py:36
  146.8 18.9 %collective-permute-start.13 = (bf16[64,6656]{1,0:T(8,128)(2,1)S(1)}, bf16[64,6656]{1,0:T(8,128)(2,1)S(1)}, u32[]{:S(2)}, u32[]{:S(2)}) collective-permute-start(bf16[64,6656]{1,0:T(8,128)(2,1)S(1)} %bitcast.172), channel_id=1, source_target_pairs={{1,2},{2,1},{5,6},{6,5},{9,10},{10,9},{13,14},{14,13},{17,18},{18,... | collective-permute-start | bytes 2555912 | tf_op jit(solution)/shard_map/ppermute | solution.py:67
  147.5 23.2 %collective-permute-start.14 = (bf16[64,6656]{1,0:T(8,128)(2,1)}, bf16[64,6656]{1,0:T(8,128)(2,1)S(1)}, u32[]{:S(2)}, u32[]{:S(2)}) collective-permute-start(bf16[64,6656]{1,0:T(8,128)(2,1)} %collective-permute-done.11.refs_2_), channel_id=1, source_target_pairs={{1,0},{2,3},{5,4},{6,7},{9,8},{10,11},{13,12},{14,15},{17,16},{18,... | collective-permute-start | bytes 2555912 | tf_op jit(solution)/shard_map/ppermute | solution.py:68
  149.1 16.5 %collective-permute-start.18 = (bf16[4,48,2048]{2,1,0:T(8,128)(2,1)S(1)}, bf16[4,48,2048]{2,1,0:T(8,128)(2,1)S(1)}, u32[]{:S(2)}, u32[]{:S(2)}) collective-permute-start(bf16[4,48,2048]{2,1,0:T(8,128)(2,1)S(1)} %get-tuple-element.263), channel_id=1, source_target_pairs={{0,4},{4,0},{8,12},{12,8},{16,20},{20,16},{24,28},{28,24},{1,5},{5... | collective-permute-start | bytes 2359304 | tf_op jit(solution)/shard_map/ppermute | solution.py:36
  149.4 16.2 %collective-permute-start.17 = (bf16[4,48,2048]{2,1,0:T(8,128)(2,1)S(1)}, bf16[4,48,2048]{2,1,0:T(8,128)(2,1)S(1)}, u32[]{:S(2)}, u32[]{:S(2)}) collective-permute-start(bf16[4,48,2048]{2,1,0:T(8,128)(2,1)S(1)} %get-tuple-element.264), channel_id=1, source_target_pairs={{0,4},{4,0},{8,12},{12,8},{16,20},{20,16},{24,28},{28,24},{1,5},{5... | collective-permute-start | bytes 2359304 | tf_op jit(solution)/shard_map/ppermute | solution.py:36
  153.4 18.8 %copy-start.8 = (bf16[4,224,256]{2,1,0:T(8,128)(2,1)}, bf16[4,224,256]{2,1,0:T(8,128)(2,1)S(1)}, u32[]{:S(2)}) copy-start(bf16[4,224,256]{2,1,0:T(8,128)(2,1)S(1)} %pad_maximum_fusion.4) | copy-start | bytes 1376260
  153.4 12.2 %collective-permute-start.16 = (bf16[4,224,256]{2,1,0:T(8,128)(2,1)S(1)}, bf16[4,224,256]{2,1,0:T(8,128)(2,1)S(1)}, u32[]{:S(2)}, u32[]{:S(2)}) collective-permute-start(bf16[4,224,256]{2,1,0:T(8,128)(2,1)S(1)} %pad_maximum_fusion.4), channel_id=1, source_target_pairs={{0,16},{4,20},{8,24},{12,28},{16,0},{20,4},{24,8},{28,12},{1,17},{... | collective-permute-start | bytes 1376264 | tf_op jit(solution)/shard_map/ppermute | solution.py:36
  172.2 29.5 %collective-permute-start.21 = (bf16[2,48,2048]{2,1,0:T(8,128)(2,1)S(1)}, bf16[2,48,2048]{2,1,0:T(8,128)(2,1)S(1)}, u32[]{:S(2)}, u32[]{:S(2)}) collective-permute-start(bf16[2,48,2048]{2,1,0:T(8,128)(2,1)S(1)} %pad_maximum_fusion.5), channel_id=1, source_target_pairs={{0,8},{4,12},{8,0},{12,4},{16,24},{20,28},{24,16},{28,20},{1,9},{5... | collective-permute-start | bytes 1179656 | tf_op jit(solution)/shard_map/ppermute | solution.py:36
  172.9 28.9 %collective-permute-start.22 = (bf16[2,48,2048]{2,1,0:T(8,128)(2,1)S(1)}, bf16[2,48,2048]{2,1,0:T(8,128)(2,1)S(1)}, u32[]{:S(2)}, u32[]{:S(2)}) collective-permute-start(bf16[2,48,2048]{2,1,0:T(8,128)(2,1)S(1)} %pad_maximum_fusion.6), channel_id=1, source_target_pairs={{0,16},{4,20},{8,24},{12,28},{16,0},{20,4},{24,8},{28,12},{1,17},{... | collective-permute-start | bytes 1179656 | tf_op jit(solution)/shard_map/ppermute | solution.py:36
  174.5 38.2 %collective-permute-start.20 = (bf16[64,6656]{1,0:T(8,128)(2,1)}, bf16[64,6656]{1,0:T(8,128)(2,1)}, u32[]{:S(2)}, u32[]{:S(2)}) collective-permute-start(bf16[64,6656]{1,0:T(8,128)(2,1)} %bitcast.31.refs_0_), channel_id=1, source_target_pairs={{0,2},{1,3},{2,0},{3,1},{4,6},{5,7},{6,4},{7,5},{8,10},{9,11},{10,... | collective-permute-start | bytes 2555912 | tf_op jit(solution)/shard_map/ppermute | solution.py:36
  174.5 38.2 %collective-permute-start.19 = (bf16[64,6656]{1,0:T(8,128)(2,1)}, bf16[64,6656]{1,0:T(8,128)(2,1)}, u32[]{:S(2)}, u32[]{:S(2)}) collective-permute-start(bf16[64,6656]{1,0:T(8,128)(2,1)} %bitcast.31.refs_0_), channel_id=1, source_target_pairs={{0,1},{1,0},{2,3},{3,2},{4,5},{5,4},{6,7},{7,6},{8,9},{9,8},{10,11... | collective-permute-start | bytes 2555912 | tf_op jit(solution)/shard_map/ppermute | solution.py:36
  203.0 9.6 %collective-permute-start.24 = (bf16[4,32,2048]{2,1,0:T(8,128)(2,1)}, bf16[4,32,2048]{2,1,0:T(8,128)(2,1)}, u32[]{:S(2)}, u32[]{:S(2)}) collective-permute-start(bf16[4,32,2048]{2,1,0:T(8,128)(2,1)} %get-tuple-element.269), channel_id=1, source_target_pairs={{0,4},{4,0},{8,12},{12,8},{16,20},{20,16},{24,28},{28,24},{1,5},{5... | collective-permute-start | bytes 1572872 | tf_op jit(solution)/shard_map/ppermute | solution.py:36
  203.0 9.6 %collective-permute-start.23 = (bf16[4,32,2048]{2,1,0:T(8,128)(2,1)}, bf16[4,32,2048]{2,1,0:T(8,128)(2,1)}, u32[]{:S(2)}, u32[]{:S(2)}) collective-permute-start(bf16[4,32,2048]{2,1,0:T(8,128)(2,1)} %get-tuple-element.270), channel_id=1, source_target_pairs={{0,4},{4,0},{8,12},{12,8},{16,20},{20,16},{24,28},{28,24},{1,5},{5... | collective-permute-start | bytes 1572872 | tf_op jit(solution)/shard_map/ppermute | solution.py:36
  219.7 16.1 %collective-permute-start.27 = (bf16[512,256]{1,0:T(8,128)(2,1)S(1)}, bf16[512,256]{1,0:T(8,128)(2,1)S(1)}, u32[]{:S(2)}, u32[]{:S(2)}) collective-permute-start(bf16[512,256]{1,0:T(8,128)(2,1)S(1)} %fusion), channel_id=1, source_target_pairs={{0,16},{4,20},{8,24},{12,28},{16,0},{20,4},{24,8},{28,12},{1,17},{... | collective-permute-start | bytes 786440 | tf_op jit(solution)/shard_map/ppermute | solution.py:36
  221.5 10.8 %collective-permute-start.28 = (bf16[1,48,2048]{2,1,0:T(8,128)(2,1)S(1)}, bf16[1,48,2048]{2,1,0:T(8,128)(2,1)S(1)}, u32[]{:S(2)}, u32[]{:S(2)}) collective-permute-start(bf16[1,48,2048]{2,1,0:T(8,128)(2,1)S(1)} %get-tuple-element.289), channel_id=1, source_target_pairs={{0,16},{4,20},{8,24},{12,28},{16,0},{20,4},{24,8},{28,12},{1,17},{... | collective-permute-start | bytes 589832 | tf_op jit(solution)/shard_map/ppermute | solution.py:36
  223.1 11.2 %copy-start.7 = (bf16[4096,256]{1,0:T(8,128)(2,1)S(1)}, bf16[4096,256]{1,0:T(8,128)(2,1)}, u32[]{:S(2)}) copy-start(bf16[4096,256]{1,0:T(8,128)(2,1)} %param.8) | copy-start | bytes 6291460
  223.1 10.7 %collective-permute-start.29 = (bf16[1,48,2048]{2,1,0:T(8,128)(2,1)S(1)}, bf16[1,48,2048]{2,1,0:T(8,128)(2,1)S(1)}, u32[]{:S(2)}, u32[]{:S(2)}) collective-permute-start(bf16[1,48,2048]{2,1,0:T(8,128)(2,1)S(1)} %get-tuple-element.287), channel_id=1, source_target_pairs={{0,8},{4,12},{8,0},{12,4},{16,24},{20,28},{24,16},{28,20},{1,9},{5... | collective-permute-start | bytes 589832 | tf_op jit(solution)/shard_map/ppermute | solution.py:36
  224.7 16.2 %collective-permute-start.25 = (bf16[64,6656]{1,0:T(8,128)(2,1)}, bf16[64,6656]{1,0:T(8,128)(2,1)S(1)}, u32[]{:S(2)}, u32[]{:S(2)}) collective-permute-start(bf16[64,6656]{1,0:T(8,128)(2,1)} %bitcast.31.refs_0_), channel_id=1, source_target_pairs={{1,2},{2,1},{5,6},{6,5},{9,10},{10,9},{13,14},{14,13},{17,18},{18,... | collective-permute-start | bytes 2555912 | tf_op jit(solution)/shard_map/ppermute | solution.py:67
  225.4 22.1 %collective-permute-start.26 = (bf16[64,6656]{1,0:T(8,128)(2,1)}, bf16[64,6656]{1,0:T(8,128)(2,1)S(1)}, u32[]{:S(2)}, u32[]{:S(2)}) collective-permute-start(bf16[64,6656]{1,0:T(8,128)(2,1)} %collective-permute-done.20.refs_2_), channel_id=1, source_target_pairs={{1,0},{2,3},{5,4},{6,7},{9,8},{10,11},{13,12},{14,15},{17,16},{18,... | collective-permute-start | bytes 2555912 | tf_op jit(solution)/shard_map/ppermute | solution.py:68
  232.2 7.4 %collective-permute-start.30 = (bf16[2,32,2048]{2,1,0:T(8,128)(2,1)S(1)}, bf16[2,32,2048]{2,1,0:T(8,128)(2,1)S(1)}, u32[]{:S(2)}, u32[]{:S(2)}) collective-permute-start(bf16[2,32,2048]{2,1,0:T(8,128)(2,1)S(1)} %pad_maximum_fusion.8), channel_id=1, source_target_pairs={{0,8},{4,12},{8,0},{12,4},{16,24},{20,28},{24,16},{28,20},{1,9},{5... | collective-permute-start | bytes 786440 | tf_op jit(solution)/shard_map/ppermute | solution.py:36
  233.8 7.1 %collective-permute-start.31 = (bf16[2,32,2048]{2,1,0:T(8,128)(2,1)S(1)}, bf16[2,32,2048]{2,1,0:T(8,128)(2,1)S(1)}, u32[]{:S(2)}, u32[]{:S(2)}) collective-permute-start(bf16[2,32,2048]{2,1,0:T(8,128)(2,1)S(1)} %pad_maximum_fusion.9), channel_id=1, source_target_pairs={{0,16},{4,20},{8,24},{12,28},{16,0},{20,4},{24,8},{28,12},{1,17},{... | collective-permute-start | bytes 786440 | tf_op jit(solution)/shard_map/ppermute | solution.py:36
  247.6 27.6 %collective-permute-start.33 = (bf16[1,32,2048]{2,1,0:T(8,128)(2,1)S(1)}, bf16[1,32,2048]{2,1,0:T(8,128)(2,1)S(1)}, u32[]{:S(2)}, u32[]{:S(2)}) collective-permute-start(bf16[1,32,2048]{2,1,0:T(8,128)(2,1)S(1)} %get-tuple-element.293), channel_id=1, source_target_pairs={{0,16},{4,20},{8,24},{12,28},{16,0},{20,4},{24,8},{28,12},{1,17},{... | collective-permute-start | bytes 393224 | tf_op jit(solution)/shard_map/ppermute | solution.py:36
  248.3 26.8 %collective-permute-start.32 = (bf16[1024,256]{1,0:T(8,128)(2,1)S(1)}, bf16[1024,256]{1,0:T(8,128)(2,1)S(1)}, u32[]{:S(2)}, u32[]{:S(2)}) collective-permute-start(bf16[1024,256]{1,0:T(8,128)(2,1)S(1)} %pad_maximum_fusion.2), channel_id=1, source_target_pairs={{0,8},{4,12},{8,0},{12,4},{16,24},{20,28},{24,16},{28,20},{1,9},{5... | collective-permute-start | bytes 1572872 | tf_op jit(solution)/shard_map/ppermute | solution.py:36
  249.1 26.0 %collective-permute-start.34 = (bf16[1,32,2048]{2,1,0:T(8,128)(2,1)S(1)}, bf16[1,32,2048]{2,1,0:T(8,128)(2,1)S(1)}, u32[]{:S(2)}, u32[]{:S(2)}) collective-permute-start(bf16[1,32,2048]{2,1,0:T(8,128)(2,1)S(1)} %get-tuple-element.291), channel_id=1, source_target_pairs={{0,8},{4,12},{8,0},{12,4},{16,24},{20,28},{24,16},{28,20},{1,9},{5... | collective-permute-start | bytes 393224 | tf_op jit(solution)/shard_map/ppermute | solution.py:36
  250.5 25.8 %slice-start = ((s8[5111808]{0:T(1024)(128)(4,1)}), s8[4194304]{0:T(1024)(128)(4,1)S(1)}, s32[]{:S(2)}) async-start(s8[5111808]{0:T(1024)(128)(4,1)} %bitcast.168), calls=%async_computation.1 | async-start | bytes 8388608
  250.6 25.7 %slice-start.1 = ((s8[5111808]{0:T(1024)(128)(4,1)}), s8[917504]{0:T(1024)(128)(4,1)S(1)}, s32[]{:S(2)}) async-start(s8[5111808]{0:T(1024)(128)(4,1)} %bitcast.168), calls=%async_computation.2 | async-start | bytes 1835008
  275.2 4.6 %collective-permute-start.36 = (bf16[4,32,2048]{2,1,0:T(8,128)(2,1)S(1)}, bf16[4,32,2048]{2,1,0:T(8,128)(2,1)S(1)}, u32[]{:S(2)}, u32[]{:S(2)}) collective-permute-start(bf16[4,32,2048]{2,1,0:T(8,128)(2,1)S(1)} %get-tuple-element.267), channel_id=1, source_target_pairs={{0,4},{4,0},{8,12},{12,8},{16,20},{20,16},{24,28},{28,24},{1,5},{5... | collective-permute-start | bytes 1572872 | tf_op jit(solution)/shard_map/ppermute | solution.py:36
  275.3 4.5 %collective-permute-start.35 = (bf16[4,32,2048]{2,1,0:T(8,128)(2,1)S(1)}, bf16[4,32,2048]{2,1,0:T(8,128)(2,1)S(1)}, u32[]{:S(2)}, u32[]{:S(2)}) collective-permute-start(bf16[4,32,2048]{2,1,0:T(8,128)(2,1)S(1)} %get-tuple-element.268), channel_id=1, source_target_pairs={{0,4},{4,0},{8,12},{12,8},{16,20},{20,16},{24,28},{28,24},{1,5},{5... | collective-permute-start | bytes 1572872 | tf_op jit(solution)/shard_map/ppermute | solution.py:36
  276.0 10.9 %collective-permute-start.39 = (bf16[2048,256]{1,0:T(8,128)(2,1)S(1)}, bf16[2048,256]{1,0:T(8,128)(2,1)S(1)}, u32[]{:S(2)}, u32[]{:S(2)}) collective-permute-start(bf16[2048,256]{1,0:T(8,128)(2,1)S(1)} %pad_maximum_fusion), channel_id=1, source_target_pairs={{0,4},{4,0},{8,12},{12,8},{16,20},{20,16},{24,28},{28,24},{1,5},{5... | collective-permute-start | bytes 3145736 | tf_op jit(solution)/shard_map/ppermute | solution.py:36
  280.2 9.4 %collective-permute-start.37 = (bf16[2,32,2048]{2,1,0:T(8,128)(2,1)S(1)}, bf16[2,32,2048]{2,1,0:T(8,128)(2,1)S(1)}, u32[]{:S(2)}, u32[]{:S(2)}) collective-permute-start(bf16[2,32,2048]{2,1,0:T(8,128)(2,1)S(1)} %pad_maximum_fusion.10), channel_id=1, source_target_pairs={{0,8},{4,12},{8,0},{12,4},{16,24},{20,28},{24,16},{28,20},{1,9},{5... | collective-permute-start | bytes 786440 | tf_op jit(solution)/shard_map/ppermute | solution.py:36
  281.0 8.7 %collective-permute-start.38 = (bf16[2,32,2048]{2,1,0:T(8,128)(2,1)S(1)}, bf16[2,32,2048]{2,1,0:T(8,128)(2,1)S(1)}, u32[]{:S(2)}, u32[]{:S(2)}) collective-permute-start(bf16[2,32,2048]{2,1,0:T(8,128)(2,1)S(1)} %pad_maximum_fusion.11), channel_id=1, source_target_pairs={{0,16},{4,20},{8,24},{12,28},{16,0},{20,4},{24,8},{28,12},{1,17},{... | collective-permute-start | bytes 786440 | tf_op jit(solution)/shard_map/ppermute | solution.py:36
  289.7 5.1 %collective-permute-start.41 = (bf16[1,32,2048]{2,1,0:T(8,128)(2,1)S(1)}, bf16[1,32,2048]{2,1,0:T(8,128)(2,1)S(1)}, u32[]{:S(2)}, u32[]{:S(2)}) collective-permute-start(bf16[1,32,2048]{2,1,0:T(8,128)(2,1)S(1)} %fusion.17), channel_id=1, source_target_pairs={{0,8},{4,12},{8,0},{12,4},{16,24},{20,28},{24,16},{28,20},{1,9},{5... | collective-permute-start | bytes 393224 | tf_op jit(solution)/shard_map/ppermute | solution.py:36
  294.0 5.0 %collective-permute-start.40 = (bf16[1,32,2048]{2,1,0:T(8,128)(2,1)S(1)}, bf16[1,32,2048]{2,1,0:T(8,128)(2,1)S(1)}, u32[]{:S(2)}, u32[]{:S(2)}) collective-permute-start(bf16[1,32,2048]{2,1,0:T(8,128)(2,1)S(1)} %fusion.16), channel_id=1, source_target_pairs={{0,16},{4,20},{8,24},{12,28},{16,0},{20,4},{24,8},{28,12},{1,17},{... | collective-permute-start | bytes 393224 | tf_op jit(solution)/shard_map/ppermute | solution.py:36
  (15 other events, 54.9 us)
